TPU v7x, 256 devices: a whole 4x4x8 slice. The times are simulated.
256 devices in a mesh: head: 16 (over y, x_lo, core), key: 16 (over x_hi, z).
Axes of the slice: x: 4 (x_hi: 2, x_lo: 2; x = x_hi * 2 + x_lo), y: 4, z: 8, core: 2. Of those that a mesh axis runs over, the one named last changes fastest.
Arguments:
- queries: bfloat16 [128, 128, 192], P(None, 'head'), may hold values from -16 to 16
- w_uk: bfloat16 [128, 128, 512], P('head'), may hold values from -0.5 to 0.5
- w_uv: bfloat16 [128, 512, 128], P('head'), may hold values from -0.25 to 0.25
- latent: bfloat16 [32768, 576], P('key'), may hold values from -5 to 5
- out_grad: bfloat16 [128, 128, 128], P(None, 'head'), may hold values from -6 to 6
- offsets: int32 [128], replicated, may hold values from 8192 to 32767, as said below
Outputs:
- d_queries: bfloat16 [128, 128, 192], P('key', 'head')
- d_latent: bfloat16 [32768, 576], P('key')
Inputs may be any that keep to these rules, and one draw needn't show every extreme that they name: Row r sees keys 0 to offsets[r].
All inputs are finite; a program needn't handle non-finite values.
Results may differ from a plain program's by a relative error of at most 0.0079.
Values may be sent and summed in bfloat16 or wider, within the bound.
No kernel may reach another device: no remote copies, remote signals or barrier semaphores. Data moves between devices by JAX's collectives and lax.ppermute only.
A program may use at most 128 MiB of HBM per device.

v0:
```python
import math

import jax
import jax.numpy as jnp
from jax import lax
from jax.sharding import PartitionSpec as P

floor_score = -1e30


def sent_to_all(value, axis):
    count = lax.axis_size(axis)
    return lax.all_to_all(
        jnp.broadcast_to(value[None], (count, *value.shape)), axis, 0, 0, tiled=True
    )


def gathered_once(value, axis):
    leaves = jax.tree.leaves(value)
    turns = sorted(range(len(leaves)), key=lambda k: -leaves[k].size)
    width = (1, *leaves[turns[0]].shape)[-1]
    lines = [
        jnp.pad(leaves[k].reshape(-1), (0, -leaves[k].size % width)).reshape(-1, width)
        for k in turns
    ]
    both, at, found = (sent_to_all(jnp.concatenate(lines), axis), 0, {})
    for k, line in zip(turns, lines):
        slab = both[:, at : at + len(line)].reshape(len(both), -1)
        found[k] = slab[:, : leaves[k].size].reshape(-1, *leaves[k].shape)
        at += len(line)
    numbers = iter(range(len(leaves)))
    return jax.tree.map(lambda _: found[next(numbers)], value)


def joined_by_halves(pieces, combine):
    while len(jax.tree.leaves(pieces)[0]) > 1:
        pieces = jax.vmap(combine)(
            *(jax.tree.map(lambda part: part[side::2], pieces) for side in (0, 1))
        )
    return jax.tree.map(lambda part: part[0], pieces)


def combined_all(value, axis, combine):
    pieces = gathered_once(value, axis)
    return joined_by_halves(pieces, combine)


def over_copies(value, axis):
    return sent_to_all(value, axis).sum(axis=0)


def cut_along(value, dim, count):
    before, after = (value.shape[:dim], value.shape[dim + 1 :])
    return jnp.moveaxis(value.reshape(*before, count, -1, *after), dim, 0)


def summed_on_arrival(value, axis, dim):
    blocks = cut_along(value, dim, lax.axis_size(axis))
    arrived = lax.all_to_all(blocks, axis, split_axis=0, concat_axis=0, tiled=True)
    return arrived.sum(axis=0)


def combine_norms(earlier, later):
    top = jnp.maximum(earlier[0], later[0])
    total = earlier[1] * jnp.exp(earlier[0] - top) + later[1] * jnp.exp(later[0] - top)
    return (top, total)


def shards(queries, w_uk, w_uv, latent, out_grad, offsets):
    rows, heads, width = queries.shape
    keys = latent.shape[0]
    nope_width = w_uk.shape[1]
    lat_width = w_uk.shape[2]
    scale = 1.0 / math.sqrt(width)
    q_lat = jnp.einsum(
        "rhd,hdc->rhc", queries[:, :, :nope_width], w_uk, preferred_element_type=jnp.float32
    ).astype(jnp.bfloat16)
    q_cat = jnp.concatenate([q_lat, queries[:, :, nope_width:]], axis=2)
    d_lat = jnp.einsum("rhe,hce->rhc", out_grad, w_uv, preferred_element_type=jnp.float32).astype(
        jnp.bfloat16
    )
    scores = jnp.einsum("rhc,kc->hrk", q_cat, latent, preferred_element_type=jnp.float32) * scale
    position = lax.axis_index("key") * keys + jnp.arange(keys, dtype=jnp.int32)
    visible = (position[None, :] <= offsets[:, None])[None]
    masked = jnp.where(visible, scores, floor_score)
    local_top = jnp.max(masked, axis=2)
    local_total = jnp.sum(jnp.where(visible, jnp.exp(masked - local_top[..., None]), 0.0), axis=2)
    top, total = combined_all((local_top, local_total), "key", combine_norms)
    log_norm = top + jnp.log(total)
    probs = jnp.where(visible, jnp.exp(masked - log_norm[..., None]), 0.0)
    d_probs = jnp.einsum(
        "rhc,kc->hrk", d_lat, latent[:, :lat_width], preferred_element_type=jnp.float32
    )
    delta = over_copies(jnp.sum(probs * d_probs, axis=2), "key")
    d_scores = (probs * (d_probs - delta[..., None])).astype(jnp.bfloat16)
    probs_b = probs.astype(jnp.bfloat16)
    up_key = w_uk.astype(jnp.float32)
    part_sum = (
        jnp.einsum("hrk,kc->rhc", d_scores, latent, preferred_element_type=jnp.float32) * scale
    )
    nope = jnp.einsum(
        "rhc,hdc->rhd", part_sum[..., :lat_width], up_key, precision=lax.Precision.HIGHEST
    )
    dq_sum = summed_on_arrival(jnp.concatenate([nope, part_sum[..., lat_width:]], axis=2), "key", 0)
    d_queries = dq_sum.astype(jnp.bfloat16)
    from_scores = (
        jnp.einsum("hrk,rhc->kc", d_scores, q_cat, preferred_element_type=jnp.float32) * scale
    )
    from_values = jnp.einsum("hrk,rhc->kc", probs_b, d_lat, preferred_element_type=jnp.float32)
    d_latent = lax.psum(
        jnp.concatenate(
            [from_scores[:, :lat_width] + from_values, from_scores[:, lat_width:]], axis=1
        ),
        "head",
    ).astype(jnp.bfloat16)
    return (d_queries, d_latent)


def solution(mesh):
    return jax.shard_map(
        shards,
        mesh=mesh,
        in_specs=(
            P(None, "head", None),
            P("head", None, None),
            P("head", None, None),
            P("key", None),
            P(None, "head", None),
            P(),
        ),
        out_specs=(P("key", "head", None), P("key", None)),
        check_vma=False,
    )
```

profile of v0, /device:TPU:1, one launch (start us, length us, event | category | flops | bytes accessed | tf_op | source)
XLA Modules:
  0.0 201.7 jit_solution(5365242685537185271)
XLA Ops:
  0.6 0.0 copy-start
  0.7 1.0 slice.80
  1.7 0.3 copy-done
  1.9 0.0 copy-start.5
  1.9 1.5 fusion.24
  3.4 0.9 broadcast_compare_fusion
  4.3 0.0 copy-done.5
  4.3 5.8 %bitcast_reduce_fusion = (f32[8,128]{1,0:T(8,128)S(1)}, f32[128,8,2048]{2,0,1:T(8,128)S(1)}) fusion(pred[128,2048]{1,0:T(8,128)(4,1)S(1)} %broadcast_compare_fusion, bf16[2048,576]{0,1:T(8,128)(2,1)} %param.9, bf16[128,8,64]{0,2,1:T(8,128)(2,1)S(1)} %slice.80, bf16[128,8,512]{0,2,1:T(8,128)(2,1)S(1)} %fusion.24), kind=kOutput, calls=%fused_computation.7 | convolution fusion | flops 2424568832 | bytes 12193792 | tf_op jit(solution)/shard_map/rhc,kc->hrk/dot_general | solution.py:82
  10.2 0.0 copy-start.1
  10.2 0.0 copy-start.3
  10.2 3.2 %copy-done.1 = f32[128,8,2048]{2,0,1:T(8,128)} copy-done((f32[128,8,2048]{2,0,1:T(8,128)}, f32[128,8,2048]{2,0,1:T(8,128)S(1)}, u32[]{:S(2)}) %copy-start.1) | copy-done | bytes 8388632
  13.4 2.5 %fusion.5 = f32[8,128]{1,0:T(8,128)S(1)} fusion(f32[128,8,2048]{2,0,1:T(8,128)S(1)} %get-tuple-element.11, f32[8,128]{1,0:T(8,128)S(1)} %get-tuple-element.10, pred[128,2048]{1,0:T(8,128)(4,1)S(1)} %broadcast_compare_fusion), kind=kLoop, calls=%fused_computation.10 | loop fusion | flops 10484736 | bytes 8658944 | tf_op jit(solution)/shard_map/reduce_sum | solution.py:87
  15.9 0.7 broadcast_in_dim.46
  16.5 11.6 %all-to-all-start = ((f32[16,16,128]{2,1,0:T(8,128)}), f32[16,16,128]{2,1,0:T(8,128)S(1)}, u32[]{:S(2)}, u32[]{:S(2)}) async-start(f32[16,16,128]{2,1,0:T(8,128)} %broadcast_in_dim.46), calls=%async_computation | async-start | bytes 262144 | tf_op jit(solution)/shard_map/all_to_all | solution.py:13
  28.1 0.0 copy-done.3
  28.1 2.4 %fusion.25 = bf16[128,8,512]{0,2,1:T(8,128)(2,1)} fusion(bf16[8,512,128]{2,1,0:T(8,128)(2,1)S(1)} %copy-done.3, bf16[128,8,128]{2,1,0:T(8,128)(2,1)} %param.10), kind=kOutput, calls=%fused_computation.32 | convolution fusion | flops 134742016 | bytes 2359296 | tf_op jit(solution)/shard_map/rhe,hce->rhc/dot_general | solution.py:79
  30.5 6.6 %all-to-all-done = f32[16,16,128]{2,1,0:T(8,128)S(1)} async-done(((f32[16,16,128]{2,1,0:T(8,128)}), f32[16,16,128]{2,1,0:T(8,128)S(1)}, u32[]{:S(2)}, u32[]{:S(2)}) %all-to-all-start) | async-done | bytes 131104 | tf_op jit(solution)/shard_map/all_to_all | solution.py:13
  37.3 12.0 %fusion = (f32[8,128]{1,0:T(8,128)S(1)}, f32[128,8,2048]{2,0,1:T(8,128)}) fusion(f32[8,128]{1,0:T(8,128)S(1)} %fusion.34, f32[128,8,2048]{2,0,1:T(8,128)} %copy-done.1, pred[128,2048]{1,0:T(8,128)(4,1)S(1)} %broadcast_compare_fusion, bf16[128,8,512]{0,2,1:T(8,128)(2,1)} %fusion.25, bf16[2048,576]{0,1:T(8,128)(2,1)} %param.9), kind=kOutput, calls=%fused_computation.2 | convolution fusion | flops 2160065536 | bytes 20455424 | tf_op jit(solution)/shard_map/rhc,kc->hrk/dot_general | solution.py:91
  49.2 12.0 %all_to_all.15 = f32[16,8,128]{2,1,0:T(8,128)S(1)} all-to-all(f32[16,8,128]{2,1,0:T(8,128)S(1)} %broadcast_in_dim.47), channel_id=1, replica_groups=mesh['head'=16,'key'=16] {'key'}, dimensions={0} | all-to-all | bytes 131072 | tf_op jit(solution)/shard_map/all_to_all | solution.py:13
  61.2 0.0 copy-start.7
  61.2 0.0 slice-start
  61.2 7.5 %fusion.2 = bf16[8,128,2048]{2,1,0:T(8,128)(2,1)S(1)} fusion(f32[128,8,2048]{2,0,1:T(8,128)} %get-tuple-element.13, f32[8,128]{1,0:T(8,128)S(1)} %reduce_sum.38, f32[8,128]{1,0:T(8,128)S(1)} %fusion.34, f32[128,8,2048]{2,0,1:T(8,128)} %copy-done.1, pred[128,2048]{1,0:T(8,128)(4,1)S(1)} %broadcast_compare_fusion), kind=kLoop, calls=%fused_computation.4 | loop fusion | flops 14680064 | bytes 21241856 | tf_op jit(solution)/shard_map/convert_element_type | solution.py:95
  68.7 0.0 copy-done.7
  68.7 0.0 copy-start.6
  68.8 0.0 slice-start.1
  68.8 2.6 %multiply_bitcast_fusion = f32[128,8,576]{0,2,1:T(8,128)S(1)} fusion(bf16[8,128,2048]{2,1,0:T(8,128)(2,1)S(1)} %fusion.2, bf16[2048,576]{0,1:T(8,128)(2,1)S(1)} %copy-done.7), kind=kOutput, calls=%fused_computation.23 | convolution fusion | flops 2416508928 | bytes 8912896 | tf_op jit(solution)/shard_map/hrk,kc->rhc/dot_general | solution.py:99
  71.4 0.0 copy-done.6
  71.4 0.0 copy-start.2
  71.4 0.0 copy-start.4
  71.5 2.7 %bitcast_multiply_fusion.1 = f32[2048,576]{0,1:T(8,128)S(1)} fusion(bf16[8,128,2048]{2,1,0:T(8,128)(2,1)S(1)} %fusion.2, bf16[128,8,64]{0,2,1:T(8,128)(2,1)S(1)} %copy-done.6, bf16[128,8,512]{0,2,1:T(8,128)(2,1)S(1)} %fusion.24), kind=kOutput, calls=%fused_computation.15 | convolution fusion | flops 2419458048 | bytes 10092544 | tf_op jit(solution)/shard_map/hrk,rhc->kc/dot_general | solution.py:107
  74.1 0.0 slice-done
  74.2 0.0 slice-done.1
  74.2 0.0 copy-done.4
  74.2 3.2 %slice_add_fusion = f32[2048,512]{0,1:T(8,128)S(1)} fusion(f32[2048,576]{0,1:T(8,128)S(1)} %bitcast_multiply_fusion.1, bf16[128,8,512]{0,2,1:T(8,128)(2,1)S(1)} %copy-done.4, f32[8,128]{1,0:T(8,128)S(1)} %fusion.34, f32[128,8,2048]{2,0,1:T(8,128)S(1)} %bitcast.70, pred[128,2048]{1,0:T(8,128)(4,1)S(1)} %broadcast_compare_fusion), kind=kOutput, calls=%fused_computation.16 | convolution fusion | flops 2159017984 | bytes 18354176 | tf_op jit(solution)/shard_map/hrk,rhc->kc/dot_general | solution.py:109
  77.4 0.0 copy-done.2
  77.5 1.3 fusion.26
  78.8 0.0 slice-start.2
  78.8 2.6 %pad_maximum_fusion = f32[2048,576]{0,1:T(8,128)} fusion(f32[2048,64]{0,1:T(8,128)S(1)} %slice.113, f32[2048,512]{0,1:T(8,128)S(1)} %slice_add_fusion), kind=kLoop, calls=%fused_computation.14 | loop fusion | flops 1179648 | bytes 9437184 | tf_op jit(solution)/shard_map/concatenate | solution.py:111
  81.4 0.0 slice-done.2
  81.4 0.1 pad_maximum_fusion.2
  81.5 1.4 copy.27
  82.9 3.7 %all-to-all-start.2 = ((f32[16,8,8,192]{3,2,1,0:T(8,128)}), f32[16,8,8,192]{3,2,1,0:T(8,128)S(1)}, u32[]{:S(2)}, u32[]{:S(2)}) async-start(f32[16,8,8,192]{3,2,1,0:T(8,128)} %bitcast.9), calls=%async_computation.2 | async-start | bytes 2097152 | tf_op jit(solution)/shard_map/all_to_all | solution.py:59
  86.6 114.4 %all-reduce.1 = bf16[2048,576]{0,1:T(8,128)(2,1)} all-reduce(f32[2048,576]{0,1:T(8,128)} %pad_maximum_fusion), channel_id=1, replica_groups=mesh['head'=16,'key'=16] {'head'}, use_global_device_ids=true, to_apply=%region_5.6 | all-reduce | flops 1179648 | bytes 7077888 | tf_op jit(solution)/shard_map/psum | solution.py:110
  201.0 0.0 all-to-all-done.2
  201.0 0.7 reduce_sum.39
  (11 shorter events, 0.1 us)
Async XLA Ops:
  0.6 1.3 copy-start
  1.9 2.4 %copy-start.5 = (bf16[128,8,64]{0,2,1:T(8,128)(2,1)}, bf16[128,8,64]{0,2,1:T(8,128)(2,1)S(1)}, u32[]{:S(2)}) copy-start(bf16[128,8,64]{0,2,1:T(8,128)(2,1)S(1)} %slice.80) | copy-start | bytes 393220
  10.2 3.2 %copy-start.1 = (f32[128,8,2048]{2,0,1:T(8,128)}, f32[128,8,2048]{2,0,1:T(8,128)S(1)}, u32[]{:S(2)}) copy-start(f32[128,8,2048]{2,0,1:T(8,128)S(1)} %get-tuple-element.11) | copy-start | bytes 25165828
  10.2 18.0 %copy-start.3 = (bf16[8,512,128]{2,1,0:T(8,128)(2,1)S(1)}, bf16[8,512,128]{2,1,0:T(8,128)(2,1)}, u32[]{:S(2)}) copy-start(bf16[8,512,128]{2,1,0:T(8,128)(2,1)} %param.8) | copy-start | bytes 3145732
  16.5 20.6 %all-to-all-start = ((f32[16,16,128]{2,1,0:T(8,128)}), f32[16,16,128]{2,1,0:T(8,128)S(1)}, u32[]{:S(2)}, u32[]{:S(2)}) async-start(f32[16,16,128]{2,1,0:T(8,128)} %broadcast_in_dim.46), calls=%async_computation | async-start | bytes 262144 | tf_op jit(solution)/shard_map/all_to_all | solution.py:13
  61.2 7.5 %copy-start.7 = (bf16[2048,576]{0,1:T(8,128)(2,1)S(1)}, bf16[2048,576]{0,1:T(8,128)(2,1)}, u32[]{:S(2)}) copy-start(bf16[2048,576]{0,1:T(8,128)(2,1)} %param.9) | copy-start | bytes 7077892
  61.2 12.9 %slice-start = ((s8[8388608]{0:T(1024)(128)(4,1)}), s8[4194304]{0:T(1024)(128)(4,1)S(1)}, s32[]{:S(2)}) async-start(s8[8388608]{0:T(1024)(128)(4,1)} %bitcast.69), calls=%async_computation.3 | async-start | bytes 8388608
  68.7 2.7 %copy-start.6 = (bf16[128,8,64]{0,2,1:T(8,128)(2,1)S(1)}, bf16[128,8,64]{0,2,1:T(8,128)(2,1)}, u32[]{:S(2)}) copy-start(bf16[128,8,64]{0,2,1:T(8,128)(2,1)} %copy-done.5) | copy-start | bytes 393220
  68.8 5.4 %slice-start.1 = ((s8[8388608]{0:T(1024)(128)(4,1)}), s8[4194304]{0:T(1024)(128)(4,1)S(1)}, s32[]{:S(2)}) async-start(s8[8388608]{0:T(1024)(128)(4,1)} %bitcast.69), calls=%async_computation.4 | async-start | bytes 8388608
  71.4 6.0 %copy-start.2 = (f32[128,8,576]{0,2,1:T(8,128)}, f32[128,8,576]{0,2,1:T(8,128)S(1)}, u32[]{:S(2)}) copy-start(f32[128,8,576]{0,2,1:T(8,128)S(1)} %multiply_bitcast_fusion) | copy-start | bytes 7077892
  71.4 2.7 %copy-start.4 = (bf16[128,8,512]{0,2,1:T(8,128)(2,1)S(1)}, bf16[128,8,512]{0,2,1:T(8,128)(2,1)}, u32[]{:S(2)}) copy-start(bf16[128,8,512]{0,2,1:T(8,128)(2,1)} %fusion.25) | copy-start | bytes 3145732
  78.8 2.6 %slice-start.2 = ((f32[128,8,576]{0,2,1:T(8,128)}), f32[128,8,64]{0,2,1:T(8,128)S(1)}, s32[]{:S(2)}) async-start(f32[128,8,576]{0,2,1:T(8,128)} %copy-done.2), calls=%async_computation.5 | async-start | bytes 524288 | tf_op jit(solution)/shard_map/slice | solution.py:104
  82.9 118.1 %all-to-all-start.2 = ((f32[16,8,8,192]{3,2,1,0:T(8,128)}), f32[16,8,8,192]{3,2,1,0:T(8,128)S(1)}, u32[]{:S(2)}, u32[]{:S(2)}) async-start(f32[16,8,8,192]{3,2,1,0:T(8,128)} %bitcast.9), calls=%async_computation.2 | async-start | bytes 2097152 | tf_op jit(solution)/shard_map/all_to_all | solution.py:59
where the time goes:
time: 205 us; the launch traced here: 202 us
  blocking collectives  126 us (61%)
  matrix products  31.5 us (15%)
  starting transfers between devices  15.2 us (7%)
  other arithmetic  14.3 us (7%)
  local copies, waits for them, and re-layouts  6.67 us (3%)
  waiting for transfers between devices  6.65 us (3%)
    psum x1, blocking collectives, shards(): lax.psum(jnp.concatenate([from_scores[:, :lat_width] + from_values, from_...  114 us
    all_to_all x1, blocking collectives, sent_to_all(): lax.all_to_all(jnp.broadcast_to(value[None], (count, *value.shape)), axis...  12 us
    dot_general x1, matrix products, shards(): jnp.einsum('rhc,kc->hrk', d_lat, latent[:, :lat_width], preferred_element...  12 us
    all_to_all x1, starting transfers between devices, sent_to_all(): lax.all_to_all(jnp.broadcast_to(value[None], (count, *value.shape)), axis...  11.6 us
    convert_element_type x1, other arithmetic, shards(): d_scores = (probs * (d_probs - delta[..., None])).astype(jnp.bfloat16)  7.51 us
    all_to_all x1, waiting for transfers between devices, sent_to_all(): lax.all_to_all(jnp.broadcast_to(value[None], (count, *value.shape)), axis...  6.65 us
    dot_general x1, matrix products, shards(): jnp.einsum('rhc,kc->hrk', q_cat, latent, preferred_element_type=jnp.float32)  5.83 us
  transfers between devices with their start and end apart: 2, of which 1 were waited for; matrix products, arithmetic and copies ran while one was open for 1% of the time, Pallas kernels for 0%

commit v1 on v0

v1 whole, which is shorter than its diff:
```python
import functools
import math

import jax
import jax.numpy as jnp
from jax import lax
from jax.experimental import pallas as pl
from jax.experimental.pallas import tpu as pltpu
from jax.sharding import PartitionSpec as P

bf16 = jnp.bfloat16
f32 = jnp.float32
floor_score = -1e30
floor_top = -1e20

HEADS = 8
ROWS = 128
NOPE = 128
ROT = 64
LAT = 512
WIDE = LAT + ROT
KEYS = 2048
BLK = 256
NBLK = KEYS // BLK
ALL = HEADS * ROWS
PEERS = 16
PART = WIDE // 3
HALF = PART // 2
SCALE = 1.0 / math.sqrt(NOPE + ROT)
SCALE2 = SCALE * math.log2(math.e)
VLIM = 60 * 1024 * 1024

NT = (((1,), (1,)), ((), ()))


def dot(a, b):
    return jnp.dot(a, b, preferred_element_type=f32)


def dot_nt(a, b):
    return lax.dot_general(a, b, NT, preferred_element_type=f32)


def params(limit=VLIM):
    return pltpu.CompilerParams(vmem_limit_bytes=limit)


def whole(shape):
    return pl.BlockSpec(shape, lambda *_: (0,) * len(shape))


KB1 = 2
CHUNK = 256


def pass_one(
    sc, off, qt, wuk, wuv, og, lat, e_out, dp_out, qcat, dlat, stat, s_scr, top, tot, dsum, offc
):
    i = pl.program_id(0)
    steps = NBLK // KB1

    @pl.when(i == 0)
    def _():
        offc[...] = jnp.broadcast_to(off[...], (ROWS, ROWS)).T - sc[0]
        for h in range(HEADS):
            rows = slice(h * ROWS, (h + 1) * ROWS)
            q = qt[h].T
            qcat[rows, :LAT] = dot(q[:, :NOPE], wuk[h]).astype(bf16)
            qcat[rows, LAT:] = q[:, NOPE:]
            dlat[rows, :] = dot_nt(og[h], wuv[h]).astype(bf16)
        top[...] = jnp.full((ALL, 128), floor_top, f32)
        tot[...] = jnp.zeros((ALL, 128), f32)
        dsum[...] = jnp.zeros((ALL, 128), f32)

    @pl.when(i < steps)
    def _():
        lane = lax.broadcasted_iota(jnp.int32, (ROWS, BLK), 1)
        for j in range(KB1):
            cols = slice(j * BLK, (j + 1) * BLK)
            at = lane + (i * KB1 + j) * BLK
            bound = jnp.concatenate([offc[...]] * (BLK // 128), axis=1)
            seen = at <= bound
            for c in range(ALL // CHUNK):
                rows = slice(c * CHUNK, (c + 1) * CHUNK)
                s = dot(qcat[rows, :], lat[:, cols]) * SCALE2
                s = jnp.where(jnp.concatenate([seen] * (CHUNK // ROWS), axis=0), s, floor_score)
                s_scr[i * KB1 + j, rows, :] = s
                best = top[rows, :]
                for k in range(BLK // 128):
                    best = jnp.maximum(best, s[:, k * 128 : (k + 1) * 128])
                top[rows, :] = best

    @pl.when(i == steps - 1)
    def _():
        top[...] = jnp.broadcast_to(jnp.max(top[...], axis=1, keepdims=True), (ALL, 128))

    @pl.when(i >= steps)
    def _():
        for j in range(KB1):
            cols = slice(j * BLK, (j + 1) * BLK)
            for c in range(ALL // CHUNK):
                rows = slice(c * CHUNK, (c + 1) * CHUNK)
                dp = dot(dlat[rows, :], lat[:LAT, cols])
                dp_out[j, rows, :] = dp
                s = s_scr[(i - steps) * KB1 + j, rows, :]
                m = top[rows, :]
                t, d = tot[rows, :], dsum[rows, :]
                for k in range(BLK // 128):
                    lanes = slice(k * 128, (k + 1) * 128)
                    e = jnp.exp2(s[:, lanes] - m)
                    e_out[j, rows, lanes] = e
                    t = t + e
                    d = d + e * dp[:, lanes]
                tot[rows, :] = t
                dsum[rows, :] = d

    @pl.when(i == 2 * steps - 1)
    def _():
        lane = lax.broadcasted_iota(jnp.int32, (ROWS, 128), 1)
        for h in range(HEADS):
            rows = slice(h * ROWS, (h + 1) * ROWS)
            t = jnp.sum(tot[rows, :], axis=1, keepdims=True)
            d = jnp.sum(dsum[rows, :], axis=1, keepdims=True)
            x = jnp.where(lane == 0, top[rows, :], jnp.where(lane == 1, t, d)).T
            for k in range(3):
                line = x[k : k + 1, :]
                for peer in range(PEERS):
                    stat[peer, k * 8 + h : k * 8 + h + 1, :] = line


def run_pass_one(base, offsets, qt, wuk, wuv, og, lat_t):
    steps = NBLK // KB1
    out_block = lambda i, sc: (jnp.maximum(i - steps, 0), 0, 0)
    return pl.pallas_call(
        pass_one,
        grid_spec=pltpu.PrefetchScalarGridSpec(
            num_scalar_prefetch=1,
            grid=(2 * steps,),
            in_specs=[
                whole((1, ROWS)),
                whole(qt.shape),
                whole(wuk.shape),
                whole(wuv.shape),
                whole(og.shape),
                pl.BlockSpec((WIDE, KB1 * BLK), lambda i, sc: (0, lax.rem(i, steps))),
            ],
            out_specs=[
                pl.BlockSpec((KB1, ALL, BLK), out_block),
                pl.BlockSpec((KB1, ALL, BLK), out_block),
                whole((ALL, WIDE)),
                whole((ALL, LAT)),
                whole((PEERS, 24, 128)),
            ],
            scratch_shapes=[
                pltpu.VMEM((NBLK, ALL, BLK), f32),
                pltpu.VMEM((ALL, 128), f32),
                pltpu.VMEM((ALL, 128), f32),
                pltpu.VMEM((ALL, 128), f32),
                pltpu.VMEM((ROWS, 128), jnp.int32),
            ],
        ),
        out_shape=[
            jax.ShapeDtypeStruct((NBLK, ALL, BLK), f32),
            jax.ShapeDtypeStruct((NBLK, ALL, BLK), f32),
            jax.ShapeDtypeStruct((ALL, WIDE), bf16),
            jax.ShapeDtypeStruct((ALL, LAT), bf16),
            jax.ShapeDtypeStruct((PEERS, 24, 128), f32),
        ],
        compiler_params=params(),
        name="pass_one",
    )(base, offsets, qt, wuk, wuv, og, lat_t)


def turn(qcat, dlat, qcat_t, dlat_t):
    for h in range(HEADS):
        rows = slice(h * ROWS, (h + 1) * ROWS)
        for k in range(LAT // 128):
            lanes = slice(k * 128, (k + 1) * 128)
            qcat_t[lanes, rows] = qcat[rows, lanes].T
            dlat_t[lanes, rows] = dlat[rows, lanes].T
        qcat_t[LAT:, rows] = qcat[rows, LAT:].T


def run_turn(qcat, dlat):
    return pl.pallas_call(
        turn,
        out_shape=[
            jax.ShapeDtypeStruct((WIDE, ALL), bf16),
            jax.ShapeDtypeStruct((LAT, ALL), bf16),
        ],
        compiler_params=params(),
        name="turn",
    )(qcat, dlat)


def place(p, r):
    order = [r[p % 3], r[(p + 1) % 3], r[(p + 2) % 3]]
    return order[0] * 4 + order[1] * 2 + order[2]


def second_core(sc, e, dp, qcat_t, dlat_t, coef, delta, x_out, ds_out, pb):
    i = pl.program_id(0)
    for c in range(ALL // CHUNK):
        rows = slice(c * CHUNK, (c + 1) * CHUNK)
        cf, dl = coef[rows, :], delta[rows, :]
        for k in range(BLK // 128):
            lanes = slice(k * 128, (k + 1) * 128)
            p = e[0, rows, lanes] * cf
            pb[rows, lanes] = p.astype(bf16)
            ds_out[0, rows, lanes] = (p * (dp[0, rows, lanes] - dl)).astype(bf16)
    scores = dot(qcat_t[...], ds_out[0]) * SCALE
    values = dot(dlat_t[...], pb[...])
    low = (scores[:LAT] + values).astype(bf16)
    high = scores[LAT:].astype(bf16)
    r0, r1 = lax.rem(i, 2), lax.div(i, 2)
    for p in range(3):
        for h in range(2):
            at = place(p, (r0, r1, jnp.bitwise_xor(sc[2], h)))
            first = p * PART + h * HALF
            if first + HALF <= LAT:
                block = low[first : first + HALF]
            elif first >= LAT:
                block = high[first - LAT : first - LAT + HALF]
            else:
                block = jnp.concatenate([low[first:], high[: first + HALF - LAT]], axis=0)
            x_out[p, at] = block


def second_first(sc, stat, e, dp, qcat_t, dlat_t, x_out, ds_out, coef, delta, pb):
    @pl.when(pl.program_id(0) == 0)
    def _():
        m = stat[:, 0:8, :]
        best = jnp.max(m, axis=0)
        w = jnp.exp2(m - best[None])
        total = jnp.sum(w * stat[:, 8:16, :], axis=0)
        dtotal = jnp.sum(w * stat[:, 16:24, :], axis=0)
        cf = jnp.exp2(stat[sc[4], 0:8, :] - best) / total
        dl = dtotal / total
        for h in range(HEADS):
            rows = slice(h * ROWS, (h + 1) * ROWS)
            coef[rows, :] = jnp.broadcast_to(cf[h : h + 1], (128, 128)).T
            delta[rows, :] = jnp.broadcast_to(dl[h : h + 1], (128, 128)).T

    second_core(sc, e, dp, qcat_t, dlat_t, coef, delta, x_out, ds_out, pb)


def second_later(sc, coef, delta, e, dp, qcat_t, dlat_t, x_out, ds_out, pb):
    second_core(sc, e, dp, qcat_t, dlat_t, coef, delta, x_out, ds_out, pb)


def key_block(i, sc):
    a0 = jnp.bitwise_xor(lax.rem(i, 2), sc[0])
    a1 = jnp.bitwise_xor(lax.div(i, 2), sc[1])
    return sc[3] * 4 + a1 * 2 + a0


def run_second(sc, heads_in, e, dp, qcat_t, dlat_t, first):
    block = pl.BlockSpec((1, ALL, BLK), lambda i, sc: (key_block(i, sc), 0, 0))
    column = jax.ShapeDtypeStruct((ALL, 128), f32)
    outs = [
        jax.ShapeDtypeStruct((3, 8, HALF, BLK), bf16),
        jax.ShapeDtypeStruct((4, ALL, BLK), bf16),
    ]
    specs = [whole((3, 8, HALF, BLK)), pl.BlockSpec((1, ALL, BLK), lambda i, sc: (i, 0, 0))]
    if first:
        outs += [column, column]
        specs += [whole(column.shape)] * 2
    return pl.pallas_call(
        second_first if first else second_later,
        grid_spec=pltpu.PrefetchScalarGridSpec(
            num_scalar_prefetch=1,
            grid=(4,),
            in_specs=[whole(a.shape) for a in heads_in]
            + [block, block, whole(qcat_t.shape), whole(dlat_t.shape)],
            out_specs=specs,
            scratch_shapes=[pltpu.VMEM((ALL, BLK), bf16)],
        ),
        out_shape=outs,
        compiler_params=params(),
        name="second_first" if first else "second_later",
    )(sc, *heads_in, e, dp, qcat_t, dlat_t)


def query_grad(sc_a, sc_b, ds_a, ds_b, lat_a, lat_b, wuk, keep, send, acc, wide):
    i = pl.program_id(0)
    part = dot_nt(ds_a[0], lat_a[...]) + dot_nt(ds_b[0], lat_b[...])

    @pl.when(i == 0)
    def _():
        acc[...] = part

    @pl.when(i > 0)
    def _():
        acc[...] += part

    @pl.when(i == 3)
    def _():
        for h in range(HEADS):
            rows = slice(h * ROWS, (h + 1) * ROWS)
            x = acc[rows, :LAT] * SCALE
            hi = x.astype(bf16)
            lo = (x - hi.astype(f32)).astype(bf16)
            wide[h, :, :NOPE] = dot_nt(hi, wuk[h]) + dot_nt(lo, wuk[h])
            wide[h, :, NOPE:] = acc[rows, LAT:] * SCALE
        for g in range(PEERS):
            bits = (g >> 3 & 1) | (g >> 2 & 1) << 1 | (g >> 1 & 1) << 2 | (g & 1) << 3
            owner = jnp.bitwise_xor(sc_a[4], bits)
            mine = wide[:, pl.ds(pl.multiple_of(owner * 8, 8), 8), :]
            block = mine.reshape(HEADS * 8, NOPE + ROT).astype(bf16)
            if g < 8:
                keep[g] = block
            else:
                send[g - 8] = block


def run_query_grad(sc_a, sc_b, ds_a, ds_b, lat_t, wuk):
    half = jax.ShapeDtypeStruct((8, HEADS * 8, NOPE + ROT), bf16)
    step = pl.BlockSpec((1, ALL, BLK), lambda i, a, b: (i, 0, 0))
    return pl.pallas_call(
        query_grad,
        grid_spec=pltpu.PrefetchScalarGridSpec(
            num_scalar_prefetch=2,
            grid=(4,),
            in_specs=[
                step,
                step,
                pl.BlockSpec((WIDE, BLK), lambda i, a, b: (0, key_block(i, a))),
                pl.BlockSpec((WIDE, BLK), lambda i, a, b: (0, key_block(i, b))),
                whole(wuk.shape),
            ],
            out_specs=[whole(half.shape)] * 2,
            scratch_shapes=[
                pltpu.VMEM((ALL, WIDE), f32),
                pltpu.VMEM((HEADS, ROWS, NOPE + ROT), f32),
            ],
        ),
        out_shape=[half, half],
        compiler_params=params(),
        name="query_grad",
    )(sc_a, sc_b, ds_a, ds_b, lat_t, lat_t, wuk)


def halve(single, *refs):
    kept, got = refs[0], refs[1 : 2 if single else 4]
    outs = refs[2 if single else 4 :]
    for p in range(3):
        n = kept.shape[1]
        for k in range(n):
            other = got[0][p, k] if single else got[p][k]
            total = (kept[p, k].astype(f32) + other.astype(f32)).astype(bf16)
            if n == 1:
                outs[p][0] = total
            elif k < n // 2:
                outs[0][p, k] = total
            else:
                outs[1 + p][k - n // 2] = total


def run_halve(kept, got):
    n = kept.shape[1]
    one = lambda k: jax.ShapeDtypeStruct((k, HALF, BLK), bf16)
    if n == 1:
        outs = [one(1)] * 3
    else:
        outs = [jax.ShapeDtypeStruct((3, n // 2, HALF, BLK), bf16)] + [one(n // 2)] * 3
    return pl.pallas_call(
        functools.partial(halve, len(got) == 1),
        out_shape=outs,
        compiler_params=params(),
        name="halve",
    )(kept, *got)


def join(last, *refs):
    n = refs[0].shape[0]
    for p in range(3):
        for src, at in ((refs[p], 0), (refs[3 + p], n)):
            refs[6 + p][at : at + n] = src[...]
            if last:
                refs[9][p, at : at + n] = src[...]


def run_join(own, got, last):
    n = 2 * own[0].shape[0]
    outs = [jax.ShapeDtypeStruct((n, HALF, BLK), bf16)] * 3
    if last:
        outs = outs + [jax.ShapeDtypeStruct((3, n, HALF, BLK), bf16)]
    return pl.pallas_call(
        functools.partial(join, last),
        out_shape=outs,
        compiler_params=params(),
        name="join",
    )(*own, *got)


def settle(sc, *refs):
    mine, mine_far, other, other_far, out = refs[0], refs[1:4], refs[4], refs[5:8], refs[8]
    for near, far, half in ((mine, mine_far, sc[3]), (other, other_far, 1 - sc[3])):
        for p in range(3):
            for i in range(8):
                r = [0, 0, 0]
                r[p % 3], r[(p + 1) % 3], r[(p + 2) % 3] = i >> 2 & 1, i >> 1 & 1, i & 1
                a = [jnp.bitwise_xor(sc[d], r[d]) for d in range(3)]
                rows = pl.ds(pl.multiple_of(p * PART + a[2] * HALF, 32), HALF)
                lanes = pl.ds(pl.multiple_of((half * 4 + a[1] * 2 + a[0]) * BLK, BLK), BLK)
                out[rows, lanes] = near[p, i] if i < 4 else far[p][i - 4]


def run_settle(sc, *pieces):
    return pl.pallas_call(
        settle,
        grid_spec=pltpu.PrefetchScalarGridSpec(
            num_scalar_prefetch=1,
            grid=(1,),
            in_specs=[whole(a.shape) for a in pieces],
            out_specs=whole((WIDE, KEYS)),
        ),
        out_shape=jax.ShapeDtypeStruct((WIDE, KEYS), bf16),
        compiler_params=params(),
        name="settle",
    )(sc, *pieces)


def cube_neighbour(k, d):
    y, rest = k >> 2, k & 3
    if d == 2:
        return k ^ 2
    gray = (y ^ (y >> 1)) ^ (1 << d)
    back = gray ^ (gray >> 1)
    return back * 4 + rest


def along(value, d):
    return lax.ppermute(value, "head", [(k, cube_neighbour(k, d)) for k in range(16)])


def to_sibling(value):
    return lax.ppermute(value, "head", [(k, k ^ 1) for k in range(16)])


def shards(queries, w_uk, w_uv, latent, out_grad, offsets):
    head = lax.axis_index("head").astype(jnp.int32)
    key = lax.axis_index("key").astype(jnp.int32)
    y = head >> 2
    gray = y ^ (y >> 1)
    core = head & 1
    sc_own = jnp.stack([gray & 1, gray >> 1, (head >> 1) & 1, core, key])
    sc_far = jnp.stack([gray & 1, gray >> 1, (head >> 1) & 1, 1 - core, key])
    lat_t = latent.T
    qt = jnp.transpose(queries, (1, 2, 0))
    og = jnp.transpose(out_grad, (1, 0, 2))
    e, dp, qcat, dlat, stat = run_pass_one(
        (key * KEYS)[None], offsets[None], qt, w_uk, w_uv, og, lat_t
    )
    stat = lax.all_to_all(stat, "key", 0, 0, tiled=True)
    qcat_t, dlat_t = run_turn(qcat, dlat)
    x_far, ds_far, coef, delta = run_second(sc_far, (stat,), e, dp, qcat_t, dlat_t, True)
    came = to_sibling(x_far)
    x_own, ds_own = run_second(sc_own, (coef, delta), e, dp, qcat_t, dlat_t, False)
    kept, *send = run_halve(x_own, [came])
    for step in range(3):
        got = [along(send[p], (p + step) % 3) for p in range(3)]
        if step == 0:
            q_keep, q_send = run_query_grad(sc_far, sc_own, ds_far, ds_own, lat_t, w_uk)
        kept, *send = run_halve(kept, got) if step < 2 else (None, *run_halve(kept, got))
    own = send
    for step in range(2):
        got = [along(own[p], (p + 2 - step) % 3) for p in range(3)]
        own = run_join(own, got, step == 1)
    near = own[3]
    far = [along(own[p], p) for p in range(3)]
    near_other = to_sibling(near)
    far_other = [to_sibling(a) for a in far]
    d_latent = run_settle(sc_own, near, *far, near_other, *far_other).T

    for flip in (1, 2, 4, 8):
        got = lax.ppermute(q_send, "key", [(k, k ^ flip) for k in range(16)])
        total = (q_keep.astype(f32) + got.astype(f32)).astype(bf16)
        n = total.shape[0] // 2
        q_keep, q_send = (total[:n], total[n:]) if n else (total, None)
    d_queries = jnp.transpose(q_keep[0].reshape(HEADS, 8, NOPE + ROT), (1, 0, 2))
    return (d_queries, d_latent)


def solution(mesh):
    return jax.shard_map(
        shards,
        mesh=mesh,
        in_specs=(
            P(None, "head", None),
            P("head", None, None),
            P("head", None, None),
            P("key", None),
            P(None, "head", None),
            P(),
        ),
        out_specs=(P("key", "head", None), P("key", None)),
        check_vma=False,
    )
```

time: 205 us -> 145 us (0.71)
  blocking collectives: 126 us -> 0 us
  Pallas kernels: 0 us -> 63 us
  matrix products: 31.5 us -> 0 us
  starting transfers between devices: 15.2 us -> 45.8 us
  waiting for transfers between devices: 6.65 us -> 22.6 us
  other arithmetic: 14.3 us -> 1.08 us
  local copies, waits for them, and re-layouts: 6.67 us -> 9.96 us
    psum x1 -> x0, blocking collectives: 114 us -> none  [shards(): lax.psum(jnp.concatenate([from_scores[:, :lat_width] + from_values, from_...]
    pallas_call x0 -> x12, Pallas kernels: none -> 63 us  [the longest x2 17.9 us: run_second(): pl.pallas_call(second_first if first else second_later, grid_spec=pltpu.P...]
    ppermute x0 -> x27, starting transfers between devices: none -> 34.2 us  [the longest x18 14.9 us: along(): lax.ppermute(value, 'head', [(k, cube_neighbour(k, d)) for k in range(16)])]
    dot_general x8 -> x0, matrix products: 31.5 us -> none  [the longest x1 12 us: shards(): jnp.einsum('rhc,kc->hrk', d_lat, latent[:, :lat_width], preferred_element...]
    ppermute x0 -> x27, waiting for transfers between devices: none -> 18 us  [the longest x18 14.4 us: along(): lax.ppermute(value, 'head', [(k, cube_neighbour(k, d)) for k in range(16)])]
    all_to_all x1 -> x0, blocking collectives: 12 us -> none  [sent_to_all(): lax.all_to_all(jnp.broadcast_to(value[None], (count, *value.shape)), axis...]
    convert_element_type x1 -> x3, other arithmetic: 7.51 us -> 1.07 us  [shards(): total = (q_keep.astype(f32) + got.astype(f32)).astype(bf16)]
    unnamed x20 -> x49, local copies, waits for them, and re-layouts: 3.51 us -> 8.11 us
  transfers between devices with their start and end apart: 2 -> 28, of which waited for: 1 -> 14; matrix products, arithmetic and copies ran while one was open for 1% -> 2% of each run, Pallas kernels for 0% -> 20%
where the time goes in v1:
time: 145 us; the launch traced here: 143 us
  Pallas kernels  63 us (43%)
  starting transfers between devices  45.8 us (32%)
  waiting for transfers between devices  22.6 us (16%)
  local copies, waits for them, and re-layouts  9.96 us (7%)
    pallas_call x2, Pallas kernels, run_second(): pl.pallas_call(second_first if first else second_later, grid_spec=pltpu.P...  17.9 us
    pallas_call x1, Pallas kernels, run_pass_one(): pl.pallas_call(pass_one, grid_spec=pltpu.PrefetchScalarGridSpec(num_scala...  15.6 us
    ppermute x18, starting transfers between devices, along(): lax.ppermute(value, 'head', [(k, cube_neighbour(k, d)) for k in range(16)])  14.9 us
    ppermute x18, waiting for transfers between devices, along(): lax.ppermute(value, 'head', [(k, cube_neighbour(k, d)) for k in range(16)])  14.4 us
    ppermute x5, starting transfers between devices, to_sibling(): return lax.ppermute(value, 'head', [(k, k ^ 1) for k in range(16)])  14.3 us
    all_to_all x1, starting transfers between devices, shards(): stat = lax.all_to_all(stat, 'key', 0, 0, tiled=True)  11.6 us
    pallas_call x1, Pallas kernels, run_query_grad(): pl.pallas_call(query_grad, grid_spec=pltpu.PrefetchScalarGridSpec(num_sca...  9.46 us
    pallas_call x4, Pallas kernels, run_halve(): pl.pallas_call(functools.partial(halve, len(got) == 1), out_shape=outs, c...  8.34 us
  transfers between devices with their start and end apart: 28, of which 14 were waited for; matrix products, arithmetic and copies ran while one was open for 2% of the time, Pallas kernels for 20%

profile of v1, /device:TPU:1, one launch (start us, length us, event | category | flops | bytes accessed | tf_op | source)
XLA Modules:
  0.0 143.2 jit_solution(3992587058045040721)
XLA Ops:
  0.6 1.7 %copy.12 = bf16[128,8,128]{2,0,1:T(8,128)(2,1)} copy(bf16[128,8,128]{2,1,0:T(8,128)(2,1)} %param.10) | data formatting | bytes 524288 | tf_op args[4]
  2.3 15.6 %pass_one.1 = (f32[8,1024,256]{2,1,0:T(8,128)}, f32[8,1024,256]{2,1,0:T(8,128)}, bf16[1024,576]{1,0:T(8,128)(2,1)}, bf16[1024,512]{1,0:T(8,128)(2,1)}, f32[16,24,128]{2,1,0:T(8,128)}) custom-call(s32[1]{0:T(128)} %bitcast.6.sc, s32[1,128]{1,0:T(1,128)} %bitcast.26, bf16[8,192,128]{2,1,0:T(8,128)(2,1)} %bitcast.24, bf16[8,128,512]{2,1,0:T(8,128)(2,1)} %wuk.3, ...), custom_call_target="tpu_custom_call" | custom-call | tf_op jit(solution)/shard_map/pass_one/pallas_call | solution.py:134
  18.0 11.6 %all-to-all-start = ((f32[16,24,128]{2,1,0:T(8,128)}), f32[16,24,128]{2,1,0:T(8,128)S(1)}, u32[]{:S(2)}, u32[]{:S(2)}) async-start(f32[16,24,128]{2,1,0:T(8,128)} %get-tuple-element.39), calls=%async_computation | async-start | bytes 393216 | tf_op jit(solution)/shard_map/all_to_all | solution.py:455
  29.6 3.8 %turn.1 = (bf16[576,1024]{1,0:T(8,128)(2,1)}, bf16[512,1024]{1,0:T(8,128)(2,1)}) custom-call(bf16[1024,576]{1,0:T(8,128)(2,1)} %get-tuple-element.42.qcat, bf16[1024,512]{1,0:T(8,128)(2,1)} %get-tuple-element.43.dlat), custom_call_target="tpu_custom_call" | custom-call | tf_op jit(solution)/shard_map/turn/pallas_call | solution.py:185
  33.3 0.6 stack.33.sc.sc_a
  33.9 4.6 %all-to-all-done.stat = f32[16,24,128]{2,1,0:T(8,128)S(1)} async-done(((f32[16,24,128]{2,1,0:T(8,128)}), f32[16,24,128]{2,1,0:T(8,128)S(1)}, u32[]{:S(2)}, u32[]{:S(2)}) %all-to-all-start) | async-done | bytes 196640 | tf_op jit(solution)/shard_map/all_to_all | solution.py:455
  38.6 0.7 copy-done.1
  39.3 9.1 %second_first.1 = (bf16[3,8,96,256]{3,2,1,0:T(8,128)(2,1)}, bf16[4,1024,256]{2,1,0:T(8,128)(2,1)}, f32[1024,128]{1,0:T(8,128)}, f32[1024,128]{1,0:T(8,128)}) custom-call(s32[5]{0:T(128)} %stack.33.sc.sc_a, f32[16,24,128]{2,1,0:T(8,128)} %copy-done.1, f32[8,1024,256]{2,1,0:T(8,128)} %get-tuple-element.40.e, f32[8,1024,256]{2,1,0:T(8,128)} %get-tuple-element.41.dp, ...), custom_call_target="tpu_custom_call" | custom-call | tf_op jit(solution)/shard_map/second_first/pallas_call | solution.py:268
  48.4 2.5 %collective-permute-start.4 = (bf16[3,8,96,256]{3,2,1,0:T(8,128)(2,1)}, bf16[3,8,96,256]{3,2,1,0:T(8,128)(2,1)S(1)}, u32[]{:S(2)}, u32[]{:S(2)}) collective-permute-start(bf16[3,8,96,256]{3,2,1,0:T(8,128)(2,1)} %get-tuple-element.53), channel_id=1, source_target_pairs={{0,16},{16,0},{32,48},{48,32},{64,80},{80,64},{96,112},{112,96},{1... | collective-permute-start | bytes 3538952 | tf_op jit(solution)/shard_map/ppermute | solution.py:438
  51.0 0.6 stack.35.sc.sc_b
  51.5 8.8 %second_later.1 = (bf16[3,8,96,256]{3,2,1,0:T(8,128)(2,1)}, bf16[4,1024,256]{2,1,0:T(8,128)(2,1)}) custom-call(s32[5]{0:T(128)} %stack.35.sc.sc_b, f32[1024,128]{1,0:T(8,128)} %get-tuple-element.47.coef, f32[1024,128]{1,0:T(8,128)} %get-tuple-element.48.delta, f32[8,1024,256]{2,1,0:T(8,128)} %get-tuple-element.40.e, f32[8,1024,256]{2,1,0:T(8,128)} %get-tuple-element.41.dp, ...), custom_call_target="tpu_custom_call" | custom-call | tf_op jit(solution)/shard_map/second_later/pallas_call | solution.py:268
  60.4 1.0 copy-done
  61.4 2.8 %halve.4 = (bf16[3,4,96,256]{3,2,1,0:T(8,128)(2,1)}, bf16[4,96,256]{2,1,0:T(8,128)(2,1)}, bf16[4,96,256]{2,1,0:T(8,128)(2,1)}, bf16[4,96,256]{2,1,0:T(8,128)(2,1)}) custom-call(bf16[3,8,96,256]{3,2,1,0:T(8,128)(2,1)} %get-tuple-element.52.refs_0_, bf16[3,8,96,256]{3,2,1,0:T(8,128)(2,1)} %copy-done), custom_call_target="tpu_custom_call" | custom-call | tf_op jit(solution)/shard_map/halve/pallas_call | solution.py:366
  64.1 1.3 collective-permute-start.5
  65.4 1.9 %collective-permute-start.6 = (bf16[4,96,256]{2,1,0:T(8,128)(2,1)}, bf16[4,96,256]{2,1,0:T(8,128)(2,1)S(1)}, u32[]{:S(2)}, u32[]{:S(2)}) collective-permute-start(bf16[4,96,256]{2,1,0:T(8,128)(2,1)} %get-tuple-element.56), channel_id=1, source_target_pairs={{0,192},{16,208},{32,224},{48,240},{64,128},{80,144},{96,160},{112... | collective-permute-start | bytes 589832 | tf_op jit(solution)/shard_map/ppermute | solution.py:434
  67.3 0.3 collective-permute-start.7
  67.7 3.2 %collective-permute-done.5.refs_1_ = bf16[4,96,256]{2,1,0:T(8,128)(2,1)S(1)} collective-permute-done((bf16[4,96,256]{2,1,0:T(8,128)(2,1)}, bf16[4,96,256]{2,1,0:T(8,128)(2,1)S(1)}, u32[]{:S(2)}, u32[]{:S(2)}) %collective-permute-start.5) | collective-permute-done | bytes 196640 | tf_op jit(solution)/shard_map/ppermute | solution.py:434
  70.9 2.2 %collective-permute-done.6.refs_2_ = bf16[4,96,256]{2,1,0:T(8,128)(2,1)S(1)} collective-permute-done((bf16[4,96,256]{2,1,0:T(8,128)(2,1)}, bf16[4,96,256]{2,1,0:T(8,128)(2,1)S(1)}, u32[]{:S(2)}, u32[]{:S(2)}) %collective-permute-start.6) | collective-permute-done | bytes 196640 | tf_op jit(solution)/shard_map/ppermute | solution.py:434
  73.1 0.4 collective-permute-done.7.refs_3_
  73.4 0.3 copy-done.10
  73.8 0.4 copy-done.11
  74.1 2.2 %halve.5 = (bf16[3,2,96,256]{3,2,1,0:T(8,128)(2,1)}, bf16[2,96,256]{2,1,0:T(8,128)(2,1)}, bf16[2,96,256]{2,1,0:T(8,128)(2,1)}, bf16[2,96,256]{2,1,0:T(8,128)(2,1)}) custom-call(bf16[3,4,96,256]{3,2,1,0:T(8,128)(2,1)} %get-tuple-element.54.refs_0_, bf16[4,96,256]{2,1,0:T(8,128)(2,1)} %copy-done.9, bf16[4,96,256]{2,1,0:T(8,128)(2,1)} %copy-done.10, ...), custom_call_target="tpu_custom_call" | custom-call | tf_op jit(solution)/shard_map/halve/pallas_call | solution.py:366
  76.3 1.6 %collective-permute-start.8 = (bf16[2,96,256]{2,1,0:T(8,128)(2,1)}, bf16[2,96,256]{2,1,0:T(8,128)(2,1)S(1)}, u32[]{:S(2)}, u32[]{:S(2)}) collective-permute-start(bf16[2,96,256]{2,1,0:T(8,128)(2,1)} %get-tuple-element.59), channel_id=1, source_target_pairs={{0,192},{16,208},{32,224},{48,240},{64,128},{80,144},{96,160},{112... | collective-permute-start | bytes 294920 | tf_op jit(solution)/shard_map/ppermute | solution.py:434
  77.9 0.3 collective-permute-start.9
  78.2 9.5 %query_grad.1 = (bf16[8,64,192]{2,1,0:T(8,128)(2,1)}, bf16[8,64,192]{2,1,0:T(8,128)(2,1)}) custom-call(s32[5]{0:T(128)} %stack.33.sc.sc_a, s32[5]{0:T(128)} %stack.35.sc.sc_b, bf16[4,1024,256]{2,1,0:T(8,128)(2,1)} %get-tuple-element.46.ds_a, bf16[4,1024,256]{2,1,0:T(8,128)(2,1)} %get-tuple-element.49.ds_b, bf16[576,2048]{1,0:T(8,128)(2,1)} %bitcast.20, ...), custom_call_target="tpu_custom_call" | custom-call | tf_op jit(solution)/shard_map/query_grad/pallas_call | solution.py:319
  87.7 1.8 %collective-permute-start = (bf16[8,64,192]{2,1,0:T(8,128)(2,1)}, bf16[8,64,192]{2,1,0:T(8,128)(2,1)S(1)}, u32[]{:S(2)}, u32[]{:S(2)}) collective-permute-start(bf16[8,64,192]{2,1,0:T(8,128)(2,1)} %get-tuple-element.51), channel_id=1, source_target_pairs={{0,1},{1,0},{2,3},{3,2},{4,5},{5,4},{6,7},{7,6},{8,9},{9,8},{10,11... | collective-permute-start | bytes 589832 | tf_op jit(solution)/shard_map/ppermute | solution.py:477
  89.5 0.6 copy-done.12
  90.2 1.8 %halve.6 = (bf16[3,1,96,256]{3,2,1,0:T(8,128)(2,1)}, bf16[1,96,256]{2,1,0:T(8,128)(2,1)}, bf16[1,96,256]{2,1,0:T(8,128)(2,1)}, bf16[1,96,256]{2,1,0:T(8,128)(2,1)}) custom-call(bf16[3,2,96,256]{3,2,1,0:T(8,128)(2,1)} %get-tuple-element.58.refs_0_, bf16[2,96,256]{2,1,0:T(8,128)(2,1)} %copy-done.12, bf16[2,96,256]{2,1,0:T(8,128)(2,1)} %copy-done.14, ...), custom_call_target="tpu_custom_call" | custom-call | tf_op jit(solution)/shard_map/halve/pallas_call | solution.py:366
  92.0 1.2 collective-permute-start.11
  93.1 1.5 %collective-permute-start.12 = (bf16[1,96,256]{2,1,0:T(8,128)(2,1)}, bf16[1,96,256]{2,1,0:T(8,128)(2,1)S(1)}, u32[]{:S(2)}, u32[]{:S(2)}) collective-permute-start(bf16[1,96,256]{2,1,0:T(8,128)(2,1)} %get-tuple-element.64), channel_id=1, source_target_pairs={{0,64},{16,80},{32,96},{48,112},{64,0},{80,16},{96,32},{112,48},{1... | collective-permute-start | bytes 147464 | tf_op jit(solution)/shard_map/ppermute | solution.py:434
  94.6 1.1 collective-permute-start.13
  95.7 0.9 collective-permute-done.12.refs_2_
  96.5 2.4 %collective-permute-done.13.refs_3_ = bf16[1,96,256]{2,1,0:T(8,128)(2,1)S(1)} collective-permute-done((bf16[1,96,256]{2,1,0:T(8,128)(2,1)}, bf16[1,96,256]{2,1,0:T(8,128)(2,1)S(1)}, u32[]{:S(2)}, u32[]{:S(2)}) %collective-permute-start.13) | collective-permute-done | bytes 49184 | tf_op jit(solution)/shard_map/ppermute | solution.py:434
  99.0 0.6 copy-done.22
  99.6 1.6 %halve.7 = (bf16[1,96,256]{2,1,0:T(8,128)(2,1)}, bf16[1,96,256]{2,1,0:T(8,128)(2,1)}, bf16[1,96,256]{2,1,0:T(8,128)(2,1)}) custom-call(bf16[3,1,96,256]{3,2,1,0:T(8,128)(2,1)} %get-tuple-element.62.refs_0_, bf16[1,96,256]{2,1,0:T(8,128)(2,1)} %copy-done.18, bf16[1,96,256]{2,1,0:T(8,128)(2,1)} %copy-done.20, bf16[1,96,256]{2,1,0:T(8,128)(2,1)} %copy-done.22), custom_call_target="tpu_custom_call" | custom-call | tf_op jit(solution)/shard_map/halve/pallas_call | solution.py:366
  101.2 0.3 collective-permute-start.14
  101.5 1.1 collective-permute-start.16
  102.6 1.8 %collective-permute-done.14.refs_3_ = bf16[1,96,256]{2,1,0:T(8,128)(2,1)S(1)} collective-permute-done((bf16[1,96,256]{2,1,0:T(8,128)(2,1)}, bf16[1,96,256]{2,1,0:T(8,128)(2,1)S(1)}, u32[]{:S(2)}, u32[]{:S(2)}) %collective-permute-start.14) | collective-permute-done | bytes 49184 | tf_op jit(solution)/shard_map/ppermute | solution.py:434
  104.3 0.3 collective-permute-done.15.refs_4_
  104.6 1.2 collective-permute-done.16.refs_5_
  105.8 0.6 copy-done.23
  106.5 1.7 %join.2 = (bf16[2,96,256]{2,1,0:T(8,128)(2,1)}, bf16[2,96,256]{2,1,0:T(8,128)(2,1)}, bf16[2,96,256]{2,1,0:T(8,128)(2,1)}) custom-call(bf16[1,96,256]{2,1,0:T(8,128)(2,1)} %get-tuple-element.66.refs_0_, bf16[1,96,256]{2,1,0:T(8,128)(2,1)} %get-tuple-element.67.refs_1_, bf16[1,96,256]{2,1,0:T(8,128)(2,1)} %get-tuple-element.68.refs_2_, ...), custom_call_target="tpu_custom_call" | custom-call | tf_op jit(solution)/shard_map/join/pallas_call | solution.py:388
  108.1 1.1 collective-permute-start.17
  109.2 1.1 collective-permute-start.18
  110.4 1.0 add_convert_fusion
  111.4 0.6 collective-permute-start.1
  112.0 1.1 collective-permute-done.17.refs_3_
  113.0 1.0 collective-permute-done.19.refs_5_
  114.0 0.6 copy-done.17
  114.7 2.2 %join.3 = (bf16[4,96,256]{2,1,0:T(8,128)(2,1)}, bf16[4,96,256]{2,1,0:T(8,128)(2,1)}, bf16[4,96,256]{2,1,0:T(8,128)(2,1)}, bf16[3,4,96,256]{3,2,1,0:T(8,128)(2,1)}) custom-call(bf16[2,96,256]{2,1,0:T(8,128)(2,1)} %get-tuple-element.69.refs_0_, bf16[2,96,256]{2,1,0:T(8,128)(2,1)} %get-tuple-element.70.refs_1_, bf16[2,96,256]{2,1,0:T(8,128)(2,1)} %get-tuple-element.71.refs_2_, ...), custom_call_target="tpu_custom_call" | custom-call | tf_op jit(solution)/shard_map/join/pallas_call | solution.py:388
  116.9 7.4 %collective-permute-start.23 = (bf16[3,4,96,256]{3,2,1,0:T(8,128)(2,1)}, bf16[3,4,96,256]{3,2,1,0:T(8,128)(2,1)S(1)}, u32[]{:S(2)}, u32[]{:S(2)}) collective-permute-start(bf16[3,4,96,256]{3,2,1,0:T(8,128)(2,1)} %get-tuple-element.72.refs_0_), channel_id=1, source_target_pairs={{0,16},{16,0},{32,48},{48,32},{64,80},{80,64},{96,112},{112,96},{1... | collective-permute-start | bytes 1769480 | tf_op jit(solution)/shard_map/ppermute | solution.py:438
  124.3 1.8 %collective-permute-start.2 = (bf16[2,64,192]{2,1,0:T(8,128)(2,1)S(1)}, bf16[2,64,192]{2,1,0:T(8,128)(2,1)S(1)}, u32[]{:S(2)}, u32[]{:S(2)}) collective-permute-start(bf16[2,64,192]{2,1,0:T(8,128)(2,1)S(1)} %slice.27), channel_id=1, source_target_pairs={{0,4},{1,5},{2,6},{3,7},{4,0},{5,1},{6,2},{7,3},{8,12},{9,13},{10,... | collective-permute-start | bytes 147464 | tf_op jit(solution)/shard_map/ppermute | solution.py:477
  126.2 0.5 collective-permute-start.20
  126.7 1.3 collective-permute-start.21
  128.0 0.3 collective-permute-start.22
  128.3 3.1 %collective-permute-done.2 = bf16[2,64,192]{2,1,0:T(8,128)(2,1)S(1)} collective-permute-done((bf16[2,64,192]{2,1,0:T(8,128)(2,1)S(1)}, bf16[2,64,192]{2,1,0:T(8,128)(2,1)S(1)}, u32[]{:S(2)}, u32[]{:S(2)}) %collective-permute-start.2) | collective-permute-done | bytes 49184 | tf_op jit(solution)/shard_map/ppermute | solution.py:477
  131.5 0.7 collective-permute-start.3
  132.2 3.7 %collective-permute-start.24 = (bf16[4,96,256]{2,1,0:T(8,128)(2,1)S(1)}, bf16[4,96,256]{2,1,0:T(8,128)(2,1)S(1)}, u32[]{:S(2)}, u32[]{:S(2)}) collective-permute-start(bf16[4,96,256]{2,1,0:T(8,128)(2,1)S(1)} %collective-permute-done.20.refs_1_), channel_id=1, source_target_pairs={{0,16},{16,0},{32,48},{48,32},{64,80},{80,64},{96,112},{112,96},{1... | collective-permute-start | bytes 589832 | tf_op jit(solution)/shard_map/ppermute | solution.py:438
  136.1 0.6 collective-permute-start.26
  136.6 0.6 copy.13
  137.3 0.3 collective-permute-done.26.refs_7_
  138.0 0.3 copy-done.8
  138.4 0.8 copy-done.2
  139.2 4.0 %settle.1 = bf16[576,2048]{1,0:T(8,128)(2,1)} custom-call(s32[5]{0:T(128)} %stack.35.sc.sc_b, bf16[3,4,96,256]{3,2,1,0:T(8,128)(2,1)} %get-tuple-element.72.refs_0_, bf16[4,96,256]{2,1,0:T(8,128)(2,1)} %copy-done.3, bf16[4,96,256]{2,1,0:T(8,128)(2,1)} %copy-done.4, bf16[4,96,256]{2,1,0:T(8,128)(2,1)} %copy-done.5, bf16[3,4,96,256]{3,2,1,0:T(8,128)(2,1)} %copy-done.2, ...), custom_call_target="tpu_custom_call" | custom-call | tf_op jit(solution)/shard_map/settle/pallas_call | solution.py:410
  (63 shorter events, 0.8 us)
Async XLA Ops:
  18.0 20.6 %all-to-all-start = ((f32[16,24,128]{2,1,0:T(8,128)}), f32[16,24,128]{2,1,0:T(8,128)S(1)}, u32[]{:S(2)}, u32[]{:S(2)}) async-start(f32[16,24,128]{2,1,0:T(8,128)} %get-tuple-element.39), calls=%async_computation | async-start | bytes 393216 | tf_op jit(solution)/shard_map/all_to_all | solution.py:455
  38.6 0.7 copy-start.1
  48.4 11.9 %collective-permute-start.4 = (bf16[3,8,96,256]{3,2,1,0:T(8,128)(2,1)}, bf16[3,8,96,256]{3,2,1,0:T(8,128)(2,1)S(1)}, u32[]{:S(2)}, u32[]{:S(2)}) collective-permute-start(bf16[3,8,96,256]{3,2,1,0:T(8,128)(2,1)} %get-tuple-element.53), channel_id=1, source_target_pairs={{0,16},{16,0},{32,48},{48,32},{64,80},{80,64},{96,112},{112,96},{1... | collective-permute-start | bytes 3538952 | tf_op jit(solution)/shard_map/ppermute | solution.py:438
  60.3 1.0 copy-start
  64.1 6.7 %collective-permute-start.5 = (bf16[4,96,256]{2,1,0:T(8,128)(2,1)}, bf16[4,96,256]{2,1,0:T(8,128)(2,1)S(1)}, u32[]{:S(2)}, u32[]{:S(2)}) collective-permute-start(bf16[4,96,256]{2,1,0:T(8,128)(2,1)} %get-tuple-element.55), channel_id=1, source_target_pairs={{0,64},{16,80},{32,96},{48,112},{64,0},{80,16},{96,32},{112,48},{1... | collective-permute-start | bytes 589832 | tf_op jit(solution)/shard_map/ppermute | solution.py:434
  65.4 7.6 %collective-permute-start.6 = (bf16[4,96,256]{2,1,0:T(8,128)(2,1)}, bf16[4,96,256]{2,1,0:T(8,128)(2,1)S(1)}, u32[]{:S(2)}, u32[]{:S(2)}) collective-permute-start(bf16[4,96,256]{2,1,0:T(8,128)(2,1)} %get-tuple-element.56), channel_id=1, source_target_pairs={{0,192},{16,208},{32,224},{48,240},{64,128},{80,144},{96,160},{112... | collective-permute-start | bytes 589832 | tf_op jit(solution)/shard_map/ppermute | solution.py:434
  67.3 6.1 %collective-permute-start.7 = (bf16[4,96,256]{2,1,0:T(8,128)(2,1)}, bf16[4,96,256]{2,1,0:T(8,128)(2,1)S(1)}, u32[]{:S(2)}, u32[]{:S(2)}) collective-permute-start(bf16[4,96,256]{2,1,0:T(8,128)(2,1)} %get-tuple-element.57), channel_id=1, source_target_pairs={{0,32},{16,48},{32,0},{48,16},{64,96},{80,112},{96,64},{112,80},{1... | collective-permute-start | bytes 589832 | tf_op jit(solution)/shard_map/ppermute | solution.py:434
  70.9 2.6 %copy-start.9 = (bf16[4,96,256]{2,1,0:T(8,128)(2,1)}, bf16[4,96,256]{2,1,0:T(8,128)(2,1)S(1)}, u32[]{:S(2)}) copy-start(bf16[4,96,256]{2,1,0:T(8,128)(2,1)S(1)} %collective-permute-done.5.refs_1_) | copy-start | bytes 589828
  73.1 0.7 copy-start.10
  73.4 0.7 copy-start.11
  76.3 13.2 %collective-permute-start.8 = (bf16[2,96,256]{2,1,0:T(8,128)(2,1)}, bf16[2,96,256]{2,1,0:T(8,128)(2,1)S(1)}, u32[]{:S(2)}, u32[]{:S(2)}) collective-permute-start(bf16[2,96,256]{2,1,0:T(8,128)(2,1)} %get-tuple-element.59), channel_id=1, source_target_pairs={{0,192},{16,208},{32,224},{48,240},{64,128},{80,144},{96,160},{112... | collective-permute-start | bytes 294920 | tf_op jit(solution)/shard_map/ppermute | solution.py:434
  77.9 11.6 %collective-permute-start.9 = (bf16[2,96,256]{2,1,0:T(8,128)(2,1)}, bf16[2,96,256]{2,1,0:T(8,128)(2,1)S(1)}, u32[]{:S(2)}, u32[]{:S(2)}) collective-permute-start(bf16[2,96,256]{2,1,0:T(8,128)(2,1)} %get-tuple-element.60), channel_id=1, source_target_pairs={{0,32},{16,48},{32,0},{48,16},{64,96},{80,112},{96,64},{112,80},{1... | collective-permute-start | bytes 294920 | tf_op jit(solution)/shard_map/ppermute | solution.py:434
  78.2 11.3 %collective-permute-start.10 = (bf16[2,96,256]{2,1,0:T(8,128)(2,1)}, bf16[2,96,256]{2,1,0:T(8,128)(2,1)S(1)}, u32[]{:S(2)}, u32[]{:S(2)}) collective-permute-start(bf16[2,96,256]{2,1,0:T(8,128)(2,1)} %get-tuple-element.61), channel_id=1, source_target_pairs={{0,64},{16,80},{32,96},{48,112},{64,0},{80,16},{96,32},{112,48},{1... | collective-permute-start | bytes 294920 | tf_op jit(solution)/shard_map/ppermute | solution.py:434
  87.7 22.7 %collective-permute-start = (bf16[8,64,192]{2,1,0:T(8,128)(2,1)}, bf16[8,64,192]{2,1,0:T(8,128)(2,1)S(1)}, u32[]{:S(2)}, u32[]{:S(2)}) collective-permute-start(bf16[8,64,192]{2,1,0:T(8,128)(2,1)} %get-tuple-element.51), channel_id=1, source_target_pairs={{0,1},{1,0},{2,3},{3,2},{4,5},{5,4},{6,7},{7,6},{8,9},{9,8},{10,11... | collective-permute-start | bytes 589832 | tf_op jit(solution)/shard_map/ppermute | solution.py:477
  89.5 0.6 copy-start.12
  89.5 0.7 copy-start.14
  89.5 0.7 copy-start.16
  92.0 3.7 %collective-permute-start.11 = (bf16[1,96,256]{2,1,0:T(8,128)(2,1)}, bf16[1,96,256]{2,1,0:T(8,128)(2,1)S(1)}, u32[]{:S(2)}, u32[]{:S(2)}) collective-permute-start(bf16[1,96,256]{2,1,0:T(8,128)(2,1)} %get-tuple-element.63), channel_id=1, source_target_pairs={{0,32},{16,48},{32,0},{48,16},{64,96},{80,112},{96,64},{112,80},{1... | collective-permute-start | bytes 147464 | tf_op jit(solution)/shard_map/ppermute | solution.py:434
  93.1 3.4 %collective-permute-start.12 = (bf16[1,96,256]{2,1,0:T(8,128)(2,1)}, bf16[1,96,256]{2,1,0:T(8,128)(2,1)S(1)}, u32[]{:S(2)}, u32[]{:S(2)}) collective-permute-start(bf16[1,96,256]{2,1,0:T(8,128)(2,1)} %get-tuple-element.64), channel_id=1, source_target_pairs={{0,64},{16,80},{32,96},{48,112},{64,0},{80,16},{96,32},{112,48},{1... | collective-permute-start | bytes 147464 | tf_op jit(solution)/shard_map/ppermute | solution.py:434
  94.6 4.4 %collective-permute-start.13 = (bf16[1,96,256]{2,1,0:T(8,128)(2,1)}, bf16[1,96,256]{2,1,0:T(8,128)(2,1)S(1)}, u32[]{:S(2)}, u32[]{:S(2)}) collective-permute-start(bf16[1,96,256]{2,1,0:T(8,128)(2,1)} %get-tuple-element.65), channel_id=1, source_target_pairs={{0,192},{16,208},{32,224},{48,240},{64,128},{80,144},{96,160},{112... | collective-permute-start | bytes 147464 | tf_op jit(solution)/shard_map/ppermute | solution.py:434
  95.7 3.3 %copy-start.18 = (bf16[1,96,256]{2,1,0:T(8,128)(2,1)}, bf16[1,96,256]{2,1,0:T(8,128)(2,1)S(1)}, u32[]{:S(2)}) copy-start(bf16[1,96,256]{2,1,0:T(8,128)(2,1)S(1)} %collective-permute-done.11.refs_1_) | copy-start | bytes 147460
  96.5 2.4 %copy-start.20 = (bf16[1,96,256]{2,1,0:T(8,128)(2,1)}, bf16[1,96,256]{2,1,0:T(8,128)(2,1)S(1)}, u32[]{:S(2)}) copy-start(bf16[1,96,256]{2,1,0:T(8,128)(2,1)S(1)} %collective-permute-done.12.refs_2_) | copy-start | bytes 147460
  99.0 0.6 copy-start.22
  101.2 3.2 %collective-permute-start.14 = (bf16[1,96,256]{2,1,0:T(8,128)(2,1)}, bf16[1,96,256]{2,1,0:T(8,128)(2,1)S(1)}, u32[]{:S(2)}, u32[]{:S(2)}) collective-permute-start(bf16[1,96,256]{2,1,0:T(8,128)(2,1)} %get-tuple-element.66.refs_0_), channel_id=1, source_target_pairs={{0,32},{16,48},{32,0},{48,16},{64,96},{80,112},{96,64},{112,80},{1... | collective-permute-start | bytes 147464 | tf_op jit(solution)/shard_map/ppermute | solution.py:434
  101.5 3.2 %collective-permute-start.15 = (bf16[1,96,256]{2,1,0:T(8,128)(2,1)}, bf16[1,96,256]{2,1,0:T(8,128)(2,1)S(1)}, u32[]{:S(2)}, u32[]{:S(2)}) collective-permute-start(bf16[1,96,256]{2,1,0:T(8,128)(2,1)} %get-tuple-element.67.refs_1_), channel_id=1, source_target_pairs={{0,64},{16,80},{32,96},{48,112},{64,0},{80,16},{96,32},{112,48},{1... | collective-permute-start | bytes 147464 | tf_op jit(solution)/shard_map/ppermute | solution.py:434
  101.5 4.4 %collective-permute-start.16 = (bf16[1,96,256]{2,1,0:T(8,128)(2,1)}, bf16[1,96,256]{2,1,0:T(8,128)(2,1)S(1)}, u32[]{:S(2)}, u32[]{:S(2)}) collective-permute-start(bf16[1,96,256]{2,1,0:T(8,128)(2,1)} %get-tuple-element.68.refs_2_), channel_id=1, source_target_pairs={{0,192},{16,208},{32,224},{48,240},{64,128},{80,144},{96,160},{112... | collective-permute-start | bytes 147464 | tf_op jit(solution)/shard_map/ppermute | solution.py:434
  104.3 1.5 %copy-start.19 = (bf16[1,96,256]{2,1,0:T(8,128)(2,1)}, bf16[1,96,256]{2,1,0:T(8,128)(2,1)S(1)}, u32[]{:S(2)}) copy-start(bf16[1,96,256]{2,1,0:T(8,128)(2,1)S(1)} %collective-permute-done.14.refs_3_) | copy-start | bytes 147460
  104.6 1.2 copy-start.21
  105.8 0.6 copy-start.23
  108.1 4.9 %collective-permute-start.17 = (bf16[2,96,256]{2,1,0:T(8,128)(2,1)}, bf16[2,96,256]{2,1,0:T(8,128)(2,1)S(1)}, u32[]{:S(2)}, u32[]{:S(2)}) collective-permute-start(bf16[2,96,256]{2,1,0:T(8,128)(2,1)} %get-tuple-element.69.refs_0_), channel_id=1, source_target_pairs={{0,192},{16,208},{32,224},{48,240},{64,128},{80,144},{96,160},{112... | collective-permute-start | bytes 294920 | tf_op jit(solution)/shard_map/ppermute | solution.py:434
  109.2 3.8 %collective-permute-start.18 = (bf16[2,96,256]{2,1,0:T(8,128)(2,1)}, bf16[2,96,256]{2,1,0:T(8,128)(2,1)S(1)}, u32[]{:S(2)}, u32[]{:S(2)}) collective-permute-start(bf16[2,96,256]{2,1,0:T(8,128)(2,1)} %get-tuple-element.70.refs_1_), channel_id=1, source_target_pairs={{0,32},{16,48},{32,0},{48,16},{64,96},{80,112},{96,64},{112,80},{1... | collective-permute-start | bytes 294920 | tf_op jit(solution)/shard_map/ppermute | solution.py:434
  110.4 3.7 %collective-permute-start.19 = (bf16[2,96,256]{2,1,0:T(8,128)(2,1)}, bf16[2,96,256]{2,1,0:T(8,128)(2,1)S(1)}, u32[]{:S(2)}, u32[]{:S(2)}) collective-permute-start(bf16[2,96,256]{2,1,0:T(8,128)(2,1)} %get-tuple-element.71.refs_2_), channel_id=1, source_target_pairs={{0,64},{16,80},{32,96},{48,112},{64,0},{80,16},{96,32},{112,48},{1... | collective-permute-start | bytes 294920 | tf_op jit(solution)/shard_map/ppermute | solution.py:434
  111.4 12.9 %collective-permute-start.1 = (bf16[4,64,192]{2,1,0:T(8,128)(2,1)S(1)}, bf16[4,64,192]{2,1,0:T(8,128)(2,1)S(1)}, u32[]{:S(2)}, u32[]{:S(2)}) collective-permute-start(bf16[4,64,192]{2,1,0:T(8,128)(2,1)S(1)} %slice.25), channel_id=1, source_target_pairs={{0,2},{1,3},{2,0},{3,1},{4,6},{5,7},{6,4},{7,5},{8,10},{9,11},{10,... | collective-permute-start | bytes 294920 | tf_op jit(solution)/shard_map/ppermute | solution.py:477
  113.0 1.0 copy-start.13
  113.0 1.0 copy-start.15
  114.0 0.6 copy-start.17
  116.9 20.8 %collective-permute-start.23 = (bf16[3,4,96,256]{3,2,1,0:T(8,128)(2,1)}, bf16[3,4,96,256]{3,2,1,0:T(8,128)(2,1)S(1)}, u32[]{:S(2)}, u32[]{:S(2)}) collective-permute-start(bf16[3,4,96,256]{3,2,1,0:T(8,128)(2,1)} %get-tuple-element.72.refs_0_), channel_id=1, source_target_pairs={{0,16},{16,0},{32,48},{48,32},{64,80},{80,64},{96,112},{112,96},{1... | collective-permute-start | bytes 1769480 | tf_op jit(solution)/shard_map/ppermute | solution.py:438
  124.3 7.1 %collective-permute-start.2 = (bf16[2,64,192]{2,1,0:T(8,128)(2,1)S(1)}, bf16[2,64,192]{2,1,0:T(8,128)(2,1)S(1)}, u32[]{:S(2)}, u32[]{:S(2)}) collective-permute-start(bf16[2,64,192]{2,1,0:T(8,128)(2,1)S(1)} %slice.27), channel_id=1, source_target_pairs={{0,4},{1,5},{2,6},{3,7},{4,0},{5,1},{6,2},{7,3},{8,12},{9,13},{10,... | collective-permute-start | bytes 147464 | tf_op jit(solution)/shard_map/ppermute | solution.py:477
  126.2 6.0 %collective-permute-start.20 = (bf16[4,96,256]{2,1,0:T(8,128)(2,1)}, bf16[4,96,256]{2,1,0:T(8,128)(2,1)S(1)}, u32[]{:S(2)}, u32[]{:S(2)}) collective-permute-start(bf16[4,96,256]{2,1,0:T(8,128)(2,1)} %get-tuple-element.73), channel_id=1, source_target_pairs={{0,64},{16,80},{32,96},{48,112},{64,0},{80,16},{96,32},{112,48},{1... | collective-permute-start | bytes 589832 | tf_op jit(solution)/shard_map/ppermute | solution.py:434
  126.7 9.2 %collective-permute-start.21 = (bf16[4,96,256]{2,1,0:T(8,128)(2,1)}, bf16[4,96,256]{2,1,0:T(8,128)(2,1)S(1)}, u32[]{:S(2)}, u32[]{:S(2)}) collective-permute-start(bf16[4,96,256]{2,1,0:T(8,128)(2,1)} %get-tuple-element.74), channel_id=1, source_target_pairs={{0,192},{16,208},{32,224},{48,240},{64,128},{80,144},{96,160},{112... | collective-permute-start | bytes 589832 | tf_op jit(solution)/shard_map/ppermute | solution.py:434
  128.0 8.0 %collective-permute-start.22 = (bf16[4,96,256]{2,1,0:T(8,128)(2,1)}, bf16[4,96,256]{2,1,0:T(8,128)(2,1)S(1)}, u32[]{:S(2)}, u32[]{:S(2)}) collective-permute-start(bf16[4,96,256]{2,1,0:T(8,128)(2,1)} %get-tuple-element.75), channel_id=1, source_target_pairs={{0,32},{16,48},{32,0},{48,16},{64,96},{80,112},{96,64},{112,80},{1... | collective-permute-start | bytes 589832 | tf_op jit(solution)/shard_map/ppermute | solution.py:434
  131.5 5.1 %collective-permute-start.3 = (bf16[1,64,192]{2,1,0:T(8,128)(2,1)S(1)}, bf16[1,64,192]{2,1,0:T(8,128)(2,1)S(1)}, u32[]{:S(2)}, u32[]{:S(2)}) collective-permute-start(bf16[1,64,192]{2,1,0:T(8,128)(2,1)S(1)} %slice.29), channel_id=1, source_target_pairs={{0,8},{1,9},{2,10},{3,11},{4,12},{5,13},{6,14},{7,15},{8,0},{9,1},... | collective-permute-start | bytes 73736 | tf_op jit(solution)/shard_map/ppermute | solution.py:477
  132.2 5.5 %copy-start.3 = (bf16[4,96,256]{2,1,0:T(8,128)(2,1)}, bf16[4,96,256]{2,1,0:T(8,128)(2,1)S(1)}, u32[]{:S(2)}) copy-start(bf16[4,96,256]{2,1,0:T(8,128)(2,1)S(1)} %collective-permute-done.20.refs_1_) | copy-start | bytes 589828
  132.2 5.0 %collective-permute-start.24 = (bf16[4,96,256]{2,1,0:T(8,128)(2,1)S(1)}, bf16[4,96,256]{2,1,0:T(8,128)(2,1)S(1)}, u32[]{:S(2)}, u32[]{:S(2)}) collective-permute-start(bf16[4,96,256]{2,1,0:T(8,128)(2,1)S(1)} %collective-permute-done.20.refs_1_), channel_id=1, source_target_pairs={{0,16},{16,0},{32,48},{48,32},{64,80},{80,64},{96,112},{112,96},{1... | collective-permute-start | bytes 589832 | tf_op jit(solution)/shard_map/ppermute | solution.py:438
  135.9 1.8 %copy-start.4 = (bf16[4,96,256]{2,1,0:T(8,128)(2,1)}, bf16[4,96,256]{2,1,0:T(8,128)(2,1)S(1)}, u32[]{:S(2)}) copy-start(bf16[4,96,256]{2,1,0:T(8,128)(2,1)S(1)} %collective-permute-done.21.refs_2_) | copy-start | bytes 589828
  135.9 1.4 %collective-permute-start.25 = (bf16[4,96,256]{2,1,0:T(8,128)(2,1)S(1)}, bf16[4,96,256]{2,1,0:T(8,128)(2,1)S(1)}, u32[]{:S(2)}, u32[]{:S(2)}) collective-permute-start(bf16[4,96,256]{2,1,0:T(8,128)(2,1)S(1)} %collective-permute-done.21.refs_2_), channel_id=1, source_target_pairs={{0,16},{16,0},{32,48},{48,32},{64,80},{80,64},{96,112},{112,96},{1... | collective-permute-start | bytes 589832 | tf_op jit(solution)/shard_map/ppermute | solution.py:438
  136.0 1.7 %copy-start.5 = (bf16[4,96,256]{2,1,0:T(8,128)(2,1)}, bf16[4,96,256]{2,1,0:T(8,128)(2,1)S(1)}, u32[]{:S(2)}) copy-start(bf16[4,96,256]{2,1,0:T(8,128)(2,1)S(1)} %collective-permute-done.22.refs_3_) | copy-start | bytes 589828
  136.1 1.6 %collective-permute-start.26 = (bf16[4,96,256]{2,1,0:T(8,128)(2,1)S(1)}, bf16[4,96,256]{2,1,0:T(8,128)(2,1)S(1)}, u32[]{:S(2)}, u32[]{:S(2)}) collective-permute-start(bf16[4,96,256]{2,1,0:T(8,128)(2,1)S(1)} %collective-permute-done.22.refs_3_), channel_id=1, source_target_pairs={{0,16},{16,0},{32,48},{48,32},{64,80},{80,64},{96,112},{112,96},{1... | collective-permute-start | bytes 589832 | tf_op jit(solution)/shard_map/ppermute | solution.py:438
  137.3 0.7 copy-start.6
  137.3 0.7 copy-start.7
  137.7 0.7 copy-start.8
  138.4 0.8 copy-start.2

commit v2 on v0

v2 whole, which is shorter than its diff:
```python
import functools
import math

import jax
import jax.numpy as jnp
from jax import lax
from jax.experimental import pallas as pl
from jax.experimental.pallas import tpu as pltpu
from jax.sharding import PartitionSpec as P

bf16 = jnp.bfloat16
f32 = jnp.float32
floor_score = -1e30
floor_top = -1e20

HEADS = 8
ROWS = 128
NOPE = 128
ROT = 64
LAT = 512
WIDE = LAT + ROT
KEYS = 2048
BLK = 256
NBLK = KEYS // BLK
ALL = HEADS * ROWS
PEERS = 16
COLS = WIDE // 2
SCALE = 1.0 / math.sqrt(NOPE + ROT)
SCALE2 = SCALE * math.log2(math.e)
VLIM = 12 * 1024 * 1024

NT = (((1,), (1,)), ((), ()))


def dot(a, b):
    return jnp.dot(a, b, preferred_element_type=f32)


def dot_nt(a, b):
    return lax.dot_general(a, b, NT, preferred_element_type=f32)


def params(limit=VLIM):
    return pltpu.CompilerParams(vmem_limit_bytes=limit)


in_vmem = pl.BlockSpec(memory_space=pltpu.VMEM)
in_hbm = pl.BlockSpec(memory_space=pltpu.HBM)
in_smem = pl.BlockSpec(memory_space=pltpu.SMEM)


def call(kernel, name, outs, args, scalars=0, scratch=(), limit=VLIM):
    return pl.pallas_call(
        kernel,
        in_specs=[in_smem] * scalars + [in_vmem] * (len(args) - scalars),
        out_specs=[in_vmem] * len(outs),
        out_shape=[jax.ShapeDtypeStruct(shape, kind) for shape, kind in outs],
        scratch_shapes=list(scratch),
        compiler_params=params(limit),
        name=name,
    )(*args)


CHUNK = 256


def pass_one(
    base, off, qt, wuk, wuv, og, lat,
    e_out, dp_out, qcat_out, dlat_out, stat,
    qt_v, wuk_v, wuv_v, og_v, lat_v, og_wide, qcat, dlat, e_v, dp_v, top, tot, dsum, hide,
    sem_in, sem_e, sem_dp, sem_q,
):
    pairs = ((qt, qt_v), (wuk, wuk_v), (og, og_v), (wuv, wuv_v), (lat, lat_v))
    loads = [pltpu.make_async_copy(a, b, sem_in.at[k]) for k, (a, b) in enumerate(pairs)]
    for copy in loads:
        copy.start()
    bound = jnp.broadcast_to(off[...], (ROWS, ROWS)).T - base[0]
    bound = jnp.concatenate([bound] * (BLK // 128), axis=1)
    lane = lax.broadcasted_iota(jnp.int32, (ROWS, BLK), 1)
    top[...] = jnp.full((ALL, 128), floor_top, f32)
    tot[...] = jnp.zeros((ALL, 128), f32)
    dsum[...] = jnp.zeros((ALL, 128), f32)
    chunks = [slice(c * CHUNK, (c + 1) * CHUNK) for c in range(ALL // CHUNK)]
    heads = [slice(h * ROWS, (h + 1) * ROWS) for h in range(HEADS)]

    loads[0].wait()
    loads[1].wait()
    for h, rows in enumerate(heads):
        q = qt_v[h].T
        qcat[rows, :LAT] = dot(q[:, :NOPE], wuk_v[h]).astype(bf16)
        qcat[rows, LAT:] = q[:, NOPE:]
    loads[2].wait()
    loads[3].wait()
    og_wide[...] = og_v[...].astype(f32)
    for h, rows in enumerate(heads):
        grad = og_wide[pl.ds(h, ROWS, stride=HEADS), :].astype(bf16)
        dlat[rows, :] = dot_nt(grad, wuv_v[h]).astype(bf16)
    loads[4].wait()
    saves = [
        pltpu.make_async_copy(qcat, qcat_out, sem_q.at[0]),
        pltpu.make_async_copy(dlat, dlat_out, sem_q.at[1]),
    ]
    for copy in saves:
        copy.start()

    def score(j, _):
        at = pl.multiple_of(j * BLK, BLK)
        hide[...] = jnp.where(lane + at <= bound, 0.0, floor_score)
        cols = lat_v[:, pl.ds(at, BLK)]
        for rows in chunks:
            s = dot(qcat[rows, :], cols)
            s = (s.reshape(CHUNK // ROWS, ROWS, BLK) + hide[...][None]).reshape(CHUNK, BLK)
            e_v[j, rows, :] = s
            best = top[rows, :]
            for k in range(BLK // 128):
                best = jnp.maximum(best, s[:, k * 128 : (k + 1) * 128])
            top[rows, :] = best
        return 0

    lax.fori_loop(0, NBLK, score, 0)
    top[...] = jnp.broadcast_to(jnp.max(top[...], axis=1, keepdims=True) * SCALE2, (ALL, 128))

    def outgoing(j):
        return (
            pltpu.make_async_copy(e_v.at[j], e_out.at[j], sem_e.at[j]),
            pltpu.make_async_copy(dp_v.at[j], dp_out.at[j], sem_dp.at[j]),
        )

    def weigh(j, _):
        cols = lat_v[:LAT, pl.ds(pl.multiple_of(j * BLK, BLK), BLK)]
        for rows in chunks:
            dp = dot(dlat[rows, :], cols)
            dp_v[j, rows, :] = dp
            s = e_v[j, rows, :]
            m = top[rows, :]
            t, d = tot[rows, :], dsum[rows, :]
            for k in range(BLK // 128):
                lanes = slice(k * 128, (k + 1) * 128)
                e = jnp.exp2(s[:, lanes] * SCALE2 - m)
                e_v[j, rows, lanes] = e
                t = t + e
                d = d + e * dp[:, lanes]
            tot[rows, :] = t
            dsum[rows, :] = d
        for copy in outgoing(j):
            copy.start()
        return 0

    lax.fori_loop(0, NBLK, weigh, 0)
    near = lane[:, :128]
    for h, rows in enumerate(heads):
        t = jnp.sum(tot[rows, :], axis=1, keepdims=True)
        d = jnp.sum(dsum[rows, :], axis=1, keepdims=True)
        x = jnp.where(near == 0, top[rows, :], jnp.where(near == 1, t, d)).T
        for k in range(3):
            line = x[k : k + 1, :]
            for peer in range(PEERS):
                stat[peer, k * 8 + h : k * 8 + h + 1, :] = line
    for j in range(NBLK):
        for copy in outgoing(j):
            copy.wait()
    for copy in saves:
        copy.wait()


def run_pass_one(base, offsets, qt, wuk, wuv, og, lat_t):
    big = (NBLK, ALL, BLK)
    outs = [(big, f32), (big, f32), ((ALL, WIDE), bf16), ((ALL, LAT), bf16)]
    outs += [((PEERS, 24, 128), f32)]
    column = pltpu.VMEM((ALL, 128), f32)
    return pl.pallas_call(
        pass_one,
        in_specs=[in_smem, in_vmem] + [in_hbm] * 5,
        out_specs=[in_hbm] * 4 + [in_vmem],
        out_shape=[jax.ShapeDtypeStruct(shape, kind) for shape, kind in outs],
        scratch_shapes=[pltpu.VMEM(a.shape, bf16) for a in (qt, wuk, wuv, og, lat_t)]
        + [
            column,
            pltpu.VMEM((ALL, WIDE), bf16),
            pltpu.VMEM((ALL, LAT), bf16),
            pltpu.VMEM(big, f32),
            pltpu.VMEM(big, f32),
            column,
            column,
            column,
            pltpu.VMEM((ROWS, BLK), f32),
            pltpu.SemaphoreType.DMA((5,)),
            pltpu.SemaphoreType.DMA((NBLK,)),
            pltpu.SemaphoreType.DMA((NBLK,)),
            pltpu.SemaphoreType.DMA((2,)),
        ],
        compiler_params=params(60 * 1024 * 1024),
        name="pass_one",
    )(base, offsets, qt, wuk, wuv, og, lat_t)


def turn(qcat, dlat, qcat_t, dlat_t):
    for h in range(HEADS):
        rows = slice(h * ROWS, (h + 1) * ROWS)
        for k in range(LAT // 128):
            lanes = slice(k * 128, (k + 1) * 128)
            qcat_t[lanes, rows] = qcat[rows, lanes].T
            dlat_t[lanes, rows] = dlat[rows, lanes].T
        qcat_t[LAT:, rows] = qcat[rows, LAT:].T


def run_turn(qcat, dlat):
    return call(turn, "turn", [((WIDE, ALL), bf16), ((LAT, ALL), bf16)], (qcat, dlat))


def place(half, r):
    return jnp.where(half == 0, r[0] * 4 + r[1] * 2 + r[2], r[1] * 4 + r[2] * 2 + r[0])


def key_block(r0, r1, sc):
    return sc[3] * 4 + jnp.bitwise_xor(sc[1], r1) * 2 + jnp.bitwise_xor(sc[0], r0)


def second_load(sc, e, dp, e_v, dp_v, sem):
    loads = []
    for i in range(4):
        kb = key_block(i & 1, i >> 1, sc)
        loads.append(
            (
                pltpu.make_async_copy(e.at[kb], e_v.at[i], sem.at[0, i]),
                pltpu.make_async_copy(dp.at[kb], dp_v.at[i], sem.at[1, i]),
            )
        )
        for copy in loads[i]:
            copy.start()
    return loads


def second_core(sc, loads, qcat_t, dlat_t, coef, delta, x_out, ds_out, e_v, dp_v, pb):
    for i in range(4):
        for copy in loads[i]:
            copy.wait()
        for c in range(ALL // CHUNK):
            rows = slice(c * CHUNK, (c + 1) * CHUNK)
            cf, dl = coef[rows, :], delta[rows, :]
            for k in range(BLK // 128):
                lanes = slice(k * 128, (k + 1) * 128)
                p = e_v[i, rows, lanes] * cf
                pb[i, rows, lanes] = p.astype(bf16)
                ds_out[i, rows, lanes] = (p * (dp_v[i, rows, lanes] - dl)).astype(bf16)
        scores = dot(qcat_t[...], ds_out[i]) * SCALE
        values = dot(dlat_t[...], pb[i])
        low = (scores[:LAT] + values).astype(bf16)
        high = scores[LAT:].astype(bf16)
        for h in range(2):
            at = place(sc[3], (i & 1, i >> 1, jnp.bitwise_xor(sc[2], h)))
            if h == 0:
                x_out[at] = low[:COLS]
            else:
                x_out[at, : LAT - COLS, :] = low[COLS:]
                x_out[at, LAT - COLS :, :] = high


def second_first(
    sc, stat, qcat_t, dlat_t, e, dp, x_out, ds_out, coef, delta, e_v, dp_v, pb, sem
):
    loads = second_load(sc, e, dp, e_v, dp_v, sem)
    m = stat[:, 0:8, :]
    best = jnp.max(m, axis=0)
    w = jnp.exp2(m - best[None])
    total = jnp.sum(w * stat[:, 8:16, :], axis=0)
    dtotal = jnp.sum(w * stat[:, 16:24, :], axis=0)
    cf = jnp.exp2(stat[sc[4], 0:8, :] - best) / total
    dl = dtotal / total
    for h in range(HEADS):
        rows = slice(h * ROWS, (h + 1) * ROWS)
        coef[rows, :] = jnp.broadcast_to(cf[h : h + 1], (128, 128)).T
        delta[rows, :] = jnp.broadcast_to(dl[h : h + 1], (128, 128)).T
    second_core(sc, loads, qcat_t, dlat_t, coef, delta, x_out, ds_out, e_v, dp_v, pb)


def second_later(
    sc, coef, delta, qcat_t, dlat_t, e, dp, x_out, ds_out, e_v, dp_v, pb, sem
):
    loads = second_load(sc, e, dp, e_v, dp_v, sem)
    second_core(sc, loads, qcat_t, dlat_t, coef, delta, x_out, ds_out, e_v, dp_v, pb)


def run_second(sc, heads_in, e, dp, qcat_t, dlat_t, first):
    outs = [((8, COLS, BLK), bf16), ((4, ALL, BLK), bf16)]
    if first:
        outs += [((ALL, 128), f32)] * 2
    return pl.pallas_call(
        second_first if first else second_later,
        in_specs=[in_smem] + [in_vmem] * (len(heads_in) + 2) + [in_hbm] * 2,
        out_specs=[in_vmem] * len(outs),
        out_shape=[jax.ShapeDtypeStruct(shape, kind) for shape, kind in outs],
        scratch_shapes=[
            pltpu.VMEM((4, ALL, BLK), f32),
            pltpu.VMEM((4, ALL, BLK), f32),
            pltpu.VMEM((4, ALL, BLK), bf16),
            pltpu.SemaphoreType.DMA((2, 4)),
        ],
        compiler_params=params(50 * 1024 * 1024),
        name="second_first" if first else "second_later",
    )(sc, *heads_in, qcat_t, dlat_t, e, dp)


def query_grad(sc_a, sc_b, ds_a, ds_b, lat, wuk, out, acc, wide):
    for n, (sc, ds) in enumerate(((sc_a, ds_a), (sc_b, ds_b))):
        for i in range(4):
            kb = key_block(i & 1, i >> 1, sc)
            part = dot_nt(ds[i], lat[:, pl.ds(pl.multiple_of(kb * BLK, BLK), BLK)])
            acc[...] = part if n + i == 0 else acc[...] + part
    for h in range(HEADS):
        rows = slice(h * ROWS, (h + 1) * ROWS)
        x = acc[rows, :LAT] * SCALE
        hi = x.astype(bf16)
        lo = (x - hi.astype(f32)).astype(bf16)
        wide[h, :, :NOPE] = dot_nt(hi, wuk[h]) + dot_nt(lo, wuk[h])
        wide[h, :, NOPE:] = acc[rows, LAT:] * SCALE
    for g in range(PEERS):
        out[g] = wide[:, g * 8 : (g + 1) * 8, :].reshape(HEADS * 8, NOPE + ROT).astype(bf16)


def run_query_grad(sc_a, sc_b, ds_a, ds_b, lat_t, wuk):
    outs = [((PEERS, HEADS * 8, NOPE + ROT), bf16)]
    scratch = [pltpu.VMEM((ALL, WIDE), f32), pltpu.VMEM((HEADS, ROWS, NOPE + ROT), f32)]
    args = (sc_a, sc_b, ds_a, ds_b, lat_t, wuk)
    return call(query_grad, "query_grad", outs, args, 2, scratch)[0]


def halve(kept, got, *outs):
    n = kept.shape[0]
    for k in range(n):
        total = (kept[k].astype(f32) + got[k].astype(f32)).astype(bf16)
        outs[k * len(outs) // n][k % (n // len(outs))] = total


def run_halve(kept, got):
    n = kept.shape[0]
    outs = [((max(n // 2, 1), COLS, BLK), bf16)] * min(n, 2)
    return call(halve, "halve", outs, (kept, got))


def join(own, got, out):
    n = own.shape[0]
    out[:n] = own[...]
    out[n:] = got[...]


def run_join(own, got):
    return call(join, "join", [((2 * own.shape[0], COLS, BLK), bf16)], (own, got))[0]


def settle(sc, mine, mine_far, other, other_far, out):
    for near, far, half in ((mine, mine_far, sc[3]), (other, other_far, 1 - sc[3])):
        for i in range(8):
            b = (i >> 2 & 1, i >> 1 & 1, i & 1)
            r = [jnp.where(half == 0, b[d], b[(d + 2) % 3]) for d in range(3)]
            a = [jnp.bitwise_xor(sc[d], r[d]) for d in range(3)]
            rows = pl.ds(pl.multiple_of(a[2] * COLS, 32), COLS)
            lanes = pl.ds(pl.multiple_of((half * 4 + a[1] * 2 + a[0]) * BLK, BLK), BLK)
            out[rows, lanes] = near[i] if i < 4 else far[i - 4]


def run_settle(sc, *pieces):
    return call(settle, "settle", [((WIDE, KEYS), bf16)], (sc, *pieces), 1)[0]


def cube_neighbour(k, d):
    y, rest = k >> 2, k & 3
    if d == 2:
        return k ^ 2
    gray = (y ^ (y >> 1)) ^ (1 << d)
    back = gray ^ (gray >> 1)
    return back * 4 + rest


def along(value, n):
    pairs = [(k, cube_neighbour(k, (n + (k & 1)) % 3)) for k in range(16)]
    return lax.ppermute(value, "head", pairs)


def to_sibling(value):
    return lax.ppermute(value, "head", [(k, k ^ 1) for k in range(16)])


def shards(queries, w_uk, w_uv, latent, out_grad, offsets):
    head = lax.axis_index("head").astype(jnp.int32)
    key = lax.axis_index("key").astype(jnp.int32)
    y = head >> 2
    gray = y ^ (y >> 1)
    core = head & 1
    sc_own = jnp.stack([gray & 1, gray >> 1, (head >> 1) & 1, core, key])
    sc_far = jnp.stack([gray & 1, gray >> 1, (head >> 1) & 1, 1 - core, key])
    lat_t = latent.T
    qt = jnp.transpose(queries, (1, 2, 0))
    og = out_grad.reshape(ALL, 128)
    e, dp, qcat, dlat, stat = run_pass_one(
        (key * KEYS)[None], offsets[None], qt, w_uk, w_uv, og, lat_t
    )
    stat = lax.all_to_all(stat, "key", 0, 0, tiled=True)
    qcat_t, dlat_t = run_turn(qcat, dlat)
    x_far, ds_far, coef, delta = run_second(sc_far, (stat,), e, dp, qcat_t, dlat_t, True)
    came = to_sibling(x_far)
    x_own, ds_own = run_second(sc_own, (coef, delta), e, dp, qcat_t, dlat_t, False)
    kept, send = run_halve(x_own, came)
    got = along(send, 0)
    dq = run_query_grad(sc_far, sc_own, ds_far, ds_own, lat_t, w_uk)
    got, dq = lax.optimization_barrier((got, dq))
    kept, send = run_halve(kept, got)
    send, dq = lax.optimization_barrier((send, dq))
    got = along(send, 1)
    dq = lax.all_to_all(dq, "key", 0, 0, tiled=True)
    kept, send = run_halve(kept, got)
    (own,) = run_halve(kept, along(send, 2))
    own = run_join(own, along(own, 2))
    own, dq = lax.optimization_barrier((own, dq))
    near = run_join(own, along(own, 1))
    far = along(near, 0)
    d_latent = run_settle(sc_own, near, far, to_sibling(near), to_sibling(far)).T

    total = jnp.sum(dq.astype(f32), axis=0).astype(bf16)
    d_queries = jnp.transpose(total.reshape(HEADS, 8, NOPE + ROT), (1, 0, 2))
    return (d_queries, d_latent)


def solution(mesh):
    return jax.shard_map(
        shards,
        mesh=mesh,
        in_specs=(
            P(None, "head", None),
            P("head", None, None),
            P("head", None, None),
            P("key", None),
            P(None, "head", None),
            P(),
        ),
        out_specs=(P("key", "head", None), P("key", None)),
        check_vma=False,
    )
```

time: 205 us -> 115 us (0.56)
  the two profiles are of different devices: /device:TPU:1 before, /device:TPU:61 now
where the time goes in v2:
time: 115 us
  Pallas kernels  40 us (35%)
  starting transfers between devices  37.3 us (32%)
  waiting for transfers between devices  29.5 us (26%)
  local copies, waits for them, and re-layouts  7 us (6%)
    ppermute x6, waiting for transfers between devices, along(): return lax.ppermute(value, 'head', pairs)  24.8 us
    ppermute x3, starting transfers between devices, to_sibling(): return lax.ppermute(value, 'head', [(k, k ^ 1) for k in range(16)])  18.1 us
    pallas_call x2, Pallas kernels, run_second(): pl.pallas_call(second_first if first else second_later, in_specs=[in_smem...  15.9 us
    pallas_call x1, Pallas kernels, run_pass_one(): pl.pallas_call(pass_one, in_specs=[in_smem, in_vmem] + [in_hbm] * 5, out_...  15 us
    all_to_all x1, starting transfers between devices, shards(): stat = lax.all_to_all(stat, 'key', 0, 0, tiled=True)  10.4 us
    pallas_call x9, Pallas kernels, call(): pl.pallas_call(kernel, in_specs=[in_smem] * scalars + [in_vmem] * (len(ar...  9.09 us
    unnamed x15, local copies, waits for them, and re-layouts  6.83 us
    all_to_all x1, starting transfers between devices, shards(): dq = lax.all_to_all(dq, 'key', 0, 0, tiled=True)  5.52 us
  transfers between devices with their start and end apart: 11, of which 8 were waited for; matrix products, arithmetic and copies ran while one was open for 1% of the time, Pallas kernels for 12%

profile of v2, /device:TPU:61, one launch (start us, length us, event | category | flops | bytes accessed | tf_op | source)
XLA Modules:
  0.0 114.7 jit_solution(4219821487074708694)
XLA Ops:
  0.6 15.0 %pass_one.1 = (f32[8,1024,256]{2,1,0:T(8,128)}, f32[8,1024,256]{2,1,0:T(8,128)}, bf16[1024,576]{1,0:T(8,128)(2,1)}, bf16[1024,512]{1,0:T(8,128)(2,1)}, f32[16,24,128]{2,1,0:T(8,128)}) custom-call(s32[1]{0:T(128)} %bitcast.6.base, s32[1,128]{1,0:T(1,128)} %bitcast.21, bf16[8,192,128]{2,1,0:T(8,128)(2,1)} %bitcast.18, bf16[8,128,512]{2,1,0:T(8,128)(2,1)} %wuk.3, ...), custom_call_target="tpu_custom_call" | custom-call | tf_op jit(solution)/shard_map/pass_one/pallas_call | solution.py:171
  15.7 10.4 %all-to-all-start = ((f32[16,24,128]{2,1,0:T(8,128)}), f32[16,24,128]{2,1,0:T(8,128)S(1)}, u32[]{:S(2)}, u32[]{:S(2)}) async-start(f32[16,24,128]{2,1,0:T(8,128)} %get-tuple-element.27), calls=%async_computation | async-start | bytes 393216 | tf_op jit(solution)/shard_map/all_to_all | solution.py:398
  26.1 0.0 copy-start.5
  26.1 1.3 %copy-done.5 = bf16[1024,576]{1,0:T(8,128)(2,1)S(1)} copy-done((bf16[1024,576]{1,0:T(8,128)(2,1)S(1)}, bf16[1024,576]{1,0:T(8,128)(2,1)}, u32[]{:S(2)}) %copy-start.5) | copy-done | bytes 1179672
  27.4 0.0 copy-start.6
  27.4 1.2 %copy-done.6 = bf16[1024,512]{1,0:T(8,128)(2,1)S(1)} copy-done((bf16[1024,512]{1,0:T(8,128)(2,1)S(1)}, bf16[1024,512]{1,0:T(8,128)(2,1)}, u32[]{:S(2)}) %copy-start.6) | copy-done | bytes 1048600
  28.6 0.7 turn.1
  29.3 0.0 copy-start.1
  29.3 1.0 copy-done.1
  30.4 0.1 stack.35.sc.sc_a
  30.4 3.8 %all-to-all-done.stat = f32[16,24,128]{2,1,0:T(8,128)S(1)} async-done(((f32[16,24,128]{2,1,0:T(8,128)}), f32[16,24,128]{2,1,0:T(8,128)S(1)}, u32[]{:S(2)}, u32[]{:S(2)}) %all-to-all-start) | async-done | bytes 196640 | tf_op jit(solution)/shard_map/all_to_all | solution.py:398
  34.2 8.0 %second_first.1 = (bf16[8,288,256]{2,1,0:T(8,128)(2,1)}, bf16[4,1024,256]{2,1,0:T(8,128)(2,1)}, f32[1024,128]{1,0:T(8,128)S(1)}, f32[1024,128]{1,0:T(8,128)S(1)}) custom-call(s32[5]{0:T(128)S(1)} %stack.35.sc.sc_a, f32[16,24,128]{2,1,0:T(8,128)S(1)} %all-to-all-done.stat, bf16[576,1024]{1,0:T(8,128)(2,1)} %copy-done.1, ...), custom_call_target="tpu_custom_call" | custom-call | tf_op jit(solution)/shard_map/second_first/pallas_call | solution.py:288
  42.2 1.9 %collective-permute-start = (bf16[8,288,256]{2,1,0:T(8,128)(2,1)}, bf16[8,288,256]{2,1,0:T(8,128)(2,1)S(1)}, u32[]{:S(2)}, u32[]{:S(2)}) collective-permute-start(bf16[8,288,256]{2,1,0:T(8,128)(2,1)} %get-tuple-element.37), channel_id=1, source_target_pairs={{0,16},{16,0},{32,48},{48,32},{64,80},{80,64},{96,112},{112,96},{1... | collective-permute-start | bytes 3538952 | tf_op jit(solution)/shard_map/ppermute | solution.py:381
  44.1 0.1 stack.33.sc.sc_b
  44.2 0.0 copy-start.2
  44.2 0.0 copy-start.3
  44.2 7.9 %second_later.1 = (bf16[8,288,256]{2,1,0:T(8,128)(2,1)S(1)}, bf16[4,1024,256]{2,1,0:T(8,128)(2,1)}) custom-call(s32[5]{0:T(128)S(1)} %stack.33.sc.sc_b, f32[1024,128]{1,0:T(8,128)S(1)} %get-tuple-element.34.coef, f32[1024,128]{1,0:T(8,128)S(1)} %get-tuple-element.35.delta, bf16[576,1024]{1,0:T(8,128)(2,1)} %copy-done.1, ...), custom_call_target="tpu_custom_call" | custom-call | tf_op jit(solution)/shard_map/second_later/pallas_call | solution.py:288
  52.1 0.0 copy-start
  52.1 0.0 collective-permute-done.got
  52.1 0.3 halve.4
  52.4 0.3 collective-permute-start.1
  52.7 0.0 copy-done.2
  52.7 0.0 copy-done.3
  52.7 1.0 copy-done
  53.8 0.0 copy-start.4
  53.8 1.6 %copy-done.4 = bf16[4,1024,256]{2,1,0:T(8,128)(2,1)S(1)} copy-done((bf16[4,1024,256]{2,1,0:T(8,128)(2,1)S(1)}, bf16[4,1024,256]{2,1,0:T(8,128)(2,1)}, u32[]{:S(2)}) %copy-start.4) | copy-done | bytes 2097176
  55.4 5.5 %query_grad.1 = bf16[16,64,192]{2,1,0:T(8,128)(2,1)} custom-call(s32[5]{0:T(128)S(1)} %stack.35.sc.sc_a, s32[5]{0:T(128)S(1)} %stack.33.sc.sc_b, bf16[4,1024,256]{2,1,0:T(8,128)(2,1)S(1)} %copy-done.3, bf16[4,1024,256]{2,1,0:T(8,128)(2,1)S(1)} %copy-done.4, bf16[576,2048]{1,0:T(8,128)(2,1)S(1)} %bitcast.16, bf16[8,128,512]{2,1,0:T(8,128)(2,1)S(1)} %copy-done.2), custom_call_target="tpu_custom_call" | custom-call | tf_op jit(solution)/shard_map/query_grad/pallas_call | solution.py:53
  60.9 1.8 %collective-permute-done.1.got = bf16[4,288,256]{2,1,0:T(8,128)(2,1)S(1)} collective-permute-done((bf16[4,288,256]{2,1,0:T(8,128)(2,1)S(1)}, bf16[4,288,256]{2,1,0:T(8,128)(2,1)S(1)}, u32[]{:S(2)}, u32[]{:S(2)}) %collective-permute-start.1) | collective-permute-done | bytes 589856 | tf_op jit(solution)/shard_map/ppermute | solution.py:377
  62.7 0.1 halve.5
  62.8 5.5 %all-to-all-start.1 = ((bf16[16,64,192]{2,1,0:T(8,128)(2,1)}), bf16[16,64,192]{2,1,0:T(8,128)(2,1)S(1)}, u32[]{:S(2)}, u32[]{:S(2)}) async-start(bf16[16,64,192]{2,1,0:T(8,128)(2,1)} %query_grad.1), calls=%async_computation.1 | async-start | bytes 1048576 | tf_op jit(solution)/shard_map/all_to_all | solution.py:410
  68.3 0.9 collective-permute-start.2
  69.2 6.2 %collective-permute-done.2.got = bf16[2,288,256]{2,1,0:T(8,128)(2,1)S(1)} collective-permute-done((bf16[2,288,256]{2,1,0:T(8,128)(2,1)S(1)}, bf16[2,288,256]{2,1,0:T(8,128)(2,1)S(1)}, u32[]{:S(2)}, u32[]{:S(2)}) %collective-permute-start.2) | collective-permute-done | bytes 294944 | tf_op jit(solution)/shard_map/ppermute | solution.py:377
  75.4 0.1 halve.6
  75.5 0.1 collective-permute-start.3
  75.6 4.3 %collective-permute-done.3.got = bf16[1,288,256]{2,1,0:T(8,128)(2,1)S(1)} collective-permute-done((bf16[1,288,256]{2,1,0:T(8,128)(2,1)S(1)}, bf16[1,288,256]{2,1,0:T(8,128)(2,1)S(1)}, u32[]{:S(2)}, u32[]{:S(2)}) %collective-permute-start.3) | collective-permute-done | bytes 147488 | tf_op jit(solution)/shard_map/ppermute | solution.py:377
  79.9 0.1 collective-permute-start.4
  80.0 4.3 %collective-permute-done.4.got = bf16[1,288,256]{2,1,0:T(8,128)(2,1)S(1)} collective-permute-done((bf16[1,288,256]{2,1,0:T(8,128)(2,1)S(1)}, bf16[1,288,256]{2,1,0:T(8,128)(2,1)S(1)}, u32[]{:S(2)}, u32[]{:S(2)}) %collective-permute-start.4) | collective-permute-done | bytes 147488 | tf_op jit(solution)/shard_map/ppermute | solution.py:377
  84.3 0.0 all-to-all-done.1
  84.3 1.8 %collective-permute-start.5 = (bf16[2,288,256]{2,1,0:T(8,128)(2,1)S(1)}, bf16[2,288,256]{2,1,0:T(8,128)(2,1)S(1)}, u32[]{:S(2)}, u32[]{:S(2)}) collective-permute-start(bf16[2,288,256]{2,1,0:T(8,128)(2,1)S(1)} %join.2.own), channel_id=1, source_target_pairs={{0,192},{16,48},{32,224},{48,16},{64,128},{80,112},{96,160},{112,8... | collective-permute-start | bytes 884744 | tf_op jit(solution)/shard_map/ppermute | solution.py:377
  86.1 5.4 %collective-permute-done.5.got = bf16[2,288,256]{2,1,0:T(8,128)(2,1)S(1)} collective-permute-done((bf16[2,288,256]{2,1,0:T(8,128)(2,1)S(1)}, bf16[2,288,256]{2,1,0:T(8,128)(2,1)S(1)}, u32[]{:S(2)}, u32[]{:S(2)}) %collective-permute-start.5) | collective-permute-done | bytes 294944 | tf_op jit(solution)/shard_map/ppermute | solution.py:377
  91.5 0.1 collective-permute-start.6
  91.6 9.4 %collective-permute-start.7 = (bf16[4,288,256]{2,1,0:T(8,128)(2,1)S(1)}, bf16[4,288,256]{2,1,0:T(8,128)(2,1)S(1)}, u32[]{:S(2)}, u32[]{:S(2)}) collective-permute-start(bf16[4,288,256]{2,1,0:T(8,128)(2,1)S(1)} %join.3.mine), channel_id=1, source_target_pairs={{0,16},{16,0},{32,48},{48,32},{64,80},{80,64},{96,112},{112,96},{1... | collective-permute-start | bytes 1769480 | tf_op jit(solution)/shard_map/ppermute | solution.py:381
  101.0 3.0 %collective-permute-done.6.mine_far = bf16[4,288,256]{2,1,0:T(8,128)(2,1)S(1)} collective-permute-done((bf16[4,288,256]{2,1,0:T(8,128)(2,1)S(1)}, bf16[4,288,256]{2,1,0:T(8,128)(2,1)S(1)}, u32[]{:S(2)}, u32[]{:S(2)}) %collective-permute-start.6) | collective-permute-done | bytes 589856 | tf_op jit(solution)/shard_map/ppermute | solution.py:377
  104.0 6.8 %collective-permute-start.8 = (bf16[4,288,256]{2,1,0:T(8,128)(2,1)S(1)}, bf16[4,288,256]{2,1,0:T(8,128)(2,1)S(1)}, u32[]{:S(2)}, u32[]{:S(2)}) collective-permute-start(bf16[4,288,256]{2,1,0:T(8,128)(2,1)S(1)} %collective-permute-done.6.mine_far), channel_id=1, source_target_pairs={{0,16},{16,0},{32,48},{48,32},{64,80},{80,64},{96,112},{112,96},{1... | collective-permute-start | bytes 1769480 | tf_op jit(solution)/shard_map/ppermute | solution.py:381
  110.8 0.1 reduce_sum.12
  110.9 0.6 copy.8
  111.5 0.0 collective-permute-done.7.other
  111.5 0.9 collective-permute-done.8.other_far
  112.4 2.3 %settle.1 = bf16[576,2048]{1,0:T(8,128)(2,1)} custom-call(s32[5]{0:T(128)S(1)} %stack.33.sc.sc_b, bf16[4,288,256]{2,1,0:T(8,128)(2,1)S(1)} %join.3.mine, bf16[4,288,256]{2,1,0:T(8,128)(2,1)S(1)} %collective-permute-done.6.mine_far, bf16[4,288,256]{2,1,0:T(8,128)(2,1)S(1)} %collective-permute-done.7.other, ...), custom_call_target="tpu_custom_call" | custom-call | tf_op jit(solution)/shard_map/settle/pallas_call | solution.py:53
  (3 shorter events, 0.1 us)
Async XLA Ops:
  15.7 18.5 %all-to-all-start = ((f32[16,24,128]{2,1,0:T(8,128)}), f32[16,24,128]{2,1,0:T(8,128)S(1)}, u32[]{:S(2)}, u32[]{:S(2)}) async-start(f32[16,24,128]{2,1,0:T(8,128)} %get-tuple-element.27), calls=%async_computation | async-start | bytes 393216 | tf_op jit(solution)/shard_map/all_to_all | solution.py:398
  26.1 1.3 %copy-start.5 = (bf16[1024,576]{1,0:T(8,128)(2,1)S(1)}, bf16[1024,576]{1,0:T(8,128)(2,1)}, u32[]{:S(2)}) copy-start(bf16[1024,576]{1,0:T(8,128)(2,1)} %get-tuple-element.28.qcat) | copy-start | bytes 3538948
  27.4 1.2 %copy-start.6 = (bf16[1024,512]{1,0:T(8,128)(2,1)S(1)}, bf16[1024,512]{1,0:T(8,128)(2,1)}, u32[]{:S(2)}) copy-start(bf16[1024,512]{1,0:T(8,128)(2,1)} %get-tuple-element.29.dlat) | copy-start | bytes 3145732
  29.3 1.0 copy-start.1
  42.2 9.9 %collective-permute-start = (bf16[8,288,256]{2,1,0:T(8,128)(2,1)}, bf16[8,288,256]{2,1,0:T(8,128)(2,1)S(1)}, u32[]{:S(2)}, u32[]{:S(2)}) collective-permute-start(bf16[8,288,256]{2,1,0:T(8,128)(2,1)} %get-tuple-element.37), channel_id=1, source_target_pairs={{0,16},{16,0},{32,48},{48,32},{64,80},{80,64},{96,112},{112,96},{1... | collective-permute-start | bytes 3538952 | tf_op jit(solution)/shard_map/ppermute | solution.py:381
  44.2 8.5 %copy-start.2 = (bf16[8,128,512]{2,1,0:T(8,128)(2,1)S(1)}, bf16[8,128,512]{2,1,0:T(8,128)(2,1)}, u32[]{:S(2)}) copy-start(bf16[8,128,512]{2,1,0:T(8,128)(2,1)} %wuk.3) | copy-start | bytes 3145732
  44.2 8.5 %copy-start.3 = (bf16[4,1024,256]{2,1,0:T(8,128)(2,1)S(1)}, bf16[4,1024,256]{2,1,0:T(8,128)(2,1)}, u32[]{:S(2)}) copy-start(bf16[4,1024,256]{2,1,0:T(8,128)(2,1)} %get-tuple-element.40.ds_a) | copy-start | bytes 6291460
  52.1 1.7 %copy-start = (bf16[2048,576]{0,1:T(8,128)(2,1)S(1)}, bf16[2048,576]{0,1:T(8,128)(2,1)}, u32[]{:S(2)}) copy-start(bf16[2048,576]{0,1:T(8,128)(2,1)} %param.9) | copy-start | bytes 7077892
  52.4 10.2 %collective-permute-start.1 = (bf16[4,288,256]{2,1,0:T(8,128)(2,1)S(1)}, bf16[4,288,256]{2,1,0:T(8,128)(2,1)S(1)}, u32[]{:S(2)}, u32[]{:S(2)}) collective-permute-start(bf16[4,288,256]{2,1,0:T(8,128)(2,1)S(1)} %get-tuple-element.39), channel_id=1, source_target_pairs={{0,64},{16,208},{32,96},{48,240},{64,0},{80,144},{96,32},{112,176}... | collective-permute-start | bytes 1769480 | tf_op jit(solution)/shard_map/ppermute | solution.py:377
  53.8 1.6 %copy-start.4 = (bf16[4,1024,256]{2,1,0:T(8,128)(2,1)S(1)}, bf16[4,1024,256]{2,1,0:T(8,128)(2,1)}, u32[]{:S(2)}) copy-start(bf16[4,1024,256]{2,1,0:T(8,128)(2,1)} %get-tuple-element.41.ds_b) | copy-start | bytes 6291460
  62.8 21.5 %all-to-all-start.1 = ((bf16[16,64,192]{2,1,0:T(8,128)(2,1)}), bf16[16,64,192]{2,1,0:T(8,128)(2,1)S(1)}, u32[]{:S(2)}, u32[]{:S(2)}) async-start(bf16[16,64,192]{2,1,0:T(8,128)(2,1)} %query_grad.1), calls=%async_computation.1 | async-start | bytes 1048576 | tf_op jit(solution)/shard_map/all_to_all | solution.py:410
  68.3 7.1 %collective-permute-start.2 = (bf16[2,288,256]{2,1,0:T(8,128)(2,1)S(1)}, bf16[2,288,256]{2,1,0:T(8,128)(2,1)S(1)}, u32[]{:S(2)}, u32[]{:S(2)}) collective-permute-start(bf16[2,288,256]{2,1,0:T(8,128)(2,1)S(1)} %get-tuple-element.46), channel_id=1, source_target_pairs={{0,192},{16,48},{32,224},{48,16},{64,128},{80,112},{96,160},{112,8... | collective-permute-start | bytes 884744 | tf_op jit(solution)/shard_map/ppermute | solution.py:377
  75.5 4.4 %collective-permute-start.3 = (bf16[1,288,256]{2,1,0:T(8,128)(2,1)S(1)}, bf16[1,288,256]{2,1,0:T(8,128)(2,1)S(1)}, u32[]{:S(2)}, u32[]{:S(2)}) collective-permute-start(bf16[1,288,256]{2,1,0:T(8,128)(2,1)S(1)} %get-tuple-element.48), channel_id=1, source_target_pairs={{0,32},{16,80},{32,0},{48,112},{64,96},{80,16},{96,64},{112,48},{1... | collective-permute-start | bytes 442376 | tf_op jit(solution)/shard_map/ppermute | solution.py:377
  79.9 4.4 %collective-permute-start.4 = (bf16[1,288,256]{2,1,0:T(8,128)(2,1)S(1)}, bf16[1,288,256]{2,1,0:T(8,128)(2,1)S(1)}, u32[]{:S(2)}, u32[]{:S(2)}) collective-permute-start(bf16[1,288,256]{2,1,0:T(8,128)(2,1)S(1)} %halve.7.own), channel_id=1, source_target_pairs={{0,32},{16,80},{32,0},{48,112},{64,96},{80,16},{96,64},{112,48},{1... | collective-permute-start | bytes 442376 | tf_op jit(solution)/shard_map/ppermute | solution.py:377
  84.3 7.2 %collective-permute-start.5 = (bf16[2,288,256]{2,1,0:T(8,128)(2,1)S(1)}, bf16[2,288,256]{2,1,0:T(8,128)(2,1)S(1)}, u32[]{:S(2)}, u32[]{:S(2)}) collective-permute-start(bf16[2,288,256]{2,1,0:T(8,128)(2,1)S(1)} %join.2.own), channel_id=1, source_target_pairs={{0,192},{16,48},{32,224},{48,16},{64,128},{80,112},{96,160},{112,8... | collective-permute-start | bytes 884744 | tf_op jit(solution)/shard_map/ppermute | solution.py:377
  91.5 12.4 %collective-permute-start.6 = (bf16[4,288,256]{2,1,0:T(8,128)(2,1)S(1)}, bf16[4,288,256]{2,1,0:T(8,128)(2,1)S(1)}, u32[]{:S(2)}, u32[]{:S(2)}) collective-permute-start(bf16[4,288,256]{2,1,0:T(8,128)(2,1)S(1)} %join.3.mine), channel_id=1, source_target_pairs={{0,64},{16,208},{32,96},{48,240},{64,0},{80,144},{96,32},{112,176}... | collective-permute-start | bytes 1769480 | tf_op jit(solution)/shard_map/ppermute | solution.py:377
  91.6 19.9 %collective-permute-start.7 = (bf16[4,288,256]{2,1,0:T(8,128)(2,1)S(1)}, bf16[4,288,256]{2,1,0:T(8,128)(2,1)S(1)}, u32[]{:S(2)}, u32[]{:S(2)}) collective-permute-start(bf16[4,288,256]{2,1,0:T(8,128)(2,1)S(1)} %join.3.mine), channel_id=1, source_target_pairs={{0,16},{16,0},{32,48},{48,32},{64,80},{80,64},{96,112},{112,96},{1... | collective-permute-start | bytes 1769480 | tf_op jit(solution)/shard_map/ppermute | solution.py:381
  104.0 8.4 %collective-permute-start.8 = (bf16[4,288,256]{2,1,0:T(8,128)(2,1)S(1)}, bf16[4,288,256]{2,1,0:T(8,128)(2,1)S(1)}, u32[]{:S(2)}, u32[]{:S(2)}) collective-permute-start(bf16[4,288,256]{2,1,0:T(8,128)(2,1)S(1)} %collective-permute-done.6.mine_far), channel_id=1, source_target_pairs={{0,16},{16,0},{32,48},{48,32},{64,80},{80,64},{96,112},{112,96},{1... | collective-permute-start | bytes 1769480 | tf_op jit(solution)/shard_map/ppermute | solution.py:381

commit v3 on v2

v3 whole, which is shorter than its diff:
```python
import functools
import math

import jax
import jax.numpy as jnp
from jax import lax
from jax.experimental import pallas as pl
from jax.experimental.pallas import tpu as pltpu
from jax.sharding import PartitionSpec as P

bf16 = jnp.bfloat16
f32 = jnp.float32
floor_score = -1e30
floor_top = -1e20

HEADS = 8
ROWS = 128
NOPE = 128
ROT = 64
LAT = 512
WIDE = LAT + ROT
KEYS = 2048
BLK = 256
NBLK = KEYS // BLK
ALL = HEADS * ROWS
PEERS = 16
COLS = WIDE // 4
CHAINS = 2
SCALE = 1.0 / math.sqrt(NOPE + ROT)
SCALE2 = SCALE * math.log2(math.e)
VLIM = 12 * 1024 * 1024

NT = (((1,), (1,)), ((), ()))


def dot(a, b):
    return jnp.dot(a, b, preferred_element_type=f32)


def dot_nt(a, b):
    return lax.dot_general(a, b, NT, preferred_element_type=f32)


def params(limit=VLIM):
    return pltpu.CompilerParams(vmem_limit_bytes=limit)


in_vmem = pl.BlockSpec(memory_space=pltpu.VMEM)
in_hbm = pl.BlockSpec(memory_space=pltpu.HBM)
in_smem = pl.BlockSpec(memory_space=pltpu.SMEM)


def call(kernel, name, outs, args, scalars=0, scratch=(), limit=VLIM):
    return pl.pallas_call(
        kernel,
        in_specs=[in_smem] * scalars + [in_vmem] * (len(args) - scalars),
        out_specs=[in_vmem] * len(outs),
        out_shape=[jax.ShapeDtypeStruct(shape, kind) for shape, kind in outs],
        scratch_shapes=list(scratch),
        compiler_params=params(limit),
        name=name,
    )(*args)


CHUNK = 256


def pass_one(
    base, off, qt, wuk, wuv, og, lat,
    e_v, dp_v, qcat_t, dlat_t, stat,
    qt_v, wuk_v, wuv_v, og_v, lat_v, og_wide, qcat, dlat, top, tot, dsum, hide, sem_in,
):
    pairs = ((qt, qt_v), (wuk, wuk_v), (og, og_v), (wuv, wuv_v), (lat, lat_v))
    loads = [pltpu.make_async_copy(a, b, sem_in.at[k]) for k, (a, b) in enumerate(pairs)]
    for copy in loads:
        copy.start()
    bound = jnp.broadcast_to(off[...], (ROWS, ROWS)).T - base[0]
    bound = jnp.concatenate([bound] * (BLK // 128), axis=1)
    lane = lax.broadcasted_iota(jnp.int32, (ROWS, BLK), 1)
    top[...] = jnp.full((ALL, 128), floor_top, f32)
    tot[...] = jnp.zeros((ALL, 128), f32)
    dsum[...] = jnp.zeros((ALL, 128), f32)
    chunks = [slice(c * CHUNK, (c + 1) * CHUNK) for c in range(ALL // CHUNK)]
    heads = [slice(h * ROWS, (h + 1) * ROWS) for h in range(HEADS)]

    loads[0].wait()
    loads[1].wait()
    for h, rows in enumerate(heads):
        q = qt_v[h].T
        qcat[rows, :LAT] = dot(q[:, :NOPE], wuk_v[h]).astype(bf16)
        qcat[rows, LAT:] = q[:, NOPE:]
    loads[2].wait()
    loads[3].wait()
    og_wide[...] = og_v[...].astype(f32)
    for h, rows in enumerate(heads):
        grad = og_wide[pl.ds(h, ROWS, stride=HEADS), :].astype(bf16)
        dlat[rows, :] = dot_nt(grad, wuv_v[h]).astype(bf16)
    loads[4].wait()
    for rows in heads:
        for k in range(LAT // 128):
            lanes = slice(k * 128, (k + 1) * 128)
            qcat_t[lanes, rows] = qcat[rows, lanes].T
            dlat_t[lanes, rows] = dlat[rows, lanes].T
        qcat_t[LAT:, rows] = qcat[rows, LAT:].T

    def score(j, _):
        at = pl.multiple_of(j * BLK, BLK)
        hide[...] = jnp.where(lane + at <= bound, 0.0, floor_score)
        cols = lat_v[:, pl.ds(at, BLK)]
        for rows in chunks:
            s = dot(qcat[rows, :], cols)
            s = (s.reshape(CHUNK // ROWS, ROWS, BLK) + hide[...][None]).reshape(CHUNK, BLK)
            e_v[j, rows, :] = s
            best = top[rows, :]
            for k in range(BLK // 128):
                best = jnp.maximum(best, s[:, k * 128 : (k + 1) * 128])
            top[rows, :] = best
        return 0

    lax.fori_loop(0, NBLK, score, 0)
    top[...] = jnp.broadcast_to(jnp.max(top[...], axis=1, keepdims=True) * SCALE2, (ALL, 128))

    def weigh(j, _):
        cols = lat_v[:LAT, pl.ds(pl.multiple_of(j * BLK, BLK), BLK)]
        for rows in chunks:
            dp = dot(dlat[rows, :], cols)
            dp_v[j, rows, :] = dp
            s = e_v[j, rows, :]
            m = top[rows, :]
            t, d = tot[rows, :], dsum[rows, :]
            for k in range(BLK // 128):
                lanes = slice(k * 128, (k + 1) * 128)
                e = jnp.exp2(s[:, lanes] * SCALE2 - m)
                e_v[j, rows, lanes] = e
                t = t + e
                d = d + e * dp[:, lanes]
            tot[rows, :] = t
            dsum[rows, :] = d
        return 0

    lax.fori_loop(0, NBLK, weigh, 0)
    near = lane[:, :128]
    for h, rows in enumerate(heads):
        t = jnp.sum(tot[rows, :], axis=1, keepdims=True)
        d = jnp.sum(dsum[rows, :], axis=1, keepdims=True)
        x = jnp.where(near == 0, top[rows, :], jnp.where(near == 1, t, d)).T
        for k in range(3):
            line = x[k : k + 1, :]
            for peer in range(PEERS):
                stat[peer, k * 8 + h : k * 8 + h + 1, :] = line


def run_pass_one(base, offsets, qt, wuk, wuv, og, lat_t):
    big = (NBLK, ALL, BLK)
    outs = [(big, f32), (big, f32), ((WIDE, ALL), bf16), ((LAT, ALL), bf16)]
    outs += [((PEERS, 24, 128), f32)]
    column = pltpu.VMEM((ALL, 128), f32)
    return pl.pallas_call(
        pass_one,
        in_specs=[in_smem, in_vmem] + [in_hbm] * 5,
        out_specs=[in_vmem] * 5,
        out_shape=[jax.ShapeDtypeStruct(shape, kind) for shape, kind in outs],
        scratch_shapes=[pltpu.VMEM(a.shape, bf16) for a in (qt, wuk, wuv, og, lat_t)]
        + [
            column,
            pltpu.VMEM((ALL, WIDE), bf16),
            pltpu.VMEM((ALL, LAT), bf16),
            column,
            column,
            column,
            pltpu.VMEM((ROWS, BLK), f32),
            pltpu.SemaphoreType.DMA((5,)),
        ],
        compiler_params=params(18 * 1024 * 1024),
        name="pass_one",
    )(base, offsets, qt, wuk, wuv, og, lat_t)


def place(half, r):
    return jnp.where(half == 0, r[0] * 4 + r[1] * 2 + r[2], r[1] * 4 + r[2] * 2 + r[0])


def key_block(r0, chain, sc):
    return sc[3] * 4 + chain * 2 + jnp.bitwise_xor(sc[0], r0)


def second(chain, sc, coef, delta, qcat_t, dlat_t, e, dp, x_out, ds_out, pb):
    for i in range(2):
        kb = key_block(i, chain, sc)
        for c in range(ALL // CHUNK):
            rows = slice(c * CHUNK, (c + 1) * CHUNK)
            cf, dl = coef[rows, :], delta[rows, :]
            for k in range(BLK // 128):
                lanes = slice(k * 128, (k + 1) * 128)
                p = e[kb, rows, lanes] * cf
                pb[i, rows, lanes] = p.astype(bf16)
                ds_out[i, rows, lanes] = (p * (dp[kb, rows, lanes] - dl)).astype(bf16)
        scores = dot(qcat_t[...], ds_out[i]) * SCALE
        values = dot(dlat_t[...], pb[i])
        low = (scores[:LAT] + values).astype(bf16)
        high = scores[LAT:].astype(bf16)
        for q in range(4):
            r = (i, jnp.bitwise_xor(sc[1], q & 1), jnp.bitwise_xor(sc[2], q >> 1))
            at = place(sc[3], r)
            if q < 3:
                x_out[at] = low[q * COLS : (q + 1) * COLS]
            else:
                x_out[at, : LAT - 3 * COLS, :] = low[3 * COLS :]
                x_out[at, LAT - 3 * COLS :, :] = high


def second_first(sc, stat, qcat_t, dlat_t, e, dp, x_out, ds_out, coef, delta, pb):
    m = stat[:, 0:8, :]
    best = jnp.max(m, axis=0)
    w = jnp.exp2(m - best[None])
    total = jnp.sum(w * stat[:, 8:16, :], axis=0)
    dtotal = jnp.sum(w * stat[:, 16:24, :], axis=0)
    cf = jnp.exp2(stat[sc[4], 0:8, :] - best) / total
    dl = dtotal / total
    for h in range(HEADS):
        rows = slice(h * ROWS, (h + 1) * ROWS)
        coef[rows, :] = jnp.broadcast_to(cf[h : h + 1], (128, 128)).T
        delta[rows, :] = jnp.broadcast_to(dl[h : h + 1], (128, 128)).T
    second(0, sc, coef, delta, qcat_t, dlat_t, e, dp, x_out, ds_out, pb)


def run_second(sc, heads_in, qcat_t, dlat_t, e, dp, chain):
    first = len(heads_in) == 1
    outs = [((8, COLS, BLK), bf16), ((2, ALL, BLK), bf16)]
    if first:
        outs += [((ALL, 128), f32)] * 2
    return call(
        second_first if first else functools.partial(second, chain),
        "second_first" if first else "second",
        outs,
        (sc, *heads_in, qcat_t, dlat_t, e, dp),
        1,
        [pltpu.VMEM((2, ALL, BLK), bf16)],
    )


def query_grad(sc_far, sc_own, far_a, own_a, far_b, own_b, lat, wuk, out, acc, wide):
    first = True
    for chain, half_ds in enumerate(((far_a, own_a), (far_b, own_b))):
        for sc, ds in zip((sc_far, sc_own), half_ds):
            for i in range(2):
                kb = key_block(i, chain, sc)
                part = dot_nt(ds[i], lat[:, pl.ds(pl.multiple_of(kb * BLK, BLK), BLK)])
                acc[...] = part if first else acc[...] + part
                first = False
    for h in range(HEADS):
        rows = slice(h * ROWS, (h + 1) * ROWS)
        x = acc[rows, :LAT] * SCALE
        hi = x.astype(bf16)
        lo = (x - hi.astype(f32)).astype(bf16)
        wide[h, :, :NOPE] = dot_nt(hi, wuk[h]) + dot_nt(lo, wuk[h])
        wide[h, :, NOPE:] = acc[rows, LAT:] * SCALE
    for g in range(PEERS):
        out[g] = wide[:, g * 8 : (g + 1) * 8, :].reshape(HEADS * 8, NOPE + ROT).astype(bf16)


def run_query_grad(*args):
    outs = [((PEERS, HEADS * 8, NOPE + ROT), bf16)]
    scratch = [pltpu.VMEM((ALL, WIDE), f32), pltpu.VMEM((HEADS, ROWS, NOPE + ROT), f32)]
    return call(query_grad, "query_grad", outs, args, 2, scratch)[0]


def halve(kept, got, *outs):
    n = kept.shape[0]
    for k in range(n):
        total = (kept[k].astype(f32) + got[k].astype(f32)).astype(bf16)
        outs[k * len(outs) // n][k % (n // len(outs))] = total


def run_halve(kept, got):
    n = kept.shape[0]
    outs = [((max(n // 2, 1), COLS, BLK), bf16)] * min(n, 2)
    return call(halve, "halve", outs, (kept, got))


def join(own, got, out):
    n = own.shape[0]
    out[:n] = own[...]
    out[n:] = got[...]


def run_join(own, got):
    return call(join, "join", [((2 * own.shape[0], COLS, BLK), bf16)], (own, got))[0]


def settle(sc, *refs):
    out = refs[-1]
    for chain in range(CHAINS):
        mine, mine_far, other, other_far = refs[4 * chain : 4 * chain + 4]
        for near, far, half in ((mine, mine_far, sc[3]), (other, other_far, 1 - sc[3])):
            for i in range(8):
                b = (i >> 2 & 1, i >> 1 & 1, i & 1)
                r = [jnp.where(half == 0, b[d], b[(d + 2) % 3]) for d in range(3)]
                a = [jnp.bitwise_xor(sc[d], r[d]) for d in range(3)]
                rows = pl.ds(pl.multiple_of((a[2] * 2 + a[1]) * COLS, 16), COLS)
                block = half * 4 + chain * 2 + a[0]
                lanes = pl.ds(pl.multiple_of(block * BLK, BLK), BLK)
                out[rows, lanes] = near[i] if i < 4 else far[i - 4]


def run_settle(sc, *pieces):
    return call(settle, "settle", [((WIDE, KEYS), bf16)], (sc, *pieces), 1)[0]


def cube_neighbour(k, d):
    y, rest = k >> 2, k & 3
    if d == 2:
        return k ^ 2
    gray = (y ^ (y >> 1)) ^ (1 << d)
    back = gray ^ (gray >> 1)
    return back * 4 + rest


def along(value, n):
    pairs = [(k, cube_neighbour(k, (n + (k & 1)) % 3)) for k in range(16)]
    return lax.ppermute(value, "head", pairs)


def to_sibling(value):
    return lax.ppermute(value, "head", [(k, k ^ 1) for k in range(16)])


def held(value):
    return pltpu.with_memory_space_constraint(value, pltpu.HBM)


def shards(queries, w_uk, w_uv, latent, out_grad, offsets):
    head = lax.axis_index("head").astype(jnp.int32)
    key = lax.axis_index("key").astype(jnp.int32)
    y = head >> 2
    gray = y ^ (y >> 1)
    core = head & 1
    sc_own = jnp.stack([gray & 1, gray >> 1, (head >> 1) & 1, core, key])
    sc_far = jnp.stack([gray & 1, gray >> 1, (head >> 1) & 1, 1 - core, key])
    lat_t = latent.T
    qt = jnp.transpose(queries, (1, 2, 0))
    og = out_grad.reshape(ALL, 128)
    e, dp, qcat_t, dlat_t, stat = run_pass_one(
        (key * KEYS)[None], offsets[None], *map(held, (qt, w_uk, w_uv, og, lat_t))
    )
    stat, sc_own, sc_far = lax.optimization_barrier((stat, sc_own, sc_far))
    stat = lax.all_to_all(stat, "key", 0, 0, tiled=True)
    turned = (qcat_t, dlat_t, e, dp)
    x_far, far_a, coef, delta = run_second(sc_far, (stat,), *turned, 0)
    came = to_sibling(x_far)
    x_own, own_a = run_second(sc_own, (coef, delta), *turned, 0)
    kept_a, send_a = run_halve(x_own, came)
    tie = lax.optimization_barrier
    sc_late, send_a = tie((sc_far, send_a))
    got_a = along(send_a, 0)
    x_far, far_b = run_second(sc_late, (coef, delta), *turned, 1)
    came = to_sibling(x_far)
    x_own, own_b = run_second(sc_own, (coef, delta), *turned, 1)
    kept_b, send_b = run_halve(x_own, came)
    got_b = along(send_b, 0)
    dq = run_query_grad(sc_far, sc_own, far_a, own_a, far_b, own_b, lat_t, w_uk)
    got_a, dq = tie((got_a, dq))
    kept_a, send_a = run_halve(kept_a, got_a)
    kept_b, send_a, dq = tie((kept_b, send_a, dq))
    got_a = along(send_a, 1)
    dq = lax.all_to_all(dq, "key", 0, 0, tiled=True)
    kept_b, send_b = run_halve(kept_b, got_b)
    kept_a, send_b = tie((kept_a, send_b))
    got_b = along(send_b, 1)
    kept_a, send_a = run_halve(kept_a, got_a)
    kept_b, send_a = tie((kept_b, send_a))
    got_a = along(send_a, 2)
    kept_b, send_b = run_halve(kept_b, got_b)
    kept_a, send_b = tie((kept_a, send_b))
    got_b = along(send_b, 2)
    (own_a,) = run_halve(kept_a, got_a)
    kept_b, own_a = tie((kept_b, own_a))
    got_a = along(own_a, 2)
    (own_b,) = run_halve(kept_b, got_b)
    own_a, own_b = tie((own_a, own_b))
    got_b = along(own_b, 2)
    own_a = run_join(own_a, got_a)
    own_b, own_a = tie((own_b, own_a))
    got_a = along(own_a, 1)
    own_b = run_join(own_b, got_b)
    own_a, own_b, dq = tie((own_a, own_b, dq))
    got_b = along(own_b, 1)
    own_a = run_join(own_a, got_a)
    own_b, own_a = tie((own_b, own_a))
    far_a, near_a = along(own_a, 0), to_sibling(own_a)
    own_b = run_join(own_b, got_b)
    far_b, near_b = along(own_b, 0), to_sibling(own_b)
    pieces = [
        (own_a, far_a, near_a, to_sibling(far_a)),
        (own_b, far_b, near_b, to_sibling(far_b)),
    ]
    d_latent = run_settle(sc_own, *pieces[0], *pieces[1]).T

    total = jnp.sum(dq.astype(f32), axis=0).astype(bf16)
    d_queries = jnp.transpose(total.reshape(HEADS, 8, NOPE + ROT), (1, 0, 2))
    return (d_queries, d_latent)


def solution(mesh):
    return jax.shard_map(
        shards,
        mesh=mesh,
        in_specs=(
            P(None, "head", None),
            P("head", None, None),
            P("head", None, None),
            P("key", None),
            P(None, "head", None),
            P(),
        ),
        out_specs=(P("key", "head", None), P("key", None)),
        check_vma=False,
    )
```

time: 115 us -> 99.6 us (0.87)
  the two profiles are of different devices: /device:TPU:61 before, /device:TPU:1 now
where the time goes in v3:
time: 99.6 us; the launch traced here: 98.5 us
  Pallas kernels  30.3 us (30%)
  waiting for transfers between devices  22.9 us (23%)
  starting transfers between devices  22.5 us (23%)
  blocking collectives  20.4 us (20%)
  local copies, waits for them, and re-layouts  1.47 us (1%)
    ppermute x12, waiting for transfers between devices, along(): return lax.ppermute(value, 'head', pairs)  22.4 us
    all_to_all x1, blocking collectives, shards(): stat = lax.all_to_all(stat, 'key', 0, 0, tiled=True)  20.4 us
    pallas_call x18, Pallas kernels, call(): pl.pallas_call(kernel, in_specs=[in_smem] * scalars + [in_vmem] * (len(ar...  17.5 us
    pallas_call x1, Pallas kernels, run_pass_one(): pl.pallas_call(pass_one, in_specs=[in_smem, in_vmem] + [in_hbm] * 5, out_...  12.8 us
    ppermute x12, starting transfers between devices, along(): return lax.ppermute(value, 'head', pairs)  9.57 us
    ppermute x6, starting transfers between devices, to_sibling(): return lax.ppermute(value, 'head', [(k, k ^ 1) for k in range(16)])  9 us
    all_to_all x1, starting transfers between devices, shards(): dq = lax.all_to_all(dq, 'key', 0, 0, tiled=True)  3.94 us
  transfers between devices with their start and end apart: 19, of which 10 were waited for; matrix products, arithmetic and copies ran while one was open for 1% of the time, Pallas kernels for 11%

profile of v3, /device:TPU:1, one launch (start us, length us, event | category | flops | bytes accessed | tf_op | source)
XLA Modules:
  0.0 98.5 jit_solution(9367547194910261227)
XLA Ops:
  0.6 0.1 stack.35.sc.sc_far
  0.7 0.1 stack.33.sc.sc_own
  0.8 0.0 copy-start.2
  0.8 0.7 copy-done.2
  1.5 12.8 %pass_one.1 = (f32[8,1024,256]{2,1,0:T(8,128)S(1)}, f32[8,1024,256]{2,1,0:T(8,128)S(1)}, bf16[576,1024]{1,0:T(8,128)(2,1)S(1)}, bf16[512,1024]{1,0:T(8,128)(2,1)S(1)}, f32[16,24,128]{2,1,0:T(8,128)S(1)}) custom-call(s32[1]{0:T(128)} %bitcast.base, s32[1,128]{1,0:T(1,128)S(1)} %bitcast.17, bf16[8,192,128]{2,1,0:T(8,128)(2,1)} %bitcast.19, ...), custom_call_target="tpu_custom_call" | custom-call | tf_op jit(solution)/shard_map/pass_one/pallas_call | solution.py:158
  14.3 20.4 %all_to_all.10.stat = f32[16,24,128]{2,1,0:T(8,128)S(1)} all-to-all(f32[16,24,128]{2,1,0:T(8,128)S(1)} %get-tuple-element.59), channel_id=1, replica_groups=mesh['head'=16,'key'=16] {'key'}, dimensions={0} | all-to-all | bytes 393216 | tf_op jit(solution)/shard_map/all_to_all | solution.py:347
  34.7 2.3 %second_first.1 = (bf16[8,144,256]{2,1,0:T(8,128)(2,1)S(1)}, bf16[2,1024,256]{2,1,0:T(8,128)(2,1)S(1)}, f32[1024,128]{1,0:T(8,128)S(1)}, f32[1024,128]{1,0:T(8,128)S(1)}) custom-call(s32[5]{0:T(128)S(1)} %stack.35.sc.sc_far, f32[16,24,128]{2,1,0:T(8,128)S(1)} %all_to_all.10.stat, bf16[576,1024]{1,0:T(8,128)(2,1)S(1)} %get-tuple-element.60.qcat_t, ...), custom_call_target="tpu_custom_call" | custom-call | tf_op jit(solution)/shard_map/second_first/pallas_call | solution.py:54
  37.0 2.5 %collective-permute-start = (bf16[8,144,256]{2,1,0:T(8,128)(2,1)S(1)}, bf16[8,144,256]{2,1,0:T(8,128)(2,1)S(1)}, u32[]{:S(2)}, u32[]{:S(2)}) collective-permute-start(bf16[8,144,256]{2,1,0:T(8,128)(2,1)S(1)} %get-tuple-element.68), channel_id=1, source_target_pairs={{0,16},{16,0},{32,48},{48,32},{64,80},{80,64},{96,112},{112,96},{1... | collective-permute-start | bytes 1769480 | tf_op jit(solution)/shard_map/ppermute | solution.py:325
  39.5 2.2 %second.4 = (bf16[8,144,256]{2,1,0:T(8,128)(2,1)S(1)}, bf16[2,1024,256]{2,1,0:T(8,128)(2,1)S(1)}) custom-call(s32[5]{0:T(128)S(1)} %stack.33.sc.sc_own, f32[1024,128]{1,0:T(8,128)S(1)} %get-tuple-element.64.coef, f32[1024,128]{1,0:T(8,128)S(1)} %get-tuple-element.65.delta, bf16[576,1024]{1,0:T(8,128)(2,1)S(1)} %get-tuple-element.60.qcat_t, ...), custom_call_target="tpu_custom_call" | custom-call | tf_op jit(solution)/shard_map/second/pallas_call | solution.py:54
  41.7 0.0 collective-permute-done.got
  41.7 0.1 halve.8
  41.9 2.2 %second.5 = (bf16[8,144,256]{2,1,0:T(8,128)(2,1)S(1)}, bf16[2,1024,256]{2,1,0:T(8,128)(2,1)S(1)}) custom-call(s32[5]{0:T(128)S(1)} %stack.35.sc.sc_far, f32[1024,128]{1,0:T(8,128)S(1)} %get-tuple-element.64.coef, f32[1024,128]{1,0:T(8,128)S(1)} %get-tuple-element.65.delta, bf16[576,1024]{1,0:T(8,128)(2,1)S(1)} %get-tuple-element.60.qcat_t, ...), custom_call_target="tpu_custom_call" | custom-call | tf_op jit(solution)/shard_map/second/pallas_call | solution.py:54
  44.0 0.0 copy-start
  44.1 0.0 copy-start.1
  44.1 0.1 collective-permute-start.1
  44.2 3.0 %collective-permute-start.2 = (bf16[4,144,256]{2,1,0:T(8,128)(2,1)S(1)}, bf16[4,144,256]{2,1,0:T(8,128)(2,1)S(1)}, u32[]{:S(2)}, u32[]{:S(2)}) collective-permute-start(bf16[4,144,256]{2,1,0:T(8,128)(2,1)S(1)} %get-tuple-element.74), channel_id=1, source_target_pairs={{0,64},{16,208},{32,96},{48,240},{64,0},{80,144},{96,32},{112,176}... | collective-permute-start | bytes 884744 | tf_op jit(solution)/shard_map/ppermute | solution.py:321
  47.2 2.2 %second.3 = (bf16[8,144,256]{2,1,0:T(8,128)(2,1)S(1)}, bf16[2,1024,256]{2,1,0:T(8,128)(2,1)S(1)}) custom-call(s32[5]{0:T(128)S(1)} %stack.33.sc.sc_own, f32[1024,128]{1,0:T(8,128)S(1)} %get-tuple-element.64.coef, f32[1024,128]{1,0:T(8,128)S(1)} %get-tuple-element.65.delta, bf16[576,1024]{1,0:T(8,128)(2,1)S(1)} %get-tuple-element.60.qcat_t, ...), custom_call_target="tpu_custom_call" | custom-call | tf_op jit(solution)/shard_map/second/pallas_call | solution.py:54
  49.4 0.0 copy-done
  49.4 0.0 copy-done.1
  49.4 5.8 %query_grad.1 = bf16[16,64,192]{2,1,0:T(8,128)(2,1)} custom-call(s32[5]{0:T(128)S(1)} %stack.35.sc.sc_far, s32[5]{0:T(128)S(1)} %stack.33.sc.sc_own, bf16[2,1024,256]{2,1,0:T(8,128)(2,1)S(1)} %get-tuple-element.75.far_a, bf16[2,1024,256]{2,1,0:T(8,128)(2,1)S(1)} %get-tuple-element.76.own_a, bf16[2,1024,256]{2,1,0:T(8,128)(2,1)S(1)} %get-tuple-element.77.far_b, ...), custom_call_target="tpu_custom_call" | custom-call | tf_op jit(solution)/shard_map/query_grad/pallas_call | solution.py:54
  55.2 0.0 collective-permute-done.2.got
  55.2 0.1 halve.10
  55.2 0.0 collective-permute-done.1.got
  55.2 0.1 halve.9
  55.4 3.9 %all-to-all-start.1 = ((bf16[16,64,192]{2,1,0:T(8,128)(2,1)}), bf16[16,64,192]{2,1,0:T(8,128)(2,1)S(1)}, u32[]{:S(2)}, u32[]{:S(2)}) async-start(bf16[16,64,192]{2,1,0:T(8,128)(2,1)} %query_grad.1), calls=%async_computation.1 | async-start | bytes 1048576 | tf_op jit(solution)/shard_map/all_to_all | solution.py:366
  59.3 0.1 collective-permute-start.3
  59.4 0.4 collective-permute-start.4
  59.9 8.2 %collective-permute-done.3.got = bf16[4,144,256]{2,1,0:T(8,128)(2,1)S(1)} collective-permute-done((bf16[4,144,256]{2,1,0:T(8,128)(2,1)S(1)}, bf16[4,144,256]{2,1,0:T(8,128)(2,1)S(1)}, u32[]{:S(2)}, u32[]{:S(2)}) %collective-permute-start.3) | collective-permute-done | bytes 294944 | tf_op jit(solution)/shard_map/ppermute | solution.py:321
  68.1 0.1 halve.11
  68.2 0.4 collective-permute-start.5
  68.6 0.0 collective-permute-done.4.got
  68.6 0.1 collective-permute-start.6
  68.7 5.5 %collective-permute-done.5.got = bf16[2,144,256]{2,1,0:T(8,128)(2,1)S(1)} collective-permute-done((bf16[2,144,256]{2,1,0:T(8,128)(2,1)S(1)}, bf16[2,144,256]{2,1,0:T(8,128)(2,1)S(1)}, u32[]{:S(2)}, u32[]{:S(2)}) %collective-permute-start.5) | collective-permute-done | bytes 147488 | tf_op jit(solution)/shard_map/ppermute | solution.py:321
  74.2 0.1 collective-permute-start.7
  74.3 0.0 collective-permute-done.6.got
  74.3 1.5 %collective-permute-start.8 = (bf16[1,144,256]{2,1,0:T(8,128)(2,1)S(1)}, bf16[1,144,256]{2,1,0:T(8,128)(2,1)S(1)}, u32[]{:S(2)}, u32[]{:S(2)}) collective-permute-start(bf16[1,144,256]{2,1,0:T(8,128)(2,1)S(1)} %halve.14.own), channel_id=1, source_target_pairs={{0,32},{16,80},{32,0},{48,112},{64,96},{80,16},{96,64},{112,48},{1... | collective-permute-start | bytes 221192 | tf_op jit(solution)/shard_map/ppermute | solution.py:321
  75.9 1.6 %collective-permute-done.7.got = bf16[1,144,256]{2,1,0:T(8,128)(2,1)S(1)} collective-permute-done((bf16[1,144,256]{2,1,0:T(8,128)(2,1)S(1)}, bf16[1,144,256]{2,1,0:T(8,128)(2,1)S(1)}, u32[]{:S(2)}, u32[]{:S(2)}) %collective-permute-start.7) | collective-permute-done | bytes 73760 | tf_op jit(solution)/shard_map/ppermute | solution.py:321
  77.5 0.2 collective-permute-start.9
  77.7 0.6 collective-permute-done.8.got
  78.3 1.0 %collective-permute-start.10 = (bf16[2,144,256]{2,1,0:T(8,128)(2,1)S(1)}, bf16[2,144,256]{2,1,0:T(8,128)(2,1)S(1)}, u32[]{:S(2)}, u32[]{:S(2)}) collective-permute-start(bf16[2,144,256]{2,1,0:T(8,128)(2,1)S(1)} %join.4.own), channel_id=1, source_target_pairs={{0,192},{16,48},{32,224},{48,16},{64,128},{80,112},{96,160},{112,8... | collective-permute-start | bytes 442376 | tf_op jit(solution)/shard_map/ppermute | solution.py:321
  79.3 1.5 %collective-permute-done.9.got = bf16[1,144,256]{2,1,0:T(8,128)(2,1)S(1)} collective-permute-done((bf16[1,144,256]{2,1,0:T(8,128)(2,1)S(1)}, bf16[1,144,256]{2,1,0:T(8,128)(2,1)S(1)}, u32[]{:S(2)}, u32[]{:S(2)}) %collective-permute-start.9) | collective-permute-done | bytes 73760 | tf_op jit(solution)/shard_map/ppermute | solution.py:321
  80.8 0.0 all-to-all-done.1
  80.8 1.0 %collective-permute-start.14 = (bf16[2,144,256]{2,1,0:T(8,128)(2,1)S(1)}, bf16[2,144,256]{2,1,0:T(8,128)(2,1)S(1)}, u32[]{:S(2)}, u32[]{:S(2)}) collective-permute-start(bf16[2,144,256]{2,1,0:T(8,128)(2,1)S(1)} %join.5.own), channel_id=1, source_target_pairs={{0,192},{16,48},{32,224},{48,16},{64,128},{80,112},{96,160},{112,8... | collective-permute-start | bytes 442376 | tf_op jit(solution)/shard_map/ppermute | solution.py:321
  81.8 0.8 collective-permute-done.10.got
  82.7 1.1 %collective-permute-start.11 = (bf16[4,144,256]{2,1,0:T(8,128)(2,1)S(1)}, bf16[4,144,256]{2,1,0:T(8,128)(2,1)S(1)}, u32[]{:S(2)}, u32[]{:S(2)}) collective-permute-start(bf16[4,144,256]{2,1,0:T(8,128)(2,1)S(1)} %join.6.refs_0_), channel_id=1, source_target_pairs={{0,64},{16,208},{32,96},{48,240},{64,0},{80,144},{96,32},{112,176}... | collective-permute-start | bytes 884744 | tf_op jit(solution)/shard_map/ppermute | solution.py:321
  83.9 1.1 %collective-permute-done.14.got = bf16[2,144,256]{2,1,0:T(8,128)(2,1)S(1)} collective-permute-done((bf16[2,144,256]{2,1,0:T(8,128)(2,1)S(1)}, bf16[2,144,256]{2,1,0:T(8,128)(2,1)S(1)}, u32[]{:S(2)}, u32[]{:S(2)}) %collective-permute-start.14) | collective-permute-done | bytes 147488 | tf_op jit(solution)/shard_map/ppermute | solution.py:321
  84.9 0.6 collective-permute-start.15
  85.6 3.0 %collective-permute-start.12 = (bf16[4,144,256]{2,1,0:T(8,128)(2,1)S(1)}, bf16[4,144,256]{2,1,0:T(8,128)(2,1)S(1)}, u32[]{:S(2)}, u32[]{:S(2)}) collective-permute-start(bf16[4,144,256]{2,1,0:T(8,128)(2,1)S(1)} %join.6.refs_0_), channel_id=1, source_target_pairs={{0,16},{16,0},{32,48},{48,32},{64,80},{80,64},{96,112},{112,96},{1... | collective-permute-start | bytes 884744 | tf_op jit(solution)/shard_map/ppermute | solution.py:325
  88.6 0.1 collective-permute-start.16
  88.7 1.2 %collective-permute-done.11.refs_1_ = bf16[4,144,256]{2,1,0:T(8,128)(2,1)S(1)} collective-permute-done((bf16[4,144,256]{2,1,0:T(8,128)(2,1)S(1)}, bf16[4,144,256]{2,1,0:T(8,128)(2,1)S(1)}, u32[]{:S(2)}, u32[]{:S(2)}) %collective-permute-start.11) | collective-permute-done | bytes 294944 | tf_op jit(solution)/shard_map/ppermute | solution.py:321
  89.9 1.3 %collective-permute-start.13 = (bf16[4,144,256]{2,1,0:T(8,128)(2,1)S(1)}, bf16[4,144,256]{2,1,0:T(8,128)(2,1)S(1)}, u32[]{:S(2)}, u32[]{:S(2)}) collective-permute-start(bf16[4,144,256]{2,1,0:T(8,128)(2,1)S(1)} %collective-permute-done.11.refs_1_), channel_id=1, source_target_pairs={{0,16},{16,0},{32,48},{48,32},{64,80},{80,64},{96,112},{112,96},{1... | collective-permute-start | bytes 884744 | tf_op jit(solution)/shard_map/ppermute | solution.py:325
  91.2 1.9 %collective-permute-done.15.refs_5_ = bf16[4,144,256]{2,1,0:T(8,128)(2,1)S(1)} collective-permute-done((bf16[4,144,256]{2,1,0:T(8,128)(2,1)S(1)}, bf16[4,144,256]{2,1,0:T(8,128)(2,1)S(1)}, u32[]{:S(2)}, u32[]{:S(2)}) %collective-permute-start.15) | collective-permute-done | bytes 294944 | tf_op jit(solution)/shard_map/ppermute | solution.py:321
  93.1 2.0 %collective-permute-start.17 = (bf16[4,144,256]{2,1,0:T(8,128)(2,1)S(1)}, bf16[4,144,256]{2,1,0:T(8,128)(2,1)S(1)}, u32[]{:S(2)}, u32[]{:S(2)}) collective-permute-start(bf16[4,144,256]{2,1,0:T(8,128)(2,1)S(1)} %collective-permute-done.15.refs_5_), channel_id=1, source_target_pairs={{0,16},{16,0},{32,48},{48,32},{64,80},{80,64},{96,112},{112,96},{1... | collective-permute-start | bytes 884744 | tf_op jit(solution)/shard_map/ppermute | solution.py:325
  95.0 0.1 reduce_sum.12
  95.1 0.6 copy.8
  95.8 0.0 collective-permute-done.12.refs_2_
  95.8 0.0 collective-permute-done.16.refs_6_
  95.8 0.0 collective-permute-done.13.refs_3_
  95.8 0.5 collective-permute-done.17.refs_7_
  96.2 2.3 %settle.1 = bf16[576,2048]{1,0:T(8,128)(2,1)} custom-call(s32[5]{0:T(128)S(1)} %stack.33.sc.sc_own, bf16[4,144,256]{2,1,0:T(8,128)(2,1)S(1)} %join.6.refs_0_, bf16[4,144,256]{2,1,0:T(8,128)(2,1)S(1)} %collective-permute-done.11.refs_1_, bf16[4,144,256]{2,1,0:T(8,128)(2,1)S(1)} %collective-permute-done.12.refs_2_, ...), custom_call_target="tpu_custom_call" | custom-call | tf_op jit(solution)/shard_map/settle/pallas_call | solution.py:54
  (8 shorter events, 0.2 us)
Async XLA Ops:
  0.8 0.7 copy-start.2
  37.0 4.7 %collective-permute-start = (bf16[8,144,256]{2,1,0:T(8,128)(2,1)S(1)}, bf16[8,144,256]{2,1,0:T(8,128)(2,1)S(1)}, u32[]{:S(2)}, u32[]{:S(2)}) collective-permute-start(bf16[8,144,256]{2,1,0:T(8,128)(2,1)S(1)} %get-tuple-element.68), channel_id=1, source_target_pairs={{0,16},{16,0},{32,48},{48,32},{64,80},{80,64},{96,112},{112,96},{1... | collective-permute-start | bytes 1769480 | tf_op jit(solution)/shard_map/ppermute | solution.py:325
  44.0 5.3 %copy-start = (bf16[2048,576]{0,1:T(8,128)(2,1)S(1)}, bf16[2048,576]{0,1:T(8,128)(2,1)}, u32[]{:S(2)}) copy-start(bf16[2048,576]{0,1:T(8,128)(2,1)} %param.9) | copy-start | bytes 7077892
  44.1 5.3 %copy-start.1 = (bf16[8,128,512]{2,1,0:T(8,128)(2,1)S(1)}, bf16[8,128,512]{2,1,0:T(8,128)(2,1)}, u32[]{:S(2)}) copy-start(bf16[8,128,512]{2,1,0:T(8,128)(2,1)} %wuk.3) | copy-start | bytes 3145732
  44.1 11.2 %collective-permute-start.1 = (bf16[8,144,256]{2,1,0:T(8,128)(2,1)S(1)}, bf16[8,144,256]{2,1,0:T(8,128)(2,1)S(1)}, u32[]{:S(2)}, u32[]{:S(2)}) collective-permute-start(bf16[8,144,256]{2,1,0:T(8,128)(2,1)S(1)} %get-tuple-element.71), channel_id=1, source_target_pairs={{0,16},{16,0},{32,48},{48,32},{64,80},{80,64},{96,112},{112,96},{1... | collective-permute-start | bytes 1769480 | tf_op jit(solution)/shard_map/ppermute | solution.py:325
  44.2 11.0 %collective-permute-start.2 = (bf16[4,144,256]{2,1,0:T(8,128)(2,1)S(1)}, bf16[4,144,256]{2,1,0:T(8,128)(2,1)S(1)}, u32[]{:S(2)}, u32[]{:S(2)}) collective-permute-start(bf16[4,144,256]{2,1,0:T(8,128)(2,1)S(1)} %get-tuple-element.74), channel_id=1, source_target_pairs={{0,64},{16,208},{32,96},{48,240},{64,0},{80,144},{96,32},{112,176}... | collective-permute-start | bytes 884744 | tf_op jit(solution)/shard_map/ppermute | solution.py:321
  55.4 25.4 %all-to-all-start.1 = ((bf16[16,64,192]{2,1,0:T(8,128)(2,1)}), bf16[16,64,192]{2,1,0:T(8,128)(2,1)S(1)}, u32[]{:S(2)}, u32[]{:S(2)}) async-start(bf16[16,64,192]{2,1,0:T(8,128)(2,1)} %query_grad.1), calls=%async_computation.1 | async-start | bytes 1048576 | tf_op jit(solution)/shard_map/all_to_all | solution.py:366
  59.3 8.7 %collective-permute-start.3 = (bf16[4,144,256]{2,1,0:T(8,128)(2,1)S(1)}, bf16[4,144,256]{2,1,0:T(8,128)(2,1)S(1)}, u32[]{:S(2)}, u32[]{:S(2)}) collective-permute-start(bf16[4,144,256]{2,1,0:T(8,128)(2,1)S(1)} %get-tuple-element.83), channel_id=1, source_target_pairs={{0,64},{16,208},{32,96},{48,240},{64,0},{80,144},{96,32},{112,176}... | collective-permute-start | bytes 884744 | tf_op jit(solution)/shard_map/ppermute | solution.py:321
  59.4 9.1 %collective-permute-start.4 = (bf16[2,144,256]{2,1,0:T(8,128)(2,1)S(1)}, bf16[2,144,256]{2,1,0:T(8,128)(2,1)S(1)}, u32[]{:S(2)}, u32[]{:S(2)}) collective-permute-start(bf16[2,144,256]{2,1,0:T(8,128)(2,1)S(1)} %get-tuple-element.88), channel_id=1, source_target_pairs={{0,192},{16,48},{32,224},{48,16},{64,128},{80,112},{96,160},{112,8... | collective-permute-start | bytes 442376 | tf_op jit(solution)/shard_map/ppermute | solution.py:321
  68.2 6.0 %collective-permute-start.5 = (bf16[2,144,256]{2,1,0:T(8,128)(2,1)S(1)}, bf16[2,144,256]{2,1,0:T(8,128)(2,1)S(1)}, u32[]{:S(2)}, u32[]{:S(2)}) collective-permute-start(bf16[2,144,256]{2,1,0:T(8,128)(2,1)S(1)} %get-tuple-element.91), channel_id=1, source_target_pairs={{0,192},{16,48},{32,224},{48,16},{64,128},{80,112},{96,160},{112,8... | collective-permute-start | bytes 442376 | tf_op jit(solution)/shard_map/ppermute | solution.py:321
  68.6 5.7 %collective-permute-start.6 = (bf16[1,144,256]{2,1,0:T(8,128)(2,1)S(1)}, bf16[1,144,256]{2,1,0:T(8,128)(2,1)S(1)}, u32[]{:S(2)}, u32[]{:S(2)}) collective-permute-start(bf16[1,144,256]{2,1,0:T(8,128)(2,1)S(1)} %get-tuple-element.96), channel_id=1, source_target_pairs={{0,32},{16,80},{32,0},{48,112},{64,96},{80,16},{96,64},{112,48},{1... | collective-permute-start | bytes 221192 | tf_op jit(solution)/shard_map/ppermute | solution.py:321
  74.2 3.3 %collective-permute-start.7 = (bf16[1,144,256]{2,1,0:T(8,128)(2,1)S(1)}, bf16[1,144,256]{2,1,0:T(8,128)(2,1)S(1)}, u32[]{:S(2)}, u32[]{:S(2)}) collective-permute-start(bf16[1,144,256]{2,1,0:T(8,128)(2,1)S(1)} %get-tuple-element.99), channel_id=1, source_target_pairs={{0,32},{16,80},{32,0},{48,112},{64,96},{80,16},{96,64},{112,48},{1... | collective-permute-start | bytes 221192 | tf_op jit(solution)/shard_map/ppermute | solution.py:321
  74.3 3.9 %collective-permute-start.8 = (bf16[1,144,256]{2,1,0:T(8,128)(2,1)S(1)}, bf16[1,144,256]{2,1,0:T(8,128)(2,1)S(1)}, u32[]{:S(2)}, u32[]{:S(2)}) collective-permute-start(bf16[1,144,256]{2,1,0:T(8,128)(2,1)S(1)} %halve.14.own), channel_id=1, source_target_pairs={{0,32},{16,80},{32,0},{48,112},{64,96},{80,16},{96,64},{112,48},{1... | collective-permute-start | bytes 221192 | tf_op jit(solution)/shard_map/ppermute | solution.py:321
  77.5 3.3 %collective-permute-start.9 = (bf16[1,144,256]{2,1,0:T(8,128)(2,1)S(1)}, bf16[1,144,256]{2,1,0:T(8,128)(2,1)S(1)}, u32[]{:S(2)}, u32[]{:S(2)}) collective-permute-start(bf16[1,144,256]{2,1,0:T(8,128)(2,1)S(1)} %halve.15.own), channel_id=1, source_target_pairs={{0,32},{16,80},{32,0},{48,112},{64,96},{80,16},{96,64},{112,48},{1... | collective-permute-start | bytes 221192 | tf_op jit(solution)/shard_map/ppermute | solution.py:321
  78.3 4.4 %collective-permute-start.10 = (bf16[2,144,256]{2,1,0:T(8,128)(2,1)S(1)}, bf16[2,144,256]{2,1,0:T(8,128)(2,1)S(1)}, u32[]{:S(2)}, u32[]{:S(2)}) collective-permute-start(bf16[2,144,256]{2,1,0:T(8,128)(2,1)S(1)} %join.4.own), channel_id=1, source_target_pairs={{0,192},{16,48},{32,224},{48,16},{64,128},{80,112},{96,160},{112,8... | collective-permute-start | bytes 442376 | tf_op jit(solution)/shard_map/ppermute | solution.py:321
  80.8 4.1 %collective-permute-start.14 = (bf16[2,144,256]{2,1,0:T(8,128)(2,1)S(1)}, bf16[2,144,256]{2,1,0:T(8,128)(2,1)S(1)}, u32[]{:S(2)}, u32[]{:S(2)}) collective-permute-start(bf16[2,144,256]{2,1,0:T(8,128)(2,1)S(1)} %join.5.own), channel_id=1, source_target_pairs={{0,192},{16,48},{32,224},{48,16},{64,128},{80,112},{96,160},{112,8... | collective-permute-start | bytes 442376 | tf_op jit(solution)/shard_map/ppermute | solution.py:321
  82.7 7.2 %collective-permute-start.11 = (bf16[4,144,256]{2,1,0:T(8,128)(2,1)S(1)}, bf16[4,144,256]{2,1,0:T(8,128)(2,1)S(1)}, u32[]{:S(2)}, u32[]{:S(2)}) collective-permute-start(bf16[4,144,256]{2,1,0:T(8,128)(2,1)S(1)} %join.6.refs_0_), channel_id=1, source_target_pairs={{0,64},{16,208},{32,96},{48,240},{64,0},{80,144},{96,32},{112,176}... | collective-permute-start | bytes 884744 | tf_op jit(solution)/shard_map/ppermute | solution.py:321
  84.9 8.1 %collective-permute-start.15 = (bf16[4,144,256]{2,1,0:T(8,128)(2,1)S(1)}, bf16[4,144,256]{2,1,0:T(8,128)(2,1)S(1)}, u32[]{:S(2)}, u32[]{:S(2)}) collective-permute-start(bf16[4,144,256]{2,1,0:T(8,128)(2,1)S(1)} %join.7.refs_4_), channel_id=1, source_target_pairs={{0,64},{16,208},{32,96},{48,240},{64,0},{80,144},{96,32},{112,176}... | collective-permute-start | bytes 884744 | tf_op jit(solution)/shard_map/ppermute | solution.py:321
  85.6 10.2 %collective-permute-start.12 = (bf16[4,144,256]{2,1,0:T(8,128)(2,1)S(1)}, bf16[4,144,256]{2,1,0:T(8,128)(2,1)S(1)}, u32[]{:S(2)}, u32[]{:S(2)}) collective-permute-start(bf16[4,144,256]{2,1,0:T(8,128)(2,1)S(1)} %join.6.refs_0_), channel_id=1, source_target_pairs={{0,16},{16,0},{32,48},{48,32},{64,80},{80,64},{96,112},{112,96},{1... | collective-permute-start | bytes 884744 | tf_op jit(solution)/shard_map/ppermute | solution.py:325
  88.6 7.1 %collective-permute-start.16 = (bf16[4,144,256]{2,1,0:T(8,128)(2,1)S(1)}, bf16[4,144,256]{2,1,0:T(8,128)(2,1)S(1)}, u32[]{:S(2)}, u32[]{:S(2)}) collective-permute-start(bf16[4,144,256]{2,1,0:T(8,128)(2,1)S(1)} %join.7.refs_4_), channel_id=1, source_target_pairs={{0,16},{16,0},{32,48},{48,32},{64,80},{80,64},{96,112},{112,96},{1... | collective-permute-start | bytes 884744 | tf_op jit(solution)/shard_map/ppermute | solution.py:325
  89.9 5.9 %collective-permute-start.13 = (bf16[4,144,256]{2,1,0:T(8,128)(2,1)S(1)}, bf16[4,144,256]{2,1,0:T(8,128)(2,1)S(1)}, u32[]{:S(2)}, u32[]{:S(2)}) collective-permute-start(bf16[4,144,256]{2,1,0:T(8,128)(2,1)S(1)} %collective-permute-done.11.refs_1_), channel_id=1, source_target_pairs={{0,16},{16,0},{32,48},{48,32},{64,80},{80,64},{96,112},{112,96},{1... | collective-permute-start | bytes 884744 | tf_op jit(solution)/shard_map/ppermute | solution.py:325
  93.1 3.2 %collective-permute-start.17 = (bf16[4,144,256]{2,1,0:T(8,128)(2,1)S(1)}, bf16[4,144,256]{2,1,0:T(8,128)(2,1)S(1)}, u32[]{:S(2)}, u32[]{:S(2)}) collective-permute-start(bf16[4,144,256]{2,1,0:T(8,128)(2,1)S(1)} %collective-permute-done.15.refs_5_), channel_id=1, source_target_pairs={{0,16},{16,0},{32,48},{48,32},{64,80},{80,64},{96,112},{112,96},{1... | collective-permute-start | bytes 884744 | tf_op jit(solution)/shard_map/ppermute | solution.py:325

commit v4 on v3

--- a/solution.py
+++ b/solution.py
@@ -28,7 +28,9 @@
 CHAINS = 2
 SCALE = 1.0 / math.sqrt(NOPE + ROT)
 SCALE2 = SCALE * math.log2(math.e)
-VLIM = 12 * 1024 * 1024
+VLIM = 14 * 1024 * 1024
+LIMIT_ONE = 34 * 1024 * 1024
+LIMIT_TWO = 28 * 1024 * 1024
 
 NT = (((1,), (1,)), ((), ()))
 
@@ -68,13 +70,14 @@
 def pass_one(
     base, off, qt, wuk, wuv, og, lat,
     e_v, dp_v, qcat_t, dlat_t, stat,
-    qt_v, wuk_v, wuv_v, og_v, lat_v, og_wide, qcat, dlat, top, tot, dsum, hide, sem_in,
+    off_v, qt_v, wuk_v, wuv_v, og_v, lat_v, og_wide, qcat, dlat, top, tot, dsum, hide, sem_in,
 ):
-    pairs = ((qt, qt_v), (wuk, wuk_v), (og, og_v), (wuv, wuv_v), (lat, lat_v))
+    pairs = ((off, off_v), (qt, qt_v), (wuk, wuk_v), (og, og_v), (wuv, wuv_v), (lat, lat_v))
     loads = [pltpu.make_async_copy(a, b, sem_in.at[k]) for k, (a, b) in enumerate(pairs)]
     for copy in loads:
         copy.start()
-    bound = jnp.broadcast_to(off[...], (ROWS, ROWS)).T - base[0]
+    loads[0].wait()
+    bound = jnp.broadcast_to(off_v[...], (ROWS, ROWS)).T - base[0]
     bound = jnp.concatenate([bound] * (BLK // 128), axis=1)
     lane = lax.broadcasted_iota(jnp.int32, (ROWS, BLK), 1)
     top[...] = jnp.full((ALL, 128), floor_top, f32)
@@ -83,19 +86,19 @@
     chunks = [slice(c * CHUNK, (c + 1) * CHUNK) for c in range(ALL // CHUNK)]
     heads = [slice(h * ROWS, (h + 1) * ROWS) for h in range(HEADS)]
 
-    loads[0].wait()
     loads[1].wait()
+    loads[2].wait()
     for h, rows in enumerate(heads):
         q = qt_v[h].T
         qcat[rows, :LAT] = dot(q[:, :NOPE], wuk_v[h]).astype(bf16)
         qcat[rows, LAT:] = q[:, NOPE:]
-    loads[2].wait()
     loads[3].wait()
+    loads[4].wait()
     og_wide[...] = og_v[...].astype(f32)
     for h, rows in enumerate(heads):
         grad = og_wide[pl.ds(h, ROWS, stride=HEADS), :].astype(bf16)
         dlat[rows, :] = dot_nt(grad, wuv_v[h]).astype(bf16)
-    loads[4].wait()
+    loads[5].wait()
     for rows in heads:
         for k in range(LAT // 128):
             lanes = slice(k * 128, (k + 1) * 128)
@@ -157,10 +160,10 @@
     column = pltpu.VMEM((ALL, 128), f32)
     return pl.pallas_call(
         pass_one,
-        in_specs=[in_smem, in_vmem] + [in_hbm] * 5,
+        in_specs=[in_smem] + [in_hbm] * 6,
         out_specs=[in_vmem] * 5,
         out_shape=[jax.ShapeDtypeStruct(shape, kind) for shape, kind in outs],
-        scratch_shapes=[pltpu.VMEM(a.shape, bf16) for a in (qt, wuk, wuv, og, lat_t)]
+        scratch_shapes=[pltpu.VMEM(a.shape, a.dtype) for a in (offsets, qt, wuk, wuv, og, lat_t)]
         + [
             column,
             pltpu.VMEM((ALL, WIDE), bf16),
@@ -169,9 +172,9 @@
             column,
             column,
             pltpu.VMEM((ROWS, BLK), f32),
-            pltpu.SemaphoreType.DMA((5,)),
+            pltpu.SemaphoreType.DMA((6,)),
         ],
-        compiler_params=params(18 * 1024 * 1024),
+        compiler_params=params(LIMIT_ONE),
         name="pass_one",
     )(base, offsets, qt, wuk, wuv, og, lat_t)
 
@@ -184,19 +187,25 @@
     return sc[3] * 4 + chain * 2 + jnp.bitwise_xor(sc[0], r0)
 
 
-def second(chain, sc, coef, delta, qcat_t, dlat_t, e, dp, x_out, ds_out, pb):
+TALL = 512
+
+
+def second(chain, sc, coef, delta, qcat_t, dlat_t, e, dp, x_out, ds_out):
     for i in range(2):
         kb = key_block(i, chain, sc)
-        for c in range(ALL // CHUNK):
-            rows = slice(c * CHUNK, (c + 1) * CHUNK)
-            cf, dl = coef[rows, :], delta[rows, :]
-            for k in range(BLK // 128):
-                lanes = slice(k * 128, (k + 1) * 128)
-                p = e[kb, rows, lanes] * cf
-                pb[i, rows, lanes] = p.astype(bf16)
-                ds_out[i, rows, lanes] = (p * (dp[kb, rows, lanes] - dl)).astype(bf16)
-        scores = dot(qcat_t[...], ds_out[i]) * SCALE
-        values = dot(dlat_t[...], pb[i])
+        scores = values = None
+        for c in range(ALL // TALL):
+            rows = slice(c * TALL, (c + 1) * TALL)
+            cf = jnp.concatenate([coef[rows, :]] * (BLK // 128), axis=1)
+            dl = jnp.concatenate([delta[rows, :]] * (BLK // 128), axis=1)
+            p = e[kb, rows, :] * cf
+            ds = (p * (dp[kb, rows, :] - dl)).astype(bf16)
+            ds_out[i, rows, :] = ds
+            from_scores = dot(qcat_t[:, rows], ds)
+            from_values = dot(dlat_t[:, rows], p.astype(bf16))
+            scores = from_scores if c == 0 else scores + from_scores
+            values = from_values if c == 0 else values + from_values
+        scores = scores * SCALE
         low = (scores[:LAT] + values).astype(bf16)
         high = scores[LAT:].astype(bf16)
         for q in range(4):
@@ -209,7 +218,7 @@
                 x_out[at, LAT - 3 * COLS :, :] = high
 
 
-def second_first(sc, stat, qcat_t, dlat_t, e, dp, x_out, ds_out, coef, delta, pb):
+def second_first(sc, stat, qcat_t, dlat_t, e, dp, x_out, ds_out, coef, delta):
     m = stat[:, 0:8, :]
     best = jnp.max(m, axis=0)
     w = jnp.exp2(m - best[None])
@@ -221,7 +230,7 @@
         rows = slice(h * ROWS, (h + 1) * ROWS)
         coef[rows, :] = jnp.broadcast_to(cf[h : h + 1], (128, 128)).T
         delta[rows, :] = jnp.broadcast_to(dl[h : h + 1], (128, 128)).T
-    second(0, sc, coef, delta, qcat_t, dlat_t, e, dp, x_out, ds_out, pb)
+    second(0, sc, coef, delta, qcat_t, dlat_t, e, dp, x_out, ds_out)
 
 
 def run_second(sc, heads_in, qcat_t, dlat_t, e, dp, chain):
@@ -235,19 +244,25 @@
         outs,
         (sc, *heads_in, qcat_t, dlat_t, e, dp),
         1,
-        [pltpu.VMEM((2, ALL, BLK), bf16)],
+        limit=LIMIT_TWO,
     )
 
 
-def query_grad(sc_far, sc_own, far_a, own_a, far_b, own_b, lat, wuk, out, acc, wide):
-    first = True
-    for chain, half_ds in enumerate(((far_a, own_a), (far_b, own_b))):
-        for sc, ds in zip((sc_far, sc_own), half_ds):
-            for i in range(2):
-                kb = key_block(i, chain, sc)
-                part = dot_nt(ds[i], lat[:, pl.ds(pl.multiple_of(kb * BLK, BLK), BLK)])
-                acc[...] = part if first else acc[...] + part
-                first = False
+def query_piece(chain, sc, ds, lat, *refs):
+    total = None if len(refs) == 1 else refs[0][...]
+    for i in range(2):
+        kb = key_block(i, chain, sc)
+        part = dot_nt(ds[i], lat[:, pl.ds(pl.multiple_of(kb * BLK, BLK), BLK)])
+        total = part if total is None else total + part
+    refs[-1][...] = total
+
+
+def run_query_piece(chain, sc, ds, lat_t, *acc):
+    kernel = functools.partial(query_piece, chain)
+    return call(kernel, "query_piece", [((ALL, WIDE), f32)], (sc, ds, lat_t, *acc), 1)[0]
+
+
+def query_last(sc, acc, wuk, keep, send, wide):
     for h in range(HEADS):
         rows = slice(h * ROWS, (h + 1) * ROWS)
         x = acc[rows, :LAT] * SCALE
@@ -256,13 +271,17 @@
         wide[h, :, :NOPE] = dot_nt(hi, wuk[h]) + dot_nt(lo, wuk[h])
         wide[h, :, NOPE:] = acc[rows, LAT:] * SCALE
     for g in range(PEERS):
-        out[g] = wide[:, g * 8 : (g + 1) * 8, :].reshape(HEADS * 8, NOPE + ROT).astype(bf16)
-
-
-def run_query_grad(*args):
-    outs = [((PEERS, HEADS * 8, NOPE + ROT), bf16)]
-    scratch = [pltpu.VMEM((ALL, WIDE), f32), pltpu.VMEM((HEADS, ROWS, NOPE + ROT), f32)]
-    return call(query_grad, "query_grad", outs, args, 2, scratch)[0]
+        bits = (g >> 3 & 1) | (g >> 2 & 1) << 1 | (g >> 1 & 1) << 2 | (g & 1) << 3
+        owner = jnp.bitwise_xor(sc[4], bits)
+        mine = wide[:, pl.ds(pl.multiple_of(owner * 8, 8), 8), :]
+        half = keep if g < 8 else send
+        half[g % 8] = mine.reshape(HEADS * 8, NOPE + ROT).astype(bf16)
+
+
+def run_query_last(sc, acc, wuk):
+    outs = [((8, HEADS * 8, NOPE + ROT), bf16)] * 2
+    scratch = [pltpu.VMEM((HEADS, ROWS, NOPE + ROT), f32)]
+    return call(query_last, "query_last", outs, (sc, acc, wuk), 1, scratch)
 
 
 def halve(kept, got, *outs):
@@ -274,7 +293,7 @@
 
 def run_halve(kept, got):
     n = kept.shape[0]
-    outs = [((max(n // 2, 1), COLS, BLK), bf16)] * min(n, 2)
+    outs = [((max(n // 2, 1), *kept.shape[1:]), bf16)] * min(n, 2)
     return call(halve, "halve", outs, (kept, got))
 
 
@@ -289,7 +308,8 @@
 
 
 def settle(sc, *refs):
-    out = refs[-1]
+    out, sem = refs[-2:]
+    copies = []
     for chain in range(CHAINS):
         mine, mine_far, other, other_far = refs[4 * chain : 4 * chain + 4]
         for near, far, half in ((mine, mine_far, sc[3]), (other, other_far, 1 - sc[3])):
@@ -300,11 +320,24 @@
                 rows = pl.ds(pl.multiple_of((a[2] * 2 + a[1]) * COLS, 16), COLS)
                 block = half * 4 + chain * 2 + a[0]
                 lanes = pl.ds(pl.multiple_of(block * BLK, BLK), BLK)
-                out[rows, lanes] = near[i] if i < 4 else far[i - 4]
+                block = near.at[i] if i < 4 else far.at[i - 4]
+                copy = pltpu.make_async_copy(block, out.at[rows, lanes], sem.at[len(copies)])
+                copy.start()
+                copies.append(copy)
+    for copy in copies:
+        copy.wait()
 
 
 def run_settle(sc, *pieces):
-    return call(settle, "settle", [((WIDE, KEYS), bf16)], (sc, *pieces), 1)[0]
+    return pl.pallas_call(
+        settle,
+        in_specs=[in_smem] + [in_vmem] * len(pieces),
+        out_specs=in_hbm,
+        out_shape=jax.ShapeDtypeStruct((WIDE, KEYS), bf16),
+        scratch_shapes=[pltpu.SemaphoreType.DMA((16 * CHAINS,))],
+        compiler_params=params(),
+        name="settle",
+    )(sc, *pieces)
 
 
 def cube_neighbour(k, d):
@@ -323,6 +356,10 @@
 
 def to_sibling(value):
     return lax.ppermute(value, "head", [(k, k ^ 1) for k in range(16)])
+
+
+def to_key(value, flip):
+    return lax.ppermute(value, "key", [(k, k ^ flip) for k in range(16)])
 
 
 def held(value):
@@ -341,7 +378,7 @@
     qt = jnp.transpose(queries, (1, 2, 0))
     og = out_grad.reshape(ALL, 128)
     e, dp, qcat_t, dlat_t, stat = run_pass_one(
-        (key * KEYS)[None], offsets[None], *map(held, (qt, w_uk, w_uv, og, lat_t))
+        (key * KEYS)[None], *map(held, (offsets[None], qt, w_uk, w_uv, og, lat_t))
     )
     stat, sc_own, sc_far = lax.optimization_barrier((stat, sc_own, sc_far))
     stat = lax.all_to_all(stat, "key", 0, 0, tiled=True)
@@ -358,15 +395,21 @@
     x_own, own_b = run_second(sc_own, (coef, delta), *turned, 1)
     kept_b, send_b = run_halve(x_own, came)
     got_b = along(send_b, 0)
-    dq = run_query_grad(sc_far, sc_own, far_a, own_a, far_b, own_b, lat_t, w_uk)
-    got_a, dq = tie((got_a, dq))
+    acc = run_query_piece(0, sc_far, far_a, lat_t)
+    acc = run_query_piece(0, sc_own, own_a, lat_t, acc)
+    got_a, acc = tie((got_a, acc))
     kept_a, send_a = run_halve(kept_a, got_a)
-    kept_b, send_a, dq = tie((kept_b, send_a, dq))
+    kept_b, send_a, acc = tie((kept_b, send_a, acc))
     got_a = along(send_a, 1)
-    dq = lax.all_to_all(dq, "key", 0, 0, tiled=True)
+    acc = run_query_piece(1, sc_far, far_b, lat_t, acc)
+    acc = run_query_piece(1, sc_own, own_b, lat_t, acc)
+    got_b, acc = tie((got_b, acc))
     kept_b, send_b = run_halve(kept_b, got_b)
-    kept_a, send_b = tie((kept_a, send_b))
+    kept_a, send_b, acc = tie((kept_a, send_b, acc))
     got_b = along(send_b, 1)
+    q_keep, q_send = run_query_last(sc_own, acc, w_uk)
+    got_a, q_send = tie((got_a, q_send))
+    q_got = to_key(q_send, 1)
     kept_a, send_a = run_halve(kept_a, got_a)
     kept_b, send_a = tie((kept_b, send_a))
     got_a = along(send_a, 2)
@@ -376,28 +419,37 @@
     (own_a,) = run_halve(kept_a, got_a)
     kept_b, own_a = tie((kept_b, own_a))
     got_a = along(own_a, 2)
+    q_keep, q_send = run_halve(q_keep, q_got)
+    got_b, q_send = tie((got_b, q_send))
+    q_got = to_key(q_send, 2)
     (own_b,) = run_halve(kept_b, got_b)
     own_a, own_b = tie((own_a, own_b))
     got_b = along(own_b, 2)
     own_a = run_join(own_a, got_a)
     own_b, own_a = tie((own_b, own_a))
     got_a = along(own_a, 1)
+    q_keep, q_send = run_halve(q_keep, q_got)
+    got_b, q_send = tie((got_b, q_send))
+    q_got = to_key(q_send, 4)
     own_b = run_join(own_b, got_b)
-    own_a, own_b, dq = tie((own_a, own_b, dq))
+    own_a, own_b = tie((own_a, own_b))
     got_b = along(own_b, 1)
     own_a = run_join(own_a, got_a)
     own_b, own_a = tie((own_b, own_a))
     far_a, near_a = along(own_a, 0), to_sibling(own_a)
+    q_keep, q_send = run_halve(q_keep, q_got)
+    got_b, q_send = tie((got_b, q_send))
+    q_got = to_key(q_send, 8)
     own_b = run_join(own_b, got_b)
     far_b, near_b = along(own_b, 0), to_sibling(own_b)
+    (dq,) = run_halve(q_keep, q_got)
     pieces = [
         (own_a, far_a, near_a, to_sibling(far_a)),
         (own_b, far_b, near_b, to_sibling(far_b)),
     ]
     d_latent = run_settle(sc_own, *pieces[0], *pieces[1]).T
 
-    total = jnp.sum(dq.astype(f32), axis=0).astype(bf16)
-    d_queries = jnp.transpose(total.reshape(HEADS, 8, NOPE + ROT), (1, 0, 2))
+    d_queries = jnp.transpose(dq.reshape(HEADS, 8, NOPE + ROT), (1, 0, 2))
     return (d_queries, d_latent)
 
 

time: 99.6 us -> 101 us (1.014); the launches traced: 98.5 us -> 101 us
  starting transfers between devices: 22.5 us -> 36.9 us
  waiting for transfers between devices: 22.9 us -> 10.9 us
    ppermute x12, waiting for transfers between devices: 22.4 us -> 1.96 us  [along(): return lax.ppermute(value, 'head', pairs)]
    ppermute x0 -> x4, waiting for transfers between devices: none -> 8.94 us  [to_key(): return lax.ppermute(value, 'key', [(k, k ^ flip) for k in range(16)])]
    ppermute x12, starting transfers between devices: 9.57 us -> 16.2 us  [along(): return lax.ppermute(value, 'head', pairs)]
    ppermute x0 -> x4, starting transfers between devices: none -> 5.98 us  [to_key(): return lax.ppermute(value, 'key', [(k, k ^ flip) for k in range(16)])]
    ppermute x6, starting transfers between devices: 9 us -> 14.7 us  [to_sibling(): return lax.ppermute(value, 'head', [(k, k ^ 1) for k in range(16)])]
    all_to_all x1 -> x0, starting transfers between devices: 3.94 us -> none  [shards(): dq = lax.all_to_all(dq, 'key', 0, 0, tiled=True)]
    pallas_call x1 -> x2, Pallas kernels: 12.8 us -> 15 us  [the longest x1 12.8 us: run_pass_one(): pl.pallas_call(pass_one, in_specs=[in_smem] + [in_hbm] * 6, out_specs=[in...]
    pallas_call x18 -> x25, Pallas kernels: 17.5 us -> 16.2 us  [call(): pl.pallas_call(kernel, in_specs=[in_smem] * scalars + [in_vmem] * (len(ar...]
  transfers between devices with their start and end apart: 19 -> 22, of which waited for: 10 -> 6; matrix products, arithmetic and copies ran while one was open for 1% -> 1% of each run, Pallas kernels for 11% -> 12%
where the time goes in v4:
time: 101 us
  starting transfers between devices  36.9 us (37%)
  Pallas kernels  31.2 us (31%)
  blocking collectives  20.4 us (20%)
  waiting for transfers between devices  10.9 us (11%)
  between operations  1.08 us (1%)
    all_to_all x1, blocking collectives, shards(): stat = lax.all_to_all(stat, 'key', 0, 0, tiled=True)  20.4 us
    pallas_call x25, Pallas kernels, call(): pl.pallas_call(kernel, in_specs=[in_smem] * scalars + [in_vmem] * (len(ar...  16.2 us
    ppermute x12, starting transfers between devices, along(): return lax.ppermute(value, 'head', pairs)  16.2 us
    ppermute x6, starting transfers between devices, to_sibling(): return lax.ppermute(value, 'head', [(k, k ^ 1) for k in range(16)])  14.7 us
    pallas_call x1, Pallas kernels, run_pass_one(): pl.pallas_call(pass_one, in_specs=[in_smem] + [in_hbm] * 6, out_specs=[in...  12.8 us
    ppermute x4, waiting for transfers between devices, to_key(): return lax.ppermute(value, 'key', [(k, k ^ flip) for k in range(16)])  8.94 us
    ppermute x4, starting transfers between devices, to_key(): return lax.ppermute(value, 'key', [(k, k ^ flip) for k in range(16)])  5.98 us
    pallas_call x1, Pallas kernels, run_settle(): pl.pallas_call(settle, in_specs=[in_smem] + [in_vmem] * len(pieces), out_...  2.22 us
  transfers between devices with their start and end apart: 22, of which 6 were waited for; matrix products, arithmetic and copies ran while one was open for 1% of the time, Pallas kernels for 12%

profile of v4, /device:TPU:1, one launch (start us, length us, event | category | flops | bytes accessed | tf_op | source)
XLA Modules:
  0.0 101.3 jit_solution(6922892510136525710)
XLA Ops:
  0.6 0.1 stack.35.sc
  0.7 0.1 stack.33.sc
  0.8 12.8 %pass_one.1 = (f32[8,1024,256]{2,1,0:T(8,128)S(1)}, f32[8,1024,256]{2,1,0:T(8,128)S(1)}, bf16[576,1024]{1,0:T(8,128)(2,1)S(1)}, bf16[512,1024]{1,0:T(8,128)(2,1)S(1)}, f32[16,24,128]{2,1,0:T(8,128)S(1)}) custom-call(s32[1]{0:T(128)} %bitcast.base, s32[1,128]{1,0:T(1,128)} %bitcast.26, bf16[8,192,128]{2,1,0:T(8,128)(2,1)} %bitcast.23, ...), custom_call_target="tpu_custom_call" | custom-call | tf_op jit(solution)/shard_map/pass_one/pallas_call | solution.py:161
  13.6 20.4 %all_to_all.5.stat = f32[16,24,128]{2,1,0:T(8,128)S(1)} all-to-all(f32[16,24,128]{2,1,0:T(8,128)S(1)} %get-tuple-element.77), channel_id=1, replica_groups=mesh['head'=16,'key'=16] {'key'}, dimensions={0} | all-to-all | bytes 393216 | tf_op jit(solution)/shard_map/all_to_all | solution.py:384
  34.0 2.1 %second_first.1 = (bf16[8,144,256]{2,1,0:T(8,128)(2,1)S(1)}, bf16[2,1024,256]{2,1,0:T(8,128)(2,1)S(1)}, f32[1024,128]{1,0:T(8,128)S(1)}, f32[1024,128]{1,0:T(8,128)S(1)}) custom-call(s32[5]{0:T(128)S(1)} %stack.35.sc, f32[16,24,128]{2,1,0:T(8,128)S(1)} %all_to_all.5.stat, bf16[576,1024]{1,0:T(8,128)(2,1)S(1)} %get-tuple-element.78.qcat_t, ...), custom_call_target="tpu_custom_call" | custom-call | tf_op jit(solution)/shard_map/second_first/pallas_call | solution.py:56
  36.2 2.5 %collective-permute-start = (bf16[8,144,256]{2,1,0:T(8,128)(2,1)S(1)}, bf16[8,144,256]{2,1,0:T(8,128)(2,1)S(1)}, u32[]{:S(2)}, u32[]{:S(2)}) collective-permute-start(bf16[8,144,256]{2,1,0:T(8,128)(2,1)S(1)} %get-tuple-element.85), channel_id=1, source_target_pairs={{0,16},{16,0},{32,48},{48,32},{64,80},{80,64},{96,112},{112,96},{1... | collective-permute-start | bytes 1769480 | tf_op jit(solution)/shard_map/ppermute | solution.py:358
  38.7 1.9 %second.3 = (bf16[8,144,256]{2,1,0:T(8,128)(2,1)S(1)}, bf16[2,1024,256]{2,1,0:T(8,128)(2,1)S(1)}) custom-call(s32[5]{0:T(128)S(1)} %stack.33.sc, f32[1024,128]{1,0:T(8,128)S(1)} %get-tuple-element.82.coef, f32[1024,128]{1,0:T(8,128)S(1)} %get-tuple-element.83.delta, bf16[576,1024]{1,0:T(8,128)(2,1)S(1)} %get-tuple-element.78.qcat_t, ...), custom_call_target="tpu_custom_call" | custom-call | tf_op jit(solution)/shard_map/second/pallas_call | solution.py:56
  40.6 0.0 collective-permute-done.got
  40.6 0.1 halve.12
  40.8 1.9 %second.5 = (bf16[8,144,256]{2,1,0:T(8,128)(2,1)S(1)}, bf16[2,1024,256]{2,1,0:T(8,128)(2,1)S(1)}) custom-call(s32[5]{0:T(128)S(1)} %stack.35.sc, f32[1024,128]{1,0:T(8,128)S(1)} %get-tuple-element.82.coef, f32[1024,128]{1,0:T(8,128)S(1)} %get-tuple-element.83.delta, bf16[576,1024]{1,0:T(8,128)(2,1)S(1)} %get-tuple-element.78.qcat_t, ...), custom_call_target="tpu_custom_call" | custom-call | tf_op jit(solution)/shard_map/second/pallas_call | solution.py:56
  42.7 0.2 collective-permute-start.2
  42.8 2.8 %collective-permute-start.1 = (bf16[4,144,256]{2,1,0:T(8,128)(2,1)S(1)}, bf16[4,144,256]{2,1,0:T(8,128)(2,1)S(1)}, u32[]{:S(2)}, u32[]{:S(2)}) collective-permute-start(bf16[4,144,256]{2,1,0:T(8,128)(2,1)S(1)} %get-tuple-element.88), channel_id=1, source_target_pairs={{0,64},{16,208},{32,96},{48,240},{64,0},{80,144},{96,32},{112,176}... | collective-permute-start | bytes 884744 | tf_op jit(solution)/shard_map/ppermute | solution.py:354
  45.6 1.9 %second.4 = (bf16[8,144,256]{2,1,0:T(8,128)(2,1)S(1)}, bf16[2,1024,256]{2,1,0:T(8,128)(2,1)S(1)}) custom-call(s32[5]{0:T(128)S(1)} %stack.33.sc, f32[1024,128]{1,0:T(8,128)S(1)} %get-tuple-element.82.coef, f32[1024,128]{1,0:T(8,128)S(1)} %get-tuple-element.83.delta, bf16[576,1024]{1,0:T(8,128)(2,1)S(1)} %get-tuple-element.78.qcat_t, ...), custom_call_target="tpu_custom_call" | custom-call | tf_op jit(solution)/shard_map/second/pallas_call | solution.py:56
  47.5 0.0 collective-permute-done.2.got
  47.5 0.1 halve.14
  47.6 0.3 collective-permute-start.3
  47.9 1.5 %query_piece.4.refs_0_ = f32[1024,576]{1,0:T(8,128)S(1)} custom-call(s32[5]{0:T(128)S(1)} %stack.35.sc, bf16[2,1024,256]{2,1,0:T(8,128)(2,1)S(1)} %get-tuple-element.90.ds, bf16[576,2048]{1,0:T(8,128)(2,1)S(1)} %bitcast.17), custom_call_target="tpu_custom_call" | custom-call | tf_op jit(solution)/shard_map/query_piece/pallas_call | solution.py:56
  49.5 1.6 %query_piece.5.refs_0_ = f32[1024,576]{1,0:T(8,128)S(1)} custom-call(s32[5]{0:T(128)S(1)} %stack.33.sc, bf16[2,1024,256]{2,1,0:T(8,128)(2,1)S(1)} %get-tuple-element.89.ds, bf16[576,2048]{1,0:T(8,128)(2,1)S(1)} %bitcast.18, f32[1024,576]{1,0:T(8,128)S(1)} %query_piece.4.refs_0_), custom_call_target="tpu_custom_call" | custom-call | tf_op jit(solution)/shard_map/query_piece/pallas_call | solution.py:56
  51.1 0.0 collective-permute-done.1.got
  51.1 0.1 halve.13
  51.1 0.4 collective-permute-start.4
  51.5 1.6 %query_piece.6.refs_0_ = f32[1024,576]{1,0:T(8,128)S(1)} custom-call(s32[5]{0:T(128)S(1)} %stack.35.sc, bf16[2,1024,256]{2,1,0:T(8,128)(2,1)S(1)} %get-tuple-element.102.ds, bf16[576,2048]{1,0:T(8,128)(2,1)S(1)} %bitcast.19, f32[1024,576]{1,0:T(8,128)S(1)} %query_piece.5.refs_0_), custom_call_target="tpu_custom_call" | custom-call | tf_op jit(solution)/shard_map/query_piece/pallas_call | solution.py:56
  53.1 0.0 copy-start.1
  53.1 1.6 %query_piece.7.acc = f32[1024,576]{1,0:T(8,128)S(1)} custom-call(s32[5]{0:T(128)S(1)} %stack.33.sc, bf16[2,1024,256]{2,1,0:T(8,128)(2,1)S(1)} %get-tuple-element.101.ds, bf16[576,2048]{1,0:T(8,128)(2,1)S(1)} %bitcast.20, f32[1024,576]{1,0:T(8,128)S(1)} %query_piece.6.refs_0_), custom_call_target="tpu_custom_call" | custom-call | tf_op jit(solution)/shard_map/query_piece/pallas_call | solution.py:56
  54.7 0.0 collective-permute-done.3.got
  54.7 0.1 halve.15
  54.8 1.2 %collective-permute-start.6 = (bf16[2,144,256]{2,1,0:T(8,128)(2,1)S(1)}, bf16[2,144,256]{2,1,0:T(8,128)(2,1)S(1)}, u32[]{:S(2)}, u32[]{:S(2)}) collective-permute-start(bf16[2,144,256]{2,1,0:T(8,128)(2,1)S(1)} %get-tuple-element.119), channel_id=1, source_target_pairs={{0,192},{16,48},{32,224},{48,16},{64,128},{80,112},{96,160},{112,8... | collective-permute-start | bytes 442376 | tf_op jit(solution)/shard_map/ppermute | solution.py:354
  56.0 1.4 %query_last.1 = (bf16[8,64,192]{2,1,0:T(8,128)(2,1)S(1)}, bf16[8,64,192]{2,1,0:T(8,128)(2,1)S(1)}) custom-call(s32[5]{0:T(128)S(1)} %stack.33.sc, f32[1024,576]{1,0:T(8,128)S(1)} %query_piece.7.acc, bf16[8,128,512]{2,1,0:T(8,128)(2,1)S(1)} %copy-done.1), custom_call_target="tpu_custom_call" | custom-call | tf_op jit(solution)/shard_map/query_last/pallas_call | solution.py:56
  57.4 0.0 collective-permute-done.4.got
  57.4 1.9 %collective-permute-start.5 = (bf16[8,64,192]{2,1,0:T(8,128)(2,1)S(1)}, bf16[8,64,192]{2,1,0:T(8,128)(2,1)S(1)}, u32[]{:S(2)}, u32[]{:S(2)}) collective-permute-start(bf16[8,64,192]{2,1,0:T(8,128)(2,1)S(1)} %get-tuple-element.111), channel_id=1, source_target_pairs={{0,1},{1,0},{2,3},{3,2},{4,5},{5,4},{6,7},{7,6},{8,9},{9,8},{10,11... | collective-permute-start | bytes 589832 | tf_op jit(solution)/shard_map/ppermute | solution.py:362
  59.4 0.0 collective-permute-done.6.got
  59.4 0.1 collective-permute-start.7
  59.5 1.5 %collective-permute-start.9 = (bf16[1,144,256]{2,1,0:T(8,128)(2,1)S(1)}, bf16[1,144,256]{2,1,0:T(8,128)(2,1)S(1)}, u32[]{:S(2)}, u32[]{:S(2)}) collective-permute-start(bf16[1,144,256]{2,1,0:T(8,128)(2,1)S(1)} %get-tuple-element.127), channel_id=1, source_target_pairs={{0,32},{16,80},{32,0},{48,112},{64,96},{80,16},{96,64},{112,48},{1... | collective-permute-start | bytes 221192 | tf_op jit(solution)/shard_map/ppermute | solution.py:354
  61.0 3.5 %collective-permute-done.5.got = bf16[8,64,192]{2,1,0:T(8,128)(2,1)S(1)} collective-permute-done((bf16[8,64,192]{2,1,0:T(8,128)(2,1)S(1)}, bf16[8,64,192]{2,1,0:T(8,128)(2,1)S(1)}, u32[]{:S(2)}, u32[]{:S(2)}) %collective-permute-start.5) | collective-permute-done | bytes 196640 | tf_op jit(solution)/shard_map/ppermute | solution.py:362
  64.5 0.1 halve.16
  64.6 0.0 collective-permute-done.7.got
  64.6 1.1 %collective-permute-start.8 = (bf16[4,64,192]{2,1,0:T(8,128)(2,1)S(1)}, bf16[4,64,192]{2,1,0:T(8,128)(2,1)S(1)}, u32[]{:S(2)}, u32[]{:S(2)}) collective-permute-start(bf16[4,64,192]{2,1,0:T(8,128)(2,1)S(1)} %get-tuple-element.123), channel_id=1, source_target_pairs={{0,2},{1,3},{2,0},{3,1},{4,6},{5,7},{6,4},{7,5},{8,10},{9,11},{10,... | collective-permute-start | bytes 294920 | tf_op jit(solution)/shard_map/ppermute | solution.py:362
  65.7 0.0 collective-permute-done.9.got
  65.8 0.1 collective-permute-start.12
  65.9 1.5 %collective-permute-start.10 = (bf16[1,144,256]{2,1,0:T(8,128)(2,1)S(1)}, bf16[1,144,256]{2,1,0:T(8,128)(2,1)S(1)}, u32[]{:S(2)}, u32[]{:S(2)}) collective-permute-start(bf16[1,144,256]{2,1,0:T(8,128)(2,1)S(1)} %halve.21.own), channel_id=1, source_target_pairs={{0,32},{16,80},{32,0},{48,112},{64,96},{80,16},{96,64},{112,48},{1... | collective-permute-start | bytes 221192 | tf_op jit(solution)/shard_map/ppermute | solution.py:354
  67.4 1.6 %collective-permute-done.12.got = bf16[1,144,256]{2,1,0:T(8,128)(2,1)S(1)} collective-permute-done((bf16[1,144,256]{2,1,0:T(8,128)(2,1)S(1)}, bf16[1,144,256]{2,1,0:T(8,128)(2,1)S(1)}, u32[]{:S(2)}, u32[]{:S(2)}) %collective-permute-start.12) | collective-permute-done | bytes 73760 | tf_op jit(solution)/shard_map/ppermute | solution.py:354
  69.1 0.5 collective-permute-start.15
  69.5 1.3 %collective-permute-done.8.got = bf16[4,64,192]{2,1,0:T(8,128)(2,1)S(1)} collective-permute-done((bf16[4,64,192]{2,1,0:T(8,128)(2,1)S(1)}, bf16[4,64,192]{2,1,0:T(8,128)(2,1)S(1)}, u32[]{:S(2)}, u32[]{:S(2)}) %collective-permute-start.8) | collective-permute-done | bytes 98336 | tf_op jit(solution)/shard_map/ppermute | solution.py:362
  70.8 0.0 collective-permute-done.10.got
  70.9 0.4 collective-permute-start.13
  71.3 1.9 %collective-permute-start.11 = (bf16[2,64,192]{2,1,0:T(8,128)(2,1)S(1)}, bf16[2,64,192]{2,1,0:T(8,128)(2,1)S(1)}, u32[]{:S(2)}, u32[]{:S(2)}) collective-permute-start(bf16[2,64,192]{2,1,0:T(8,128)(2,1)S(1)} %get-tuple-element.133), channel_id=1, source_target_pairs={{0,4},{1,5},{2,6},{3,7},{4,0},{5,1},{6,2},{7,3},{8,12},{9,13},{10,... | collective-permute-start | bytes 147464 | tf_op jit(solution)/shard_map/ppermute | solution.py:362
  73.2 0.3 collective-permute-done.15.got
  73.5 4.0 %collective-permute-start.16 = (bf16[4,144,256]{2,1,0:T(8,128)(2,1)S(1)}, bf16[4,144,256]{2,1,0:T(8,128)(2,1)S(1)}, u32[]{:S(2)}, u32[]{:S(2)}) collective-permute-start(bf16[4,144,256]{2,1,0:T(8,128)(2,1)S(1)} %join.6.refs_0_), channel_id=1, source_target_pairs={{0,64},{16,208},{32,96},{48,240},{64,0},{80,144},{96,32},{112,176}... | collective-permute-start | bytes 884744 | tf_op jit(solution)/shard_map/ppermute | solution.py:354
  77.5 0.9 collective-permute-done.11.got
  78.4 0.0 collective-permute-done.13.got
  78.4 3.4 %collective-permute-start.19 = (bf16[4,144,256]{2,1,0:T(8,128)(2,1)S(1)}, bf16[4,144,256]{2,1,0:T(8,128)(2,1)S(1)}, u32[]{:S(2)}, u32[]{:S(2)}) collective-permute-start(bf16[4,144,256]{2,1,0:T(8,128)(2,1)S(1)} %join.7.refs_4_), channel_id=1, source_target_pairs={{0,64},{16,208},{32,96},{48,240},{64,0},{80,144},{96,32},{112,176}... | collective-permute-start | bytes 884744 | tf_op jit(solution)/shard_map/ppermute | solution.py:354
  81.9 5.4 %collective-permute-start.17 = (bf16[4,144,256]{2,1,0:T(8,128)(2,1)S(1)}, bf16[4,144,256]{2,1,0:T(8,128)(2,1)S(1)}, u32[]{:S(2)}, u32[]{:S(2)}) collective-permute-start(bf16[4,144,256]{2,1,0:T(8,128)(2,1)S(1)} %join.6.refs_0_), channel_id=1, source_target_pairs={{0,16},{16,0},{32,48},{48,32},{64,80},{80,64},{96,112},{112,96},{1... | collective-permute-start | bytes 884744 | tf_op jit(solution)/shard_map/ppermute | solution.py:358
  87.3 0.1 collective-permute-start.20
  87.4 0.0 collective-permute-done.16.refs_1_
  87.4 2.6 %collective-permute-start.18 = (bf16[4,144,256]{2,1,0:T(8,128)(2,1)S(1)}, bf16[4,144,256]{2,1,0:T(8,128)(2,1)S(1)}, u32[]{:S(2)}, u32[]{:S(2)}) collective-permute-start(bf16[4,144,256]{2,1,0:T(8,128)(2,1)S(1)} %collective-permute-done.16.refs_1_), channel_id=1, source_target_pairs={{0,16},{16,0},{32,48},{48,32},{64,80},{80,64},{96,112},{112,96},{1... | collective-permute-start | bytes 884744 | tf_op jit(solution)/shard_map/ppermute | solution.py:358
  90.0 0.0 collective-permute-done.19.refs_5_
  90.0 3.9 %collective-permute-start.21 = (bf16[4,144,256]{2,1,0:T(8,128)(2,1)S(1)}, bf16[4,144,256]{2,1,0:T(8,128)(2,1)S(1)}, u32[]{:S(2)}, u32[]{:S(2)}) collective-permute-start(bf16[4,144,256]{2,1,0:T(8,128)(2,1)S(1)} %collective-permute-done.19.refs_5_), channel_id=1, source_target_pairs={{0,16},{16,0},{32,48},{48,32},{64,80},{80,64},{96,112},{112,96},{1... | collective-permute-start | bytes 884744 | tf_op jit(solution)/shard_map/ppermute | solution.py:358
  94.0 1.0 %collective-permute-start.14 = (bf16[1,64,192]{2,1,0:T(8,128)(2,1)S(1)}, bf16[1,64,192]{2,1,0:T(8,128)(2,1)S(1)}, u32[]{:S(2)}, u32[]{:S(2)}) collective-permute-start(bf16[1,64,192]{2,1,0:T(8,128)(2,1)S(1)} %get-tuple-element.141), channel_id=1, source_target_pairs={{0,8},{1,9},{2,10},{3,11},{4,12},{5,13},{6,14},{7,15},{8,0},{9,1},... | collective-permute-start | bytes 73736 | tf_op jit(solution)/shard_map/ppermute | solution.py:362
  95.0 3.2 %collective-permute-done.14.got = bf16[1,64,192]{2,1,0:T(8,128)(2,1)S(1)} collective-permute-done((bf16[1,64,192]{2,1,0:T(8,128)(2,1)S(1)}, bf16[1,64,192]{2,1,0:T(8,128)(2,1)S(1)}, u32[]{:S(2)}, u32[]{:S(2)}) %collective-permute-start.14) | collective-permute-done | bytes 24608 | tf_op jit(solution)/shard_map/ppermute | solution.py:362
  98.2 0.6 copy.10
  98.9 0.0 collective-permute-done.17.refs_2_
  98.9 0.0 collective-permute-done.20.refs_6_
  98.9 0.0 collective-permute-done.21.refs_7_
  98.9 2.2 %settle.1 = bf16[576,2048]{1,0:T(8,128)(2,1)} custom-call(s32[5]{0:T(128)S(1)} %stack.33.sc, bf16[4,144,256]{2,1,0:T(8,128)(2,1)S(1)} %join.6.refs_0_, bf16[4,144,256]{2,1,0:T(8,128)(2,1)S(1)} %collective-permute-done.16.refs_1_, bf16[4,144,256]{2,1,0:T(8,128)(2,1)S(1)} %collective-permute-done.17.refs_2_, ...), custom_call_target="tpu_custom_call" | custom-call | tf_op jit(solution)/shard_map/settle/pallas_call | solution.py:332
  (15 shorter events, 0.3 us)
Async XLA Ops:
  36.2 4.4 %collective-permute-start = (bf16[8,144,256]{2,1,0:T(8,128)(2,1)S(1)}, bf16[8,144,256]{2,1,0:T(8,128)(2,1)S(1)}, u32[]{:S(2)}, u32[]{:S(2)}) collective-permute-start(bf16[8,144,256]{2,1,0:T(8,128)(2,1)S(1)} %get-tuple-element.85), channel_id=1, source_target_pairs={{0,16},{16,0},{32,48},{48,32},{64,80},{80,64},{96,112},{112,96},{1... | collective-permute-start | bytes 1769480 | tf_op jit(solution)/shard_map/ppermute | solution.py:358
  42.7 4.8 %collective-permute-start.2 = (bf16[8,144,256]{2,1,0:T(8,128)(2,1)S(1)}, bf16[8,144,256]{2,1,0:T(8,128)(2,1)S(1)}, u32[]{:S(2)}, u32[]{:S(2)}) collective-permute-start(bf16[8,144,256]{2,1,0:T(8,128)(2,1)S(1)} %get-tuple-element.95), channel_id=1, source_target_pairs={{0,16},{16,0},{32,48},{48,32},{64,80},{80,64},{96,112},{112,96},{1... | collective-permute-start | bytes 1769480 | tf_op jit(solution)/shard_map/ppermute | solution.py:358
  42.8 8.2 %collective-permute-start.1 = (bf16[4,144,256]{2,1,0:T(8,128)(2,1)S(1)}, bf16[4,144,256]{2,1,0:T(8,128)(2,1)S(1)}, u32[]{:S(2)}, u32[]{:S(2)}) collective-permute-start(bf16[4,144,256]{2,1,0:T(8,128)(2,1)S(1)} %get-tuple-element.88), channel_id=1, source_target_pairs={{0,64},{16,208},{32,96},{48,240},{64,0},{80,144},{96,32},{112,176}... | collective-permute-start | bytes 884744 | tf_op jit(solution)/shard_map/ppermute | solution.py:354
  45.6 2.4 %copy-start = (bf16[2048,576]{0,1:T(8,128)(2,1)S(1)}, bf16[2048,576]{0,1:T(8,128)(2,1)}, u32[]{:S(2)}) copy-start(bf16[2048,576]{0,1:T(8,128)(2,1)} %param.9) | copy-start | bytes 7077892
  47.6 7.1 %collective-permute-start.3 = (bf16[4,144,256]{2,1,0:T(8,128)(2,1)S(1)}, bf16[4,144,256]{2,1,0:T(8,128)(2,1)S(1)}, u32[]{:S(2)}, u32[]{:S(2)}) collective-permute-start(bf16[4,144,256]{2,1,0:T(8,128)(2,1)S(1)} %get-tuple-element.100), channel_id=1, source_target_pairs={{0,64},{16,208},{32,96},{48,240},{64,0},{80,144},{96,32},{112,176}... | collective-permute-start | bytes 884744 | tf_op jit(solution)/shard_map/ppermute | solution.py:354
  51.1 6.3 %collective-permute-start.4 = (bf16[2,144,256]{2,1,0:T(8,128)(2,1)S(1)}, bf16[2,144,256]{2,1,0:T(8,128)(2,1)S(1)}, u32[]{:S(2)}, u32[]{:S(2)}) collective-permute-start(bf16[2,144,256]{2,1,0:T(8,128)(2,1)S(1)} %get-tuple-element.109), channel_id=1, source_target_pairs={{0,192},{16,48},{32,224},{48,16},{64,128},{80,112},{96,160},{112,8... | collective-permute-start | bytes 442376 | tf_op jit(solution)/shard_map/ppermute | solution.py:354
  53.1 2.9 %copy-start.1 = (bf16[8,128,512]{2,1,0:T(8,128)(2,1)S(1)}, bf16[8,128,512]{2,1,0:T(8,128)(2,1)}, u32[]{:S(2)}) copy-start(bf16[8,128,512]{2,1,0:T(8,128)(2,1)} %wuk.3) | copy-start | bytes 3145732
  54.8 4.6 %collective-permute-start.6 = (bf16[2,144,256]{2,1,0:T(8,128)(2,1)S(1)}, bf16[2,144,256]{2,1,0:T(8,128)(2,1)S(1)}, u32[]{:S(2)}, u32[]{:S(2)}) collective-permute-start(bf16[2,144,256]{2,1,0:T(8,128)(2,1)S(1)} %get-tuple-element.119), channel_id=1, source_target_pairs={{0,192},{16,48},{32,224},{48,16},{64,128},{80,112},{96,160},{112,8... | collective-permute-start | bytes 442376 | tf_op jit(solution)/shard_map/ppermute | solution.py:354
  57.4 7.1 %collective-permute-start.5 = (bf16[8,64,192]{2,1,0:T(8,128)(2,1)S(1)}, bf16[8,64,192]{2,1,0:T(8,128)(2,1)S(1)}, u32[]{:S(2)}, u32[]{:S(2)}) collective-permute-start(bf16[8,64,192]{2,1,0:T(8,128)(2,1)S(1)} %get-tuple-element.111), channel_id=1, source_target_pairs={{0,1},{1,0},{2,3},{3,2},{4,5},{5,4},{6,7},{7,6},{8,9},{9,8},{10,11... | collective-permute-start | bytes 589832 | tf_op jit(solution)/shard_map/ppermute | solution.py:362
  59.4 5.1 %collective-permute-start.7 = (bf16[1,144,256]{2,1,0:T(8,128)(2,1)S(1)}, bf16[1,144,256]{2,1,0:T(8,128)(2,1)S(1)}, u32[]{:S(2)}, u32[]{:S(2)}) collective-permute-start(bf16[1,144,256]{2,1,0:T(8,128)(2,1)S(1)} %get-tuple-element.121), channel_id=1, source_target_pairs={{0,32},{16,80},{32,0},{48,112},{64,96},{80,16},{96,64},{112,48},{1... | collective-permute-start | bytes 221192 | tf_op jit(solution)/shard_map/ppermute | solution.py:354
  59.5 6.2 %collective-permute-start.9 = (bf16[1,144,256]{2,1,0:T(8,128)(2,1)S(1)}, bf16[1,144,256]{2,1,0:T(8,128)(2,1)S(1)}, u32[]{:S(2)}, u32[]{:S(2)}) collective-permute-start(bf16[1,144,256]{2,1,0:T(8,128)(2,1)S(1)} %get-tuple-element.127), channel_id=1, source_target_pairs={{0,32},{16,80},{32,0},{48,112},{64,96},{80,16},{96,64},{112,48},{1... | collective-permute-start | bytes 221192 | tf_op jit(solution)/shard_map/ppermute | solution.py:354
  64.6 6.2 %collective-permute-start.8 = (bf16[4,64,192]{2,1,0:T(8,128)(2,1)S(1)}, bf16[4,64,192]{2,1,0:T(8,128)(2,1)S(1)}, u32[]{:S(2)}, u32[]{:S(2)}) collective-permute-start(bf16[4,64,192]{2,1,0:T(8,128)(2,1)S(1)} %get-tuple-element.123), channel_id=1, source_target_pairs={{0,2},{1,3},{2,0},{3,1},{4,6},{5,7},{6,4},{7,5},{8,10},{9,11},{10,... | collective-permute-start | bytes 294920 | tf_op jit(solution)/shard_map/ppermute | solution.py:362
  65.8 3.3 %collective-permute-start.12 = (bf16[1,144,256]{2,1,0:T(8,128)(2,1)S(1)}, bf16[1,144,256]{2,1,0:T(8,128)(2,1)S(1)}, u32[]{:S(2)}, u32[]{:S(2)}) collective-permute-start(bf16[1,144,256]{2,1,0:T(8,128)(2,1)S(1)} %halve.20.own), channel_id=1, source_target_pairs={{0,32},{16,80},{32,0},{48,112},{64,96},{80,16},{96,64},{112,48},{1... | collective-permute-start | bytes 221192 | tf_op jit(solution)/shard_map/ppermute | solution.py:354
  65.9 5.0 %collective-permute-start.10 = (bf16[1,144,256]{2,1,0:T(8,128)(2,1)S(1)}, bf16[1,144,256]{2,1,0:T(8,128)(2,1)S(1)}, u32[]{:S(2)}, u32[]{:S(2)}) collective-permute-start(bf16[1,144,256]{2,1,0:T(8,128)(2,1)S(1)} %halve.21.own), channel_id=1, source_target_pairs={{0,32},{16,80},{32,0},{48,112},{64,96},{80,16},{96,64},{112,48},{1... | collective-permute-start | bytes 221192 | tf_op jit(solution)/shard_map/ppermute | solution.py:354
  69.1 4.4 %collective-permute-start.15 = (bf16[2,144,256]{2,1,0:T(8,128)(2,1)S(1)}, bf16[2,144,256]{2,1,0:T(8,128)(2,1)S(1)}, u32[]{:S(2)}, u32[]{:S(2)}) collective-permute-start(bf16[2,144,256]{2,1,0:T(8,128)(2,1)S(1)} %join.4.own), channel_id=1, source_target_pairs={{0,192},{16,48},{32,224},{48,16},{64,128},{80,112},{96,160},{112,8... | collective-permute-start | bytes 442376 | tf_op jit(solution)/shard_map/ppermute | solution.py:354
  70.9 7.5 %collective-permute-start.13 = (bf16[2,144,256]{2,1,0:T(8,128)(2,1)S(1)}, bf16[2,144,256]{2,1,0:T(8,128)(2,1)S(1)}, u32[]{:S(2)}, u32[]{:S(2)}) collective-permute-start(bf16[2,144,256]{2,1,0:T(8,128)(2,1)S(1)} %join.5.own), channel_id=1, source_target_pairs={{0,192},{16,48},{32,224},{48,16},{64,128},{80,112},{96,160},{112,8... | collective-permute-start | bytes 442376 | tf_op jit(solution)/shard_map/ppermute | solution.py:354
  71.3 7.1 %collective-permute-start.11 = (bf16[2,64,192]{2,1,0:T(8,128)(2,1)S(1)}, bf16[2,64,192]{2,1,0:T(8,128)(2,1)S(1)}, u32[]{:S(2)}, u32[]{:S(2)}) collective-permute-start(bf16[2,64,192]{2,1,0:T(8,128)(2,1)S(1)} %get-tuple-element.133), channel_id=1, source_target_pairs={{0,4},{1,5},{2,6},{3,7},{4,0},{5,1},{6,2},{7,3},{8,12},{9,13},{10,... | collective-permute-start | bytes 147464 | tf_op jit(solution)/shard_map/ppermute | solution.py:362
  73.5 13.9 %collective-permute-start.16 = (bf16[4,144,256]{2,1,0:T(8,128)(2,1)S(1)}, bf16[4,144,256]{2,1,0:T(8,128)(2,1)S(1)}, u32[]{:S(2)}, u32[]{:S(2)}) collective-permute-start(bf16[4,144,256]{2,1,0:T(8,128)(2,1)S(1)} %join.6.refs_0_), channel_id=1, source_target_pairs={{0,64},{16,208},{32,96},{48,240},{64,0},{80,144},{96,32},{112,176}... | collective-permute-start | bytes 884744 | tf_op jit(solution)/shard_map/ppermute | solution.py:354
  78.4 11.6 %collective-permute-start.19 = (bf16[4,144,256]{2,1,0:T(8,128)(2,1)S(1)}, bf16[4,144,256]{2,1,0:T(8,128)(2,1)S(1)}, u32[]{:S(2)}, u32[]{:S(2)}) collective-permute-start(bf16[4,144,256]{2,1,0:T(8,128)(2,1)S(1)} %join.7.refs_4_), channel_id=1, source_target_pairs={{0,64},{16,208},{32,96},{48,240},{64,0},{80,144},{96,32},{112,176}... | collective-permute-start | bytes 884744 | tf_op jit(solution)/shard_map/ppermute | solution.py:354
  81.9 17.0 %collective-permute-start.17 = (bf16[4,144,256]{2,1,0:T(8,128)(2,1)S(1)}, bf16[4,144,256]{2,1,0:T(8,128)(2,1)S(1)}, u32[]{:S(2)}, u32[]{:S(2)}) collective-permute-start(bf16[4,144,256]{2,1,0:T(8,128)(2,1)S(1)} %join.6.refs_0_), channel_id=1, source_target_pairs={{0,16},{16,0},{32,48},{48,32},{64,80},{80,64},{96,112},{112,96},{1... | collective-permute-start | bytes 884744 | tf_op jit(solution)/shard_map/ppermute | solution.py:358
  87.3 11.5 %collective-permute-start.20 = (bf16[4,144,256]{2,1,0:T(8,128)(2,1)S(1)}, bf16[4,144,256]{2,1,0:T(8,128)(2,1)S(1)}, u32[]{:S(2)}, u32[]{:S(2)}) collective-permute-start(bf16[4,144,256]{2,1,0:T(8,128)(2,1)S(1)} %join.7.refs_4_), channel_id=1, source_target_pairs={{0,16},{16,0},{32,48},{48,32},{64,80},{80,64},{96,112},{112,96},{1... | collective-permute-start | bytes 884744 | tf_op jit(solution)/shard_map/ppermute | solution.py:358
  87.4 11.4 %collective-permute-start.18 = (bf16[4,144,256]{2,1,0:T(8,128)(2,1)S(1)}, bf16[4,144,256]{2,1,0:T(8,128)(2,1)S(1)}, u32[]{:S(2)}, u32[]{:S(2)}) collective-permute-start(bf16[4,144,256]{2,1,0:T(8,128)(2,1)S(1)} %collective-permute-done.16.refs_1_), channel_id=1, source_target_pairs={{0,16},{16,0},{32,48},{48,32},{64,80},{80,64},{96,112},{112,96},{1... | collective-permute-start | bytes 884744 | tf_op jit(solution)/shard_map/ppermute | solution.py:358
  90.0 8.8 %collective-permute-start.21 = (bf16[4,144,256]{2,1,0:T(8,128)(2,1)S(1)}, bf16[4,144,256]{2,1,0:T(8,128)(2,1)S(1)}, u32[]{:S(2)}, u32[]{:S(2)}) collective-permute-start(bf16[4,144,256]{2,1,0:T(8,128)(2,1)S(1)} %collective-permute-done.19.refs_5_), channel_id=1, source_target_pairs={{0,16},{16,0},{32,48},{48,32},{64,80},{80,64},{96,112},{112,96},{1... | collective-permute-start | bytes 884744 | tf_op jit(solution)/shard_map/ppermute | solution.py:358
  94.0 4.3 %collective-permute-start.14 = (bf16[1,64,192]{2,1,0:T(8,128)(2,1)S(1)}, bf16[1,64,192]{2,1,0:T(8,128)(2,1)S(1)}, u32[]{:S(2)}, u32[]{:S(2)}) collective-permute-start(bf16[1,64,192]{2,1,0:T(8,128)(2,1)S(1)} %get-tuple-element.141), channel_id=1, source_target_pairs={{0,8},{1,9},{2,10},{3,11},{4,12},{5,13},{6,14},{7,15},{8,0},{9,1},... | collective-permute-start | bytes 73736 | tf_op jit(solution)/shard_map/ppermute | solution.py:362

commit v5 on v4

--- a/solution.py
+++ b/solution.py
@@ -25,7 +25,6 @@
 ALL = HEADS * ROWS
 PEERS = 16
 COLS = WIDE // 4
-CHAINS = 2
 SCALE = 1.0 / math.sqrt(NOPE + ROT)
 SCALE2 = SCALE * math.log2(math.e)
 VLIM = 14 * 1024 * 1024
@@ -120,7 +119,7 @@
             top[rows, :] = best
         return 0
 
-    lax.fori_loop(0, NBLK, score, 0)
+    lax.fori_loop(0, NBLK, score, 0, unroll=NBLK)
     top[...] = jnp.broadcast_to(jnp.max(top[...], axis=1, keepdims=True) * SCALE2, (ALL, 128))
 
     def weigh(j, _):
@@ -141,7 +140,7 @@
             dsum[rows, :] = d
         return 0
 
-    lax.fori_loop(0, NBLK, weigh, 0)
+    lax.fori_loop(0, NBLK, weigh, 0, unroll=NBLK)
     near = lane[:, :128]
     for h, rows in enumerate(heads):
         t = jnp.sum(tot[rows, :], axis=1, keepdims=True)
@@ -262,7 +261,7 @@
     return call(kernel, "query_piece", [((ALL, WIDE), f32)], (sc, ds, lat_t, *acc), 1)[0]
 
 
-def query_last(sc, acc, wuk, keep, send, wide):
+def query_last(acc, wuk, out, wide):
     for h in range(HEADS):
         rows = slice(h * ROWS, (h + 1) * ROWS)
         x = acc[rows, :LAT] * SCALE
@@ -271,17 +270,13 @@
         wide[h, :, :NOPE] = dot_nt(hi, wuk[h]) + dot_nt(lo, wuk[h])
         wide[h, :, NOPE:] = acc[rows, LAT:] * SCALE
     for g in range(PEERS):
-        bits = (g >> 3 & 1) | (g >> 2 & 1) << 1 | (g >> 1 & 1) << 2 | (g & 1) << 3
-        owner = jnp.bitwise_xor(sc[4], bits)
-        mine = wide[:, pl.ds(pl.multiple_of(owner * 8, 8), 8), :]
-        half = keep if g < 8 else send
-        half[g % 8] = mine.reshape(HEADS * 8, NOPE + ROT).astype(bf16)
-
-
-def run_query_last(sc, acc, wuk):
-    outs = [((8, HEADS * 8, NOPE + ROT), bf16)] * 2
+        out[g] = wide[:, g * 8 : (g + 1) * 8, :].reshape(HEADS * 8, NOPE + ROT).astype(bf16)
+
+
+def run_query_last(acc, wuk):
+    outs = [((PEERS, HEADS * 8, NOPE + ROT), bf16)]
     scratch = [pltpu.VMEM((HEADS, ROWS, NOPE + ROT), f32)]
-    return call(query_last, "query_last", outs, (sc, acc, wuk), 1, scratch)
+    return call(query_last, "query_last", outs, (acc, wuk), 0, scratch)[0]
 
 
 def halve(kept, got, *outs):
@@ -307,37 +302,35 @@
     return call(join, "join", [((2 * own.shape[0], COLS, BLK), bf16)], (own, got))[0]
 
 
-def settle(sc, *refs):
+def settle(chain, sc, mine, mine_far, other, other_far, *refs):
     out, sem = refs[-2:]
     copies = []
-    for chain in range(CHAINS):
-        mine, mine_far, other, other_far = refs[4 * chain : 4 * chain + 4]
-        for near, far, half in ((mine, mine_far, sc[3]), (other, other_far, 1 - sc[3])):
-            for i in range(8):
-                b = (i >> 2 & 1, i >> 1 & 1, i & 1)
-                r = [jnp.where(half == 0, b[d], b[(d + 2) % 3]) for d in range(3)]
-                a = [jnp.bitwise_xor(sc[d], r[d]) for d in range(3)]
-                rows = pl.ds(pl.multiple_of((a[2] * 2 + a[1]) * COLS, 16), COLS)
-                block = half * 4 + chain * 2 + a[0]
-                lanes = pl.ds(pl.multiple_of(block * BLK, BLK), BLK)
-                block = near.at[i] if i < 4 else far.at[i - 4]
-                copy = pltpu.make_async_copy(block, out.at[rows, lanes], sem.at[len(copies)])
-                copy.start()
-                copies.append(copy)
+    for near, far, half in ((mine, mine_far, sc[3]), (other, other_far, 1 - sc[3])):
+        for i in range(8):
+            b = (i >> 2 & 1, i >> 1 & 1, i & 1)
+            r = [jnp.where(half == 0, b[d], b[(d + 2) % 3]) for d in range(3)]
+            a = [jnp.bitwise_xor(sc[d], r[d]) for d in range(3)]
+            rows = pl.ds(pl.multiple_of((a[2] * 2 + a[1]) * COLS, 16), COLS)
+            lanes = pl.ds(pl.multiple_of((half * 4 + chain * 2 + a[0]) * BLK, BLK), BLK)
+            block = near.at[i] if i < 4 else far.at[i - 4]
+            copy = pltpu.make_async_copy(block, out.at[rows, lanes], sem.at[len(copies)])
+            copy.start()
+            copies.append(copy)
     for copy in copies:
         copy.wait()
 
 
-def run_settle(sc, *pieces):
+def run_settle(chain, sc, pieces, *earlier):
     return pl.pallas_call(
-        settle,
-        in_specs=[in_smem] + [in_vmem] * len(pieces),
+        functools.partial(settle, chain),
+        in_specs=[in_smem] + [in_vmem] * len(pieces) + [in_hbm] * len(earlier),
         out_specs=in_hbm,
         out_shape=jax.ShapeDtypeStruct((WIDE, KEYS), bf16),
-        scratch_shapes=[pltpu.SemaphoreType.DMA((16 * CHAINS,))],
+        scratch_shapes=[pltpu.SemaphoreType.DMA((16,))],
+        input_output_aliases={5: 0} if earlier else {},
         compiler_params=params(),
         name="settle",
-    )(sc, *pieces)
+    )(sc, *pieces, *earlier)
 
 
 def cube_neighbour(k, d):
@@ -356,10 +349,6 @@
 
 def to_sibling(value):
     return lax.ppermute(value, "head", [(k, k ^ 1) for k in range(16)])
-
-
-def to_key(value, flip):
-    return lax.ppermute(value, "key", [(k, k ^ flip) for k in range(16)])
 
 
 def held(value):
@@ -407,9 +396,9 @@
     kept_b, send_b = run_halve(kept_b, got_b)
     kept_a, send_b, acc = tie((kept_a, send_b, acc))
     got_b = along(send_b, 1)
-    q_keep, q_send = run_query_last(sc_own, acc, w_uk)
-    got_a, q_send = tie((got_a, q_send))
-    q_got = to_key(q_send, 1)
+    dq = run_query_last(acc, w_uk)
+    got_a, dq = tie((got_a, dq))
+    dq = lax.all_to_all(dq, "key", 0, 0, tiled=True)
     kept_a, send_a = run_halve(kept_a, got_a)
     kept_b, send_a = tie((kept_b, send_a))
     got_a = along(send_a, 2)
@@ -419,36 +408,27 @@
     (own_a,) = run_halve(kept_a, got_a)
     kept_b, own_a = tie((kept_b, own_a))
     got_a = along(own_a, 2)
-    q_keep, q_send = run_halve(q_keep, q_got)
-    got_b, q_send = tie((got_b, q_send))
-    q_got = to_key(q_send, 2)
     (own_b,) = run_halve(kept_b, got_b)
     own_a, own_b = tie((own_a, own_b))
     got_b = along(own_b, 2)
     own_a = run_join(own_a, got_a)
     own_b, own_a = tie((own_b, own_a))
     got_a = along(own_a, 1)
-    q_keep, q_send = run_halve(q_keep, q_got)
-    got_b, q_send = tie((got_b, q_send))
-    q_got = to_key(q_send, 4)
     own_b = run_join(own_b, got_b)
-    own_a, own_b = tie((own_a, own_b))
+    own_a, own_b, dq = tie((own_a, own_b, dq))
     got_b = along(own_b, 1)
     own_a = run_join(own_a, got_a)
     own_b, own_a = tie((own_b, own_a))
     far_a, near_a = along(own_a, 0), to_sibling(own_a)
-    q_keep, q_send = run_halve(q_keep, q_got)
-    got_b, q_send = tie((got_b, q_send))
-    q_got = to_key(q_send, 8)
     own_b = run_join(own_b, got_b)
     far_b, near_b = along(own_b, 0), to_sibling(own_b)
-    (dq,) = run_halve(q_keep, q_got)
     pieces = [
         (own_a, far_a, near_a, to_sibling(far_a)),
         (own_b, far_b, near_b, to_sibling(far_b)),
     ]
-    d_latent = run_settle(sc_own, *pieces[0], *pieces[1]).T
-
+    d_latent = run_settle(1, sc_own, pieces[1], run_settle(0, sc_own, pieces[0])).T
+
+    dq = jnp.sum(dq.astype(f32), axis=0).astype(bf16)
     d_queries = jnp.transpose(dq.reshape(HEADS, 8, NOPE + ROT), (1, 0, 2))
     return (d_queries, d_latent)
 

time: 101 us -> 97.5 us (0.965)
  starting transfers between devices: 36.9 us -> 31.5 us
  waiting for transfers between devices: 10.9 us -> 13.8 us
  Pallas kernels: 31.2 us -> 29.7 us
    ppermute x12, waiting for transfers between devices: 1.96 us -> 11.8 us  [along(): return lax.ppermute(value, 'head', pairs)]
    ppermute x4 -> x0, waiting for transfers between devices: 8.94 us -> none  [to_key(): return lax.ppermute(value, 'key', [(k, k ^ flip) for k in range(16)])]
    ppermute x4 -> x0, starting transfers between devices: 5.98 us -> none  [to_key(): return lax.ppermute(value, 'key', [(k, k ^ flip) for k in range(16)])]
    ppermute x12, starting transfers between devices: 16.2 us -> 11.5 us  [along(): return lax.ppermute(value, 'head', pairs)]
    all_to_all x0 -> x1, starting transfers between devices: none -> 4.52 us  [shards(): dq = lax.all_to_all(dq, 'key', 0, 0, tiled=True)]
    pallas_call x1, Pallas kernels: 12.8 us -> 10 us  [run_pass_one(): pl.pallas_call(pass_one, in_specs=[in_smem] + [in_hbm] * 6, out_specs=[in...]
    all_to_all x0 -> x1, waiting for transfers between devices: none -> 1.99 us  [shards(): dq = lax.all_to_all(dq, 'key', 0, 0, tiled=True)]
    pallas_call x1 -> x2, Pallas kernels: 2.22 us -> 3.38 us  [run_settle(): pl.pallas_call(functools.partial(settle, chain), in_specs=[in_smem] + [in...]
  transfers between devices with their start and end apart: 22 -> 19, of which waited for: 6 -> 7; matrix products, arithmetic and copies ran while one was open for 1% -> 1% of each run, Pallas kernels for 12% -> 14%
where the time goes in v5:
time: 97.5 us; the launch traced here: 97.3 us
  starting transfers between devices  31.5 us (32%)
  Pallas kernels  29.7 us (30%)
  blocking collectives  20.4 us (21%)
  waiting for transfers between devices  13.8 us (14%)
  between operations  1.04 us (1%)
    all_to_all x1, blocking collectives, shards(): stat = lax.all_to_all(stat, 'key', 0, 0, tiled=True)  20.4 us
    pallas_call x21, Pallas kernels, call(): pl.pallas_call(kernel, in_specs=[in_smem] * scalars + [in_vmem] * (len(ar...  16.2 us
    ppermute x6, starting transfers between devices, to_sibling(): return lax.ppermute(value, 'head', [(k, k ^ 1) for k in range(16)])  15.4 us
    ppermute x12, waiting for transfers between devices, along(): return lax.ppermute(value, 'head', pairs)  11.8 us
    ppermute x12, starting transfers between devices, along(): return lax.ppermute(value, 'head', pairs)  11.5 us
    pallas_call x1, Pallas kernels, run_pass_one(): pl.pallas_call(pass_one, in_specs=[in_smem] + [in_hbm] * 6, out_specs=[in...  10 us
    all_to_all x1, starting transfers between devices, shards(): dq = lax.all_to_all(dq, 'key', 0, 0, tiled=True)  4.52 us
    pallas_call x2, Pallas kernels, run_settle(): pl.pallas_call(functools.partial(settle, chain), in_specs=[in_smem] + [in...  3.38 us
  transfers between devices with their start and end apart: 19, of which 7 were waited for; matrix products, arithmetic and copies ran while one was open for 1% of the time, Pallas kernels for 14%

profile of v5, /device:TPU:1, one launch (start us, length us, event | category | flops | bytes accessed | tf_op | source)
XLA Modules:
  0.0 97.3 jit_solution(1066592242471846285)
XLA Ops:
  0.6 0.1 stack.35.sc
  0.7 0.1 stack.33.sc
  0.8 10.0 %pass_one.1 = (f32[8,1024,256]{2,1,0:T(8,128)S(1)}, f32[8,1024,256]{2,1,0:T(8,128)S(1)}, bf16[576,1024]{1,0:T(8,128)(2,1)S(1)}, bf16[512,1024]{1,0:T(8,128)(2,1)S(1)}, f32[16,24,128]{2,1,0:T(8,128)S(1)}) custom-call(s32[1]{0:T(128)} %bitcast.base, s32[1,128]{1,0:T(1,128)} %bitcast.24, bf16[8,192,128]{2,1,0:T(8,128)(2,1)} %bitcast.21, ...), custom_call_target="tpu_custom_call" | custom-call | tf_op jit(solution)/shard_map/pass_one/pallas_call | solution.py:160
  10.9 20.4 %all_to_all.10.stat = f32[16,24,128]{2,1,0:T(8,128)S(1)} all-to-all(f32[16,24,128]{2,1,0:T(8,128)S(1)} %get-tuple-element.64), channel_id=1, replica_groups=mesh['head'=16,'key'=16] {'key'}, dimensions={0} | all-to-all | bytes 393216 | tf_op jit(solution)/shard_map/all_to_all | solution.py:373
  31.3 2.1 %second_first.1 = (bf16[8,144,256]{2,1,0:T(8,128)(2,1)S(1)}, bf16[2,1024,256]{2,1,0:T(8,128)(2,1)S(1)}, f32[1024,128]{1,0:T(8,128)S(1)}, f32[1024,128]{1,0:T(8,128)S(1)}) custom-call(s32[5]{0:T(128)S(1)} %stack.35.sc, f32[16,24,128]{2,1,0:T(8,128)S(1)} %all_to_all.10.stat, bf16[576,1024]{1,0:T(8,128)(2,1)S(1)} %get-tuple-element.65.qcat_t, ...), custom_call_target="tpu_custom_call" | custom-call | tf_op jit(solution)/shard_map/second_first/pallas_call | solution.py:55
  33.4 2.7 %collective-permute-start = (bf16[8,144,256]{2,1,0:T(8,128)(2,1)S(1)}, bf16[8,144,256]{2,1,0:T(8,128)(2,1)S(1)}, u32[]{:S(2)}, u32[]{:S(2)}) collective-permute-start(bf16[8,144,256]{2,1,0:T(8,128)(2,1)S(1)} %get-tuple-element.73), channel_id=1, source_target_pairs={{0,16},{16,0},{32,48},{48,32},{64,80},{80,64},{96,112},{112,96},{1... | collective-permute-start | bytes 1769480 | tf_op jit(solution)/shard_map/ppermute | solution.py:351
  36.1 1.9 %second.4 = (bf16[8,144,256]{2,1,0:T(8,128)(2,1)S(1)}, bf16[2,1024,256]{2,1,0:T(8,128)(2,1)S(1)}) custom-call(s32[5]{0:T(128)S(1)} %stack.33.sc, f32[1024,128]{1,0:T(8,128)S(1)} %get-tuple-element.69.coef, f32[1024,128]{1,0:T(8,128)S(1)} %get-tuple-element.70.delta, bf16[576,1024]{1,0:T(8,128)(2,1)S(1)} %get-tuple-element.65.qcat_t, ...), custom_call_target="tpu_custom_call" | custom-call | tf_op jit(solution)/shard_map/second/pallas_call | solution.py:55
  38.0 0.0 collective-permute-done.got
  38.0 0.1 halve.8
  38.2 1.9 %second.5 = (bf16[8,144,256]{2,1,0:T(8,128)(2,1)S(1)}, bf16[2,1024,256]{2,1,0:T(8,128)(2,1)S(1)}) custom-call(s32[5]{0:T(128)S(1)} %stack.35.sc, f32[1024,128]{1,0:T(8,128)S(1)} %get-tuple-element.69.coef, f32[1024,128]{1,0:T(8,128)S(1)} %get-tuple-element.70.delta, bf16[576,1024]{1,0:T(8,128)(2,1)S(1)} %get-tuple-element.65.qcat_t, ...), custom_call_target="tpu_custom_call" | custom-call | tf_op jit(solution)/shard_map/second/pallas_call | solution.py:55
  40.1 0.2 collective-permute-start.1
  40.3 2.8 %collective-permute-start.2 = (bf16[4,144,256]{2,1,0:T(8,128)(2,1)S(1)}, bf16[4,144,256]{2,1,0:T(8,128)(2,1)S(1)}, u32[]{:S(2)}, u32[]{:S(2)}) collective-permute-start(bf16[4,144,256]{2,1,0:T(8,128)(2,1)S(1)} %get-tuple-element.79), channel_id=1, source_target_pairs={{0,64},{16,208},{32,96},{48,240},{64,0},{80,144},{96,32},{112,176}... | collective-permute-start | bytes 884744 | tf_op jit(solution)/shard_map/ppermute | solution.py:347
  43.0 0.0 copy-start
  43.0 1.9 %second.3 = (bf16[8,144,256]{2,1,0:T(8,128)(2,1)S(1)}, bf16[2,1024,256]{2,1,0:T(8,128)(2,1)S(1)}) custom-call(s32[5]{0:T(128)S(1)} %stack.33.sc, f32[1024,128]{1,0:T(8,128)S(1)} %get-tuple-element.69.coef, f32[1024,128]{1,0:T(8,128)S(1)} %get-tuple-element.70.delta, bf16[576,1024]{1,0:T(8,128)(2,1)S(1)} %get-tuple-element.65.qcat_t, ...), custom_call_target="tpu_custom_call" | custom-call | tf_op jit(solution)/shard_map/second/pallas_call | solution.py:55
  44.9 0.0 collective-permute-done.1.got
  44.9 0.1 halve.9
  45.1 0.1 collective-permute-start.3
  45.2 0.0 copy-done
  45.2 1.5 %query_piece.4.refs_0_ = f32[1024,576]{1,0:T(8,128)S(1)} custom-call(s32[5]{0:T(128)S(1)} %stack.35.sc, bf16[2,1024,256]{2,1,0:T(8,128)(2,1)S(1)} %get-tuple-element.81.ds, bf16[576,2048]{1,0:T(8,128)(2,1)S(1)} %bitcast.16), custom_call_target="tpu_custom_call" | custom-call | tf_op jit(solution)/shard_map/query_piece/pallas_call | solution.py:55
  46.7 1.6 %query_piece.5.refs_0_ = f32[1024,576]{1,0:T(8,128)S(1)} custom-call(s32[5]{0:T(128)S(1)} %stack.33.sc, bf16[2,1024,256]{2,1,0:T(8,128)(2,1)S(1)} %get-tuple-element.80.ds, bf16[576,2048]{1,0:T(8,128)(2,1)S(1)} %bitcast.17, f32[1024,576]{1,0:T(8,128)S(1)} %query_piece.4.refs_0_), custom_call_target="tpu_custom_call" | custom-call | tf_op jit(solution)/shard_map/query_piece/pallas_call | solution.py:55
  48.3 0.0 collective-permute-done.2.got
  48.3 0.1 halve.10
  48.4 0.4 collective-permute-start.4
  48.8 1.6 %query_piece.6.refs_0_ = f32[1024,576]{1,0:T(8,128)S(1)} custom-call(s32[5]{0:T(128)S(1)} %stack.35.sc, bf16[2,1024,256]{2,1,0:T(8,128)(2,1)S(1)} %get-tuple-element.88.ds, bf16[576,2048]{1,0:T(8,128)(2,1)S(1)} %bitcast.18, f32[1024,576]{1,0:T(8,128)S(1)} %query_piece.5.refs_0_), custom_call_target="tpu_custom_call" | custom-call | tf_op jit(solution)/shard_map/query_piece/pallas_call | solution.py:55
  50.3 0.0 copy-start.1
  50.4 1.6 %query_piece.7.acc = f32[1024,576]{1,0:T(8,128)S(1)} custom-call(s32[5]{0:T(128)S(1)} %stack.33.sc, bf16[2,1024,256]{2,1,0:T(8,128)(2,1)S(1)} %get-tuple-element.87.ds, bf16[576,2048]{1,0:T(8,128)(2,1)S(1)} %bitcast.19, f32[1024,576]{1,0:T(8,128)S(1)} %query_piece.6.refs_0_), custom_call_target="tpu_custom_call" | custom-call | tf_op jit(solution)/shard_map/query_piece/pallas_call | solution.py:55
  51.9 0.0 collective-permute-done.3.got
  52.0 0.1 halve.11
  52.0 0.0 copy-done.1
  52.0 1.6 %query_last.1 = bf16[16,64,192]{2,1,0:T(8,128)(2,1)} custom-call(f32[1024,576]{1,0:T(8,128)S(1)} %query_piece.7.acc, bf16[8,128,512]{2,1,0:T(8,128)(2,1)S(1)} %copy-done.1), custom_call_target="tpu_custom_call" | custom-call | tf_op jit(solution)/shard_map/query_last/pallas_call | solution.py:55
  53.7 0.0 collective-permute-done.4.got
  53.7 4.5 %all-to-all-start.1 = ((bf16[16,64,192]{2,1,0:T(8,128)(2,1)}), bf16[16,64,192]{2,1,0:T(8,128)(2,1)S(1)}, u32[]{:S(2)}, u32[]{:S(2)}) async-start(bf16[16,64,192]{2,1,0:T(8,128)(2,1)} %query_last.1), calls=%async_computation.1 | async-start | bytes 1048576 | tf_op jit(solution)/shard_map/all_to_all | solution.py:401
  58.2 0.5 collective-permute-start.5
  58.7 0.3 collective-permute-start.6
  59.1 4.3 %collective-permute-done.5.got = bf16[2,144,256]{2,1,0:T(8,128)(2,1)S(1)} collective-permute-done((bf16[2,144,256]{2,1,0:T(8,128)(2,1)S(1)}, bf16[2,144,256]{2,1,0:T(8,128)(2,1)S(1)}, u32[]{:S(2)}, u32[]{:S(2)}) %collective-permute-start.5) | collective-permute-done | bytes 147488 | tf_op jit(solution)/shard_map/ppermute | solution.py:347
  63.4 0.4 collective-permute-start.7
  63.8 0.0 collective-permute-done.6.got
  63.8 1.3 %collective-permute-start.8 = (bf16[1,144,256]{2,1,0:T(8,128)(2,1)S(1)}, bf16[1,144,256]{2,1,0:T(8,128)(2,1)S(1)}, u32[]{:S(2)}, u32[]{:S(2)}) collective-permute-start(bf16[1,144,256]{2,1,0:T(8,128)(2,1)S(1)} %halve.14.own), channel_id=1, source_target_pairs={{0,32},{16,80},{32,0},{48,112},{64,96},{80,16},{96,64},{112,48},{1... | collective-permute-start | bytes 221192 | tf_op jit(solution)/shard_map/ppermute | solution.py:347
  65.0 1.9 %collective-permute-done.7.got = bf16[1,144,256]{2,1,0:T(8,128)(2,1)S(1)} collective-permute-done((bf16[1,144,256]{2,1,0:T(8,128)(2,1)S(1)}, bf16[1,144,256]{2,1,0:T(8,128)(2,1)S(1)}, u32[]{:S(2)}, u32[]{:S(2)}) %collective-permute-start.7) | collective-permute-done | bytes 73760 | tf_op jit(solution)/shard_map/ppermute | solution.py:347
  67.0 0.4 collective-permute-start.9
  67.4 0.4 collective-permute-done.8.got
  67.8 0.1 collective-permute-start.10
  67.9 2.7 %collective-permute-done.9.got = bf16[1,144,256]{2,1,0:T(8,128)(2,1)S(1)} collective-permute-done((bf16[1,144,256]{2,1,0:T(8,128)(2,1)S(1)}, bf16[1,144,256]{2,1,0:T(8,128)(2,1)S(1)}, u32[]{:S(2)}, u32[]{:S(2)}) %collective-permute-start.9) | collective-permute-done | bytes 73760 | tf_op jit(solution)/shard_map/ppermute | solution.py:347
  70.6 2.0 %all-to-all-done.1 = bf16[16,64,192]{2,1,0:T(8,128)(2,1)S(1)} async-done(((bf16[16,64,192]{2,1,0:T(8,128)(2,1)}), bf16[16,64,192]{2,1,0:T(8,128)(2,1)S(1)}, u32[]{:S(2)}, u32[]{:S(2)}) %all-to-all-start.1) | async-done | bytes 393248 | tf_op jit(solution)/shard_map/all_to_all | solution.py:401
  72.6 0.5 collective-permute-start.11
  73.1 1.5 %collective-permute-done.10.got = bf16[2,144,256]{2,1,0:T(8,128)(2,1)S(1)} collective-permute-done((bf16[2,144,256]{2,1,0:T(8,128)(2,1)S(1)}, bf16[2,144,256]{2,1,0:T(8,128)(2,1)S(1)}, u32[]{:S(2)}, u32[]{:S(2)}) %collective-permute-start.10) | collective-permute-done | bytes 147488 | tf_op jit(solution)/shard_map/ppermute | solution.py:347
  74.6 2.0 %collective-permute-start.15 = (bf16[4,144,256]{2,1,0:T(8,128)(2,1)S(1)}, bf16[4,144,256]{2,1,0:T(8,128)(2,1)S(1)}, u32[]{:S(2)}, u32[]{:S(2)}) collective-permute-start(bf16[4,144,256]{2,1,0:T(8,128)(2,1)S(1)} %join.6.mine), channel_id=1, source_target_pairs={{0,64},{16,208},{32,96},{48,240},{64,0},{80,144},{96,32},{112,176}... | collective-permute-start | bytes 884744 | tf_op jit(solution)/shard_map/ppermute | solution.py:347
  76.6 1.0 %collective-permute-done.11.got = bf16[2,144,256]{2,1,0:T(8,128)(2,1)S(1)} collective-permute-done((bf16[2,144,256]{2,1,0:T(8,128)(2,1)S(1)}, bf16[2,144,256]{2,1,0:T(8,128)(2,1)S(1)}, u32[]{:S(2)}, u32[]{:S(2)}) %collective-permute-start.11) | collective-permute-done | bytes 147488 | tf_op jit(solution)/shard_map/ppermute | solution.py:347
  77.6 2.8 %collective-permute-start.12 = (bf16[4,144,256]{2,1,0:T(8,128)(2,1)S(1)}, bf16[4,144,256]{2,1,0:T(8,128)(2,1)S(1)}, u32[]{:S(2)}, u32[]{:S(2)}) collective-permute-start(bf16[4,144,256]{2,1,0:T(8,128)(2,1)S(1)} %join.7.mine), channel_id=1, source_target_pairs={{0,64},{16,208},{32,96},{48,240},{64,0},{80,144},{96,32},{112,176}... | collective-permute-start | bytes 884744 | tf_op jit(solution)/shard_map/ppermute | solution.py:347
  80.4 6.0 %collective-permute-start.16 = (bf16[4,144,256]{2,1,0:T(8,128)(2,1)S(1)}, bf16[4,144,256]{2,1,0:T(8,128)(2,1)S(1)}, u32[]{:S(2)}, u32[]{:S(2)}) collective-permute-start(bf16[4,144,256]{2,1,0:T(8,128)(2,1)S(1)} %join.6.mine), channel_id=1, source_target_pairs={{0,16},{16,0},{32,48},{48,32},{64,80},{80,64},{96,112},{112,96},{1... | collective-permute-start | bytes 884744 | tf_op jit(solution)/shard_map/ppermute | solution.py:351
  86.4 0.0 collective-permute-done.15.mine_far
  86.4 3.2 %collective-permute-start.17 = (bf16[4,144,256]{2,1,0:T(8,128)(2,1)S(1)}, bf16[4,144,256]{2,1,0:T(8,128)(2,1)S(1)}, u32[]{:S(2)}, u32[]{:S(2)}) collective-permute-start(bf16[4,144,256]{2,1,0:T(8,128)(2,1)S(1)} %collective-permute-done.15.mine_far), channel_id=1, source_target_pairs={{0,16},{16,0},{32,48},{48,32},{64,80},{80,64},{96,112},{112,96},{1... | collective-permute-start | bytes 884744 | tf_op jit(solution)/shard_map/ppermute | solution.py:351
  89.6 0.0 collective-permute-start.13
  89.6 0.0 collective-permute-done.12.mine_far
  89.6 3.4 %collective-permute-start.14 = (bf16[4,144,256]{2,1,0:T(8,128)(2,1)S(1)}, bf16[4,144,256]{2,1,0:T(8,128)(2,1)S(1)}, u32[]{:S(2)}, u32[]{:S(2)}) collective-permute-start(bf16[4,144,256]{2,1,0:T(8,128)(2,1)S(1)} %collective-permute-done.12.mine_far), channel_id=1, source_target_pairs={{0,16},{16,0},{32,48},{48,32},{64,80},{80,64},{96,112},{112,96},{1... | collective-permute-start | bytes 884744 | tf_op jit(solution)/shard_map/ppermute | solution.py:351
  93.0 0.1 reduce_sum.12
  93.1 0.6 copy.9
  93.7 0.0 collective-permute-done.16.other
  93.7 0.0 collective-permute-done.17.other_far
  93.7 1.7 %settle.2.refs_0_ = bf16[576,2048]{1,0:T(8,128)(2,1)} custom-call(s32[5]{0:T(128)S(1)} %stack.33.sc, bf16[4,144,256]{2,1,0:T(8,128)(2,1)S(1)} %join.6.mine, bf16[4,144,256]{2,1,0:T(8,128)(2,1)S(1)} %collective-permute-done.15.mine_far, bf16[4,144,256]{2,1,0:T(8,128)(2,1)S(1)} %collective-permute-done.16.other, ...), custom_call_target="tpu_custom_call" | custom-call | tf_op jit(solution)/shard_map/settle/pallas_call | solution.py:324
  95.4 0.0 collective-permute-done.13.other
  95.4 0.0 collective-permute-done.14.other_far
  95.4 1.7 %settle.3 = bf16[576,2048]{1,0:T(8,128)(2,1)} custom-call(s32[5]{0:T(128)S(1)} %stack.33.sc, bf16[4,144,256]{2,1,0:T(8,128)(2,1)S(1)} %join.7.mine, bf16[4,144,256]{2,1,0:T(8,128)(2,1)S(1)} %collective-permute-done.12.mine_far, bf16[4,144,256]{2,1,0:T(8,128)(2,1)S(1)} %collective-permute-done.13.other, ...), custom_call_target="tpu_custom_call", output_to_operand_aliasing={{}: (5, {})} | custom-call | tf_op jit(solution)/shard_map/settle/pallas_call | solution.py:324
  (8 shorter events, 0.2 us)
Async XLA Ops:
  33.4 4.6 %collective-permute-start = (bf16[8,144,256]{2,1,0:T(8,128)(2,1)S(1)}, bf16[8,144,256]{2,1,0:T(8,128)(2,1)S(1)}, u32[]{:S(2)}, u32[]{:S(2)}) collective-permute-start(bf16[8,144,256]{2,1,0:T(8,128)(2,1)S(1)} %get-tuple-element.73), channel_id=1, source_target_pairs={{0,16},{16,0},{32,48},{48,32},{64,80},{80,64},{96,112},{112,96},{1... | collective-permute-start | bytes 1769480 | tf_op jit(solution)/shard_map/ppermute | solution.py:351
  40.1 4.8 %collective-permute-start.1 = (bf16[8,144,256]{2,1,0:T(8,128)(2,1)S(1)}, bf16[8,144,256]{2,1,0:T(8,128)(2,1)S(1)}, u32[]{:S(2)}, u32[]{:S(2)}) collective-permute-start(bf16[8,144,256]{2,1,0:T(8,128)(2,1)S(1)} %get-tuple-element.76), channel_id=1, source_target_pairs={{0,16},{16,0},{32,48},{48,32},{64,80},{80,64},{96,112},{112,96},{1... | collective-permute-start | bytes 1769480 | tf_op jit(solution)/shard_map/ppermute | solution.py:351
  40.3 8.1 %collective-permute-start.2 = (bf16[4,144,256]{2,1,0:T(8,128)(2,1)S(1)}, bf16[4,144,256]{2,1,0:T(8,128)(2,1)S(1)}, u32[]{:S(2)}, u32[]{:S(2)}) collective-permute-start(bf16[4,144,256]{2,1,0:T(8,128)(2,1)S(1)} %get-tuple-element.79), channel_id=1, source_target_pairs={{0,64},{16,208},{32,96},{48,240},{64,0},{80,144},{96,32},{112,176}... | collective-permute-start | bytes 884744 | tf_op jit(solution)/shard_map/ppermute | solution.py:347
  43.0 2.2 %copy-start = (bf16[2048,576]{0,1:T(8,128)(2,1)S(1)}, bf16[2048,576]{0,1:T(8,128)(2,1)}, u32[]{:S(2)}) copy-start(bf16[2048,576]{0,1:T(8,128)(2,1)} %param.9) | copy-start | bytes 7077892
  45.1 6.9 %collective-permute-start.3 = (bf16[4,144,256]{2,1,0:T(8,128)(2,1)S(1)}, bf16[4,144,256]{2,1,0:T(8,128)(2,1)S(1)}, u32[]{:S(2)}, u32[]{:S(2)}) collective-permute-start(bf16[4,144,256]{2,1,0:T(8,128)(2,1)S(1)} %get-tuple-element.86), channel_id=1, source_target_pairs={{0,64},{16,208},{32,96},{48,240},{64,0},{80,144},{96,32},{112,176}... | collective-permute-start | bytes 884744 | tf_op jit(solution)/shard_map/ppermute | solution.py:347
  48.4 5.3 %collective-permute-start.4 = (bf16[2,144,256]{2,1,0:T(8,128)(2,1)S(1)}, bf16[2,144,256]{2,1,0:T(8,128)(2,1)S(1)}, u32[]{:S(2)}, u32[]{:S(2)}) collective-permute-start(bf16[2,144,256]{2,1,0:T(8,128)(2,1)S(1)} %get-tuple-element.96), channel_id=1, source_target_pairs={{0,192},{16,48},{32,224},{48,16},{64,128},{80,112},{96,160},{112,8... | collective-permute-start | bytes 442376 | tf_op jit(solution)/shard_map/ppermute | solution.py:347
  50.3 1.7 %copy-start.1 = (bf16[8,128,512]{2,1,0:T(8,128)(2,1)S(1)}, bf16[8,128,512]{2,1,0:T(8,128)(2,1)}, u32[]{:S(2)}) copy-start(bf16[8,128,512]{2,1,0:T(8,128)(2,1)} %wuk.3) | copy-start | bytes 3145732
  53.7 18.9 %all-to-all-start.1 = ((bf16[16,64,192]{2,1,0:T(8,128)(2,1)}), bf16[16,64,192]{2,1,0:T(8,128)(2,1)S(1)}, u32[]{:S(2)}, u32[]{:S(2)}) async-start(bf16[16,64,192]{2,1,0:T(8,128)(2,1)} %query_last.1), calls=%async_computation.1 | async-start | bytes 1048576 | tf_op jit(solution)/shard_map/all_to_all | solution.py:401
  58.2 5.1 %collective-permute-start.5 = (bf16[2,144,256]{2,1,0:T(8,128)(2,1)S(1)}, bf16[2,144,256]{2,1,0:T(8,128)(2,1)S(1)}, u32[]{:S(2)}, u32[]{:S(2)}) collective-permute-start(bf16[2,144,256]{2,1,0:T(8,128)(2,1)S(1)} %get-tuple-element.101), channel_id=1, source_target_pairs={{0,192},{16,48},{32,224},{48,16},{64,128},{80,112},{96,160},{112,8... | collective-permute-start | bytes 442376 | tf_op jit(solution)/shard_map/ppermute | solution.py:347
  58.7 5.0 %collective-permute-start.6 = (bf16[1,144,256]{2,1,0:T(8,128)(2,1)S(1)}, bf16[1,144,256]{2,1,0:T(8,128)(2,1)S(1)}, u32[]{:S(2)}, u32[]{:S(2)}) collective-permute-start(bf16[1,144,256]{2,1,0:T(8,128)(2,1)S(1)} %get-tuple-element.106), channel_id=1, source_target_pairs={{0,32},{16,80},{32,0},{48,112},{64,96},{80,16},{96,64},{112,48},{1... | collective-permute-start | bytes 221192 | tf_op jit(solution)/shard_map/ppermute | solution.py:347
  63.4 3.6 %collective-permute-start.7 = (bf16[1,144,256]{2,1,0:T(8,128)(2,1)S(1)}, bf16[1,144,256]{2,1,0:T(8,128)(2,1)S(1)}, u32[]{:S(2)}, u32[]{:S(2)}) collective-permute-start(bf16[1,144,256]{2,1,0:T(8,128)(2,1)S(1)} %get-tuple-element.109), channel_id=1, source_target_pairs={{0,32},{16,80},{32,0},{48,112},{64,96},{80,16},{96,64},{112,48},{1... | collective-permute-start | bytes 221192 | tf_op jit(solution)/shard_map/ppermute | solution.py:347
  63.8 4.0 %collective-permute-start.8 = (bf16[1,144,256]{2,1,0:T(8,128)(2,1)S(1)}, bf16[1,144,256]{2,1,0:T(8,128)(2,1)S(1)}, u32[]{:S(2)}, u32[]{:S(2)}) collective-permute-start(bf16[1,144,256]{2,1,0:T(8,128)(2,1)S(1)} %halve.14.own), channel_id=1, source_target_pairs={{0,32},{16,80},{32,0},{48,112},{64,96},{80,16},{96,64},{112,48},{1... | collective-permute-start | bytes 221192 | tf_op jit(solution)/shard_map/ppermute | solution.py:347
  67.0 3.6 %collective-permute-start.9 = (bf16[1,144,256]{2,1,0:T(8,128)(2,1)S(1)}, bf16[1,144,256]{2,1,0:T(8,128)(2,1)S(1)}, u32[]{:S(2)}, u32[]{:S(2)}) collective-permute-start(bf16[1,144,256]{2,1,0:T(8,128)(2,1)S(1)} %halve.15.own), channel_id=1, source_target_pairs={{0,32},{16,80},{32,0},{48,112},{64,96},{80,16},{96,64},{112,48},{1... | collective-permute-start | bytes 221192 | tf_op jit(solution)/shard_map/ppermute | solution.py:347
  67.8 6.8 %collective-permute-start.10 = (bf16[2,144,256]{2,1,0:T(8,128)(2,1)S(1)}, bf16[2,144,256]{2,1,0:T(8,128)(2,1)S(1)}, u32[]{:S(2)}, u32[]{:S(2)}) collective-permute-start(bf16[2,144,256]{2,1,0:T(8,128)(2,1)S(1)} %join.4.own), channel_id=1, source_target_pairs={{0,192},{16,48},{32,224},{48,16},{64,128},{80,112},{96,160},{112,8... | collective-permute-start | bytes 442376 | tf_op jit(solution)/shard_map/ppermute | solution.py:347
  72.6 5.0 %collective-permute-start.11 = (bf16[2,144,256]{2,1,0:T(8,128)(2,1)S(1)}, bf16[2,144,256]{2,1,0:T(8,128)(2,1)S(1)}, u32[]{:S(2)}, u32[]{:S(2)}) collective-permute-start(bf16[2,144,256]{2,1,0:T(8,128)(2,1)S(1)} %join.5.own), channel_id=1, source_target_pairs={{0,192},{16,48},{32,224},{48,16},{64,128},{80,112},{96,160},{112,8... | collective-permute-start | bytes 442376 | tf_op jit(solution)/shard_map/ppermute | solution.py:347
  74.6 11.8 %collective-permute-start.15 = (bf16[4,144,256]{2,1,0:T(8,128)(2,1)S(1)}, bf16[4,144,256]{2,1,0:T(8,128)(2,1)S(1)}, u32[]{:S(2)}, u32[]{:S(2)}) collective-permute-start(bf16[4,144,256]{2,1,0:T(8,128)(2,1)S(1)} %join.6.mine), channel_id=1, source_target_pairs={{0,64},{16,208},{32,96},{48,240},{64,0},{80,144},{96,32},{112,176}... | collective-permute-start | bytes 884744 | tf_op jit(solution)/shard_map/ppermute | solution.py:347
  77.6 12.0 %collective-permute-start.12 = (bf16[4,144,256]{2,1,0:T(8,128)(2,1)S(1)}, bf16[4,144,256]{2,1,0:T(8,128)(2,1)S(1)}, u32[]{:S(2)}, u32[]{:S(2)}) collective-permute-start(bf16[4,144,256]{2,1,0:T(8,128)(2,1)S(1)} %join.7.mine), channel_id=1, source_target_pairs={{0,64},{16,208},{32,96},{48,240},{64,0},{80,144},{96,32},{112,176}... | collective-permute-start | bytes 884744 | tf_op jit(solution)/shard_map/ppermute | solution.py:347
  80.4 13.3 %collective-permute-start.16 = (bf16[4,144,256]{2,1,0:T(8,128)(2,1)S(1)}, bf16[4,144,256]{2,1,0:T(8,128)(2,1)S(1)}, u32[]{:S(2)}, u32[]{:S(2)}) collective-permute-start(bf16[4,144,256]{2,1,0:T(8,128)(2,1)S(1)} %join.6.mine), channel_id=1, source_target_pairs={{0,16},{16,0},{32,48},{48,32},{64,80},{80,64},{96,112},{112,96},{1... | collective-permute-start | bytes 884744 | tf_op jit(solution)/shard_map/ppermute | solution.py:351
  86.4 7.3 %collective-permute-start.17 = (bf16[4,144,256]{2,1,0:T(8,128)(2,1)S(1)}, bf16[4,144,256]{2,1,0:T(8,128)(2,1)S(1)}, u32[]{:S(2)}, u32[]{:S(2)}) collective-permute-start(bf16[4,144,256]{2,1,0:T(8,128)(2,1)S(1)} %collective-permute-done.15.mine_far), channel_id=1, source_target_pairs={{0,16},{16,0},{32,48},{48,32},{64,80},{80,64},{96,112},{112,96},{1... | collective-permute-start | bytes 884744 | tf_op jit(solution)/shard_map/ppermute | solution.py:351
  89.6 5.8 %collective-permute-start.13 = (bf16[4,144,256]{2,1,0:T(8,128)(2,1)S(1)}, bf16[4,144,256]{2,1,0:T(8,128)(2,1)S(1)}, u32[]{:S(2)}, u32[]{:S(2)}) collective-permute-start(bf16[4,144,256]{2,1,0:T(8,128)(2,1)S(1)} %join.7.mine), channel_id=1, source_target_pairs={{0,16},{16,0},{32,48},{48,32},{64,80},{80,64},{96,112},{112,96},{1... | collective-permute-start | bytes 884744 | tf_op jit(solution)/shard_map/ppermute | solution.py:351
  89.6 5.8 %collective-permute-start.14 = (bf16[4,144,256]{2,1,0:T(8,128)(2,1)S(1)}, bf16[4,144,256]{2,1,0:T(8,128)(2,1)S(1)}, u32[]{:S(2)}, u32[]{:S(2)}) collective-permute-start(bf16[4,144,256]{2,1,0:T(8,128)(2,1)S(1)} %collective-permute-done.12.mine_far), channel_id=1, source_target_pairs={{0,16},{16,0},{32,48},{48,32},{64,80},{80,64},{96,112},{112,96},{1... | collective-permute-start | bytes 884744 | tf_op jit(solution)/shard_map/ppermute | solution.py:351

commit v6 on v5

--- a/solution.py
+++ b/solution.py
@@ -292,14 +292,33 @@
     return call(halve, "halve", outs, (kept, got))
 
 
-def join(own, got, out):
-    n = own.shape[0]
-    out[:n] = own[...]
-    out[n:] = got[...]
-
-
-def run_join(own, got):
-    return call(join, "join", [((2 * own.shape[0], COLS, BLK), bf16)], (own, got))[0]
+def quarter(kept_a, got_a, kept_b, got_b, keep, first, second_, both):
+    for c, (kept, got) in enumerate(((kept_a, got_a), (kept_b, got_b))):
+        for k, out in enumerate((keep, second_, first, both)):
+            out[c] = (kept[k].astype(f32) + got[k].astype(f32)).astype(bf16)
+
+
+def run_quarter(*args):
+    return call(quarter, "quarter", [((2, COLS, BLK), bf16)] * 4, args)
+
+
+def whole_sum(keep, first, second_, both, out):
+    total = keep[...].astype(f32) + first[...].astype(f32)
+    out[...] = (total + (second_[...].astype(f32) + both[...].astype(f32))).astype(bf16)
+
+
+def run_whole_sum(*args):
+    return call(whole_sum, "whole_sum", [((2, COLS, BLK), bf16)], args)[0]
+
+
+def join(own, first, second_, both, *outs):
+    for k, part in enumerate((own, second_, first, both)):
+        for c, out in enumerate(outs):
+            out[k] = part[c]
+
+
+def run_join(*args):
+    return call(join, "join", [((4, COLS, BLK), bf16)] * 2, args)
 
 
 def settle(chain, sc, mine, mine_far, other, other_far, *refs):
@@ -345,6 +364,19 @@
 def along(value, n):
     pairs = [(k, cube_neighbour(k, (n + (k & 1)) % 3)) for k in range(16)]
     return lax.ppermute(value, "head", pairs)
+
+
+def to_three(values):
+    got = []
+    for value, flips in zip(values, ((1,), (2,), (1, 2))):
+        pairs = []
+        for k in range(16):
+            other = k
+            for n in flips:
+                other = cube_neighbour(other, (n + (k & 1)) % 3)
+            pairs.append((k, other))
+        got.append(lax.ppermute(value, "head", pairs))
+    return got
 
 
 def to_sibling(value):
@@ -386,41 +418,18 @@
     got_b = along(send_b, 0)
     acc = run_query_piece(0, sc_far, far_a, lat_t)
     acc = run_query_piece(0, sc_own, own_a, lat_t, acc)
-    got_a, acc = tie((got_a, acc))
-    kept_a, send_a = run_halve(kept_a, got_a)
-    kept_b, send_a, acc = tie((kept_b, send_a, acc))
-    got_a = along(send_a, 1)
     acc = run_query_piece(1, sc_far, far_b, lat_t, acc)
     acc = run_query_piece(1, sc_own, own_b, lat_t, acc)
     got_b, acc = tie((got_b, acc))
-    kept_b, send_b = run_halve(kept_b, got_b)
-    kept_a, send_b, acc = tie((kept_a, send_b, acc))
-    got_b = along(send_b, 1)
+    keep, *sends = run_quarter(kept_a, got_a, kept_b, got_b)
+    *sends, acc = tie((*sends, acc))
+    got = to_three(sends)
     dq = run_query_last(acc, w_uk)
-    got_a, dq = tie((got_a, dq))
     dq = lax.all_to_all(dq, "key", 0, 0, tiled=True)
-    kept_a, send_a = run_halve(kept_a, got_a)
-    kept_b, send_a = tie((kept_b, send_a))
-    got_a = along(send_a, 2)
-    kept_b, send_b = run_halve(kept_b, got_b)
-    kept_a, send_b = tie((kept_a, send_b))
-    got_b = along(send_b, 2)
-    (own_a,) = run_halve(kept_a, got_a)
-    kept_b, own_a = tie((kept_b, own_a))
-    got_a = along(own_a, 2)
-    (own_b,) = run_halve(kept_b, got_b)
-    own_a, own_b = tie((own_a, own_b))
-    got_b = along(own_b, 2)
-    own_a = run_join(own_a, got_a)
-    own_b, own_a = tie((own_b, own_a))
-    got_a = along(own_a, 1)
-    own_b = run_join(own_b, got_b)
+    own = run_whole_sum(keep, *got)
+    own_a, own_b = run_join(own, *to_three([own] * 3))
     own_a, own_b, dq = tie((own_a, own_b, dq))
-    got_b = along(own_b, 1)
-    own_a = run_join(own_a, got_a)
-    own_b, own_a = tie((own_b, own_a))
     far_a, near_a = along(own_a, 0), to_sibling(own_a)
-    own_b = run_join(own_b, got_b)
     far_b, near_b = along(own_b, 0), to_sibling(own_b)
     pieces = [
         (own_a, far_a, near_a, to_sibling(far_a)),

time: 97.5 us -> 101 us (1.036)
  starting transfers between devices: 31.5 us -> 36.1 us
  waiting for transfers between devices: 13.8 us -> 12.6 us
    ppermute x0 -> x6, waiting for transfers between devices: none -> 11.6 us  [to_three(): got.append(lax.ppermute(value, 'head', pairs))]
    ppermute x12 -> x4, waiting for transfers between devices: 11.8 us -> 0.92 us  [along(): return lax.ppermute(value, 'head', pairs)]
    ppermute x0 -> x6, starting transfers between devices: none -> 5.46 us  [to_three(): got.append(lax.ppermute(value, 'head', pairs))]
    ppermute x12 -> x4, starting transfers between devices: 11.5 us -> 6.91 us  [along(): return lax.ppermute(value, 'head', pairs)]
    ppermute x6, starting transfers between devices: 15.4 us -> 19.9 us  [to_sibling(): return lax.ppermute(value, 'head', [(k, k ^ 1) for k in range(16)])]
    all_to_all x1, waiting for transfers between devices: 1.99 us -> 0.01 us  [shards(): dq = lax.all_to_all(dq, 'key', 0, 0, tiled=True)]
    pallas_call x21 -> x14, Pallas kernels: 16.2 us -> 16.1 us  [call(): pl.pallas_call(kernel, in_specs=[in_smem] * scalars + [in_vmem] * (len(ar...]
  transfers between devices with their start and end apart: 19 -> 17, of which waited for: 7 -> 5; matrix products, arithmetic and copies ran while one was open for 1% -> 1% of each run, Pallas kernels for 14% -> 12%
where the time goes in v6:
time: 101 us
  starting transfers between devices  36.1 us (36%)
  Pallas kernels  29.6 us (29%)
  blocking collectives  20.4 us (20%)
  waiting for transfers between devices  12.6 us (12%)
    all_to_all x1, blocking collectives, shards(): stat = lax.all_to_all(stat, 'key', 0, 0, tiled=True)  20.4 us
    ppermute x6, starting transfers between devices, to_sibling(): return lax.ppermute(value, 'head', [(k, k ^ 1) for k in range(16)])  19.9 us
    pallas_call x14, Pallas kernels, call(): pl.pallas_call(kernel, in_specs=[in_smem] * scalars + [in_vmem] * (len(ar...  16.1 us
    ppermute x6, waiting for transfers between devices, to_three(): got.append(lax.ppermute(value, 'head', pairs))  11.6 us
    pallas_call x1, Pallas kernels, run_pass_one(): pl.pallas_call(pass_one, in_specs=[in_smem] + [in_hbm] * 6, out_specs=[in...  10 us
    ppermute x4, starting transfers between devices, along(): return lax.ppermute(value, 'head', pairs)  6.91 us
    ppermute x6, starting transfers between devices, to_three(): got.append(lax.ppermute(value, 'head', pairs))  5.46 us
    all_to_all x1, starting transfers between devices, shards(): dq = lax.all_to_all(dq, 'key', 0, 0, tiled=True)  3.92 us
  transfers between devices with their start and end apart: 17, of which 5 were waited for; matrix products, arithmetic and copies ran while one was open for 1% of the time, Pallas kernels for 12%

profile of v6, /device:TPU:1, one launch (start us, length us, event | category | flops | bytes accessed | tf_op | source)
XLA Modules:
  0.0 100.6 jit_solution(7627033165454826947)
XLA Ops:
  0.6 0.1 stack.35.sc
  0.7 0.1 stack.33.sc
  0.8 10.0 %pass_one.1 = (f32[8,1024,256]{2,1,0:T(8,128)S(1)}, f32[8,1024,256]{2,1,0:T(8,128)S(1)}, bf16[576,1024]{1,0:T(8,128)(2,1)S(1)}, bf16[512,1024]{1,0:T(8,128)(2,1)S(1)}, f32[16,24,128]{2,1,0:T(8,128)S(1)}) custom-call(s32[1]{0:T(128)} %bitcast.base, s32[1,128]{1,0:T(1,128)} %bitcast.24, bf16[8,192,128]{2,1,0:T(8,128)(2,1)} %bitcast.21, ...), custom_call_target="tpu_custom_call" | custom-call | tf_op jit(solution)/shard_map/pass_one/pallas_call | solution.py:160
  10.9 20.4 %all_to_all.10.stat = f32[16,24,128]{2,1,0:T(8,128)S(1)} all-to-all(f32[16,24,128]{2,1,0:T(8,128)S(1)} %get-tuple-element.44), channel_id=1, replica_groups=mesh['head'=16,'key'=16] {'key'}, dimensions={0} | all-to-all | bytes 393216 | tf_op jit(solution)/shard_map/all_to_all | solution.py:405
  31.3 2.1 %second_first.1 = (bf16[8,144,256]{2,1,0:T(8,128)(2,1)S(1)}, bf16[2,1024,256]{2,1,0:T(8,128)(2,1)S(1)}, f32[1024,128]{1,0:T(8,128)S(1)}, f32[1024,128]{1,0:T(8,128)S(1)}) custom-call(s32[5]{0:T(128)S(1)} %stack.35.sc, f32[16,24,128]{2,1,0:T(8,128)S(1)} %all_to_all.10.stat, bf16[576,1024]{1,0:T(8,128)(2,1)S(1)} %get-tuple-element.45.qcat_t, ...), custom_call_target="tpu_custom_call" | custom-call | tf_op jit(solution)/shard_map/second_first/pallas_call | solution.py:55
  33.4 2.7 %collective-permute-start = (bf16[8,144,256]{2,1,0:T(8,128)(2,1)S(1)}, bf16[8,144,256]{2,1,0:T(8,128)(2,1)S(1)}, u32[]{:S(2)}, u32[]{:S(2)}) collective-permute-start(bf16[8,144,256]{2,1,0:T(8,128)(2,1)S(1)} %get-tuple-element.52), channel_id=1, source_target_pairs={{0,16},{16,0},{32,48},{48,32},{64,80},{80,64},{96,112},{112,96},{1... | collective-permute-start | bytes 1769480 | tf_op jit(solution)/shard_map/ppermute | solution.py:383
  36.1 1.9 %second.3 = (bf16[8,144,256]{2,1,0:T(8,128)(2,1)S(1)}, bf16[2,1024,256]{2,1,0:T(8,128)(2,1)S(1)}) custom-call(s32[5]{0:T(128)S(1)} %stack.33.sc, f32[1024,128]{1,0:T(8,128)S(1)} %get-tuple-element.49.coef, f32[1024,128]{1,0:T(8,128)S(1)} %get-tuple-element.50.delta, bf16[576,1024]{1,0:T(8,128)(2,1)S(1)} %get-tuple-element.45.qcat_t, ...), custom_call_target="tpu_custom_call" | custom-call | tf_op jit(solution)/shard_map/second/pallas_call | solution.py:55
  38.0 0.0 collective-permute-done.got
  38.0 0.1 halve.2
  38.2 1.9 %second.5 = (bf16[8,144,256]{2,1,0:T(8,128)(2,1)S(1)}, bf16[2,1024,256]{2,1,0:T(8,128)(2,1)S(1)}) custom-call(s32[5]{0:T(128)S(1)} %stack.35.sc, f32[1024,128]{1,0:T(8,128)S(1)} %get-tuple-element.49.coef, f32[1024,128]{1,0:T(8,128)S(1)} %get-tuple-element.50.delta, bf16[576,1024]{1,0:T(8,128)(2,1)S(1)} %get-tuple-element.45.qcat_t, ...), custom_call_target="tpu_custom_call" | custom-call | tf_op jit(solution)/shard_map/second/pallas_call | solution.py:55
  40.1 0.2 collective-permute-start.2
  40.3 0.0 copy-start
  40.3 1.9 %second.4 = (bf16[8,144,256]{2,1,0:T(8,128)(2,1)S(1)}, bf16[2,1024,256]{2,1,0:T(8,128)(2,1)S(1)}) custom-call(s32[5]{0:T(128)S(1)} %stack.33.sc, f32[1024,128]{1,0:T(8,128)S(1)} %get-tuple-element.49.coef, f32[1024,128]{1,0:T(8,128)S(1)} %get-tuple-element.50.delta, bf16[576,1024]{1,0:T(8,128)(2,1)S(1)} %get-tuple-element.45.qcat_t, ...), custom_call_target="tpu_custom_call" | custom-call | tf_op jit(solution)/shard_map/second/pallas_call | solution.py:55
  42.2 0.0 collective-permute-done.2.got
  42.2 0.1 halve.3
  42.3 2.8 %collective-permute-start.3 = (bf16[4,144,256]{2,1,0:T(8,128)(2,1)S(1)}, bf16[4,144,256]{2,1,0:T(8,128)(2,1)S(1)}, u32[]{:S(2)}, u32[]{:S(2)}) collective-permute-start(bf16[4,144,256]{2,1,0:T(8,128)(2,1)S(1)} %get-tuple-element.60), channel_id=1, source_target_pairs={{0,64},{16,208},{32,96},{48,240},{64,0},{80,144},{96,32},{112,176}... | collective-permute-start | bytes 884744 | tf_op jit(solution)/shard_map/ppermute | solution.py:366
  45.2 0.1 collective-permute-start.1
  45.3 0.0 copy-done
  45.3 1.5 %query_piece.4.refs_0_ = f32[1024,576]{1,0:T(8,128)S(1)} custom-call(s32[5]{0:T(128)S(1)} %stack.35.sc, bf16[2,1024,256]{2,1,0:T(8,128)(2,1)S(1)} %get-tuple-element.64.ds, bf16[576,2048]{1,0:T(8,128)(2,1)S(1)} %bitcast.16), custom_call_target="tpu_custom_call" | custom-call | tf_op jit(solution)/shard_map/query_piece/pallas_call | solution.py:55
  46.8 1.6 %query_piece.5.refs_0_ = f32[1024,576]{1,0:T(8,128)S(1)} custom-call(s32[5]{0:T(128)S(1)} %stack.33.sc, bf16[2,1024,256]{2,1,0:T(8,128)(2,1)S(1)} %get-tuple-element.63.ds, bf16[576,2048]{1,0:T(8,128)(2,1)S(1)} %bitcast.17, f32[1024,576]{1,0:T(8,128)S(1)} %query_piece.4.refs_0_), custom_call_target="tpu_custom_call" | custom-call | tf_op jit(solution)/shard_map/query_piece/pallas_call | solution.py:55
  48.4 1.6 %query_piece.6.refs_0_ = f32[1024,576]{1,0:T(8,128)S(1)} custom-call(s32[5]{0:T(128)S(1)} %stack.35.sc, bf16[2,1024,256]{2,1,0:T(8,128)(2,1)S(1)} %get-tuple-element.62.ds, bf16[576,2048]{1,0:T(8,128)(2,1)S(1)} %bitcast.18, f32[1024,576]{1,0:T(8,128)S(1)} %query_piece.5.refs_0_), custom_call_target="tpu_custom_call" | custom-call | tf_op jit(solution)/shard_map/query_piece/pallas_call | solution.py:55
  49.9 0.0 copy-start.1
  49.9 1.6 %query_piece.7.acc = f32[1024,576]{1,0:T(8,128)S(1)} custom-call(s32[5]{0:T(128)S(1)} %stack.33.sc, bf16[2,1024,256]{2,1,0:T(8,128)(2,1)S(1)} %get-tuple-element.61.ds, bf16[576,2048]{1,0:T(8,128)(2,1)S(1)} %bitcast.19, f32[1024,576]{1,0:T(8,128)S(1)} %query_piece.6.refs_0_), custom_call_target="tpu_custom_call" | custom-call | tf_op jit(solution)/shard_map/query_piece/pallas_call | solution.py:55
  51.5 0.0 collective-permute-done.3.got_b
  51.5 0.9 collective-permute-done.1.got_a
  52.4 0.1 quarter.1
  52.6 0.0 copy-done.1
  52.6 1.6 %query_last.1 = bf16[16,64,192]{2,1,0:T(8,128)(2,1)} custom-call(f32[1024,576]{1,0:T(8,128)S(1)} %query_piece.7.acc, bf16[8,128,512]{2,1,0:T(8,128)(2,1)S(1)} %copy-done.1), custom_call_target="tpu_custom_call" | custom-call | tf_op jit(solution)/shard_map/query_last/pallas_call | solution.py:55
  54.2 3.9 %all-to-all-start.1 = ((bf16[16,64,192]{2,1,0:T(8,128)(2,1)}), bf16[16,64,192]{2,1,0:T(8,128)(2,1)S(1)}, u32[]{:S(2)}, u32[]{:S(2)}) async-start(bf16[16,64,192]{2,1,0:T(8,128)(2,1)} %query_last.1), calls=%async_computation.1 | async-start | bytes 1048576 | tf_op jit(solution)/shard_map/all_to_all | solution.py:428
  58.1 0.4 collective-permute-start.4
  58.5 0.3 collective-permute-start.5
  58.8 2.0 %collective-permute-start.6 = (bf16[2,144,256]{2,1,0:T(8,128)(2,1)S(1)}, bf16[2,144,256]{2,1,0:T(8,128)(2,1)S(1)}, u32[]{:S(2)}, u32[]{:S(2)}) collective-permute-start(bf16[2,144,256]{2,1,0:T(8,128)(2,1)S(1)} %get-tuple-element.73), channel_id=1, source_target_pairs={{0,224},{16,112},{32,192},{48,80},{64,160},{80,48},{96,128},{112,1... | collective-permute-start | bytes 442376 | tf_op jit(solution)/shard_map/ppermute | solution.py:378
  60.8 2.3 %collective-permute-done.4.first = bf16[2,144,256]{2,1,0:T(8,128)(2,1)S(1)} collective-permute-done((bf16[2,144,256]{2,1,0:T(8,128)(2,1)S(1)}, bf16[2,144,256]{2,1,0:T(8,128)(2,1)S(1)}, u32[]{:S(2)}, u32[]{:S(2)}) %collective-permute-start.4) | collective-permute-done | bytes 147488 | tf_op jit(solution)/shard_map/ppermute | solution.py:378
  63.2 0.0 collective-permute-done.5.second_
  63.2 4.8 %collective-permute-done.6.both = bf16[2,144,256]{2,1,0:T(8,128)(2,1)S(1)} collective-permute-done((bf16[2,144,256]{2,1,0:T(8,128)(2,1)S(1)}, bf16[2,144,256]{2,1,0:T(8,128)(2,1)S(1)}, u32[]{:S(2)}, u32[]{:S(2)}) %collective-permute-start.6) | collective-permute-done | bytes 147488 | tf_op jit(solution)/shard_map/ppermute | solution.py:378
  67.9 0.1 whole_sum.1.own
  68.0 0.1 collective-permute-start.9
  68.1 0.8 collective-permute-start.8
  68.9 1.8 %collective-permute-start.7 = (bf16[2,144,256]{2,1,0:T(8,128)(2,1)S(1)}, bf16[2,144,256]{2,1,0:T(8,128)(2,1)S(1)}, u32[]{:S(2)}, u32[]{:S(2)}) collective-permute-start(bf16[2,144,256]{2,1,0:T(8,128)(2,1)S(1)} %whole_sum.1.own), channel_id=1, source_target_pairs={{0,192},{16,48},{32,224},{48,16},{64,128},{80,112},{96,160},{112,8... | collective-permute-start | bytes 442376 | tf_op jit(solution)/shard_map/ppermute | solution.py:378
  70.7 3.3 %collective-permute-done.9.both = bf16[2,144,256]{2,1,0:T(8,128)(2,1)S(1)} collective-permute-done((bf16[2,144,256]{2,1,0:T(8,128)(2,1)S(1)}, bf16[2,144,256]{2,1,0:T(8,128)(2,1)S(1)}, u32[]{:S(2)}, u32[]{:S(2)}) %collective-permute-start.9) | collective-permute-done | bytes 147488 | tf_op jit(solution)/shard_map/ppermute | solution.py:378
  74.1 0.0 collective-permute-done.8.second_
  74.1 1.2 %collective-permute-done.7.first = bf16[2,144,256]{2,1,0:T(8,128)(2,1)S(1)} collective-permute-done((bf16[2,144,256]{2,1,0:T(8,128)(2,1)S(1)}, bf16[2,144,256]{2,1,0:T(8,128)(2,1)S(1)}, u32[]{:S(2)}, u32[]{:S(2)}) %collective-permute-start.7) | collective-permute-done | bytes 147488 | tf_op jit(solution)/shard_map/ppermute | solution.py:378
  75.3 0.0 all-to-all-done.1
  75.3 3.9 %collective-permute-start.13 = (bf16[4,144,256]{2,1,0:T(8,128)(2,1)S(1)}, bf16[4,144,256]{2,1,0:T(8,128)(2,1)S(1)}, u32[]{:S(2)}, u32[]{:S(2)}) collective-permute-start(bf16[4,144,256]{2,1,0:T(8,128)(2,1)S(1)} %get-tuple-element.79.mine), channel_id=1, source_target_pairs={{0,64},{16,208},{32,96},{48,240},{64,0},{80,144},{96,32},{112,176}... | collective-permute-start | bytes 884744 | tf_op jit(solution)/shard_map/ppermute | solution.py:366
  79.2 0.1 collective-permute-start.10
  79.3 9.1 %collective-permute-start.14 = (bf16[4,144,256]{2,1,0:T(8,128)(2,1)S(1)}, bf16[4,144,256]{2,1,0:T(8,128)(2,1)S(1)}, u32[]{:S(2)}, u32[]{:S(2)}) collective-permute-start(bf16[4,144,256]{2,1,0:T(8,128)(2,1)S(1)} %get-tuple-element.79.mine), channel_id=1, source_target_pairs={{0,16},{16,0},{32,48},{48,32},{64,80},{80,64},{96,112},{112,96},{1... | collective-permute-start | bytes 884744 | tf_op jit(solution)/shard_map/ppermute | solution.py:383
  88.4 0.0 collective-permute-done.13.mine_far
  88.4 4.7 %collective-permute-start.15 = (bf16[4,144,256]{2,1,0:T(8,128)(2,1)S(1)}, bf16[4,144,256]{2,1,0:T(8,128)(2,1)S(1)}, u32[]{:S(2)}, u32[]{:S(2)}) collective-permute-start(bf16[4,144,256]{2,1,0:T(8,128)(2,1)S(1)} %collective-permute-done.13.mine_far), channel_id=1, source_target_pairs={{0,16},{16,0},{32,48},{48,32},{64,80},{80,64},{96,112},{112,96},{1... | collective-permute-start | bytes 884744 | tf_op jit(solution)/shard_map/ppermute | solution.py:383
  93.1 0.0 collective-permute-start.11
  93.1 0.0 collective-permute-done.10.mine_far
  93.1 3.2 %collective-permute-start.12 = (bf16[4,144,256]{2,1,0:T(8,128)(2,1)S(1)}, bf16[4,144,256]{2,1,0:T(8,128)(2,1)S(1)}, u32[]{:S(2)}, u32[]{:S(2)}) collective-permute-start(bf16[4,144,256]{2,1,0:T(8,128)(2,1)S(1)} %collective-permute-done.10.mine_far), channel_id=1, source_target_pairs={{0,16},{16,0},{32,48},{48,32},{64,80},{80,64},{96,112},{112,96},{1... | collective-permute-start | bytes 884744 | tf_op jit(solution)/shard_map/ppermute | solution.py:383
  96.3 0.1 reduce_sum.12
  96.4 0.6 copy.9
  97.0 0.0 collective-permute-done.14.other
  97.0 0.0 collective-permute-done.15.other_far
  97.0 1.7 %settle.2.refs_0_ = bf16[576,2048]{1,0:T(8,128)(2,1)} custom-call(s32[5]{0:T(128)S(1)} %stack.33.sc, bf16[4,144,256]{2,1,0:T(8,128)(2,1)S(1)} %get-tuple-element.79.mine, bf16[4,144,256]{2,1,0:T(8,128)(2,1)S(1)} %collective-permute-done.13.mine_far, bf16[4,144,256]{2,1,0:T(8,128)(2,1)S(1)} %collective-permute-done.14.other, ...), custom_call_target="tpu_custom_call" | custom-call | tf_op jit(solution)/shard_map/settle/pallas_call | solution.py:343
  98.7 0.0 collective-permute-done.11.other
  98.7 0.0 collective-permute-done.12.other_far
  98.7 1.7 %settle.3 = bf16[576,2048]{1,0:T(8,128)(2,1)} custom-call(s32[5]{0:T(128)S(1)} %stack.33.sc, bf16[4,144,256]{2,1,0:T(8,128)(2,1)S(1)} %get-tuple-element.78.mine, bf16[4,144,256]{2,1,0:T(8,128)(2,1)S(1)} %collective-permute-done.10.mine_far, bf16[4,144,256]{2,1,0:T(8,128)(2,1)S(1)} %collective-permute-done.11.other, ...), custom_call_target="tpu_custom_call", output_to_operand_aliasing={{}: (5, {})} | custom-call | tf_op jit(solution)/shard_map/settle/pallas_call | solution.py:343
  (1 shorter events, 0.0 us)
Async XLA Ops:
  33.4 4.6 %collective-permute-start = (bf16[8,144,256]{2,1,0:T(8,128)(2,1)S(1)}, bf16[8,144,256]{2,1,0:T(8,128)(2,1)S(1)}, u32[]{:S(2)}, u32[]{:S(2)}) collective-permute-start(bf16[8,144,256]{2,1,0:T(8,128)(2,1)S(1)} %get-tuple-element.52), channel_id=1, source_target_pairs={{0,16},{16,0},{32,48},{48,32},{64,80},{80,64},{96,112},{112,96},{1... | collective-permute-start | bytes 1769480 | tf_op jit(solution)/shard_map/ppermute | solution.py:383
  40.1 2.1 %collective-permute-start.2 = (bf16[8,144,256]{2,1,0:T(8,128)(2,1)S(1)}, bf16[8,144,256]{2,1,0:T(8,128)(2,1)S(1)}, u32[]{:S(2)}, u32[]{:S(2)}) collective-permute-start(bf16[8,144,256]{2,1,0:T(8,128)(2,1)S(1)} %get-tuple-element.58), channel_id=1, source_target_pairs={{0,16},{16,0},{32,48},{48,32},{64,80},{80,64},{96,112},{112,96},{1... | collective-permute-start | bytes 1769480 | tf_op jit(solution)/shard_map/ppermute | solution.py:383
  40.3 5.0 %copy-start = (bf16[2048,576]{0,1:T(8,128)(2,1)S(1)}, bf16[2048,576]{0,1:T(8,128)(2,1)}, u32[]{:S(2)}) copy-start(bf16[2048,576]{0,1:T(8,128)(2,1)} %param.9) | copy-start | bytes 7077892
  42.3 9.2 %collective-permute-start.3 = (bf16[4,144,256]{2,1,0:T(8,128)(2,1)S(1)}, bf16[4,144,256]{2,1,0:T(8,128)(2,1)S(1)}, u32[]{:S(2)}, u32[]{:S(2)}) collective-permute-start(bf16[4,144,256]{2,1,0:T(8,128)(2,1)S(1)} %get-tuple-element.60), channel_id=1, source_target_pairs={{0,64},{16,208},{32,96},{48,240},{64,0},{80,144},{96,32},{112,176}... | collective-permute-start | bytes 884744 | tf_op jit(solution)/shard_map/ppermute | solution.py:366
  45.2 7.3 %collective-permute-start.1 = (bf16[4,144,256]{2,1,0:T(8,128)(2,1)S(1)}, bf16[4,144,256]{2,1,0:T(8,128)(2,1)S(1)}, u32[]{:S(2)}, u32[]{:S(2)}) collective-permute-start(bf16[4,144,256]{2,1,0:T(8,128)(2,1)S(1)} %get-tuple-element.55), channel_id=1, source_target_pairs={{0,64},{16,208},{32,96},{48,240},{64,0},{80,144},{96,32},{112,176}... | collective-permute-start | bytes 884744 | tf_op jit(solution)/shard_map/ppermute | solution.py:366
  49.9 2.6 %copy-start.1 = (bf16[8,128,512]{2,1,0:T(8,128)(2,1)S(1)}, bf16[8,128,512]{2,1,0:T(8,128)(2,1)}, u32[]{:S(2)}) copy-start(bf16[8,128,512]{2,1,0:T(8,128)(2,1)} %wuk.3) | copy-start | bytes 3145732
  54.2 21.2 %all-to-all-start.1 = ((bf16[16,64,192]{2,1,0:T(8,128)(2,1)}), bf16[16,64,192]{2,1,0:T(8,128)(2,1)S(1)}, u32[]{:S(2)}, u32[]{:S(2)}) async-start(bf16[16,64,192]{2,1,0:T(8,128)(2,1)} %query_last.1), calls=%async_computation.1 | async-start | bytes 1048576 | tf_op jit(solution)/shard_map/all_to_all | solution.py:428
  58.1 5.1 %collective-permute-start.4 = (bf16[2,144,256]{2,1,0:T(8,128)(2,1)S(1)}, bf16[2,144,256]{2,1,0:T(8,128)(2,1)S(1)}, u32[]{:S(2)}, u32[]{:S(2)}) collective-permute-start(bf16[2,144,256]{2,1,0:T(8,128)(2,1)S(1)} %get-tuple-element.71), channel_id=1, source_target_pairs={{0,192},{16,48},{32,224},{48,16},{64,128},{80,112},{96,160},{112,8... | collective-permute-start | bytes 442376 | tf_op jit(solution)/shard_map/ppermute | solution.py:378
  58.5 4.7 %collective-permute-start.5 = (bf16[2,144,256]{2,1,0:T(8,128)(2,1)S(1)}, bf16[2,144,256]{2,1,0:T(8,128)(2,1)S(1)}, u32[]{:S(2)}, u32[]{:S(2)}) collective-permute-start(bf16[2,144,256]{2,1,0:T(8,128)(2,1)S(1)} %get-tuple-element.72), channel_id=1, source_target_pairs={{0,32},{16,80},{32,0},{48,112},{64,96},{80,16},{96,64},{112,48},{1... | collective-permute-start | bytes 442376 | tf_op jit(solution)/shard_map/ppermute | solution.py:378
  58.8 9.1 %collective-permute-start.6 = (bf16[2,144,256]{2,1,0:T(8,128)(2,1)S(1)}, bf16[2,144,256]{2,1,0:T(8,128)(2,1)S(1)}, u32[]{:S(2)}, u32[]{:S(2)}) collective-permute-start(bf16[2,144,256]{2,1,0:T(8,128)(2,1)S(1)} %get-tuple-element.73), channel_id=1, source_target_pairs={{0,224},{16,112},{32,192},{48,80},{64,160},{80,48},{96,128},{112,1... | collective-permute-start | bytes 442376 | tf_op jit(solution)/shard_map/ppermute | solution.py:378
  68.0 6.1 %collective-permute-start.9 = (bf16[2,144,256]{2,1,0:T(8,128)(2,1)S(1)}, bf16[2,144,256]{2,1,0:T(8,128)(2,1)S(1)}, u32[]{:S(2)}, u32[]{:S(2)}) collective-permute-start(bf16[2,144,256]{2,1,0:T(8,128)(2,1)S(1)} %whole_sum.1.own), channel_id=1, source_target_pairs={{0,224},{16,112},{32,192},{48,80},{64,160},{80,48},{96,128},{112,1... | collective-permute-start | bytes 442376 | tf_op jit(solution)/shard_map/ppermute | solution.py:378
  68.1 6.0 %collective-permute-start.8 = (bf16[2,144,256]{2,1,0:T(8,128)(2,1)S(1)}, bf16[2,144,256]{2,1,0:T(8,128)(2,1)S(1)}, u32[]{:S(2)}, u32[]{:S(2)}) collective-permute-start(bf16[2,144,256]{2,1,0:T(8,128)(2,1)S(1)} %whole_sum.1.own), channel_id=1, source_target_pairs={{0,32},{16,80},{32,0},{48,112},{64,96},{80,16},{96,64},{112,48},{1... | collective-permute-start | bytes 442376 | tf_op jit(solution)/shard_map/ppermute | solution.py:378
  68.9 6.4 %collective-permute-start.7 = (bf16[2,144,256]{2,1,0:T(8,128)(2,1)S(1)}, bf16[2,144,256]{2,1,0:T(8,128)(2,1)S(1)}, u32[]{:S(2)}, u32[]{:S(2)}) collective-permute-start(bf16[2,144,256]{2,1,0:T(8,128)(2,1)S(1)} %whole_sum.1.own), channel_id=1, source_target_pairs={{0,192},{16,48},{32,224},{48,16},{64,128},{80,112},{96,160},{112,8... | collective-permute-start | bytes 442376 | tf_op jit(solution)/shard_map/ppermute | solution.py:378
  75.3 13.1 %collective-permute-start.13 = (bf16[4,144,256]{2,1,0:T(8,128)(2,1)S(1)}, bf16[4,144,256]{2,1,0:T(8,128)(2,1)S(1)}, u32[]{:S(2)}, u32[]{:S(2)}) collective-permute-start(bf16[4,144,256]{2,1,0:T(8,128)(2,1)S(1)} %get-tuple-element.79.mine), channel_id=1, source_target_pairs={{0,64},{16,208},{32,96},{48,240},{64,0},{80,144},{96,32},{112,176}... | collective-permute-start | bytes 884744 | tf_op jit(solution)/shard_map/ppermute | solution.py:366
  79.2 13.9 %collective-permute-start.10 = (bf16[4,144,256]{2,1,0:T(8,128)(2,1)S(1)}, bf16[4,144,256]{2,1,0:T(8,128)(2,1)S(1)}, u32[]{:S(2)}, u32[]{:S(2)}) collective-permute-start(bf16[4,144,256]{2,1,0:T(8,128)(2,1)S(1)} %get-tuple-element.78.mine), channel_id=1, source_target_pairs={{0,64},{16,208},{32,96},{48,240},{64,0},{80,144},{96,32},{112,176}... | collective-permute-start | bytes 884744 | tf_op jit(solution)/shard_map/ppermute | solution.py:366
  79.3 17.7 %collective-permute-start.14 = (bf16[4,144,256]{2,1,0:T(8,128)(2,1)S(1)}, bf16[4,144,256]{2,1,0:T(8,128)(2,1)S(1)}, u32[]{:S(2)}, u32[]{:S(2)}) collective-permute-start(bf16[4,144,256]{2,1,0:T(8,128)(2,1)S(1)} %get-tuple-element.79.mine), channel_id=1, source_target_pairs={{0,16},{16,0},{32,48},{48,32},{64,80},{80,64},{96,112},{112,96},{1... | collective-permute-start | bytes 884744 | tf_op jit(solution)/shard_map/ppermute | solution.py:383
  88.4 8.6 %collective-permute-start.15 = (bf16[4,144,256]{2,1,0:T(8,128)(2,1)S(1)}, bf16[4,144,256]{2,1,0:T(8,128)(2,1)S(1)}, u32[]{:S(2)}, u32[]{:S(2)}) collective-permute-start(bf16[4,144,256]{2,1,0:T(8,128)(2,1)S(1)} %collective-permute-done.13.mine_far), channel_id=1, source_target_pairs={{0,16},{16,0},{32,48},{48,32},{64,80},{80,64},{96,112},{112,96},{1... | collective-permute-start | bytes 884744 | tf_op jit(solution)/shard_map/ppermute | solution.py:383
  93.1 5.6 %collective-permute-start.11 = (bf16[4,144,256]{2,1,0:T(8,128)(2,1)S(1)}, bf16[4,144,256]{2,1,0:T(8,128)(2,1)S(1)}, u32[]{:S(2)}, u32[]{:S(2)}) collective-permute-start(bf16[4,144,256]{2,1,0:T(8,128)(2,1)S(1)} %get-tuple-element.78.mine), channel_id=1, source_target_pairs={{0,16},{16,0},{32,48},{48,32},{64,80},{80,64},{96,112},{112,96},{1... | collective-permute-start | bytes 884744 | tf_op jit(solution)/shard_map/ppermute | solution.py:383
  93.1 5.6 %collective-permute-start.12 = (bf16[4,144,256]{2,1,0:T(8,128)(2,1)S(1)}, bf16[4,144,256]{2,1,0:T(8,128)(2,1)S(1)}, u32[]{:S(2)}, u32[]{:S(2)}) collective-permute-start(bf16[4,144,256]{2,1,0:T(8,128)(2,1)S(1)} %collective-permute-done.10.mine_far), channel_id=1, source_target_pairs={{0,16},{16,0},{32,48},{48,32},{64,80},{80,64},{96,112},{112,96},{1... | collective-permute-start | bytes 884744 | tf_op jit(solution)/shard_map/ppermute | solution.py:383

commit v7 on v5

--- a/solution.py
+++ b/solution.py
@@ -398,7 +398,6 @@
     got_b = along(send_b, 1)
     dq = run_query_last(acc, w_uk)
     got_a, dq = tie((got_a, dq))
-    dq = lax.all_to_all(dq, "key", 0, 0, tiled=True)
     kept_a, send_a = run_halve(kept_a, got_a)
     kept_b, send_a = tie((kept_b, send_a))
     got_a = along(send_a, 2)
@@ -411,11 +410,13 @@
     (own_b,) = run_halve(kept_b, got_b)
     own_a, own_b = tie((own_a, own_b))
     got_b = along(own_b, 2)
+    got_a, dq = tie((got_a, dq))
+    dq = lax.all_to_all(dq, "key", 0, 0, tiled=True)
     own_a = run_join(own_a, got_a)
     own_b, own_a = tie((own_b, own_a))
     got_a = along(own_a, 1)
     own_b = run_join(own_b, got_b)
-    own_a, own_b, dq = tie((own_a, own_b, dq))
+    own_a, own_b = tie((own_a, own_b))
     got_b = along(own_b, 1)
     own_a = run_join(own_a, got_a)
     own_b, own_a = tie((own_b, own_a))

time: 97.5 us -> 93.6 us (0.960)
  waiting for transfers between devices: 13.8 us -> 10.3 us
    all_to_all x1, waiting for transfers between devices: 1.99 us -> 0.01 us  [shards(): dq = lax.all_to_all(dq, 'key', 0, 0, tiled=True)]
    ppermute x12, waiting for transfers between devices: 11.8 us -> 10.3 us  [along(): return lax.ppermute(value, 'head', pairs)]
  transfers between devices with their start and end apart: 19 -> 19, of which waited for: 7 -> 6; matrix products, arithmetic and copies ran while one was open for 1% -> 1% of each run, Pallas kernels for 14% -> 15%
where the time goes in v7:
time: 93.6 us; the launch traced here: 93.3 us
  starting transfers between devices  31 us (33%)
  Pallas kernels  29.7 us (32%)
  blocking collectives  20.4 us (22%)
  waiting for transfers between devices  10.3 us (11%)
  between operations  1.03 us (1%)
    all_to_all x1, blocking collectives, shards(): stat = lax.all_to_all(stat, 'key', 0, 0, tiled=True)  20.4 us
    pallas_call x21, Pallas kernels, call(): pl.pallas_call(kernel, in_specs=[in_smem] * scalars + [in_vmem] * (len(ar...  16.3 us
    ppermute x6, starting transfers between devices, to_sibling(): return lax.ppermute(value, 'head', [(k, k ^ 1) for k in range(16)])  14.8 us
    ppermute x12, starting transfers between devices, along(): return lax.ppermute(value, 'head', pairs)  12.3 us
    ppermute x12, waiting for transfers between devices, along(): return lax.ppermute(value, 'head', pairs)  10.3 us
    pallas_call x1, Pallas kernels, run_pass_one(): pl.pallas_call(pass_one, in_specs=[in_smem] + [in_hbm] * 6, out_specs=[in...  10 us
    all_to_all x1, starting transfers between devices, shards(): dq = lax.all_to_all(dq, 'key', 0, 0, tiled=True)  3.92 us
    pallas_call x2, Pallas kernels, run_settle(): pl.pallas_call(functools.partial(settle, chain), in_specs=[in_smem] + [in...  3.38 us
  transfers between devices with their start and end apart: 19, of which 6 were waited for; matrix products, arithmetic and copies ran while one was open for 1% of the time, Pallas kernels for 15%

profile of v7, /device:TPU:1, one launch (start us, length us, event | category | flops | bytes accessed | tf_op | source)
XLA Modules:
  0.0 93.3 jit_solution(3467443687663631034)
XLA Ops:
  0.6 0.1 stack.35.sc
  0.7 0.1 stack.33.sc
  0.8 10.0 %pass_one.1 = (f32[8,1024,256]{2,1,0:T(8,128)S(1)}, f32[8,1024,256]{2,1,0:T(8,128)S(1)}, bf16[576,1024]{1,0:T(8,128)(2,1)S(1)}, bf16[512,1024]{1,0:T(8,128)(2,1)S(1)}, f32[16,24,128]{2,1,0:T(8,128)S(1)}) custom-call(s32[1]{0:T(128)} %bitcast.base, s32[1,128]{1,0:T(1,128)} %bitcast.24, bf16[8,192,128]{2,1,0:T(8,128)(2,1)} %bitcast.21, ...), custom_call_target="tpu_custom_call" | custom-call | tf_op jit(solution)/shard_map/pass_one/pallas_call | solution.py:160
  10.9 20.4 %all_to_all.10.stat = f32[16,24,128]{2,1,0:T(8,128)S(1)} all-to-all(f32[16,24,128]{2,1,0:T(8,128)S(1)} %get-tuple-element.65), channel_id=1, replica_groups=mesh['head'=16,'key'=16] {'key'}, dimensions={0} | all-to-all | bytes 393216 | tf_op jit(solution)/shard_map/all_to_all | solution.py:373
  31.3 2.1 %second_first.1 = (bf16[8,144,256]{2,1,0:T(8,128)(2,1)S(1)}, bf16[2,1024,256]{2,1,0:T(8,128)(2,1)S(1)}, f32[1024,128]{1,0:T(8,128)S(1)}, f32[1024,128]{1,0:T(8,128)S(1)}) custom-call(s32[5]{0:T(128)S(1)} %stack.35.sc, f32[16,24,128]{2,1,0:T(8,128)S(1)} %all_to_all.10.stat, bf16[576,1024]{1,0:T(8,128)(2,1)S(1)} %get-tuple-element.66.qcat_t, ...), custom_call_target="tpu_custom_call" | custom-call | tf_op jit(solution)/shard_map/second_first/pallas_call | solution.py:55
  33.4 2.7 %collective-permute-start = (bf16[8,144,256]{2,1,0:T(8,128)(2,1)S(1)}, bf16[8,144,256]{2,1,0:T(8,128)(2,1)S(1)}, u32[]{:S(2)}, u32[]{:S(2)}) collective-permute-start(bf16[8,144,256]{2,1,0:T(8,128)(2,1)S(1)} %get-tuple-element.74), channel_id=1, source_target_pairs={{0,16},{16,0},{32,48},{48,32},{64,80},{80,64},{96,112},{112,96},{1... | collective-permute-start | bytes 1769480 | tf_op jit(solution)/shard_map/ppermute | solution.py:351
  36.1 1.9 %second.4 = (bf16[8,144,256]{2,1,0:T(8,128)(2,1)S(1)}, bf16[2,1024,256]{2,1,0:T(8,128)(2,1)S(1)}) custom-call(s32[5]{0:T(128)S(1)} %stack.33.sc, f32[1024,128]{1,0:T(8,128)S(1)} %get-tuple-element.70.coef, f32[1024,128]{1,0:T(8,128)S(1)} %get-tuple-element.71.delta, bf16[576,1024]{1,0:T(8,128)(2,1)S(1)} %get-tuple-element.66.qcat_t, ...), custom_call_target="tpu_custom_call" | custom-call | tf_op jit(solution)/shard_map/second/pallas_call | solution.py:55
  38.0 0.0 collective-permute-done.got
  38.0 0.1 halve.8
  38.2 1.9 %second.5 = (bf16[8,144,256]{2,1,0:T(8,128)(2,1)S(1)}, bf16[2,1024,256]{2,1,0:T(8,128)(2,1)S(1)}) custom-call(s32[5]{0:T(128)S(1)} %stack.35.sc, f32[1024,128]{1,0:T(8,128)S(1)} %get-tuple-element.70.coef, f32[1024,128]{1,0:T(8,128)S(1)} %get-tuple-element.71.delta, bf16[576,1024]{1,0:T(8,128)(2,1)S(1)} %get-tuple-element.66.qcat_t, ...), custom_call_target="tpu_custom_call" | custom-call | tf_op jit(solution)/shard_map/second/pallas_call | solution.py:55
  40.1 0.2 collective-permute-start.1
  40.3 2.8 %collective-permute-start.2 = (bf16[4,144,256]{2,1,0:T(8,128)(2,1)S(1)}, bf16[4,144,256]{2,1,0:T(8,128)(2,1)S(1)}, u32[]{:S(2)}, u32[]{:S(2)}) collective-permute-start(bf16[4,144,256]{2,1,0:T(8,128)(2,1)S(1)} %get-tuple-element.80), channel_id=1, source_target_pairs={{0,64},{16,208},{32,96},{48,240},{64,0},{80,144},{96,32},{112,176}... | collective-permute-start | bytes 884744 | tf_op jit(solution)/shard_map/ppermute | solution.py:347
  43.0 0.0 copy-start
  43.0 1.9 %second.3 = (bf16[8,144,256]{2,1,0:T(8,128)(2,1)S(1)}, bf16[2,1024,256]{2,1,0:T(8,128)(2,1)S(1)}) custom-call(s32[5]{0:T(128)S(1)} %stack.33.sc, f32[1024,128]{1,0:T(8,128)S(1)} %get-tuple-element.70.coef, f32[1024,128]{1,0:T(8,128)S(1)} %get-tuple-element.71.delta, bf16[576,1024]{1,0:T(8,128)(2,1)S(1)} %get-tuple-element.66.qcat_t, ...), custom_call_target="tpu_custom_call" | custom-call | tf_op jit(solution)/shard_map/second/pallas_call | solution.py:55
  44.9 0.0 collective-permute-done.1.got
  44.9 0.1 halve.9
  45.1 0.1 collective-permute-start.3
  45.2 0.0 copy-done
  45.2 1.5 %query_piece.4.refs_0_ = f32[1024,576]{1,0:T(8,128)S(1)} custom-call(s32[5]{0:T(128)S(1)} %stack.35.sc, bf16[2,1024,256]{2,1,0:T(8,128)(2,1)S(1)} %get-tuple-element.82.ds, bf16[576,2048]{1,0:T(8,128)(2,1)S(1)} %bitcast.16), custom_call_target="tpu_custom_call" | custom-call | tf_op jit(solution)/shard_map/query_piece/pallas_call | solution.py:55
  46.7 1.6 %query_piece.5.refs_0_ = f32[1024,576]{1,0:T(8,128)S(1)} custom-call(s32[5]{0:T(128)S(1)} %stack.33.sc, bf16[2,1024,256]{2,1,0:T(8,128)(2,1)S(1)} %get-tuple-element.81.ds, bf16[576,2048]{1,0:T(8,128)(2,1)S(1)} %bitcast.17, f32[1024,576]{1,0:T(8,128)S(1)} %query_piece.4.refs_0_), custom_call_target="tpu_custom_call" | custom-call | tf_op jit(solution)/shard_map/query_piece/pallas_call | solution.py:55
  48.3 0.0 collective-permute-done.2.got
  48.3 0.1 halve.10
  48.4 0.4 collective-permute-start.4
  48.8 1.6 %query_piece.6.refs_0_ = f32[1024,576]{1,0:T(8,128)S(1)} custom-call(s32[5]{0:T(128)S(1)} %stack.35.sc, bf16[2,1024,256]{2,1,0:T(8,128)(2,1)S(1)} %get-tuple-element.89.ds, bf16[576,2048]{1,0:T(8,128)(2,1)S(1)} %bitcast.18, f32[1024,576]{1,0:T(8,128)S(1)} %query_piece.5.refs_0_), custom_call_target="tpu_custom_call" | custom-call | tf_op jit(solution)/shard_map/query_piece/pallas_call | solution.py:55
  50.3 0.0 copy-start.1
  50.4 1.6 %query_piece.7.acc = f32[1024,576]{1,0:T(8,128)S(1)} custom-call(s32[5]{0:T(128)S(1)} %stack.33.sc, bf16[2,1024,256]{2,1,0:T(8,128)(2,1)S(1)} %get-tuple-element.88.ds, bf16[576,2048]{1,0:T(8,128)(2,1)S(1)} %bitcast.19, f32[1024,576]{1,0:T(8,128)S(1)} %query_piece.6.refs_0_), custom_call_target="tpu_custom_call" | custom-call | tf_op jit(solution)/shard_map/query_piece/pallas_call | solution.py:55
  51.9 0.0 collective-permute-done.3.got
  52.0 0.1 halve.11
  52.0 1.2 %collective-permute-start.5 = (bf16[2,144,256]{2,1,0:T(8,128)(2,1)S(1)}, bf16[2,144,256]{2,1,0:T(8,128)(2,1)S(1)}, u32[]{:S(2)}, u32[]{:S(2)}) collective-permute-start(bf16[2,144,256]{2,1,0:T(8,128)(2,1)S(1)} %get-tuple-element.102), channel_id=1, source_target_pairs={{0,192},{16,48},{32,224},{48,16},{64,128},{80,112},{96,160},{112,8... | collective-permute-start | bytes 442376 | tf_op jit(solution)/shard_map/ppermute | solution.py:347
  53.3 0.0 copy-done.1
  53.3 1.6 %query_last.1 = bf16[16,64,192]{2,1,0:T(8,128)(2,1)} custom-call(f32[1024,576]{1,0:T(8,128)S(1)} %query_piece.7.acc, bf16[8,128,512]{2,1,0:T(8,128)(2,1)S(1)} %copy-done.1), custom_call_target="tpu_custom_call" | custom-call | tf_op jit(solution)/shard_map/query_last/pallas_call | solution.py:55
  54.9 0.0 collective-permute-done.4.got
  54.9 0.1 collective-permute-start.6
  55.0 1.1 %collective-permute-done.5.got = bf16[2,144,256]{2,1,0:T(8,128)(2,1)S(1)} collective-permute-done((bf16[2,144,256]{2,1,0:T(8,128)(2,1)S(1)}, bf16[2,144,256]{2,1,0:T(8,128)(2,1)S(1)}, u32[]{:S(2)}, u32[]{:S(2)}) %collective-permute-start.5) | collective-permute-done | bytes 147488 | tf_op jit(solution)/shard_map/ppermute | solution.py:347
  56.2 0.7 collective-permute-start.8
  56.8 1.4 %collective-permute-done.6.got = bf16[1,144,256]{2,1,0:T(8,128)(2,1)S(1)} collective-permute-done((bf16[1,144,256]{2,1,0:T(8,128)(2,1)S(1)}, bf16[1,144,256]{2,1,0:T(8,128)(2,1)S(1)}, u32[]{:S(2)}, u32[]{:S(2)}) %collective-permute-start.6) | collective-permute-done | bytes 73760 | tf_op jit(solution)/shard_map/ppermute | solution.py:347
  58.2 0.4 collective-permute-start.7
  58.6 1.3 %collective-permute-done.8.got = bf16[1,144,256]{2,1,0:T(8,128)(2,1)S(1)} collective-permute-done((bf16[1,144,256]{2,1,0:T(8,128)(2,1)S(1)}, bf16[1,144,256]{2,1,0:T(8,128)(2,1)S(1)}, u32[]{:S(2)}, u32[]{:S(2)}) %collective-permute-start.8) | collective-permute-done | bytes 73760 | tf_op jit(solution)/shard_map/ppermute | solution.py:347
  60.0 0.5 collective-permute-start.9
  60.4 1.1 %collective-permute-done.7.got = bf16[1,144,256]{2,1,0:T(8,128)(2,1)S(1)} collective-permute-done((bf16[1,144,256]{2,1,0:T(8,128)(2,1)S(1)}, bf16[1,144,256]{2,1,0:T(8,128)(2,1)S(1)}, u32[]{:S(2)}, u32[]{:S(2)}) %collective-permute-start.7) | collective-permute-done | bytes 73760 | tf_op jit(solution)/shard_map/ppermute | solution.py:347
  61.5 3.9 %all-to-all-start.1 = ((bf16[16,64,192]{2,1,0:T(8,128)(2,1)}), bf16[16,64,192]{2,1,0:T(8,128)(2,1)S(1)}, u32[]{:S(2)}, u32[]{:S(2)}) async-start(bf16[16,64,192]{2,1,0:T(8,128)(2,1)} %query_last.1), calls=%async_computation.1 | async-start | bytes 1048576 | tf_op jit(solution)/shard_map/all_to_all | solution.py:414
  65.5 0.4 collective-permute-start.10
  65.9 0.0 collective-permute-done.9.got
  65.9 1.3 %collective-permute-start.11 = (bf16[2,144,256]{2,1,0:T(8,128)(2,1)S(1)}, bf16[2,144,256]{2,1,0:T(8,128)(2,1)S(1)}, u32[]{:S(2)}, u32[]{:S(2)}) collective-permute-start(bf16[2,144,256]{2,1,0:T(8,128)(2,1)S(1)} %join.5.own), channel_id=1, source_target_pairs={{0,192},{16,48},{32,224},{48,16},{64,128},{80,112},{96,160},{112,8... | collective-permute-start | bytes 442376 | tf_op jit(solution)/shard_map/ppermute | solution.py:347
  67.2 3.9 %collective-permute-done.10.got = bf16[2,144,256]{2,1,0:T(8,128)(2,1)S(1)} collective-permute-done((bf16[2,144,256]{2,1,0:T(8,128)(2,1)S(1)}, bf16[2,144,256]{2,1,0:T(8,128)(2,1)S(1)}, u32[]{:S(2)}, u32[]{:S(2)}) %collective-permute-start.10) | collective-permute-done | bytes 147488 | tf_op jit(solution)/shard_map/ppermute | solution.py:347
  71.1 2.2 %collective-permute-start.15 = (bf16[4,144,256]{2,1,0:T(8,128)(2,1)S(1)}, bf16[4,144,256]{2,1,0:T(8,128)(2,1)S(1)}, u32[]{:S(2)}, u32[]{:S(2)}) collective-permute-start(bf16[4,144,256]{2,1,0:T(8,128)(2,1)S(1)} %join.6.mine), channel_id=1, source_target_pairs={{0,64},{16,208},{32,96},{48,240},{64,0},{80,144},{96,32},{112,176}... | collective-permute-start | bytes 884744 | tf_op jit(solution)/shard_map/ppermute | solution.py:347
  73.3 1.4 %collective-permute-done.11.got = bf16[2,144,256]{2,1,0:T(8,128)(2,1)S(1)} collective-permute-done((bf16[2,144,256]{2,1,0:T(8,128)(2,1)S(1)}, bf16[2,144,256]{2,1,0:T(8,128)(2,1)S(1)}, u32[]{:S(2)}, u32[]{:S(2)}) %collective-permute-start.11) | collective-permute-done | bytes 147488 | tf_op jit(solution)/shard_map/ppermute | solution.py:347
  74.8 2.3 %collective-permute-start.12 = (bf16[4,144,256]{2,1,0:T(8,128)(2,1)S(1)}, bf16[4,144,256]{2,1,0:T(8,128)(2,1)S(1)}, u32[]{:S(2)}, u32[]{:S(2)}) collective-permute-start(bf16[4,144,256]{2,1,0:T(8,128)(2,1)S(1)} %join.7.mine), channel_id=1, source_target_pairs={{0,64},{16,208},{32,96},{48,240},{64,0},{80,144},{96,32},{112,176}... | collective-permute-start | bytes 884744 | tf_op jit(solution)/shard_map/ppermute | solution.py:347
  77.1 5.3 %collective-permute-start.16 = (bf16[4,144,256]{2,1,0:T(8,128)(2,1)S(1)}, bf16[4,144,256]{2,1,0:T(8,128)(2,1)S(1)}, u32[]{:S(2)}, u32[]{:S(2)}) collective-permute-start(bf16[4,144,256]{2,1,0:T(8,128)(2,1)S(1)} %join.6.mine), channel_id=1, source_target_pairs={{0,16},{16,0},{32,48},{48,32},{64,80},{80,64},{96,112},{112,96},{1... | collective-permute-start | bytes 884744 | tf_op jit(solution)/shard_map/ppermute | solution.py:351
  82.4 0.0 collective-permute-done.15.mine_far
  82.4 3.5 %collective-permute-start.17 = (bf16[4,144,256]{2,1,0:T(8,128)(2,1)S(1)}, bf16[4,144,256]{2,1,0:T(8,128)(2,1)S(1)}, u32[]{:S(2)}, u32[]{:S(2)}) collective-permute-start(bf16[4,144,256]{2,1,0:T(8,128)(2,1)S(1)} %collective-permute-done.15.mine_far), channel_id=1, source_target_pairs={{0,16},{16,0},{32,48},{48,32},{64,80},{80,64},{96,112},{112,96},{1... | collective-permute-start | bytes 884744 | tf_op jit(solution)/shard_map/ppermute | solution.py:351
  85.9 0.0 collective-permute-start.13
  85.9 0.0 collective-permute-done.12.mine_far
  85.9 3.2 %collective-permute-start.14 = (bf16[4,144,256]{2,1,0:T(8,128)(2,1)S(1)}, bf16[4,144,256]{2,1,0:T(8,128)(2,1)S(1)}, u32[]{:S(2)}, u32[]{:S(2)}) collective-permute-start(bf16[4,144,256]{2,1,0:T(8,128)(2,1)S(1)} %collective-permute-done.12.mine_far), channel_id=1, source_target_pairs={{0,16},{16,0},{32,48},{48,32},{64,80},{80,64},{96,112},{112,96},{1... | collective-permute-start | bytes 884744 | tf_op jit(solution)/shard_map/ppermute | solution.py:351
  89.0 0.0 all-to-all-done.1
  89.0 0.1 reduce_sum.12
  89.1 0.6 copy.9
  89.8 0.0 collective-permute-done.16.other
  89.8 0.0 collective-permute-done.17.other_far
  89.8 1.7 %settle.2.refs_0_ = bf16[576,2048]{1,0:T(8,128)(2,1)} custom-call(s32[5]{0:T(128)S(1)} %stack.33.sc, bf16[4,144,256]{2,1,0:T(8,128)(2,1)S(1)} %join.6.mine, bf16[4,144,256]{2,1,0:T(8,128)(2,1)S(1)} %collective-permute-done.15.mine_far, bf16[4,144,256]{2,1,0:T(8,128)(2,1)S(1)} %collective-permute-done.16.other, ...), custom_call_target="tpu_custom_call" | custom-call | tf_op jit(solution)/shard_map/settle/pallas_call | solution.py:324
  91.5 0.0 collective-permute-done.13.other
  91.5 0.0 collective-permute-done.14.other_far
  91.5 1.7 %settle.3 = bf16[576,2048]{1,0:T(8,128)(2,1)} custom-call(s32[5]{0:T(128)S(1)} %stack.33.sc, bf16[4,144,256]{2,1,0:T(8,128)(2,1)S(1)} %join.7.mine, bf16[4,144,256]{2,1,0:T(8,128)(2,1)S(1)} %collective-permute-done.12.mine_far, bf16[4,144,256]{2,1,0:T(8,128)(2,1)S(1)} %collective-permute-done.13.other, ...), custom_call_target="tpu_custom_call", output_to_operand_aliasing={{}: (5, {})} | custom-call | tf_op jit(solution)/shard_map/settle/pallas_call | solution.py:324
  (8 shorter events, 0.2 us)
Async XLA Ops:
  33.4 4.6 %collective-permute-start = (bf16[8,144,256]{2,1,0:T(8,128)(2,1)S(1)}, bf16[8,144,256]{2,1,0:T(8,128)(2,1)S(1)}, u32[]{:S(2)}, u32[]{:S(2)}) collective-permute-start(bf16[8,144,256]{2,1,0:T(8,128)(2,1)S(1)} %get-tuple-element.74), channel_id=1, source_target_pairs={{0,16},{16,0},{32,48},{48,32},{64,80},{80,64},{96,112},{112,96},{1... | collective-permute-start | bytes 1769480 | tf_op jit(solution)/shard_map/ppermute | solution.py:351
  40.1 4.8 %collective-permute-start.1 = (bf16[8,144,256]{2,1,0:T(8,128)(2,1)S(1)}, bf16[8,144,256]{2,1,0:T(8,128)(2,1)S(1)}, u32[]{:S(2)}, u32[]{:S(2)}) collective-permute-start(bf16[8,144,256]{2,1,0:T(8,128)(2,1)S(1)} %get-tuple-element.77), channel_id=1, source_target_pairs={{0,16},{16,0},{32,48},{48,32},{64,80},{80,64},{96,112},{112,96},{1... | collective-permute-start | bytes 1769480 | tf_op jit(solution)/shard_map/ppermute | solution.py:351
  40.3 8.1 %collective-permute-start.2 = (bf16[4,144,256]{2,1,0:T(8,128)(2,1)S(1)}, bf16[4,144,256]{2,1,0:T(8,128)(2,1)S(1)}, u32[]{:S(2)}, u32[]{:S(2)}) collective-permute-start(bf16[4,144,256]{2,1,0:T(8,128)(2,1)S(1)} %get-tuple-element.80), channel_id=1, source_target_pairs={{0,64},{16,208},{32,96},{48,240},{64,0},{80,144},{96,32},{112,176}... | collective-permute-start | bytes 884744 | tf_op jit(solution)/shard_map/ppermute | solution.py:347
  43.0 2.2 %copy-start = (bf16[2048,576]{0,1:T(8,128)(2,1)S(1)}, bf16[2048,576]{0,1:T(8,128)(2,1)}, u32[]{:S(2)}) copy-start(bf16[2048,576]{0,1:T(8,128)(2,1)} %param.9) | copy-start | bytes 7077892
  45.1 6.9 %collective-permute-start.3 = (bf16[4,144,256]{2,1,0:T(8,128)(2,1)S(1)}, bf16[4,144,256]{2,1,0:T(8,128)(2,1)S(1)}, u32[]{:S(2)}, u32[]{:S(2)}) collective-permute-start(bf16[4,144,256]{2,1,0:T(8,128)(2,1)S(1)} %get-tuple-element.87), channel_id=1, source_target_pairs={{0,64},{16,208},{32,96},{48,240},{64,0},{80,144},{96,32},{112,176}... | collective-permute-start | bytes 884744 | tf_op jit(solution)/shard_map/ppermute | solution.py:347
  48.4 6.5 %collective-permute-start.4 = (bf16[2,144,256]{2,1,0:T(8,128)(2,1)S(1)}, bf16[2,144,256]{2,1,0:T(8,128)(2,1)S(1)}, u32[]{:S(2)}, u32[]{:S(2)}) collective-permute-start(bf16[2,144,256]{2,1,0:T(8,128)(2,1)S(1)} %get-tuple-element.97), channel_id=1, source_target_pairs={{0,192},{16,48},{32,224},{48,16},{64,128},{80,112},{96,160},{112,8... | collective-permute-start | bytes 442376 | tf_op jit(solution)/shard_map/ppermute | solution.py:347
  50.3 2.9 %copy-start.1 = (bf16[8,128,512]{2,1,0:T(8,128)(2,1)S(1)}, bf16[8,128,512]{2,1,0:T(8,128)(2,1)}, u32[]{:S(2)}) copy-start(bf16[8,128,512]{2,1,0:T(8,128)(2,1)} %wuk.3) | copy-start | bytes 3145732
  52.0 4.1 %collective-permute-start.5 = (bf16[2,144,256]{2,1,0:T(8,128)(2,1)S(1)}, bf16[2,144,256]{2,1,0:T(8,128)(2,1)S(1)}, u32[]{:S(2)}, u32[]{:S(2)}) collective-permute-start(bf16[2,144,256]{2,1,0:T(8,128)(2,1)S(1)} %get-tuple-element.102), channel_id=1, source_target_pairs={{0,192},{16,48},{32,224},{48,16},{64,128},{80,112},{96,160},{112,8... | collective-permute-start | bytes 442376 | tf_op jit(solution)/shard_map/ppermute | solution.py:347
  54.9 3.3 %collective-permute-start.6 = (bf16[1,144,256]{2,1,0:T(8,128)(2,1)S(1)}, bf16[1,144,256]{2,1,0:T(8,128)(2,1)S(1)}, u32[]{:S(2)}, u32[]{:S(2)}) collective-permute-start(bf16[1,144,256]{2,1,0:T(8,128)(2,1)S(1)} %get-tuple-element.107), channel_id=1, source_target_pairs={{0,32},{16,80},{32,0},{48,112},{64,96},{80,16},{96,64},{112,48},{1... | collective-permute-start | bytes 221192 | tf_op jit(solution)/shard_map/ppermute | solution.py:347
  56.2 3.8 %collective-permute-start.8 = (bf16[1,144,256]{2,1,0:T(8,128)(2,1)S(1)}, bf16[1,144,256]{2,1,0:T(8,128)(2,1)S(1)}, u32[]{:S(2)}, u32[]{:S(2)}) collective-permute-start(bf16[1,144,256]{2,1,0:T(8,128)(2,1)S(1)} %get-tuple-element.112), channel_id=1, source_target_pairs={{0,32},{16,80},{32,0},{48,112},{64,96},{80,16},{96,64},{112,48},{1... | collective-permute-start | bytes 221192 | tf_op jit(solution)/shard_map/ppermute | solution.py:347
  58.2 3.3 %collective-permute-start.7 = (bf16[1,144,256]{2,1,0:T(8,128)(2,1)S(1)}, bf16[1,144,256]{2,1,0:T(8,128)(2,1)S(1)}, u32[]{:S(2)}, u32[]{:S(2)}) collective-permute-start(bf16[1,144,256]{2,1,0:T(8,128)(2,1)S(1)} %halve.14.own), channel_id=1, source_target_pairs={{0,32},{16,80},{32,0},{48,112},{64,96},{80,16},{96,64},{112,48},{1... | collective-permute-start | bytes 221192 | tf_op jit(solution)/shard_map/ppermute | solution.py:347
  60.0 5.9 %collective-permute-start.9 = (bf16[1,144,256]{2,1,0:T(8,128)(2,1)S(1)}, bf16[1,144,256]{2,1,0:T(8,128)(2,1)S(1)}, u32[]{:S(2)}, u32[]{:S(2)}) collective-permute-start(bf16[1,144,256]{2,1,0:T(8,128)(2,1)S(1)} %halve.15.own), channel_id=1, source_target_pairs={{0,32},{16,80},{32,0},{48,112},{64,96},{80,16},{96,64},{112,48},{1... | collective-permute-start | bytes 221192 | tf_op jit(solution)/shard_map/ppermute | solution.py:347
  61.5 27.5 %all-to-all-start.1 = ((bf16[16,64,192]{2,1,0:T(8,128)(2,1)}), bf16[16,64,192]{2,1,0:T(8,128)(2,1)S(1)}, u32[]{:S(2)}, u32[]{:S(2)}) async-start(bf16[16,64,192]{2,1,0:T(8,128)(2,1)} %query_last.1), calls=%async_computation.1 | async-start | bytes 1048576 | tf_op jit(solution)/shard_map/all_to_all | solution.py:414
  65.5 5.6 %collective-permute-start.10 = (bf16[2,144,256]{2,1,0:T(8,128)(2,1)S(1)}, bf16[2,144,256]{2,1,0:T(8,128)(2,1)S(1)}, u32[]{:S(2)}, u32[]{:S(2)}) collective-permute-start(bf16[2,144,256]{2,1,0:T(8,128)(2,1)S(1)} %join.4.own), channel_id=1, source_target_pairs={{0,192},{16,48},{32,224},{48,16},{64,128},{80,112},{96,160},{112,8... | collective-permute-start | bytes 442376 | tf_op jit(solution)/shard_map/ppermute | solution.py:347
  65.9 8.9 %collective-permute-start.11 = (bf16[2,144,256]{2,1,0:T(8,128)(2,1)S(1)}, bf16[2,144,256]{2,1,0:T(8,128)(2,1)S(1)}, u32[]{:S(2)}, u32[]{:S(2)}) collective-permute-start(bf16[2,144,256]{2,1,0:T(8,128)(2,1)S(1)} %join.5.own), channel_id=1, source_target_pairs={{0,192},{16,48},{32,224},{48,16},{64,128},{80,112},{96,160},{112,8... | collective-permute-start | bytes 442376 | tf_op jit(solution)/shard_map/ppermute | solution.py:347
  71.1 11.3 %collective-permute-start.15 = (bf16[4,144,256]{2,1,0:T(8,128)(2,1)S(1)}, bf16[4,144,256]{2,1,0:T(8,128)(2,1)S(1)}, u32[]{:S(2)}, u32[]{:S(2)}) collective-permute-start(bf16[4,144,256]{2,1,0:T(8,128)(2,1)S(1)} %join.6.mine), channel_id=1, source_target_pairs={{0,64},{16,208},{32,96},{48,240},{64,0},{80,144},{96,32},{112,176}... | collective-permute-start | bytes 884744 | tf_op jit(solution)/shard_map/ppermute | solution.py:347
  74.8 11.1 %collective-permute-start.12 = (bf16[4,144,256]{2,1,0:T(8,128)(2,1)S(1)}, bf16[4,144,256]{2,1,0:T(8,128)(2,1)S(1)}, u32[]{:S(2)}, u32[]{:S(2)}) collective-permute-start(bf16[4,144,256]{2,1,0:T(8,128)(2,1)S(1)} %join.7.mine), channel_id=1, source_target_pairs={{0,64},{16,208},{32,96},{48,240},{64,0},{80,144},{96,32},{112,176}... | collective-permute-start | bytes 884744 | tf_op jit(solution)/shard_map/ppermute | solution.py:347
  77.1 12.7 %collective-permute-start.16 = (bf16[4,144,256]{2,1,0:T(8,128)(2,1)S(1)}, bf16[4,144,256]{2,1,0:T(8,128)(2,1)S(1)}, u32[]{:S(2)}, u32[]{:S(2)}) collective-permute-start(bf16[4,144,256]{2,1,0:T(8,128)(2,1)S(1)} %join.6.mine), channel_id=1, source_target_pairs={{0,16},{16,0},{32,48},{48,32},{64,80},{80,64},{96,112},{112,96},{1... | collective-permute-start | bytes 884744 | tf_op jit(solution)/shard_map/ppermute | solution.py:351
  82.4 7.4 %collective-permute-start.17 = (bf16[4,144,256]{2,1,0:T(8,128)(2,1)S(1)}, bf16[4,144,256]{2,1,0:T(8,128)(2,1)S(1)}, u32[]{:S(2)}, u32[]{:S(2)}) collective-permute-start(bf16[4,144,256]{2,1,0:T(8,128)(2,1)S(1)} %collective-permute-done.15.mine_far), channel_id=1, source_target_pairs={{0,16},{16,0},{32,48},{48,32},{64,80},{80,64},{96,112},{112,96},{1... | collective-permute-start | bytes 884744 | tf_op jit(solution)/shard_map/ppermute | solution.py:351
  85.9 5.6 %collective-permute-start.13 = (bf16[4,144,256]{2,1,0:T(8,128)(2,1)S(1)}, bf16[4,144,256]{2,1,0:T(8,128)(2,1)S(1)}, u32[]{:S(2)}, u32[]{:S(2)}) collective-permute-start(bf16[4,144,256]{2,1,0:T(8,128)(2,1)S(1)} %join.7.mine), channel_id=1, source_target_pairs={{0,16},{16,0},{32,48},{48,32},{64,80},{80,64},{96,112},{112,96},{1... | collective-permute-start | bytes 884744 | tf_op jit(solution)/shard_map/ppermute | solution.py:351
  85.9 5.6 %collective-permute-start.14 = (bf16[4,144,256]{2,1,0:T(8,128)(2,1)S(1)}, bf16[4,144,256]{2,1,0:T(8,128)(2,1)S(1)}, u32[]{:S(2)}, u32[]{:S(2)}) collective-permute-start(bf16[4,144,256]{2,1,0:T(8,128)(2,1)S(1)} %collective-permute-done.12.mine_far), channel_id=1, source_target_pairs={{0,16},{16,0},{32,48},{48,32},{64,80},{80,64},{96,112},{112,96},{1... | collective-permute-start | bytes 884744 | tf_op jit(solution)/shard_map/ppermute | solution.py:351

commit v8 on v7

--- a/solution.py
+++ b/solution.py
@@ -69,13 +69,20 @@
 def pass_one(
     base, off, qt, wuk, wuv, og, lat,
     e_v, dp_v, qcat_t, dlat_t, stat,
-    off_v, qt_v, wuk_v, wuv_v, og_v, lat_v, og_wide, qcat, dlat, top, tot, dsum, hide, sem_in,
+    off_v, qt_v, wuk_v, wuv_v, og_v, lat_v, og_wide, qcat, dlat, top, tot, dsum, hide,
+    sem_in, sem_lat,
 ):
-    pairs = ((off, off_v), (qt, qt_v), (wuk, wuk_v), (og, og_v), (wuv, wuv_v), (lat, lat_v))
-    loads = [pltpu.make_async_copy(a, b, sem_in.at[k]) for k, (a, b) in enumerate(pairs)]
-    for copy in loads:
+    def load(source, target, sem):
+        copy = pltpu.make_async_copy(source, target, sem)
         copy.start()
-    loads[0].wait()
+        return copy
+
+    pairs = ((off, off_v), (qt, qt_v), (wuk, wuk_v))
+    ahead = [load(*pair, sem_in.at[k]) for k, pair in enumerate(pairs)]
+    blocks = [slice(j * BLK, (j + 1) * BLK) for j in range(NBLK)]
+    lat_loads = [load(lat.at[:, c], lat_v.at[:, c], sem_lat.at[j]) for j, c in enumerate(blocks)]
+    behind = [load(og, og_v, sem_in.at[3]), load(wuv, wuv_v, sem_in.at[4])]
+    ahead[0].wait()
     bound = jnp.broadcast_to(off_v[...], (ROWS, ROWS)).T - base[0]
     bound = jnp.concatenate([bound] * (BLK // 128), axis=1)
     lane = lax.broadcasted_iota(jnp.int32, (ROWS, BLK), 1)
@@ -85,47 +92,38 @@
     chunks = [slice(c * CHUNK, (c + 1) * CHUNK) for c in range(ALL // CHUNK)]
     heads = [slice(h * ROWS, (h + 1) * ROWS) for h in range(HEADS)]
 
-    loads[1].wait()
-    loads[2].wait()
+    ahead[1].wait()
+    ahead[2].wait()
     for h, rows in enumerate(heads):
         q = qt_v[h].T
         qcat[rows, :LAT] = dot(q[:, :NOPE], wuk_v[h]).astype(bf16)
         qcat[rows, LAT:] = q[:, NOPE:]
-    loads[3].wait()
-    loads[4].wait()
-    og_wide[...] = og_v[...].astype(f32)
-    for h, rows in enumerate(heads):
-        grad = og_wide[pl.ds(h, ROWS, stride=HEADS), :].astype(bf16)
-        dlat[rows, :] = dot_nt(grad, wuv_v[h]).astype(bf16)
-    loads[5].wait()
-    for rows in heads:
-        for k in range(LAT // 128):
-            lanes = slice(k * 128, (k + 1) * 128)
-            qcat_t[lanes, rows] = qcat[rows, lanes].T
-            dlat_t[lanes, rows] = dlat[rows, lanes].T
-        qcat_t[LAT:, rows] = qcat[rows, LAT:].T
-
-    def score(j, _):
-        at = pl.multiple_of(j * BLK, BLK)
-        hide[...] = jnp.where(lane + at <= bound, 0.0, floor_score)
-        cols = lat_v[:, pl.ds(at, BLK)]
+    for j, cols in enumerate(blocks):
+        lat_loads[j].wait()
+        hide[j] = jnp.where(lane + j * BLK <= bound, 0.0, floor_score)
         for rows in chunks:
-            s = dot(qcat[rows, :], cols)
-            s = (s.reshape(CHUNK // ROWS, ROWS, BLK) + hide[...][None]).reshape(CHUNK, BLK)
+            s = dot(qcat[rows, :], lat_v[:, cols])
+            s = (s.reshape(CHUNK // ROWS, ROWS, BLK) + hide[j][None]).reshape(CHUNK, BLK)
             e_v[j, rows, :] = s
             best = top[rows, :]
             for k in range(BLK // 128):
                 best = jnp.maximum(best, s[:, k * 128 : (k + 1) * 128])
             top[rows, :] = best
-        return 0
-
-    lax.fori_loop(0, NBLK, score, 0, unroll=NBLK)
+        rows = heads[j]
+        for k in range(LAT // 128):
+            lanes = slice(k * 128, (k + 1) * 128)
+            qcat_t[lanes, rows] = qcat[rows, lanes].T
+        qcat_t[LAT:, rows] = qcat[rows, LAT:].T
+    for copy in behind:
+        copy.wait()
+    og_wide[...] = og_v[...].astype(f32)
+    for h, rows in enumerate(heads):
+        grad = og_wide[pl.ds(h, ROWS, stride=HEADS), :].astype(bf16)
+        dlat[rows, :] = dot_nt(grad, wuv_v[h]).astype(bf16)
     top[...] = jnp.broadcast_to(jnp.max(top[...], axis=1, keepdims=True) * SCALE2, (ALL, 128))
-
-    def weigh(j, _):
-        cols = lat_v[:LAT, pl.ds(pl.multiple_of(j * BLK, BLK), BLK)]
+    for j, cols in enumerate(blocks):
         for rows in chunks:
-            dp = dot(dlat[rows, :], cols)
+            dp = dot(dlat[rows, :], lat_v[:LAT, cols])
             dp_v[j, rows, :] = dp
             s = e_v[j, rows, :]
             m = top[rows, :]
@@ -138,9 +136,10 @@
                 d = d + e * dp[:, lanes]
             tot[rows, :] = t
             dsum[rows, :] = d
-        return 0
-
-    lax.fori_loop(0, NBLK, weigh, 0, unroll=NBLK)
+        rows = heads[j]
+        for k in range(LAT // 128):
+            lanes = slice(k * 128, (k + 1) * 128)
+            dlat_t[lanes, rows] = dlat[rows, lanes].T
     near = lane[:, :128]
     for h, rows in enumerate(heads):
         t = jnp.sum(tot[rows, :], axis=1, keepdims=True)
@@ -170,8 +169,9 @@
             column,
             column,
             column,
-            pltpu.VMEM((ROWS, BLK), f32),
-            pltpu.SemaphoreType.DMA((6,)),
+            pltpu.VMEM((NBLK, ROWS, BLK), f32),
+            pltpu.SemaphoreType.DMA((5,)),
+            pltpu.SemaphoreType.DMA((NBLK,)),
         ],
         compiler_params=params(LIMIT_ONE),
         name="pass_one",
@@ -302,32 +302,32 @@
     return call(join, "join", [((2 * own.shape[0], COLS, BLK), bf16)], (own, got))[0]
 
 
-def settle(chain, sc, mine, mine_far, other, other_far, *refs):
+def settle(parts, sc, *refs):
     out, sem = refs[-2:]
     copies = []
-    for near, far, half in ((mine, mine_far, sc[3]), (other, other_far, 1 - sc[3])):
-        for i in range(8):
-            b = (i >> 2 & 1, i >> 1 & 1, i & 1)
+    for (chain, mine, far), piece in zip(parts, refs):
+        half = sc[3] if mine else 1 - sc[3]
+        for i in range(4):
+            b = (far, i >> 1, i & 1)
             r = [jnp.where(half == 0, b[d], b[(d + 2) % 3]) for d in range(3)]
             a = [jnp.bitwise_xor(sc[d], r[d]) for d in range(3)]
             rows = pl.ds(pl.multiple_of((a[2] * 2 + a[1]) * COLS, 16), COLS)
             lanes = pl.ds(pl.multiple_of((half * 4 + chain * 2 + a[0]) * BLK, BLK), BLK)
-            block = near.at[i] if i < 4 else far.at[i - 4]
-            copy = pltpu.make_async_copy(block, out.at[rows, lanes], sem.at[len(copies)])
+            copy = pltpu.make_async_copy(piece.at[i], out.at[rows, lanes], sem.at[len(copies)])
             copy.start()
             copies.append(copy)
     for copy in copies:
         copy.wait()
 
 
-def run_settle(chain, sc, pieces, *earlier):
+def run_settle(parts, sc, pieces, *earlier):
     return pl.pallas_call(
-        functools.partial(settle, chain),
+        functools.partial(settle, parts),
         in_specs=[in_smem] + [in_vmem] * len(pieces) + [in_hbm] * len(earlier),
         out_specs=in_hbm,
         out_shape=jax.ShapeDtypeStruct((WIDE, KEYS), bf16),
-        scratch_shapes=[pltpu.SemaphoreType.DMA((16,))],
-        input_output_aliases={5: 0} if earlier else {},
+        scratch_shapes=[pltpu.SemaphoreType.DMA((4 * len(pieces),))],
+        input_output_aliases={1 + len(pieces): 0} if earlier else {},
         compiler_params=params(),
         name="settle",
     )(sc, *pieces, *earlier)
@@ -423,11 +423,14 @@
     far_a, near_a = along(own_a, 0), to_sibling(own_a)
     own_b = run_join(own_b, got_b)
     far_b, near_b = along(own_b, 0), to_sibling(own_b)
-    pieces = [
-        (own_a, far_a, near_a, to_sibling(far_a)),
-        (own_b, far_b, near_b, to_sibling(far_b)),
-    ]
-    d_latent = run_settle(1, sc_own, pieces[1], run_settle(0, sc_own, pieces[0])).T
+    near_parts = ((0, True, 0), (0, False, 0), (1, True, 0), (1, False, 0))
+    out = run_settle(near_parts, sc_own, (own_a, near_a, own_b, near_b))
+    other_a = to_sibling(far_a)
+    far_b, out = tie((far_b, out))
+    other_b = to_sibling(far_b)
+    out = run_settle(((0, True, 1), (0, False, 1)), sc_own, (far_a, other_a), out)
+    out = run_settle(((1, True, 1), (1, False, 1)), sc_own, (far_b, other_b), out)
+    d_latent = out.T
 
     dq = jnp.sum(dq.astype(f32), axis=0).astype(bf16)
     d_queries = jnp.transpose(dq.reshape(HEADS, 8, NOPE + ROT), (1, 0, 2))

time: 93.6 us -> 92.3 us (0.986)
  Pallas kernels: 29.7 us -> 32.3 us
  starting transfers between devices: 31 us -> 28.6 us
  waiting for transfers between devices: 10.3 us -> 8.27 us
    ppermute x12, waiting for transfers between devices: 10.3 us -> 8.25 us  [along(): return lax.ppermute(value, 'head', pairs)]
    ppermute x12, starting transfers between devices: 12.3 us -> 10.6 us  [along(): return lax.ppermute(value, 'head', pairs)]
    pallas_call x1, Pallas kernels: 10 us -> 11.4 us  [run_pass_one(): pl.pallas_call(pass_one, in_specs=[in_smem] + [in_hbm] * 6, out_specs=[in...]
    pallas_call x2 -> x3, Pallas kernels: 3.38 us -> 4.54 us  [run_settle(): pl.pallas_call(functools.partial(settle, parts), in_specs=[in_smem] + [in...]
    ppermute x6, starting transfers between devices: 14.8 us -> 13.7 us  [to_sibling(): return lax.ppermute(value, 'head', [(k, k ^ 1) for k in range(16)])]
  transfers between devices with their start and end apart: 19 -> 19, of which waited for: 6 -> 6; matrix products, arithmetic and copies ran while one was open for 1% -> 1% of each run, Pallas kernels for 15% -> 17%
where the time goes in v8:
time: 92.3 us; the launch traced here: 91.5 us
  Pallas kernels  32.3 us (35%)
  starting transfers between devices  28.6 us (31%)
  blocking collectives  20.4 us (22%)
  waiting for transfers between devices  8.27 us (9%)
  between operations  1.03 us (1%)
    all_to_all x1, blocking collectives, shards(): stat = lax.all_to_all(stat, 'key', 0, 0, tiled=True)  20.4 us
    pallas_call x21, Pallas kernels, call(): pl.pallas_call(kernel, in_specs=[in_smem] * scalars + [in_vmem] * (len(ar...  16.3 us
    ppermute x6, starting transfers between devices, to_sibling(): return lax.ppermute(value, 'head', [(k, k ^ 1) for k in range(16)])  13.7 us
    pallas_call x1, Pallas kernels, run_pass_one(): pl.pallas_call(pass_one, in_specs=[in_smem] + [in_hbm] * 6, out_specs=[in...  11.4 us
    ppermute x12, starting transfers between devices, along(): return lax.ppermute(value, 'head', pairs)  10.6 us
    ppermute x12, waiting for transfers between devices, along(): return lax.ppermute(value, 'head', pairs)  8.25 us
    pallas_call x3, Pallas kernels, run_settle(): pl.pallas_call(functools.partial(settle, parts), in_specs=[in_smem] + [in...  4.54 us
    all_to_all x1, starting transfers between devices, shards(): dq = lax.all_to_all(dq, 'key', 0, 0, tiled=True)  4.23 us
  transfers between devices with their start and end apart: 19, of which 6 were waited for; matrix products, arithmetic and copies ran while one was open for 1% of the time, Pallas kernels for 17%

profile of v8, /device:TPU:1, one launch (start us, length us, event | category | flops | bytes accessed | tf_op | source)
XLA Modules:
  0.0 91.5 jit_solution(1327072350311107780)
XLA Ops:
  0.6 0.1 stack.35.sc
  0.7 0.1 stack.33.sc
  0.8 11.4 %pass_one.1 = (f32[8,1024,256]{2,1,0:T(8,128)S(1)}, f32[8,1024,256]{2,1,0:T(8,128)S(1)}, bf16[576,1024]{1,0:T(8,128)(2,1)S(1)}, bf16[512,1024]{1,0:T(8,128)(2,1)S(1)}, f32[16,24,128]{2,1,0:T(8,128)S(1)}) custom-call(s32[1]{0:T(128)} %bitcast.base, s32[1,128]{1,0:T(1,128)} %bitcast.24, bf16[8,192,128]{2,1,0:T(8,128)(2,1)} %bitcast.21, ...), custom_call_target="tpu_custom_call" | custom-call | tf_op jit(solution)/shard_map/pass_one/pallas_call | solution.py:159
  12.3 20.4 %all_to_all.10.stat = f32[16,24,128]{2,1,0:T(8,128)S(1)} all-to-all(f32[16,24,128]{2,1,0:T(8,128)S(1)} %get-tuple-element.67), channel_id=1, replica_groups=mesh['head'=16,'key'=16] {'key'}, dimensions={0} | all-to-all | bytes 393216 | tf_op jit(solution)/shard_map/all_to_all | solution.py:373
  32.7 2.1 %second_first.1 = (bf16[8,144,256]{2,1,0:T(8,128)(2,1)S(1)}, bf16[2,1024,256]{2,1,0:T(8,128)(2,1)S(1)}, f32[1024,128]{1,0:T(8,128)S(1)}, f32[1024,128]{1,0:T(8,128)S(1)}) custom-call(s32[5]{0:T(128)S(1)} %stack.35.sc, f32[16,24,128]{2,1,0:T(8,128)S(1)} %all_to_all.10.stat, bf16[576,1024]{1,0:T(8,128)(2,1)S(1)} %get-tuple-element.68.qcat_t, ...), custom_call_target="tpu_custom_call" | custom-call | tf_op jit(solution)/shard_map/second_first/pallas_call | solution.py:55
  34.8 2.7 %collective-permute-start = (bf16[8,144,256]{2,1,0:T(8,128)(2,1)S(1)}, bf16[8,144,256]{2,1,0:T(8,128)(2,1)S(1)}, u32[]{:S(2)}, u32[]{:S(2)}) collective-permute-start(bf16[8,144,256]{2,1,0:T(8,128)(2,1)S(1)} %get-tuple-element.76), channel_id=1, source_target_pairs={{0,16},{16,0},{32,48},{48,32},{64,80},{80,64},{96,112},{112,96},{1... | collective-permute-start | bytes 1769480 | tf_op jit(solution)/shard_map/ppermute | solution.py:351
  37.5 1.9 %second.4 = (bf16[8,144,256]{2,1,0:T(8,128)(2,1)S(1)}, bf16[2,1024,256]{2,1,0:T(8,128)(2,1)S(1)}) custom-call(s32[5]{0:T(128)S(1)} %stack.33.sc, f32[1024,128]{1,0:T(8,128)S(1)} %get-tuple-element.72.coef, f32[1024,128]{1,0:T(8,128)S(1)} %get-tuple-element.73.delta, bf16[576,1024]{1,0:T(8,128)(2,1)S(1)} %get-tuple-element.68.qcat_t, ...), custom_call_target="tpu_custom_call" | custom-call | tf_op jit(solution)/shard_map/second/pallas_call | solution.py:55
  39.4 0.0 collective-permute-done.got
  39.4 0.1 halve.8
  39.6 1.9 %second.5 = (bf16[8,144,256]{2,1,0:T(8,128)(2,1)S(1)}, bf16[2,1024,256]{2,1,0:T(8,128)(2,1)S(1)}) custom-call(s32[5]{0:T(128)S(1)} %stack.35.sc, f32[1024,128]{1,0:T(8,128)S(1)} %get-tuple-element.72.coef, f32[1024,128]{1,0:T(8,128)S(1)} %get-tuple-element.73.delta, bf16[576,1024]{1,0:T(8,128)(2,1)S(1)} %get-tuple-element.68.qcat_t, ...), custom_call_target="tpu_custom_call" | custom-call | tf_op jit(solution)/shard_map/second/pallas_call | solution.py:55
  41.5 0.2 collective-permute-start.1
  41.7 2.8 %collective-permute-start.2 = (bf16[4,144,256]{2,1,0:T(8,128)(2,1)S(1)}, bf16[4,144,256]{2,1,0:T(8,128)(2,1)S(1)}, u32[]{:S(2)}, u32[]{:S(2)}) collective-permute-start(bf16[4,144,256]{2,1,0:T(8,128)(2,1)S(1)} %get-tuple-element.82), channel_id=1, source_target_pairs={{0,64},{16,208},{32,96},{48,240},{64,0},{80,144},{96,32},{112,176}... | collective-permute-start | bytes 884744 | tf_op jit(solution)/shard_map/ppermute | solution.py:347
  44.4 0.0 copy-start
  44.4 1.9 %second.3 = (bf16[8,144,256]{2,1,0:T(8,128)(2,1)S(1)}, bf16[2,1024,256]{2,1,0:T(8,128)(2,1)S(1)}) custom-call(s32[5]{0:T(128)S(1)} %stack.33.sc, f32[1024,128]{1,0:T(8,128)S(1)} %get-tuple-element.72.coef, f32[1024,128]{1,0:T(8,128)S(1)} %get-tuple-element.73.delta, bf16[576,1024]{1,0:T(8,128)(2,1)S(1)} %get-tuple-element.68.qcat_t, ...), custom_call_target="tpu_custom_call" | custom-call | tf_op jit(solution)/shard_map/second/pallas_call | solution.py:55
  46.3 0.0 collective-permute-done.1.got
  46.3 0.1 halve.9
  46.5 0.1 collective-permute-start.3
  46.6 0.0 copy-done
  46.6 1.5 %query_piece.4.refs_0_ = f32[1024,576]{1,0:T(8,128)S(1)} custom-call(s32[5]{0:T(128)S(1)} %stack.35.sc, bf16[2,1024,256]{2,1,0:T(8,128)(2,1)S(1)} %get-tuple-element.84.ds, bf16[576,2048]{1,0:T(8,128)(2,1)S(1)} %bitcast.16), custom_call_target="tpu_custom_call" | custom-call | tf_op jit(solution)/shard_map/query_piece/pallas_call | solution.py:55
  48.1 1.6 %query_piece.5.refs_0_ = f32[1024,576]{1,0:T(8,128)S(1)} custom-call(s32[5]{0:T(128)S(1)} %stack.33.sc, bf16[2,1024,256]{2,1,0:T(8,128)(2,1)S(1)} %get-tuple-element.83.ds, bf16[576,2048]{1,0:T(8,128)(2,1)S(1)} %bitcast.17, f32[1024,576]{1,0:T(8,128)S(1)} %query_piece.4.refs_0_), custom_call_target="tpu_custom_call" | custom-call | tf_op jit(solution)/shard_map/query_piece/pallas_call | solution.py:55
  49.7 0.0 collective-permute-done.2.got
  49.7 0.1 halve.10
  49.8 0.4 collective-permute-start.4
  50.2 1.6 %query_piece.6.refs_0_ = f32[1024,576]{1,0:T(8,128)S(1)} custom-call(s32[5]{0:T(128)S(1)} %stack.35.sc, bf16[2,1024,256]{2,1,0:T(8,128)(2,1)S(1)} %get-tuple-element.91.ds, bf16[576,2048]{1,0:T(8,128)(2,1)S(1)} %bitcast.18, f32[1024,576]{1,0:T(8,128)S(1)} %query_piece.5.refs_0_), custom_call_target="tpu_custom_call" | custom-call | tf_op jit(solution)/shard_map/query_piece/pallas_call | solution.py:55
  51.7 0.0 copy-start.1
  51.8 1.6 %query_piece.7.acc = f32[1024,576]{1,0:T(8,128)S(1)} custom-call(s32[5]{0:T(128)S(1)} %stack.33.sc, bf16[2,1024,256]{2,1,0:T(8,128)(2,1)S(1)} %get-tuple-element.90.ds, bf16[576,2048]{1,0:T(8,128)(2,1)S(1)} %bitcast.19, f32[1024,576]{1,0:T(8,128)S(1)} %query_piece.6.refs_0_), custom_call_target="tpu_custom_call" | custom-call | tf_op jit(solution)/shard_map/query_piece/pallas_call | solution.py:55
  53.3 0.0 collective-permute-done.3.got
  53.4 0.1 halve.11
  53.4 1.2 %collective-permute-start.5 = (bf16[2,144,256]{2,1,0:T(8,128)(2,1)S(1)}, bf16[2,144,256]{2,1,0:T(8,128)(2,1)S(1)}, u32[]{:S(2)}, u32[]{:S(2)}) collective-permute-start(bf16[2,144,256]{2,1,0:T(8,128)(2,1)S(1)} %get-tuple-element.104), channel_id=1, source_target_pairs={{0,192},{16,48},{32,224},{48,16},{64,128},{80,112},{96,160},{112,8... | collective-permute-start | bytes 442376 | tf_op jit(solution)/shard_map/ppermute | solution.py:347
  54.7 0.0 copy-done.1
  54.7 1.6 %query_last.1 = bf16[16,64,192]{2,1,0:T(8,128)(2,1)} custom-call(f32[1024,576]{1,0:T(8,128)S(1)} %query_piece.7.acc, bf16[8,128,512]{2,1,0:T(8,128)(2,1)S(1)} %copy-done.1), custom_call_target="tpu_custom_call" | custom-call | tf_op jit(solution)/shard_map/query_last/pallas_call | solution.py:55
  56.3 0.0 collective-permute-done.4.got
  56.4 0.1 collective-permute-start.6
  56.5 1.0 %collective-permute-done.5.got = bf16[2,144,256]{2,1,0:T(8,128)(2,1)S(1)} collective-permute-done((bf16[2,144,256]{2,1,0:T(8,128)(2,1)S(1)}, bf16[2,144,256]{2,1,0:T(8,128)(2,1)S(1)}, u32[]{:S(2)}, u32[]{:S(2)}) %collective-permute-start.5) | collective-permute-done | bytes 147488 | tf_op jit(solution)/shard_map/ppermute | solution.py:347
  57.5 0.7 collective-permute-start.8
  58.3 1.4 %collective-permute-done.6.got = bf16[1,144,256]{2,1,0:T(8,128)(2,1)S(1)} collective-permute-done((bf16[1,144,256]{2,1,0:T(8,128)(2,1)S(1)}, bf16[1,144,256]{2,1,0:T(8,128)(2,1)S(1)}, u32[]{:S(2)}, u32[]{:S(2)}) %collective-permute-start.6) | collective-permute-done | bytes 73760 | tf_op jit(solution)/shard_map/ppermute | solution.py:347
  59.7 0.4 collective-permute-start.7
  60.1 1.3 %collective-permute-done.8.got = bf16[1,144,256]{2,1,0:T(8,128)(2,1)S(1)} collective-permute-done((bf16[1,144,256]{2,1,0:T(8,128)(2,1)S(1)}, bf16[1,144,256]{2,1,0:T(8,128)(2,1)S(1)}, u32[]{:S(2)}, u32[]{:S(2)}) %collective-permute-start.8) | collective-permute-done | bytes 73760 | tf_op jit(solution)/shard_map/ppermute | solution.py:347
  61.4 0.5 collective-permute-start.9
  61.9 1.1 %collective-permute-done.7.got = bf16[1,144,256]{2,1,0:T(8,128)(2,1)S(1)} collective-permute-done((bf16[1,144,256]{2,1,0:T(8,128)(2,1)S(1)}, bf16[1,144,256]{2,1,0:T(8,128)(2,1)S(1)}, u32[]{:S(2)}, u32[]{:S(2)}) %collective-permute-start.7) | collective-permute-done | bytes 73760 | tf_op jit(solution)/shard_map/ppermute | solution.py:347
  63.0 0.4 collective-permute-start.10
  63.4 1.3 %collective-permute-done.9.got = bf16[1,144,256]{2,1,0:T(8,128)(2,1)S(1)} collective-permute-done((bf16[1,144,256]{2,1,0:T(8,128)(2,1)S(1)}, bf16[1,144,256]{2,1,0:T(8,128)(2,1)S(1)}, u32[]{:S(2)}, u32[]{:S(2)}) %collective-permute-start.9) | collective-permute-done | bytes 73760 | tf_op jit(solution)/shard_map/ppermute | solution.py:347
  64.7 0.9 %collective-permute-start.11 = (bf16[2,144,256]{2,1,0:T(8,128)(2,1)S(1)}, bf16[2,144,256]{2,1,0:T(8,128)(2,1)S(1)}, u32[]{:S(2)}, u32[]{:S(2)}) collective-permute-start(bf16[2,144,256]{2,1,0:T(8,128)(2,1)S(1)} %join.5.own), channel_id=1, source_target_pairs={{0,192},{16,48},{32,224},{48,16},{64,128},{80,112},{96,160},{112,8... | collective-permute-start | bytes 442376 | tf_op jit(solution)/shard_map/ppermute | solution.py:347
  65.6 4.2 %all-to-all-start.1 = ((bf16[16,64,192]{2,1,0:T(8,128)(2,1)}), bf16[16,64,192]{2,1,0:T(8,128)(2,1)S(1)}, u32[]{:S(2)}, u32[]{:S(2)}) async-start(bf16[16,64,192]{2,1,0:T(8,128)(2,1)} %query_last.1), calls=%async_computation.1 | async-start | bytes 1048576 | tf_op jit(solution)/shard_map/all_to_all | solution.py:414
  69.9 0.0 collective-permute-done.10.got
  69.9 3.0 %collective-permute-start.16 = (bf16[4,144,256]{2,1,0:T(8,128)(2,1)S(1)}, bf16[4,144,256]{2,1,0:T(8,128)(2,1)S(1)}, u32[]{:S(2)}, u32[]{:S(2)}) collective-permute-start(bf16[4,144,256]{2,1,0:T(8,128)(2,1)S(1)} %join.6.refs_0_), channel_id=1, source_target_pairs={{0,64},{16,208},{32,96},{48,240},{64,0},{80,144},{96,32},{112,176}... | collective-permute-start | bytes 884744 | tf_op jit(solution)/shard_map/ppermute | solution.py:347
  72.9 4.3 %collective-permute-start.13 = (bf16[4,144,256]{2,1,0:T(8,128)(2,1)S(1)}, bf16[4,144,256]{2,1,0:T(8,128)(2,1)S(1)}, u32[]{:S(2)}, u32[]{:S(2)}) collective-permute-start(bf16[4,144,256]{2,1,0:T(8,128)(2,1)S(1)} %join.6.refs_0_), channel_id=1, source_target_pairs={{0,16},{16,0},{32,48},{48,32},{64,80},{80,64},{96,112},{112,96},{1... | collective-permute-start | bytes 884744 | tf_op jit(solution)/shard_map/ppermute | solution.py:351
  77.2 0.0 collective-permute-done.11.got
  77.3 3.3 %collective-permute-start.14 = (bf16[4,144,256]{2,1,0:T(8,128)(2,1)S(1)}, bf16[4,144,256]{2,1,0:T(8,128)(2,1)S(1)}, u32[]{:S(2)}, u32[]{:S(2)}) collective-permute-start(bf16[4,144,256]{2,1,0:T(8,128)(2,1)S(1)} %join.7.refs_2_), channel_id=1, source_target_pairs={{0,16},{16,0},{32,48},{48,32},{64,80},{80,64},{96,112},{112,96},{1... | collective-permute-start | bytes 884744 | tf_op jit(solution)/shard_map/ppermute | solution.py:351
  80.6 0.0 collective-permute-start.12
  80.6 0.0 collective-permute-done.16.refs_0_
  80.6 3.2 %collective-permute-start.17 = (bf16[4,144,256]{2,1,0:T(8,128)(2,1)S(1)}, bf16[4,144,256]{2,1,0:T(8,128)(2,1)S(1)}, u32[]{:S(2)}, u32[]{:S(2)}) collective-permute-start(bf16[4,144,256]{2,1,0:T(8,128)(2,1)S(1)} %collective-permute-done.16.refs_0_), channel_id=1, source_target_pairs={{0,16},{16,0},{32,48},{48,32},{64,80},{80,64},{96,112},{112,96},{1... | collective-permute-start | bytes 884744 | tf_op jit(solution)/shard_map/ppermute | solution.py:351
  83.9 0.0 collective-permute-done.13.refs_1_
  83.9 0.0 collective-permute-done.14.refs_3_
  83.9 1.7 %settle.3.refs_2_ = bf16[576,2048]{1,0:T(8,128)(2,1)} custom-call(s32[5]{0:T(128)S(1)} %stack.33.sc, bf16[4,144,256]{2,1,0:T(8,128)(2,1)S(1)} %join.6.refs_0_, bf16[4,144,256]{2,1,0:T(8,128)(2,1)S(1)} %collective-permute-done.13.refs_1_, bf16[4,144,256]{2,1,0:T(8,128)(2,1)S(1)} %join.7.refs_2_, bf16[4,144,256]{2,1,0:T(8,128)(2,1)S(1)} %collective-permute-done.14.refs_3_), custom_call_target="tpu_custom_call" | custom-call | tf_op jit(solution)/shard_map/settle/pallas_call | solution.py:324
  85.6 2.1 %collective-permute-done.12.refs_0_ = bf16[4,144,256]{2,1,0:T(8,128)(2,1)S(1)} collective-permute-done((bf16[4,144,256]{2,1,0:T(8,128)(2,1)S(1)}, bf16[4,144,256]{2,1,0:T(8,128)(2,1)S(1)}, u32[]{:S(2)}, u32[]{:S(2)}) %collective-permute-start.12) | collective-permute-done | bytes 294944 | tf_op jit(solution)/shard_map/ppermute | solution.py:347
  87.7 0.0 collective-permute-start.15
  87.7 0.0 all-to-all-done.1
  87.7 0.1 reduce_sum.12
  87.8 0.6 copy.10
  88.4 0.0 collective-permute-done.17.refs_1_
  88.4 1.4 %settle.4.refs_2_ = bf16[576,2048]{1,0:T(8,128)(2,1)} custom-call(s32[5]{0:T(128)S(1)} %stack.33.sc, bf16[4,144,256]{2,1,0:T(8,128)(2,1)S(1)} %collective-permute-done.16.refs_0_, bf16[4,144,256]{2,1,0:T(8,128)(2,1)S(1)} %collective-permute-done.17.refs_1_, bf16[576,2048]{1,0:T(8,128)(2,1)} %settle.3.refs_2_), custom_call_target="tpu_custom_call", output_to_operand_aliasing={{}: (3, {})} | custom-call | tf_op jit(solution)/shard_map/settle/pallas_call | solution.py:324
  89.9 0.0 collective-permute-done.15.refs_1_
  89.9 1.4 %settle.5 = bf16[576,2048]{1,0:T(8,128)(2,1)} custom-call(s32[5]{0:T(128)S(1)} %stack.33.sc, bf16[4,144,256]{2,1,0:T(8,128)(2,1)S(1)} %collective-permute-done.12.refs_0_, bf16[4,144,256]{2,1,0:T(8,128)(2,1)S(1)} %collective-permute-done.15.refs_1_, bf16[576,2048]{1,0:T(8,128)(2,1)} %settle.4.refs_2_), custom_call_target="tpu_custom_call", output_to_operand_aliasing={{}: (3, {})} | custom-call | tf_op jit(solution)/shard_map/settle/pallas_call | solution.py:324
  (8 shorter events, 0.2 us)
Async XLA Ops:
  34.8 4.6 %collective-permute-start = (bf16[8,144,256]{2,1,0:T(8,128)(2,1)S(1)}, bf16[8,144,256]{2,1,0:T(8,128)(2,1)S(1)}, u32[]{:S(2)}, u32[]{:S(2)}) collective-permute-start(bf16[8,144,256]{2,1,0:T(8,128)(2,1)S(1)} %get-tuple-element.76), channel_id=1, source_target_pairs={{0,16},{16,0},{32,48},{48,32},{64,80},{80,64},{96,112},{112,96},{1... | collective-permute-start | bytes 1769480 | tf_op jit(solution)/shard_map/ppermute | solution.py:351
  41.5 4.8 %collective-permute-start.1 = (bf16[8,144,256]{2,1,0:T(8,128)(2,1)S(1)}, bf16[8,144,256]{2,1,0:T(8,128)(2,1)S(1)}, u32[]{:S(2)}, u32[]{:S(2)}) collective-permute-start(bf16[8,144,256]{2,1,0:T(8,128)(2,1)S(1)} %get-tuple-element.79), channel_id=1, source_target_pairs={{0,16},{16,0},{32,48},{48,32},{64,80},{80,64},{96,112},{112,96},{1... | collective-permute-start | bytes 1769480 | tf_op jit(solution)/shard_map/ppermute | solution.py:351
  41.7 8.1 %collective-permute-start.2 = (bf16[4,144,256]{2,1,0:T(8,128)(2,1)S(1)}, bf16[4,144,256]{2,1,0:T(8,128)(2,1)S(1)}, u32[]{:S(2)}, u32[]{:S(2)}) collective-permute-start(bf16[4,144,256]{2,1,0:T(8,128)(2,1)S(1)} %get-tuple-element.82), channel_id=1, source_target_pairs={{0,64},{16,208},{32,96},{48,240},{64,0},{80,144},{96,32},{112,176}... | collective-permute-start | bytes 884744 | tf_op jit(solution)/shard_map/ppermute | solution.py:347
  44.4 2.2 %copy-start = (bf16[2048,576]{0,1:T(8,128)(2,1)S(1)}, bf16[2048,576]{0,1:T(8,128)(2,1)}, u32[]{:S(2)}) copy-start(bf16[2048,576]{0,1:T(8,128)(2,1)} %param.9) | copy-start | bytes 7077892
  46.5 6.9 %collective-permute-start.3 = (bf16[4,144,256]{2,1,0:T(8,128)(2,1)S(1)}, bf16[4,144,256]{2,1,0:T(8,128)(2,1)S(1)}, u32[]{:S(2)}, u32[]{:S(2)}) collective-permute-start(bf16[4,144,256]{2,1,0:T(8,128)(2,1)S(1)} %get-tuple-element.89), channel_id=1, source_target_pairs={{0,64},{16,208},{32,96},{48,240},{64,0},{80,144},{96,32},{112,176}... | collective-permute-start | bytes 884744 | tf_op jit(solution)/shard_map/ppermute | solution.py:347
  49.8 6.5 %collective-permute-start.4 = (bf16[2,144,256]{2,1,0:T(8,128)(2,1)S(1)}, bf16[2,144,256]{2,1,0:T(8,128)(2,1)S(1)}, u32[]{:S(2)}, u32[]{:S(2)}) collective-permute-start(bf16[2,144,256]{2,1,0:T(8,128)(2,1)S(1)} %get-tuple-element.99), channel_id=1, source_target_pairs={{0,192},{16,48},{32,224},{48,16},{64,128},{80,112},{96,160},{112,8... | collective-permute-start | bytes 442376 | tf_op jit(solution)/shard_map/ppermute | solution.py:347
  51.7 2.9 %copy-start.1 = (bf16[8,128,512]{2,1,0:T(8,128)(2,1)S(1)}, bf16[8,128,512]{2,1,0:T(8,128)(2,1)}, u32[]{:S(2)}) copy-start(bf16[8,128,512]{2,1,0:T(8,128)(2,1)} %wuk.3) | copy-start | bytes 3145732
  53.4 4.1 %collective-permute-start.5 = (bf16[2,144,256]{2,1,0:T(8,128)(2,1)S(1)}, bf16[2,144,256]{2,1,0:T(8,128)(2,1)S(1)}, u32[]{:S(2)}, u32[]{:S(2)}) collective-permute-start(bf16[2,144,256]{2,1,0:T(8,128)(2,1)S(1)} %get-tuple-element.104), channel_id=1, source_target_pairs={{0,192},{16,48},{32,224},{48,16},{64,128},{80,112},{96,160},{112,8... | collective-permute-start | bytes 442376 | tf_op jit(solution)/shard_map/ppermute | solution.py:347
  56.4 3.3 %collective-permute-start.6 = (bf16[1,144,256]{2,1,0:T(8,128)(2,1)S(1)}, bf16[1,144,256]{2,1,0:T(8,128)(2,1)S(1)}, u32[]{:S(2)}, u32[]{:S(2)}) collective-permute-start(bf16[1,144,256]{2,1,0:T(8,128)(2,1)S(1)} %get-tuple-element.109), channel_id=1, source_target_pairs={{0,32},{16,80},{32,0},{48,112},{64,96},{80,16},{96,64},{112,48},{1... | collective-permute-start | bytes 221192 | tf_op jit(solution)/shard_map/ppermute | solution.py:347
  57.5 3.8 %collective-permute-start.8 = (bf16[1,144,256]{2,1,0:T(8,128)(2,1)S(1)}, bf16[1,144,256]{2,1,0:T(8,128)(2,1)S(1)}, u32[]{:S(2)}, u32[]{:S(2)}) collective-permute-start(bf16[1,144,256]{2,1,0:T(8,128)(2,1)S(1)} %get-tuple-element.114), channel_id=1, source_target_pairs={{0,32},{16,80},{32,0},{48,112},{64,96},{80,16},{96,64},{112,48},{1... | collective-permute-start | bytes 221192 | tf_op jit(solution)/shard_map/ppermute | solution.py:347
  59.7 3.3 %collective-permute-start.7 = (bf16[1,144,256]{2,1,0:T(8,128)(2,1)S(1)}, bf16[1,144,256]{2,1,0:T(8,128)(2,1)S(1)}, u32[]{:S(2)}, u32[]{:S(2)}) collective-permute-start(bf16[1,144,256]{2,1,0:T(8,128)(2,1)S(1)} %halve.14.own), channel_id=1, source_target_pairs={{0,32},{16,80},{32,0},{48,112},{64,96},{80,16},{96,64},{112,48},{1... | collective-permute-start | bytes 221192 | tf_op jit(solution)/shard_map/ppermute | solution.py:347
  61.4 3.3 %collective-permute-start.9 = (bf16[1,144,256]{2,1,0:T(8,128)(2,1)S(1)}, bf16[1,144,256]{2,1,0:T(8,128)(2,1)S(1)}, u32[]{:S(2)}, u32[]{:S(2)}) collective-permute-start(bf16[1,144,256]{2,1,0:T(8,128)(2,1)S(1)} %halve.15.own), channel_id=1, source_target_pairs={{0,32},{16,80},{32,0},{48,112},{64,96},{80,16},{96,64},{112,48},{1... | collective-permute-start | bytes 221192 | tf_op jit(solution)/shard_map/ppermute | solution.py:347
  63.0 6.9 %collective-permute-start.10 = (bf16[2,144,256]{2,1,0:T(8,128)(2,1)S(1)}, bf16[2,144,256]{2,1,0:T(8,128)(2,1)S(1)}, u32[]{:S(2)}, u32[]{:S(2)}) collective-permute-start(bf16[2,144,256]{2,1,0:T(8,128)(2,1)S(1)} %join.4.own), channel_id=1, source_target_pairs={{0,192},{16,48},{32,224},{48,16},{64,128},{80,112},{96,160},{112,8... | collective-permute-start | bytes 442376 | tf_op jit(solution)/shard_map/ppermute | solution.py:347
  64.7 12.6 %collective-permute-start.11 = (bf16[2,144,256]{2,1,0:T(8,128)(2,1)S(1)}, bf16[2,144,256]{2,1,0:T(8,128)(2,1)S(1)}, u32[]{:S(2)}, u32[]{:S(2)}) collective-permute-start(bf16[2,144,256]{2,1,0:T(8,128)(2,1)S(1)} %join.5.own), channel_id=1, source_target_pairs={{0,192},{16,48},{32,224},{48,16},{64,128},{80,112},{96,160},{112,8... | collective-permute-start | bytes 442376 | tf_op jit(solution)/shard_map/ppermute | solution.py:347
  65.6 22.1 %all-to-all-start.1 = ((bf16[16,64,192]{2,1,0:T(8,128)(2,1)}), bf16[16,64,192]{2,1,0:T(8,128)(2,1)S(1)}, u32[]{:S(2)}, u32[]{:S(2)}) async-start(bf16[16,64,192]{2,1,0:T(8,128)(2,1)} %query_last.1), calls=%async_computation.1 | async-start | bytes 1048576 | tf_op jit(solution)/shard_map/all_to_all | solution.py:414
  69.9 10.7 %collective-permute-start.16 = (bf16[4,144,256]{2,1,0:T(8,128)(2,1)S(1)}, bf16[4,144,256]{2,1,0:T(8,128)(2,1)S(1)}, u32[]{:S(2)}, u32[]{:S(2)}) collective-permute-start(bf16[4,144,256]{2,1,0:T(8,128)(2,1)S(1)} %join.6.refs_0_), channel_id=1, source_target_pairs={{0,64},{16,208},{32,96},{48,240},{64,0},{80,144},{96,32},{112,176}... | collective-permute-start | bytes 884744 | tf_op jit(solution)/shard_map/ppermute | solution.py:347
  72.9 10.9 %collective-permute-start.13 = (bf16[4,144,256]{2,1,0:T(8,128)(2,1)S(1)}, bf16[4,144,256]{2,1,0:T(8,128)(2,1)S(1)}, u32[]{:S(2)}, u32[]{:S(2)}) collective-permute-start(bf16[4,144,256]{2,1,0:T(8,128)(2,1)S(1)} %join.6.refs_0_), channel_id=1, source_target_pairs={{0,16},{16,0},{32,48},{48,32},{64,80},{80,64},{96,112},{112,96},{1... | collective-permute-start | bytes 884744 | tf_op jit(solution)/shard_map/ppermute | solution.py:351
  77.3 6.6 %collective-permute-start.14 = (bf16[4,144,256]{2,1,0:T(8,128)(2,1)S(1)}, bf16[4,144,256]{2,1,0:T(8,128)(2,1)S(1)}, u32[]{:S(2)}, u32[]{:S(2)}) collective-permute-start(bf16[4,144,256]{2,1,0:T(8,128)(2,1)S(1)} %join.7.refs_2_), channel_id=1, source_target_pairs={{0,16},{16,0},{32,48},{48,32},{64,80},{80,64},{96,112},{112,96},{1... | collective-permute-start | bytes 884744 | tf_op jit(solution)/shard_map/ppermute | solution.py:351
  80.6 7.1 %collective-permute-start.12 = (bf16[4,144,256]{2,1,0:T(8,128)(2,1)S(1)}, bf16[4,144,256]{2,1,0:T(8,128)(2,1)S(1)}, u32[]{:S(2)}, u32[]{:S(2)}) collective-permute-start(bf16[4,144,256]{2,1,0:T(8,128)(2,1)S(1)} %join.7.refs_2_), channel_id=1, source_target_pairs={{0,64},{16,208},{32,96},{48,240},{64,0},{80,144},{96,32},{112,176}... | collective-permute-start | bytes 884744 | tf_op jit(solution)/shard_map/ppermute | solution.py:347
  80.6 7.8 %collective-permute-start.17 = (bf16[4,144,256]{2,1,0:T(8,128)(2,1)S(1)}, bf16[4,144,256]{2,1,0:T(8,128)(2,1)S(1)}, u32[]{:S(2)}, u32[]{:S(2)}) collective-permute-start(bf16[4,144,256]{2,1,0:T(8,128)(2,1)S(1)} %collective-permute-done.16.refs_0_), channel_id=1, source_target_pairs={{0,16},{16,0},{32,48},{48,32},{64,80},{80,64},{96,112},{112,96},{1... | collective-permute-start | bytes 884744 | tf_op jit(solution)/shard_map/ppermute | solution.py:351
  87.7 2.2 %collective-permute-start.15 = (bf16[4,144,256]{2,1,0:T(8,128)(2,1)S(1)}, bf16[4,144,256]{2,1,0:T(8,128)(2,1)S(1)}, u32[]{:S(2)}, u32[]{:S(2)}) collective-permute-start(bf16[4,144,256]{2,1,0:T(8,128)(2,1)S(1)} %collective-permute-done.12.refs_0_), channel_id=1, source_target_pairs={{0,16},{16,0},{32,48},{48,32},{64,80},{80,64},{96,112},{112,96},{1... | collective-permute-start | bytes 884744 | tf_op jit(solution)/shard_map/ppermute | solution.py:351

commit v9 on v7

--- a/solution.py
+++ b/solution.py
@@ -302,32 +302,32 @@
     return call(join, "join", [((2 * own.shape[0], COLS, BLK), bf16)], (own, got))[0]
 
 
-def settle(chain, sc, mine, mine_far, other, other_far, *refs):
+def settle(parts, sc, *refs):
     out, sem = refs[-2:]
     copies = []
-    for near, far, half in ((mine, mine_far, sc[3]), (other, other_far, 1 - sc[3])):
-        for i in range(8):
-            b = (i >> 2 & 1, i >> 1 & 1, i & 1)
+    for (chain, mine, far), piece in zip(parts, refs):
+        half = sc[3] if mine else 1 - sc[3]
+        for i in range(4):
+            b = (far, i >> 1, i & 1)
             r = [jnp.where(half == 0, b[d], b[(d + 2) % 3]) for d in range(3)]
             a = [jnp.bitwise_xor(sc[d], r[d]) for d in range(3)]
             rows = pl.ds(pl.multiple_of((a[2] * 2 + a[1]) * COLS, 16), COLS)
             lanes = pl.ds(pl.multiple_of((half * 4 + chain * 2 + a[0]) * BLK, BLK), BLK)
-            block = near.at[i] if i < 4 else far.at[i - 4]
-            copy = pltpu.make_async_copy(block, out.at[rows, lanes], sem.at[len(copies)])
+            copy = pltpu.make_async_copy(piece.at[i], out.at[rows, lanes], sem.at[len(copies)])
             copy.start()
             copies.append(copy)
     for copy in copies:
         copy.wait()
 
 
-def run_settle(chain, sc, pieces, *earlier):
+def run_settle(parts, sc, pieces, *earlier):
     return pl.pallas_call(
-        functools.partial(settle, chain),
+        functools.partial(settle, parts),
         in_specs=[in_smem] + [in_vmem] * len(pieces) + [in_hbm] * len(earlier),
         out_specs=in_hbm,
         out_shape=jax.ShapeDtypeStruct((WIDE, KEYS), bf16),
-        scratch_shapes=[pltpu.SemaphoreType.DMA((16,))],
-        input_output_aliases={5: 0} if earlier else {},
+        scratch_shapes=[pltpu.SemaphoreType.DMA((4 * len(pieces),))],
+        input_output_aliases={1 + len(pieces): 0} if earlier else {},
         compiler_params=params(),
         name="settle",
     )(sc, *pieces, *earlier)
@@ -408,10 +408,10 @@
     kept_b, own_a = tie((kept_b, own_a))
     got_a = along(own_a, 2)
     (own_b,) = run_halve(kept_b, got_b)
+    own_b, dq = tie((own_b, dq))
+    dq = lax.all_to_all(dq, "key", 0, 0, tiled=True)
     own_a, own_b = tie((own_a, own_b))
     got_b = along(own_b, 2)
-    got_a, dq = tie((got_a, dq))
-    dq = lax.all_to_all(dq, "key", 0, 0, tiled=True)
     own_a = run_join(own_a, got_a)
     own_b, own_a = tie((own_b, own_a))
     got_a = along(own_a, 1)
@@ -423,11 +423,14 @@
     far_a, near_a = along(own_a, 0), to_sibling(own_a)
     own_b = run_join(own_b, got_b)
     far_b, near_b = along(own_b, 0), to_sibling(own_b)
-    pieces = [
-        (own_a, far_a, near_a, to_sibling(far_a)),
-        (own_b, far_b, near_b, to_sibling(far_b)),
-    ]
-    d_latent = run_settle(1, sc_own, pieces[1], run_settle(0, sc_own, pieces[0])).T
+    near_parts = ((0, True, 0), (0, False, 0), (1, True, 0), (1, False, 0))
+    out = run_settle(near_parts, sc_own, (own_a, near_a, own_b, near_b))
+    other_a = to_sibling(far_a)
+    far_b, out = tie((far_b, out))
+    other_b = to_sibling(far_b)
+    far_parts = ((0, True, 1), (0, False, 1), (1, True, 1), (1, False, 1))
+    out = run_settle(far_parts, sc_own, (far_a, other_a, far_b, other_b), out)
+    d_latent = out.T
 
     dq = jnp.sum(dq.astype(f32), axis=0).astype(bf16)
     d_queries = jnp.transpose(dq.reshape(HEADS, 8, NOPE + ROT), (1, 0, 2))

time: 93.6 us -> 89.7 us (0.958)
  starting transfers between devices: 31 us -> 24.7 us
  waiting for transfers between devices: 10.3 us -> 12.7 us
    ppermute x6, starting transfers between devices: 14.8 us -> 10.2 us  [to_sibling(): return lax.ppermute(value, 'head', [(k, k ^ 1) for k in range(16)])]
    ppermute x12, starting transfers between devices: 12.3 us -> 10.3 us  [along(): return lax.ppermute(value, 'head', pairs)]
    ppermute x12, waiting for transfers between devices: 10.3 us -> 11.8 us  [along(): return lax.ppermute(value, 'head', pairs)]
  transfers between devices with their start and end apart: 19 -> 19, of which waited for: 6 -> 8; matrix products, arithmetic and copies ran while one was open for 1% -> 1% of each run, Pallas kernels for 15% -> 15%
where the time goes in v9:
time: 89.7 us; the launch traced here: 89.4 us
  Pallas kernels  29.7 us (33%)
  starting transfers between devices  24.7 us (28%)
  blocking collectives  20.4 us (23%)
  waiting for transfers between devices  12.7 us (14%)
  between operations  1.03 us (1%)
    all_to_all x1, blocking collectives, shards(): stat = lax.all_to_all(stat, 'key', 0, 0, tiled=True)  20.4 us
    pallas_call x21, Pallas kernels, call(): pl.pallas_call(kernel, in_specs=[in_smem] * scalars + [in_vmem] * (len(ar...  16.3 us
    ppermute x12, waiting for transfers between devices, along(): return lax.ppermute(value, 'head', pairs)  11.8 us
    ppermute x12, starting transfers between devices, along(): return lax.ppermute(value, 'head', pairs)  10.3 us
    ppermute x6, starting transfers between devices, to_sibling(): return lax.ppermute(value, 'head', [(k, k ^ 1) for k in range(16)])  10.2 us
    pallas_call x1, Pallas kernels, run_pass_one(): pl.pallas_call(pass_one, in_specs=[in_smem] + [in_hbm] * 6, out_specs=[in...  10 us
    all_to_all x1, starting transfers between devices, shards(): dq = lax.all_to_all(dq, 'key', 0, 0, tiled=True)  4.22 us
    pallas_call x2, Pallas kernels, run_settle(): pl.pallas_call(functools.partial(settle, parts), in_specs=[in_smem] + [in...  3.38 us
  transfers between devices with their start and end apart: 19, of which 8 were waited for; matrix products, arithmetic and copies ran while one was open for 1% of the time, Pallas kernels for 15%

profile of v9, /device:TPU:1, one launch (start us, length us, event | category | flops | bytes accessed | tf_op | source)
XLA Modules:
  0.0 89.4 jit_solution(18415772085201070791)
XLA Ops:
  0.6 0.1 stack.35.sc
  0.7 0.1 stack.33.sc
  0.8 10.0 %pass_one.1 = (f32[8,1024,256]{2,1,0:T(8,128)S(1)}, f32[8,1024,256]{2,1,0:T(8,128)S(1)}, bf16[576,1024]{1,0:T(8,128)(2,1)S(1)}, bf16[512,1024]{1,0:T(8,128)(2,1)S(1)}, f32[16,24,128]{2,1,0:T(8,128)S(1)}) custom-call(s32[1]{0:T(128)} %bitcast.base, s32[1,128]{1,0:T(1,128)} %bitcast.24, bf16[8,192,128]{2,1,0:T(8,128)(2,1)} %bitcast.21, ...), custom_call_target="tpu_custom_call" | custom-call | tf_op jit(solution)/shard_map/pass_one/pallas_call | solution.py:160
  10.9 20.4 %all_to_all.10.stat = f32[16,24,128]{2,1,0:T(8,128)S(1)} all-to-all(f32[16,24,128]{2,1,0:T(8,128)S(1)} %get-tuple-element.67), channel_id=1, replica_groups=mesh['head'=16,'key'=16] {'key'}, dimensions={0} | all-to-all | bytes 393216 | tf_op jit(solution)/shard_map/all_to_all | solution.py:373
  31.3 2.1 %second_first.1 = (bf16[8,144,256]{2,1,0:T(8,128)(2,1)S(1)}, bf16[2,1024,256]{2,1,0:T(8,128)(2,1)S(1)}, f32[1024,128]{1,0:T(8,128)S(1)}, f32[1024,128]{1,0:T(8,128)S(1)}) custom-call(s32[5]{0:T(128)S(1)} %stack.35.sc, f32[16,24,128]{2,1,0:T(8,128)S(1)} %all_to_all.10.stat, bf16[576,1024]{1,0:T(8,128)(2,1)S(1)} %get-tuple-element.68.qcat_t, ...), custom_call_target="tpu_custom_call" | custom-call | tf_op jit(solution)/shard_map/second_first/pallas_call | solution.py:55
  33.4 2.7 %collective-permute-start = (bf16[8,144,256]{2,1,0:T(8,128)(2,1)S(1)}, bf16[8,144,256]{2,1,0:T(8,128)(2,1)S(1)}, u32[]{:S(2)}, u32[]{:S(2)}) collective-permute-start(bf16[8,144,256]{2,1,0:T(8,128)(2,1)S(1)} %get-tuple-element.76), channel_id=1, source_target_pairs={{0,16},{16,0},{32,48},{48,32},{64,80},{80,64},{96,112},{112,96},{1... | collective-permute-start | bytes 1769480 | tf_op jit(solution)/shard_map/ppermute | solution.py:351
  36.1 1.9 %second.4 = (bf16[8,144,256]{2,1,0:T(8,128)(2,1)S(1)}, bf16[2,1024,256]{2,1,0:T(8,128)(2,1)S(1)}) custom-call(s32[5]{0:T(128)S(1)} %stack.33.sc, f32[1024,128]{1,0:T(8,128)S(1)} %get-tuple-element.72.coef, f32[1024,128]{1,0:T(8,128)S(1)} %get-tuple-element.73.delta, bf16[576,1024]{1,0:T(8,128)(2,1)S(1)} %get-tuple-element.68.qcat_t, ...), custom_call_target="tpu_custom_call" | custom-call | tf_op jit(solution)/shard_map/second/pallas_call | solution.py:55
  38.0 0.0 collective-permute-done.got
  38.0 0.1 halve.8
  38.2 1.9 %second.5 = (bf16[8,144,256]{2,1,0:T(8,128)(2,1)S(1)}, bf16[2,1024,256]{2,1,0:T(8,128)(2,1)S(1)}) custom-call(s32[5]{0:T(128)S(1)} %stack.35.sc, f32[1024,128]{1,0:T(8,128)S(1)} %get-tuple-element.72.coef, f32[1024,128]{1,0:T(8,128)S(1)} %get-tuple-element.73.delta, bf16[576,1024]{1,0:T(8,128)(2,1)S(1)} %get-tuple-element.68.qcat_t, ...), custom_call_target="tpu_custom_call" | custom-call | tf_op jit(solution)/shard_map/second/pallas_call | solution.py:55
  40.1 0.2 collective-permute-start.1
  40.3 2.8 %collective-permute-start.2 = (bf16[4,144,256]{2,1,0:T(8,128)(2,1)S(1)}, bf16[4,144,256]{2,1,0:T(8,128)(2,1)S(1)}, u32[]{:S(2)}, u32[]{:S(2)}) collective-permute-start(bf16[4,144,256]{2,1,0:T(8,128)(2,1)S(1)} %get-tuple-element.82), channel_id=1, source_target_pairs={{0,64},{16,208},{32,96},{48,240},{64,0},{80,144},{96,32},{112,176}... | collective-permute-start | bytes 884744 | tf_op jit(solution)/shard_map/ppermute | solution.py:347
  43.0 0.0 copy-start
  43.0 1.9 %second.3 = (bf16[8,144,256]{2,1,0:T(8,128)(2,1)S(1)}, bf16[2,1024,256]{2,1,0:T(8,128)(2,1)S(1)}) custom-call(s32[5]{0:T(128)S(1)} %stack.33.sc, f32[1024,128]{1,0:T(8,128)S(1)} %get-tuple-element.72.coef, f32[1024,128]{1,0:T(8,128)S(1)} %get-tuple-element.73.delta, bf16[576,1024]{1,0:T(8,128)(2,1)S(1)} %get-tuple-element.68.qcat_t, ...), custom_call_target="tpu_custom_call" | custom-call | tf_op jit(solution)/shard_map/second/pallas_call | solution.py:55
  44.9 0.0 collective-permute-done.1.got
  44.9 0.1 halve.9
  45.1 0.1 collective-permute-start.3
  45.2 0.0 copy-done
  45.2 1.5 %query_piece.4.refs_0_ = f32[1024,576]{1,0:T(8,128)S(1)} custom-call(s32[5]{0:T(128)S(1)} %stack.35.sc, bf16[2,1024,256]{2,1,0:T(8,128)(2,1)S(1)} %get-tuple-element.84.ds, bf16[576,2048]{1,0:T(8,128)(2,1)S(1)} %bitcast.16), custom_call_target="tpu_custom_call" | custom-call | tf_op jit(solution)/shard_map/query_piece/pallas_call | solution.py:55
  46.7 1.6 %query_piece.5.refs_0_ = f32[1024,576]{1,0:T(8,128)S(1)} custom-call(s32[5]{0:T(128)S(1)} %stack.33.sc, bf16[2,1024,256]{2,1,0:T(8,128)(2,1)S(1)} %get-tuple-element.83.ds, bf16[576,2048]{1,0:T(8,128)(2,1)S(1)} %bitcast.17, f32[1024,576]{1,0:T(8,128)S(1)} %query_piece.4.refs_0_), custom_call_target="tpu_custom_call" | custom-call | tf_op jit(solution)/shard_map/query_piece/pallas_call | solution.py:55
  48.3 0.0 collective-permute-done.2.got
  48.3 0.1 halve.10
  48.4 0.4 collective-permute-start.4
  48.8 1.6 %query_piece.6.refs_0_ = f32[1024,576]{1,0:T(8,128)S(1)} custom-call(s32[5]{0:T(128)S(1)} %stack.35.sc, bf16[2,1024,256]{2,1,0:T(8,128)(2,1)S(1)} %get-tuple-element.91.ds, bf16[576,2048]{1,0:T(8,128)(2,1)S(1)} %bitcast.18, f32[1024,576]{1,0:T(8,128)S(1)} %query_piece.5.refs_0_), custom_call_target="tpu_custom_call" | custom-call | tf_op jit(solution)/shard_map/query_piece/pallas_call | solution.py:55
  50.3 0.0 copy-start.1
  50.4 1.6 %query_piece.7.acc = f32[1024,576]{1,0:T(8,128)S(1)} custom-call(s32[5]{0:T(128)S(1)} %stack.33.sc, bf16[2,1024,256]{2,1,0:T(8,128)(2,1)S(1)} %get-tuple-element.90.ds, bf16[576,2048]{1,0:T(8,128)(2,1)S(1)} %bitcast.19, f32[1024,576]{1,0:T(8,128)S(1)} %query_piece.6.refs_0_), custom_call_target="tpu_custom_call" | custom-call | tf_op jit(solution)/shard_map/query_piece/pallas_call | solution.py:55
  51.9 0.0 collective-permute-done.3.got
  52.0 0.1 halve.11
  52.0 1.2 %collective-permute-start.5 = (bf16[2,144,256]{2,1,0:T(8,128)(2,1)S(1)}, bf16[2,144,256]{2,1,0:T(8,128)(2,1)S(1)}, u32[]{:S(2)}, u32[]{:S(2)}) collective-permute-start(bf16[2,144,256]{2,1,0:T(8,128)(2,1)S(1)} %get-tuple-element.104), channel_id=1, source_target_pairs={{0,192},{16,48},{32,224},{48,16},{64,128},{80,112},{96,160},{112,8... | collective-permute-start | bytes 442376 | tf_op jit(solution)/shard_map/ppermute | solution.py:347
  53.3 0.0 copy-done.1
  53.3 1.6 %query_last.1 = bf16[16,64,192]{2,1,0:T(8,128)(2,1)} custom-call(f32[1024,576]{1,0:T(8,128)S(1)} %query_piece.7.acc, bf16[8,128,512]{2,1,0:T(8,128)(2,1)S(1)} %copy-done.1), custom_call_target="tpu_custom_call" | custom-call | tf_op jit(solution)/shard_map/query_last/pallas_call | solution.py:55
  54.9 0.0 collective-permute-done.4.got
  55.0 0.1 collective-permute-start.6
  55.1 1.1 %collective-permute-done.5.got = bf16[2,144,256]{2,1,0:T(8,128)(2,1)S(1)} collective-permute-done((bf16[2,144,256]{2,1,0:T(8,128)(2,1)S(1)}, bf16[2,144,256]{2,1,0:T(8,128)(2,1)S(1)}, u32[]{:S(2)}, u32[]{:S(2)}) %collective-permute-start.5) | collective-permute-done | bytes 147488 | tf_op jit(solution)/shard_map/ppermute | solution.py:347
  56.2 0.7 collective-permute-start.7
  56.9 1.4 %collective-permute-done.6.got = bf16[1,144,256]{2,1,0:T(8,128)(2,1)S(1)} collective-permute-done((bf16[1,144,256]{2,1,0:T(8,128)(2,1)S(1)}, bf16[1,144,256]{2,1,0:T(8,128)(2,1)S(1)}, u32[]{:S(2)}, u32[]{:S(2)}) %collective-permute-start.6) | collective-permute-done | bytes 73760 | tf_op jit(solution)/shard_map/ppermute | solution.py:347
  58.3 0.4 collective-permute-start.8
  58.7 1.3 %collective-permute-done.7.got = bf16[1,144,256]{2,1,0:T(8,128)(2,1)S(1)} collective-permute-done((bf16[1,144,256]{2,1,0:T(8,128)(2,1)S(1)}, bf16[1,144,256]{2,1,0:T(8,128)(2,1)S(1)}, u32[]{:S(2)}, u32[]{:S(2)}) %collective-permute-start.7) | collective-permute-done | bytes 73760 | tf_op jit(solution)/shard_map/ppermute | solution.py:347
  60.0 0.5 collective-permute-start.9
  60.5 1.1 %collective-permute-done.8.got = bf16[1,144,256]{2,1,0:T(8,128)(2,1)S(1)} collective-permute-done((bf16[1,144,256]{2,1,0:T(8,128)(2,1)S(1)}, bf16[1,144,256]{2,1,0:T(8,128)(2,1)S(1)}, u32[]{:S(2)}, u32[]{:S(2)}) %collective-permute-start.8) | collective-permute-done | bytes 73760 | tf_op jit(solution)/shard_map/ppermute | solution.py:347
  61.6 0.4 collective-permute-start.10
  62.0 1.3 %collective-permute-done.9.got = bf16[1,144,256]{2,1,0:T(8,128)(2,1)S(1)} collective-permute-done((bf16[1,144,256]{2,1,0:T(8,128)(2,1)S(1)}, bf16[1,144,256]{2,1,0:T(8,128)(2,1)S(1)}, u32[]{:S(2)}, u32[]{:S(2)}) %collective-permute-start.9) | collective-permute-done | bytes 73760 | tf_op jit(solution)/shard_map/ppermute | solution.py:347
  63.3 0.9 %collective-permute-start.13 = (bf16[2,144,256]{2,1,0:T(8,128)(2,1)S(1)}, bf16[2,144,256]{2,1,0:T(8,128)(2,1)S(1)}, u32[]{:S(2)}, u32[]{:S(2)}) collective-permute-start(bf16[2,144,256]{2,1,0:T(8,128)(2,1)S(1)} %join.5.own), channel_id=1, source_target_pairs={{0,192},{16,48},{32,224},{48,16},{64,128},{80,112},{96,160},{112,8... | collective-permute-start | bytes 442376 | tf_op jit(solution)/shard_map/ppermute | solution.py:347
  64.2 4.2 %all-to-all-start.1 = ((bf16[16,64,192]{2,1,0:T(8,128)(2,1)}), bf16[16,64,192]{2,1,0:T(8,128)(2,1)S(1)}, u32[]{:S(2)}, u32[]{:S(2)}) async-start(bf16[16,64,192]{2,1,0:T(8,128)(2,1)} %query_last.1), calls=%async_computation.1 | async-start | bytes 1048576 | tf_op jit(solution)/shard_map/all_to_all | solution.py:412
  68.5 0.0 collective-permute-done.10.got
  68.5 7.2 %collective-permute-start.15 = (bf16[4,144,256]{2,1,0:T(8,128)(2,1)S(1)}, bf16[4,144,256]{2,1,0:T(8,128)(2,1)S(1)}, u32[]{:S(2)}, u32[]{:S(2)}) collective-permute-start(bf16[4,144,256]{2,1,0:T(8,128)(2,1)S(1)} %join.6.refs_0_), channel_id=1, source_target_pairs={{0,16},{16,0},{32,48},{48,32},{64,80},{80,64},{96,112},{112,96},{1... | collective-permute-start | bytes 884744 | tf_op jit(solution)/shard_map/ppermute | solution.py:351
  75.7 2.5 %collective-permute-start.11 = (bf16[4,144,256]{2,1,0:T(8,128)(2,1)S(1)}, bf16[4,144,256]{2,1,0:T(8,128)(2,1)S(1)}, u32[]{:S(2)}, u32[]{:S(2)}) collective-permute-start(bf16[4,144,256]{2,1,0:T(8,128)(2,1)S(1)} %join.6.refs_0_), channel_id=1, source_target_pairs={{0,64},{16,208},{32,96},{48,240},{64,0},{80,144},{96,32},{112,176}... | collective-permute-start | bytes 884744 | tf_op jit(solution)/shard_map/ppermute | solution.py:347
  78.2 0.0 collective-permute-done.13.got
  78.2 0.1 collective-permute-start.16
  78.3 0.3 collective-permute-start.14
  78.6 4.2 %collective-permute-done.11.refs_0_ = bf16[4,144,256]{2,1,0:T(8,128)(2,1)S(1)} collective-permute-done((bf16[4,144,256]{2,1,0:T(8,128)(2,1)S(1)}, bf16[4,144,256]{2,1,0:T(8,128)(2,1)S(1)}, u32[]{:S(2)}, u32[]{:S(2)}) %collective-permute-start.11) | collective-permute-done | bytes 294944 | tf_op jit(solution)/shard_map/ppermute | solution.py:347
  82.8 0.0 collective-permute-start.12
  82.8 0.0 collective-permute-done.15.refs_1_
  82.8 0.0 collective-permute-done.16.refs_3_
  82.8 1.7 %settle.2.refs_4_ = bf16[576,2048]{1,0:T(8,128)(2,1)} custom-call(s32[5]{0:T(128)S(1)} %stack.33.sc, bf16[4,144,256]{2,1,0:T(8,128)(2,1)S(1)} %join.6.refs_0_, bf16[4,144,256]{2,1,0:T(8,128)(2,1)S(1)} %collective-permute-done.15.refs_1_, bf16[4,144,256]{2,1,0:T(8,128)(2,1)S(1)} %join.7.refs_2_, bf16[4,144,256]{2,1,0:T(8,128)(2,1)S(1)} %collective-permute-done.16.refs_3_), custom_call_target="tpu_custom_call" | custom-call | tf_op jit(solution)/shard_map/settle/pallas_call | solution.py:324
  84.5 1.4 %collective-permute-done.14.refs_2_ = bf16[4,144,256]{2,1,0:T(8,128)(2,1)S(1)} collective-permute-done((bf16[4,144,256]{2,1,0:T(8,128)(2,1)S(1)}, bf16[4,144,256]{2,1,0:T(8,128)(2,1)S(1)}, u32[]{:S(2)}, u32[]{:S(2)}) %collective-permute-start.14) | collective-permute-done | bytes 294944 | tf_op jit(solution)/shard_map/ppermute | solution.py:347
  85.9 0.0 collective-permute-start.17
  85.9 0.0 all-to-all-done.1
  85.9 0.1 reduce_sum.12
  86.0 0.6 copy.9
  86.6 0.0 collective-permute-done.12.refs_1_
  86.7 0.8 collective-permute-done.17.refs_3_
  87.5 1.7 %settle.3 = bf16[576,2048]{1,0:T(8,128)(2,1)} custom-call(s32[5]{0:T(128)S(1)} %stack.33.sc, bf16[4,144,256]{2,1,0:T(8,128)(2,1)S(1)} %collective-permute-done.11.refs_0_, bf16[4,144,256]{2,1,0:T(8,128)(2,1)S(1)} %collective-permute-done.12.refs_1_, bf16[4,144,256]{2,1,0:T(8,128)(2,1)S(1)} %collective-permute-done.14.refs_2_, ...), custom_call_target="tpu_custom_call", output_to_operand_aliasing={{}: (5, {})} | custom-call | tf_op jit(solution)/shard_map/settle/pallas_call | solution.py:324
  (8 shorter events, 0.2 us)
Async XLA Ops:
  33.4 4.6 %collective-permute-start = (bf16[8,144,256]{2,1,0:T(8,128)(2,1)S(1)}, bf16[8,144,256]{2,1,0:T(8,128)(2,1)S(1)}, u32[]{:S(2)}, u32[]{:S(2)}) collective-permute-start(bf16[8,144,256]{2,1,0:T(8,128)(2,1)S(1)} %get-tuple-element.76), channel_id=1, source_target_pairs={{0,16},{16,0},{32,48},{48,32},{64,80},{80,64},{96,112},{112,96},{1... | collective-permute-start | bytes 1769480 | tf_op jit(solution)/shard_map/ppermute | solution.py:351
  40.1 4.8 %collective-permute-start.1 = (bf16[8,144,256]{2,1,0:T(8,128)(2,1)S(1)}, bf16[8,144,256]{2,1,0:T(8,128)(2,1)S(1)}, u32[]{:S(2)}, u32[]{:S(2)}) collective-permute-start(bf16[8,144,256]{2,1,0:T(8,128)(2,1)S(1)} %get-tuple-element.79), channel_id=1, source_target_pairs={{0,16},{16,0},{32,48},{48,32},{64,80},{80,64},{96,112},{112,96},{1... | collective-permute-start | bytes 1769480 | tf_op jit(solution)/shard_map/ppermute | solution.py:351
  40.3 8.1 %collective-permute-start.2 = (bf16[4,144,256]{2,1,0:T(8,128)(2,1)S(1)}, bf16[4,144,256]{2,1,0:T(8,128)(2,1)S(1)}, u32[]{:S(2)}, u32[]{:S(2)}) collective-permute-start(bf16[4,144,256]{2,1,0:T(8,128)(2,1)S(1)} %get-tuple-element.82), channel_id=1, source_target_pairs={{0,64},{16,208},{32,96},{48,240},{64,0},{80,144},{96,32},{112,176}... | collective-permute-start | bytes 884744 | tf_op jit(solution)/shard_map/ppermute | solution.py:347
  43.0 2.2 %copy-start = (bf16[2048,576]{0,1:T(8,128)(2,1)S(1)}, bf16[2048,576]{0,1:T(8,128)(2,1)}, u32[]{:S(2)}) copy-start(bf16[2048,576]{0,1:T(8,128)(2,1)} %param.9) | copy-start | bytes 7077892
  45.1 6.9 %collective-permute-start.3 = (bf16[4,144,256]{2,1,0:T(8,128)(2,1)S(1)}, bf16[4,144,256]{2,1,0:T(8,128)(2,1)S(1)}, u32[]{:S(2)}, u32[]{:S(2)}) collective-permute-start(bf16[4,144,256]{2,1,0:T(8,128)(2,1)S(1)} %get-tuple-element.89), channel_id=1, source_target_pairs={{0,64},{16,208},{32,96},{48,240},{64,0},{80,144},{96,32},{112,176}... | collective-permute-start | bytes 884744 | tf_op jit(solution)/shard_map/ppermute | solution.py:347
  48.4 6.5 %collective-permute-start.4 = (bf16[2,144,256]{2,1,0:T(8,128)(2,1)S(1)}, bf16[2,144,256]{2,1,0:T(8,128)(2,1)S(1)}, u32[]{:S(2)}, u32[]{:S(2)}) collective-permute-start(bf16[2,144,256]{2,1,0:T(8,128)(2,1)S(1)} %get-tuple-element.99), channel_id=1, source_target_pairs={{0,192},{16,48},{32,224},{48,16},{64,128},{80,112},{96,160},{112,8... | collective-permute-start | bytes 442376 | tf_op jit(solution)/shard_map/ppermute | solution.py:347
  50.3 2.9 %copy-start.1 = (bf16[8,128,512]{2,1,0:T(8,128)(2,1)S(1)}, bf16[8,128,512]{2,1,0:T(8,128)(2,1)}, u32[]{:S(2)}) copy-start(bf16[8,128,512]{2,1,0:T(8,128)(2,1)} %wuk.3) | copy-start | bytes 3145732
  52.0 4.1 %collective-permute-start.5 = (bf16[2,144,256]{2,1,0:T(8,128)(2,1)S(1)}, bf16[2,144,256]{2,1,0:T(8,128)(2,1)S(1)}, u32[]{:S(2)}, u32[]{:S(2)}) collective-permute-start(bf16[2,144,256]{2,1,0:T(8,128)(2,1)S(1)} %get-tuple-element.104), channel_id=1, source_target_pairs={{0,192},{16,48},{32,224},{48,16},{64,128},{80,112},{96,160},{112,8... | collective-permute-start | bytes 442376 | tf_op jit(solution)/shard_map/ppermute | solution.py:347
  55.0 3.3 %collective-permute-start.6 = (bf16[1,144,256]{2,1,0:T(8,128)(2,1)S(1)}, bf16[1,144,256]{2,1,0:T(8,128)(2,1)S(1)}, u32[]{:S(2)}, u32[]{:S(2)}) collective-permute-start(bf16[1,144,256]{2,1,0:T(8,128)(2,1)S(1)} %get-tuple-element.109), channel_id=1, source_target_pairs={{0,32},{16,80},{32,0},{48,112},{64,96},{80,16},{96,64},{112,48},{1... | collective-permute-start | bytes 221192 | tf_op jit(solution)/shard_map/ppermute | solution.py:347
  56.2 3.8 %collective-permute-start.7 = (bf16[1,144,256]{2,1,0:T(8,128)(2,1)S(1)}, bf16[1,144,256]{2,1,0:T(8,128)(2,1)S(1)}, u32[]{:S(2)}, u32[]{:S(2)}) collective-permute-start(bf16[1,144,256]{2,1,0:T(8,128)(2,1)S(1)} %get-tuple-element.111), channel_id=1, source_target_pairs={{0,32},{16,80},{32,0},{48,112},{64,96},{80,16},{96,64},{112,48},{1... | collective-permute-start | bytes 221192 | tf_op jit(solution)/shard_map/ppermute | solution.py:347
  58.3 3.3 %collective-permute-start.8 = (bf16[1,144,256]{2,1,0:T(8,128)(2,1)S(1)}, bf16[1,144,256]{2,1,0:T(8,128)(2,1)S(1)}, u32[]{:S(2)}, u32[]{:S(2)}) collective-permute-start(bf16[1,144,256]{2,1,0:T(8,128)(2,1)S(1)} %halve.14.own), channel_id=1, source_target_pairs={{0,32},{16,80},{32,0},{48,112},{64,96},{80,16},{96,64},{112,48},{1... | collective-permute-start | bytes 221192 | tf_op jit(solution)/shard_map/ppermute | solution.py:347
  60.0 3.3 %collective-permute-start.9 = (bf16[1,144,256]{2,1,0:T(8,128)(2,1)S(1)}, bf16[1,144,256]{2,1,0:T(8,128)(2,1)S(1)}, u32[]{:S(2)}, u32[]{:S(2)}) collective-permute-start(bf16[1,144,256]{2,1,0:T(8,128)(2,1)S(1)} %halve.15.own), channel_id=1, source_target_pairs={{0,32},{16,80},{32,0},{48,112},{64,96},{80,16},{96,64},{112,48},{1... | collective-permute-start | bytes 221192 | tf_op jit(solution)/shard_map/ppermute | solution.py:347
  61.6 6.9 %collective-permute-start.10 = (bf16[2,144,256]{2,1,0:T(8,128)(2,1)S(1)}, bf16[2,144,256]{2,1,0:T(8,128)(2,1)S(1)}, u32[]{:S(2)}, u32[]{:S(2)}) collective-permute-start(bf16[2,144,256]{2,1,0:T(8,128)(2,1)S(1)} %join.4.own), channel_id=1, source_target_pairs={{0,192},{16,48},{32,224},{48,16},{64,128},{80,112},{96,160},{112,8... | collective-permute-start | bytes 442376 | tf_op jit(solution)/shard_map/ppermute | solution.py:347
  63.3 14.9 %collective-permute-start.13 = (bf16[2,144,256]{2,1,0:T(8,128)(2,1)S(1)}, bf16[2,144,256]{2,1,0:T(8,128)(2,1)S(1)}, u32[]{:S(2)}, u32[]{:S(2)}) collective-permute-start(bf16[2,144,256]{2,1,0:T(8,128)(2,1)S(1)} %join.5.own), channel_id=1, source_target_pairs={{0,192},{16,48},{32,224},{48,16},{64,128},{80,112},{96,160},{112,8... | collective-permute-start | bytes 442376 | tf_op jit(solution)/shard_map/ppermute | solution.py:347
  64.2 21.7 %all-to-all-start.1 = ((bf16[16,64,192]{2,1,0:T(8,128)(2,1)}), bf16[16,64,192]{2,1,0:T(8,128)(2,1)S(1)}, u32[]{:S(2)}, u32[]{:S(2)}) async-start(bf16[16,64,192]{2,1,0:T(8,128)(2,1)} %query_last.1), calls=%async_computation.1 | async-start | bytes 1048576 | tf_op jit(solution)/shard_map/all_to_all | solution.py:412
  68.5 14.3 %collective-permute-start.15 = (bf16[4,144,256]{2,1,0:T(8,128)(2,1)S(1)}, bf16[4,144,256]{2,1,0:T(8,128)(2,1)S(1)}, u32[]{:S(2)}, u32[]{:S(2)}) collective-permute-start(bf16[4,144,256]{2,1,0:T(8,128)(2,1)S(1)} %join.6.refs_0_), channel_id=1, source_target_pairs={{0,16},{16,0},{32,48},{48,32},{64,80},{80,64},{96,112},{112,96},{1... | collective-permute-start | bytes 884744 | tf_op jit(solution)/shard_map/ppermute | solution.py:351
  75.7 7.1 %collective-permute-start.11 = (bf16[4,144,256]{2,1,0:T(8,128)(2,1)S(1)}, bf16[4,144,256]{2,1,0:T(8,128)(2,1)S(1)}, u32[]{:S(2)}, u32[]{:S(2)}) collective-permute-start(bf16[4,144,256]{2,1,0:T(8,128)(2,1)S(1)} %join.6.refs_0_), channel_id=1, source_target_pairs={{0,64},{16,208},{32,96},{48,240},{64,0},{80,144},{96,32},{112,176}... | collective-permute-start | bytes 884744 | tf_op jit(solution)/shard_map/ppermute | solution.py:347
  78.2 4.6 %collective-permute-start.16 = (bf16[4,144,256]{2,1,0:T(8,128)(2,1)S(1)}, bf16[4,144,256]{2,1,0:T(8,128)(2,1)S(1)}, u32[]{:S(2)}, u32[]{:S(2)}) collective-permute-start(bf16[4,144,256]{2,1,0:T(8,128)(2,1)S(1)} %join.7.refs_2_), channel_id=1, source_target_pairs={{0,16},{16,0},{32,48},{48,32},{64,80},{80,64},{96,112},{112,96},{1... | collective-permute-start | bytes 884744 | tf_op jit(solution)/shard_map/ppermute | solution.py:351
  78.3 7.6 %collective-permute-start.14 = (bf16[4,144,256]{2,1,0:T(8,128)(2,1)S(1)}, bf16[4,144,256]{2,1,0:T(8,128)(2,1)S(1)}, u32[]{:S(2)}, u32[]{:S(2)}) collective-permute-start(bf16[4,144,256]{2,1,0:T(8,128)(2,1)S(1)} %join.7.refs_2_), channel_id=1, source_target_pairs={{0,64},{16,208},{32,96},{48,240},{64,0},{80,144},{96,32},{112,176}... | collective-permute-start | bytes 884744 | tf_op jit(solution)/shard_map/ppermute | solution.py:347
  82.8 3.9 %collective-permute-start.12 = (bf16[4,144,256]{2,1,0:T(8,128)(2,1)S(1)}, bf16[4,144,256]{2,1,0:T(8,128)(2,1)S(1)}, u32[]{:S(2)}, u32[]{:S(2)}) collective-permute-start(bf16[4,144,256]{2,1,0:T(8,128)(2,1)S(1)} %collective-permute-done.11.refs_0_), channel_id=1, source_target_pairs={{0,16},{16,0},{32,48},{48,32},{64,80},{80,64},{96,112},{112,96},{1... | collective-permute-start | bytes 884744 | tf_op jit(solution)/shard_map/ppermute | solution.py:351
  85.9 1.6 %collective-permute-start.17 = (bf16[4,144,256]{2,1,0:T(8,128)(2,1)S(1)}, bf16[4,144,256]{2,1,0:T(8,128)(2,1)S(1)}, u32[]{:S(2)}, u32[]{:S(2)}) collective-permute-start(bf16[4,144,256]{2,1,0:T(8,128)(2,1)S(1)} %collective-permute-done.14.refs_2_), channel_id=1, source_target_pairs={{0,16},{16,0},{32,48},{48,32},{64,80},{80,64},{96,112},{112,96},{1... | collective-permute-start | bytes 884744 | tf_op jit(solution)/shard_map/ppermute | solution.py:351

commit v10 on v9

--- a/solution.py
+++ b/solution.py
@@ -302,10 +302,9 @@
     return call(join, "join", [((2 * own.shape[0], COLS, BLK), bf16)], (own, got))[0]
 
 
-def settle(parts, sc, *refs):
-    out, sem = refs[-2:]
+def settle_start(parts, sc, pieces, out, sem):
     copies = []
-    for (chain, mine, far), piece in zip(parts, refs):
+    for (chain, mine, far), piece in zip(parts, pieces):
         half = sc[3] if mine else 1 - sc[3]
         for i in range(4):
             b = (far, i >> 1, i & 1)
@@ -316,21 +315,59 @@
             copy = pltpu.make_async_copy(piece.at[i], out.at[rows, lanes], sem.at[len(copies)])
             copy.start()
             copies.append(copy)
+    return copies
+
+
+def settle_near(parts, sc, *refs):
+    for copy in settle_start(parts, sc, refs[:4], *refs[4:]):
+        copy.wait()
+
+
+def settle_far(parts, sc, a, b, c, d, dq, earlier, out, dq_out, sem, low, high):
+    copies = settle_start(parts, sc, (a, b, c, d), out, sem)
+    total = dq[0].astype(f32)
+    for g in range(1, PEERS):
+        total = total + dq[g].astype(f32)
+    low[...] = total[:, :NOPE]
+    high[:, :ROT] = total[:, NOPE:]
+    for r in range(8):
+        rows = pl.ds(r, HEADS, stride=8)
+        dq_out[r, :, :NOPE] = low[rows, :].astype(bf16)
+        dq_out[r, :, NOPE:] = high[rows, :][:, :ROT].astype(bf16)
     for copy in copies:
         copy.wait()
 
 
-def run_settle(parts, sc, pieces, *earlier):
+def run_settle_near(parts, sc, pieces):
     return pl.pallas_call(
-        functools.partial(settle, parts),
-        in_specs=[in_smem] + [in_vmem] * len(pieces) + [in_hbm] * len(earlier),
+        functools.partial(settle_near, parts),
+        in_specs=[in_smem] + [in_vmem] * 4,
         out_specs=in_hbm,
         out_shape=jax.ShapeDtypeStruct((WIDE, KEYS), bf16),
-        scratch_shapes=[pltpu.SemaphoreType.DMA((4 * len(pieces),))],
-        input_output_aliases={1 + len(pieces): 0} if earlier else {},
+        scratch_shapes=[pltpu.SemaphoreType.DMA((16,))],
         compiler_params=params(),
-        name="settle",
-    )(sc, *pieces, *earlier)
+        name="settle_near",
+    )(sc, *pieces)
+
+
+def run_settle_far(parts, sc, pieces, dq, earlier):
+    return pl.pallas_call(
+        functools.partial(settle_far, parts),
+        in_specs=[in_smem] + [in_vmem] * 5 + [in_hbm],
+        out_specs=[in_hbm, in_vmem],
+        out_shape=[
+            jax.ShapeDtypeStruct((WIDE, KEYS), bf16),
+            jax.ShapeDtypeStruct((8, HEADS, NOPE + ROT), bf16),
+        ],
+        scratch_shapes=[
+            pltpu.SemaphoreType.DMA((16,)),
+            pltpu.VMEM((HEADS * 8, 128), f32),
+            pltpu.VMEM((HEADS * 8, 128), f32),
+        ],
+        input_output_aliases={6: 0},
+        compiler_params=params(),
+        name="settle_far",
+    )(sc, *pieces, dq, earlier)
 
 
 def cube_neighbour(k, d):
@@ -424,16 +461,15 @@
     own_b = run_join(own_b, got_b)
     far_b, near_b = along(own_b, 0), to_sibling(own_b)
     near_parts = ((0, True, 0), (0, False, 0), (1, True, 0), (1, False, 0))
-    out = run_settle(near_parts, sc_own, (own_a, near_a, own_b, near_b))
+    out = run_settle_near(near_parts, sc_own, (own_a, near_a, own_b, near_b))
     other_a = to_sibling(far_a)
     far_b, out = tie((far_b, out))
     other_b = to_sibling(far_b)
     far_parts = ((0, True, 1), (0, False, 1), (1, True, 1), (1, False, 1))
-    out = run_settle(far_parts, sc_own, (far_a, other_a, far_b, other_b), out)
+    pieces = (far_a, other_a, far_b, other_b)
+    out, d_queries = run_settle_far(far_parts, sc_own, pieces, dq, out)
     d_latent = out.T
 
-    dq = jnp.sum(dq.astype(f32), axis=0).astype(bf16)
-    d_queries = jnp.transpose(dq.reshape(HEADS, 8, NOPE + ROT), (1, 0, 2))
     return (d_queries, d_latent)
 
 

time: 89.7 us -> 90.2 us (level)
  transfers between devices with their start and end apart: 19 -> 19, of which waited for: 8 -> 8; matrix products, arithmetic and copies ran while one was open for 1% -> 0% of each run, Pallas kernels for 15% -> 15%
where the time goes in v10:
time: 90.2 us; the launch traced here: 90 us
  Pallas kernels  30.3 us (34%)
  starting transfers between devices  24.6 us (27%)
  blocking collectives  20.4 us (23%)
  waiting for transfers between devices  13.5 us (15%)
  between operations  1.03 us (1%)
    all_to_all x1, blocking collectives, shards(): stat = lax.all_to_all(stat, 'key', 0, 0, tiled=True)  20.4 us
    pallas_call x21, Pallas kernels, call(): pl.pallas_call(kernel, in_specs=[in_smem] * scalars + [in_vmem] * (len(ar...  16.2 us
    ppermute x12, waiting for transfers between devices, along(): return lax.ppermute(value, 'head', pairs)  11.9 us
    ppermute x12, starting transfers between devices, along(): return lax.ppermute(value, 'head', pairs)  10.2 us
    ppermute x6, starting transfers between devices, to_sibling(): return lax.ppermute(value, 'head', [(k, k ^ 1) for k in range(16)])  10.2 us
    pallas_call x1, Pallas kernels, run_pass_one(): pl.pallas_call(pass_one, in_specs=[in_smem] + [in_hbm] * 6, out_specs=[in...  10 us
    all_to_all x1, starting transfers between devices, shards(): dq = lax.all_to_all(dq, 'key', 0, 0, tiled=True)  4.22 us
    pallas_call x1, Pallas kernels, run_settle_far(): pl.pallas_call(functools.partial(settle_far, parts), in_specs=[in_smem] +...  2.3 us
  transfers between devices with their start and end apart: 19, of which 8 were waited for; matrix products, arithmetic and copies ran while one was open for 0% of the time, Pallas kernels for 15%

profile of v10, /device:TPU:1, one launch (start us, length us, event | category | flops | bytes accessed | tf_op | source)
XLA Modules:
  0.0 90.0 jit_solution(11133329142737744075)
XLA Ops:
  0.6 0.1 stack.35.sc
  0.7 0.1 stack.33.sc
  0.8 10.0 %pass_one.1 = (f32[8,1024,256]{2,1,0:T(8,128)S(1)}, f32[8,1024,256]{2,1,0:T(8,128)S(1)}, bf16[576,1024]{1,0:T(8,128)(2,1)S(1)}, bf16[512,1024]{1,0:T(8,128)(2,1)S(1)}, f32[16,24,128]{2,1,0:T(8,128)S(1)}) custom-call(s32[1]{0:T(128)} %bitcast.base, s32[1,128]{1,0:T(1,128)} %bitcast.20, bf16[8,192,128]{2,1,0:T(8,128)(2,1)} %bitcast.18, ...), custom_call_target="tpu_custom_call" | custom-call | tf_op jit(solution)/shard_map/pass_one/pallas_call | solution.py:160
  10.9 20.4 %all_to_all.10.stat = f32[16,24,128]{2,1,0:T(8,128)S(1)} all-to-all(f32[16,24,128]{2,1,0:T(8,128)S(1)} %get-tuple-element.69), channel_id=1, replica_groups=mesh['head'=16,'key'=16] {'key'}, dimensions={0} | all-to-all | bytes 393216 | tf_op jit(solution)/shard_map/all_to_all | solution.py:410
  31.3 2.1 %second_first.1 = (bf16[8,144,256]{2,1,0:T(8,128)(2,1)S(1)}, bf16[2,1024,256]{2,1,0:T(8,128)(2,1)S(1)}, f32[1024,128]{1,0:T(8,128)S(1)}, f32[1024,128]{1,0:T(8,128)S(1)}) custom-call(s32[5]{0:T(128)S(1)} %stack.35.sc, f32[16,24,128]{2,1,0:T(8,128)S(1)} %all_to_all.10.stat, bf16[576,1024]{1,0:T(8,128)(2,1)S(1)} %get-tuple-element.70.qcat_t, ...), custom_call_target="tpu_custom_call" | custom-call | tf_op jit(solution)/shard_map/second_first/pallas_call | solution.py:55
  33.4 2.7 %collective-permute-start = (bf16[8,144,256]{2,1,0:T(8,128)(2,1)S(1)}, bf16[8,144,256]{2,1,0:T(8,128)(2,1)S(1)}, u32[]{:S(2)}, u32[]{:S(2)}) collective-permute-start(bf16[8,144,256]{2,1,0:T(8,128)(2,1)S(1)} %get-tuple-element.78), channel_id=1, source_target_pairs={{0,16},{16,0},{32,48},{48,32},{64,80},{80,64},{96,112},{112,96},{1... | collective-permute-start | bytes 1769480 | tf_op jit(solution)/shard_map/ppermute | solution.py:388
  36.1 1.9 %second.4 = (bf16[8,144,256]{2,1,0:T(8,128)(2,1)S(1)}, bf16[2,1024,256]{2,1,0:T(8,128)(2,1)S(1)}) custom-call(s32[5]{0:T(128)S(1)} %stack.33.sc, f32[1024,128]{1,0:T(8,128)S(1)} %get-tuple-element.74.coef, f32[1024,128]{1,0:T(8,128)S(1)} %get-tuple-element.75.delta, bf16[576,1024]{1,0:T(8,128)(2,1)S(1)} %get-tuple-element.70.qcat_t, ...), custom_call_target="tpu_custom_call" | custom-call | tf_op jit(solution)/shard_map/second/pallas_call | solution.py:55
  38.0 0.0 collective-permute-done.got
  38.0 0.1 halve.8
  38.2 1.9 %second.5 = (bf16[8,144,256]{2,1,0:T(8,128)(2,1)S(1)}, bf16[2,1024,256]{2,1,0:T(8,128)(2,1)S(1)}) custom-call(s32[5]{0:T(128)S(1)} %stack.35.sc, f32[1024,128]{1,0:T(8,128)S(1)} %get-tuple-element.74.coef, f32[1024,128]{1,0:T(8,128)S(1)} %get-tuple-element.75.delta, bf16[576,1024]{1,0:T(8,128)(2,1)S(1)} %get-tuple-element.70.qcat_t, ...), custom_call_target="tpu_custom_call" | custom-call | tf_op jit(solution)/shard_map/second/pallas_call | solution.py:55
  40.1 0.2 collective-permute-start.1
  40.3 2.8 %collective-permute-start.2 = (bf16[4,144,256]{2,1,0:T(8,128)(2,1)S(1)}, bf16[4,144,256]{2,1,0:T(8,128)(2,1)S(1)}, u32[]{:S(2)}, u32[]{:S(2)}) collective-permute-start(bf16[4,144,256]{2,1,0:T(8,128)(2,1)S(1)} %get-tuple-element.84), channel_id=1, source_target_pairs={{0,64},{16,208},{32,96},{48,240},{64,0},{80,144},{96,32},{112,176}... | collective-permute-start | bytes 884744 | tf_op jit(solution)/shard_map/ppermute | solution.py:384
  43.0 0.0 copy-start
  43.0 1.9 %second.3 = (bf16[8,144,256]{2,1,0:T(8,128)(2,1)S(1)}, bf16[2,1024,256]{2,1,0:T(8,128)(2,1)S(1)}) custom-call(s32[5]{0:T(128)S(1)} %stack.33.sc, f32[1024,128]{1,0:T(8,128)S(1)} %get-tuple-element.74.coef, f32[1024,128]{1,0:T(8,128)S(1)} %get-tuple-element.75.delta, bf16[576,1024]{1,0:T(8,128)(2,1)S(1)} %get-tuple-element.70.qcat_t, ...), custom_call_target="tpu_custom_call" | custom-call | tf_op jit(solution)/shard_map/second/pallas_call | solution.py:55
  44.9 0.0 collective-permute-done.1.got
  44.9 0.1 halve.9
  45.1 0.1 collective-permute-start.3
  45.2 0.0 copy-done
  45.2 1.5 %query_piece.4.refs_0_ = f32[1024,576]{1,0:T(8,128)S(1)} custom-call(s32[5]{0:T(128)S(1)} %stack.35.sc, bf16[2,1024,256]{2,1,0:T(8,128)(2,1)S(1)} %get-tuple-element.86.ds, bf16[576,2048]{1,0:T(8,128)(2,1)S(1)} %bitcast.13), custom_call_target="tpu_custom_call" | custom-call | tf_op jit(solution)/shard_map/query_piece/pallas_call | solution.py:55
  46.7 1.6 %query_piece.5.refs_0_ = f32[1024,576]{1,0:T(8,128)S(1)} custom-call(s32[5]{0:T(128)S(1)} %stack.33.sc, bf16[2,1024,256]{2,1,0:T(8,128)(2,1)S(1)} %get-tuple-element.85.ds, bf16[576,2048]{1,0:T(8,128)(2,1)S(1)} %bitcast.14, f32[1024,576]{1,0:T(8,128)S(1)} %query_piece.4.refs_0_), custom_call_target="tpu_custom_call" | custom-call | tf_op jit(solution)/shard_map/query_piece/pallas_call | solution.py:55
  48.3 0.0 collective-permute-done.2.got
  48.3 0.1 halve.10
  48.4 0.4 collective-permute-start.4
  48.8 1.6 %query_piece.6.refs_0_ = f32[1024,576]{1,0:T(8,128)S(1)} custom-call(s32[5]{0:T(128)S(1)} %stack.35.sc, bf16[2,1024,256]{2,1,0:T(8,128)(2,1)S(1)} %get-tuple-element.93.ds, bf16[576,2048]{1,0:T(8,128)(2,1)S(1)} %bitcast.15, f32[1024,576]{1,0:T(8,128)S(1)} %query_piece.5.refs_0_), custom_call_target="tpu_custom_call" | custom-call | tf_op jit(solution)/shard_map/query_piece/pallas_call | solution.py:55
  50.3 0.0 copy-start.1
  50.4 1.6 %query_piece.7.acc = f32[1024,576]{1,0:T(8,128)S(1)} custom-call(s32[5]{0:T(128)S(1)} %stack.33.sc, bf16[2,1024,256]{2,1,0:T(8,128)(2,1)S(1)} %get-tuple-element.92.ds, bf16[576,2048]{1,0:T(8,128)(2,1)S(1)} %bitcast.16, f32[1024,576]{1,0:T(8,128)S(1)} %query_piece.6.refs_0_), custom_call_target="tpu_custom_call" | custom-call | tf_op jit(solution)/shard_map/query_piece/pallas_call | solution.py:55
  51.9 0.0 collective-permute-done.3.got
  52.0 0.1 halve.11
  52.0 1.2 %collective-permute-start.5 = (bf16[2,144,256]{2,1,0:T(8,128)(2,1)S(1)}, bf16[2,144,256]{2,1,0:T(8,128)(2,1)S(1)}, u32[]{:S(2)}, u32[]{:S(2)}) collective-permute-start(bf16[2,144,256]{2,1,0:T(8,128)(2,1)S(1)} %get-tuple-element.106), channel_id=1, source_target_pairs={{0,192},{16,48},{32,224},{48,16},{64,128},{80,112},{96,160},{112,8... | collective-permute-start | bytes 442376 | tf_op jit(solution)/shard_map/ppermute | solution.py:384
  53.3 0.0 copy-done.1
  53.3 1.6 %query_last.1 = bf16[16,64,192]{2,1,0:T(8,128)(2,1)} custom-call(f32[1024,576]{1,0:T(8,128)S(1)} %query_piece.7.acc, bf16[8,128,512]{2,1,0:T(8,128)(2,1)S(1)} %copy-done.1), custom_call_target="tpu_custom_call" | custom-call | tf_op jit(solution)/shard_map/query_last/pallas_call | solution.py:55
  54.9 0.0 collective-permute-done.4.got
  54.9 0.1 collective-permute-start.6
  55.0 1.1 %collective-permute-done.5.got = bf16[2,144,256]{2,1,0:T(8,128)(2,1)S(1)} collective-permute-done((bf16[2,144,256]{2,1,0:T(8,128)(2,1)S(1)}, bf16[2,144,256]{2,1,0:T(8,128)(2,1)S(1)}, u32[]{:S(2)}, u32[]{:S(2)}) %collective-permute-start.5) | collective-permute-done | bytes 147488 | tf_op jit(solution)/shard_map/ppermute | solution.py:384
  56.2 0.7 collective-permute-start.7
  56.8 1.4 %collective-permute-done.6.got = bf16[1,144,256]{2,1,0:T(8,128)(2,1)S(1)} collective-permute-done((bf16[1,144,256]{2,1,0:T(8,128)(2,1)S(1)}, bf16[1,144,256]{2,1,0:T(8,128)(2,1)S(1)}, u32[]{:S(2)}, u32[]{:S(2)}) %collective-permute-start.6) | collective-permute-done | bytes 73760 | tf_op jit(solution)/shard_map/ppermute | solution.py:384
  58.2 0.4 collective-permute-start.8
  58.6 1.3 %collective-permute-done.7.got = bf16[1,144,256]{2,1,0:T(8,128)(2,1)S(1)} collective-permute-done((bf16[1,144,256]{2,1,0:T(8,128)(2,1)S(1)}, bf16[1,144,256]{2,1,0:T(8,128)(2,1)S(1)}, u32[]{:S(2)}, u32[]{:S(2)}) %collective-permute-start.7) | collective-permute-done | bytes 73760 | tf_op jit(solution)/shard_map/ppermute | solution.py:384
  60.0 0.5 collective-permute-start.9
  60.4 1.1 %collective-permute-done.8.got = bf16[1,144,256]{2,1,0:T(8,128)(2,1)S(1)} collective-permute-done((bf16[1,144,256]{2,1,0:T(8,128)(2,1)S(1)}, bf16[1,144,256]{2,1,0:T(8,128)(2,1)S(1)}, u32[]{:S(2)}, u32[]{:S(2)}) %collective-permute-start.8) | collective-permute-done | bytes 73760 | tf_op jit(solution)/shard_map/ppermute | solution.py:384
  61.5 0.4 collective-permute-start.10
  62.0 1.3 %collective-permute-done.9.got = bf16[1,144,256]{2,1,0:T(8,128)(2,1)S(1)} collective-permute-done((bf16[1,144,256]{2,1,0:T(8,128)(2,1)S(1)}, bf16[1,144,256]{2,1,0:T(8,128)(2,1)S(1)}, u32[]{:S(2)}, u32[]{:S(2)}) %collective-permute-start.9) | collective-permute-done | bytes 73760 | tf_op jit(solution)/shard_map/ppermute | solution.py:384
  63.3 0.9 %collective-permute-start.13 = (bf16[2,144,256]{2,1,0:T(8,128)(2,1)S(1)}, bf16[2,144,256]{2,1,0:T(8,128)(2,1)S(1)}, u32[]{:S(2)}, u32[]{:S(2)}) collective-permute-start(bf16[2,144,256]{2,1,0:T(8,128)(2,1)S(1)} %join.5.own), channel_id=1, source_target_pairs={{0,192},{16,48},{32,224},{48,16},{64,128},{80,112},{96,160},{112,8... | collective-permute-start | bytes 442376 | tf_op jit(solution)/shard_map/ppermute | solution.py:384
  64.2 4.2 %all-to-all-start.1 = ((bf16[16,64,192]{2,1,0:T(8,128)(2,1)}), bf16[16,64,192]{2,1,0:T(8,128)(2,1)S(1)}, u32[]{:S(2)}, u32[]{:S(2)}) async-start(bf16[16,64,192]{2,1,0:T(8,128)(2,1)} %query_last.1), calls=%async_computation.1 | async-start | bytes 1048576 | tf_op jit(solution)/shard_map/all_to_all | solution.py:449
  68.5 0.0 collective-permute-done.10.got
  68.5 7.2 %collective-permute-start.15 = (bf16[4,144,256]{2,1,0:T(8,128)(2,1)S(1)}, bf16[4,144,256]{2,1,0:T(8,128)(2,1)S(1)}, u32[]{:S(2)}, u32[]{:S(2)}) collective-permute-start(bf16[4,144,256]{2,1,0:T(8,128)(2,1)S(1)} %join.6.refs_0_), channel_id=1, source_target_pairs={{0,16},{16,0},{32,48},{48,32},{64,80},{80,64},{96,112},{112,96},{1... | collective-permute-start | bytes 884744 | tf_op jit(solution)/shard_map/ppermute | solution.py:388
  75.7 2.5 %collective-permute-start.11 = (bf16[4,144,256]{2,1,0:T(8,128)(2,1)S(1)}, bf16[4,144,256]{2,1,0:T(8,128)(2,1)S(1)}, u32[]{:S(2)}, u32[]{:S(2)}) collective-permute-start(bf16[4,144,256]{2,1,0:T(8,128)(2,1)S(1)} %join.6.refs_0_), channel_id=1, source_target_pairs={{0,64},{16,208},{32,96},{48,240},{64,0},{80,144},{96,32},{112,176}... | collective-permute-start | bytes 884744 | tf_op jit(solution)/shard_map/ppermute | solution.py:384
  78.2 0.0 collective-permute-done.13.got
  78.2 0.1 collective-permute-start.16
  78.3 0.3 collective-permute-start.14
  78.6 4.2 %collective-permute-done.11.a = bf16[4,144,256]{2,1,0:T(8,128)(2,1)S(1)} collective-permute-done((bf16[4,144,256]{2,1,0:T(8,128)(2,1)S(1)}, bf16[4,144,256]{2,1,0:T(8,128)(2,1)S(1)}, u32[]{:S(2)}, u32[]{:S(2)}) %collective-permute-start.11) | collective-permute-done | bytes 294944 | tf_op jit(solution)/shard_map/ppermute | solution.py:384
  82.8 0.0 collective-permute-start.12
  82.8 0.0 collective-permute-done.15.refs_1_
  82.8 0.0 collective-permute-done.16.refs_3_
  82.8 1.7 %settle_near.1.earlier = bf16[576,2048]{1,0:T(8,128)(2,1)} custom-call(s32[5]{0:T(128)S(1)} %stack.33.sc, bf16[4,144,256]{2,1,0:T(8,128)(2,1)S(1)} %join.6.refs_0_, bf16[4,144,256]{2,1,0:T(8,128)(2,1)S(1)} %collective-permute-done.15.refs_1_, bf16[4,144,256]{2,1,0:T(8,128)(2,1)S(1)} %join.7.refs_2_, bf16[4,144,256]{2,1,0:T(8,128)(2,1)S(1)} %collective-permute-done.16.refs_3_), custom_call_target="tpu_custom_call" | custom-call | tf_op jit(solution)/shard_map/settle_near/pallas_call | solution.py:342
  84.5 1.4 %collective-permute-done.14.c = bf16[4,144,256]{2,1,0:T(8,128)(2,1)S(1)} collective-permute-done((bf16[4,144,256]{2,1,0:T(8,128)(2,1)S(1)}, bf16[4,144,256]{2,1,0:T(8,128)(2,1)S(1)}, u32[]{:S(2)}, u32[]{:S(2)}) %collective-permute-start.14) | collective-permute-done | bytes 294944 | tf_op jit(solution)/shard_map/ppermute | solution.py:384
  85.9 0.0 collective-permute-start.17
  85.9 0.0 all-to-all-done.1.dq
  85.9 0.0 collective-permute-done.12.b
  86.0 1.6 %collective-permute-done.17.d = bf16[4,144,256]{2,1,0:T(8,128)(2,1)S(1)} collective-permute-done((bf16[4,144,256]{2,1,0:T(8,128)(2,1)S(1)}, bf16[4,144,256]{2,1,0:T(8,128)(2,1)S(1)}, u32[]{:S(2)}, u32[]{:S(2)}) %collective-permute-start.17) | collective-permute-done | bytes 294944 | tf_op jit(solution)/shard_map/ppermute | solution.py:388
  87.5 2.3 %settle_far.1 = (bf16[576,2048]{1,0:T(8,128)(2,1)}, bf16[8,8,192]{2,1,0:T(8,128)(2,1)}) custom-call(s32[5]{0:T(128)S(1)} %stack.33.sc, bf16[4,144,256]{2,1,0:T(8,128)(2,1)S(1)} %collective-permute-done.11.a, bf16[4,144,256]{2,1,0:T(8,128)(2,1)S(1)} %collective-permute-done.12.b, ...), custom_call_target="tpu_custom_call", output_to_operand_aliasing={{0}: (6, {})} | custom-call | tf_op jit(solution)/shard_map/settle_far/pallas_call | solution.py:354
  (8 shorter events, 0.2 us)
Async XLA Ops:
  33.4 4.6 %collective-permute-start = (bf16[8,144,256]{2,1,0:T(8,128)(2,1)S(1)}, bf16[8,144,256]{2,1,0:T(8,128)(2,1)S(1)}, u32[]{:S(2)}, u32[]{:S(2)}) collective-permute-start(bf16[8,144,256]{2,1,0:T(8,128)(2,1)S(1)} %get-tuple-element.78), channel_id=1, source_target_pairs={{0,16},{16,0},{32,48},{48,32},{64,80},{80,64},{96,112},{112,96},{1... | collective-permute-start | bytes 1769480 | tf_op jit(solution)/shard_map/ppermute | solution.py:388
  40.1 4.8 %collective-permute-start.1 = (bf16[8,144,256]{2,1,0:T(8,128)(2,1)S(1)}, bf16[8,144,256]{2,1,0:T(8,128)(2,1)S(1)}, u32[]{:S(2)}, u32[]{:S(2)}) collective-permute-start(bf16[8,144,256]{2,1,0:T(8,128)(2,1)S(1)} %get-tuple-element.81), channel_id=1, source_target_pairs={{0,16},{16,0},{32,48},{48,32},{64,80},{80,64},{96,112},{112,96},{1... | collective-permute-start | bytes 1769480 | tf_op jit(solution)/shard_map/ppermute | solution.py:388
  40.3 8.1 %collective-permute-start.2 = (bf16[4,144,256]{2,1,0:T(8,128)(2,1)S(1)}, bf16[4,144,256]{2,1,0:T(8,128)(2,1)S(1)}, u32[]{:S(2)}, u32[]{:S(2)}) collective-permute-start(bf16[4,144,256]{2,1,0:T(8,128)(2,1)S(1)} %get-tuple-element.84), channel_id=1, source_target_pairs={{0,64},{16,208},{32,96},{48,240},{64,0},{80,144},{96,32},{112,176}... | collective-permute-start | bytes 884744 | tf_op jit(solution)/shard_map/ppermute | solution.py:384
  43.0 2.2 %copy-start = (bf16[2048,576]{0,1:T(8,128)(2,1)S(1)}, bf16[2048,576]{0,1:T(8,128)(2,1)}, u32[]{:S(2)}) copy-start(bf16[2048,576]{0,1:T(8,128)(2,1)} %param.9) | copy-start | bytes 7077892
  45.1 6.9 %collective-permute-start.3 = (bf16[4,144,256]{2,1,0:T(8,128)(2,1)S(1)}, bf16[4,144,256]{2,1,0:T(8,128)(2,1)S(1)}, u32[]{:S(2)}, u32[]{:S(2)}) collective-permute-start(bf16[4,144,256]{2,1,0:T(8,128)(2,1)S(1)} %get-tuple-element.91), channel_id=1, source_target_pairs={{0,64},{16,208},{32,96},{48,240},{64,0},{80,144},{96,32},{112,176}... | collective-permute-start | bytes 884744 | tf_op jit(solution)/shard_map/ppermute | solution.py:384
  48.4 6.5 %collective-permute-start.4 = (bf16[2,144,256]{2,1,0:T(8,128)(2,1)S(1)}, bf16[2,144,256]{2,1,0:T(8,128)(2,1)S(1)}, u32[]{:S(2)}, u32[]{:S(2)}) collective-permute-start(bf16[2,144,256]{2,1,0:T(8,128)(2,1)S(1)} %get-tuple-element.101), channel_id=1, source_target_pairs={{0,192},{16,48},{32,224},{48,16},{64,128},{80,112},{96,160},{112,8... | collective-permute-start | bytes 442376 | tf_op jit(solution)/shard_map/ppermute | solution.py:384
  50.3 2.9 %copy-start.1 = (bf16[8,128,512]{2,1,0:T(8,128)(2,1)S(1)}, bf16[8,128,512]{2,1,0:T(8,128)(2,1)}, u32[]{:S(2)}) copy-start(bf16[8,128,512]{2,1,0:T(8,128)(2,1)} %wuk.3) | copy-start | bytes 3145732
  52.0 4.1 %collective-permute-start.5 = (bf16[2,144,256]{2,1,0:T(8,128)(2,1)S(1)}, bf16[2,144,256]{2,1,0:T(8,128)(2,1)S(1)}, u32[]{:S(2)}, u32[]{:S(2)}) collective-permute-start(bf16[2,144,256]{2,1,0:T(8,128)(2,1)S(1)} %get-tuple-element.106), channel_id=1, source_target_pairs={{0,192},{16,48},{32,224},{48,16},{64,128},{80,112},{96,160},{112,8... | collective-permute-start | bytes 442376 | tf_op jit(solution)/shard_map/ppermute | solution.py:384
  54.9 3.3 %collective-permute-start.6 = (bf16[1,144,256]{2,1,0:T(8,128)(2,1)S(1)}, bf16[1,144,256]{2,1,0:T(8,128)(2,1)S(1)}, u32[]{:S(2)}, u32[]{:S(2)}) collective-permute-start(bf16[1,144,256]{2,1,0:T(8,128)(2,1)S(1)} %get-tuple-element.111), channel_id=1, source_target_pairs={{0,32},{16,80},{32,0},{48,112},{64,96},{80,16},{96,64},{112,48},{1... | collective-permute-start | bytes 221192 | tf_op jit(solution)/shard_map/ppermute | solution.py:384
  56.2 3.8 %collective-permute-start.7 = (bf16[1,144,256]{2,1,0:T(8,128)(2,1)S(1)}, bf16[1,144,256]{2,1,0:T(8,128)(2,1)S(1)}, u32[]{:S(2)}, u32[]{:S(2)}) collective-permute-start(bf16[1,144,256]{2,1,0:T(8,128)(2,1)S(1)} %get-tuple-element.114), channel_id=1, source_target_pairs={{0,32},{16,80},{32,0},{48,112},{64,96},{80,16},{96,64},{112,48},{1... | collective-permute-start | bytes 221192 | tf_op jit(solution)/shard_map/ppermute | solution.py:384
  58.2 3.3 %collective-permute-start.8 = (bf16[1,144,256]{2,1,0:T(8,128)(2,1)S(1)}, bf16[1,144,256]{2,1,0:T(8,128)(2,1)S(1)}, u32[]{:S(2)}, u32[]{:S(2)}) collective-permute-start(bf16[1,144,256]{2,1,0:T(8,128)(2,1)S(1)} %halve.14.own), channel_id=1, source_target_pairs={{0,32},{16,80},{32,0},{48,112},{64,96},{80,16},{96,64},{112,48},{1... | collective-permute-start | bytes 221192 | tf_op jit(solution)/shard_map/ppermute | solution.py:384
  60.0 3.3 %collective-permute-start.9 = (bf16[1,144,256]{2,1,0:T(8,128)(2,1)S(1)}, bf16[1,144,256]{2,1,0:T(8,128)(2,1)S(1)}, u32[]{:S(2)}, u32[]{:S(2)}) collective-permute-start(bf16[1,144,256]{2,1,0:T(8,128)(2,1)S(1)} %halve.15.own), channel_id=1, source_target_pairs={{0,32},{16,80},{32,0},{48,112},{64,96},{80,16},{96,64},{112,48},{1... | collective-permute-start | bytes 221192 | tf_op jit(solution)/shard_map/ppermute | solution.py:384
  61.5 6.9 %collective-permute-start.10 = (bf16[2,144,256]{2,1,0:T(8,128)(2,1)S(1)}, bf16[2,144,256]{2,1,0:T(8,128)(2,1)S(1)}, u32[]{:S(2)}, u32[]{:S(2)}) collective-permute-start(bf16[2,144,256]{2,1,0:T(8,128)(2,1)S(1)} %join.4.own), channel_id=1, source_target_pairs={{0,192},{16,48},{32,224},{48,16},{64,128},{80,112},{96,160},{112,8... | collective-permute-start | bytes 442376 | tf_op jit(solution)/shard_map/ppermute | solution.py:384
  63.3 14.9 %collective-permute-start.13 = (bf16[2,144,256]{2,1,0:T(8,128)(2,1)S(1)}, bf16[2,144,256]{2,1,0:T(8,128)(2,1)S(1)}, u32[]{:S(2)}, u32[]{:S(2)}) collective-permute-start(bf16[2,144,256]{2,1,0:T(8,128)(2,1)S(1)} %join.5.own), channel_id=1, source_target_pairs={{0,192},{16,48},{32,224},{48,16},{64,128},{80,112},{96,160},{112,8... | collective-permute-start | bytes 442376 | tf_op jit(solution)/shard_map/ppermute | solution.py:384
  64.2 21.7 %all-to-all-start.1 = ((bf16[16,64,192]{2,1,0:T(8,128)(2,1)}), bf16[16,64,192]{2,1,0:T(8,128)(2,1)S(1)}, u32[]{:S(2)}, u32[]{:S(2)}) async-start(bf16[16,64,192]{2,1,0:T(8,128)(2,1)} %query_last.1), calls=%async_computation.1 | async-start | bytes 1048576 | tf_op jit(solution)/shard_map/all_to_all | solution.py:449
  68.5 14.3 %collective-permute-start.15 = (bf16[4,144,256]{2,1,0:T(8,128)(2,1)S(1)}, bf16[4,144,256]{2,1,0:T(8,128)(2,1)S(1)}, u32[]{:S(2)}, u32[]{:S(2)}) collective-permute-start(bf16[4,144,256]{2,1,0:T(8,128)(2,1)S(1)} %join.6.refs_0_), channel_id=1, source_target_pairs={{0,16},{16,0},{32,48},{48,32},{64,80},{80,64},{96,112},{112,96},{1... | collective-permute-start | bytes 884744 | tf_op jit(solution)/shard_map/ppermute | solution.py:388
  75.7 7.1 %collective-permute-start.11 = (bf16[4,144,256]{2,1,0:T(8,128)(2,1)S(1)}, bf16[4,144,256]{2,1,0:T(8,128)(2,1)S(1)}, u32[]{:S(2)}, u32[]{:S(2)}) collective-permute-start(bf16[4,144,256]{2,1,0:T(8,128)(2,1)S(1)} %join.6.refs_0_), channel_id=1, source_target_pairs={{0,64},{16,208},{32,96},{48,240},{64,0},{80,144},{96,32},{112,176}... | collective-permute-start | bytes 884744 | tf_op jit(solution)/shard_map/ppermute | solution.py:384
  78.2 4.6 %collective-permute-start.16 = (bf16[4,144,256]{2,1,0:T(8,128)(2,1)S(1)}, bf16[4,144,256]{2,1,0:T(8,128)(2,1)S(1)}, u32[]{:S(2)}, u32[]{:S(2)}) collective-permute-start(bf16[4,144,256]{2,1,0:T(8,128)(2,1)S(1)} %join.7.refs_2_), channel_id=1, source_target_pairs={{0,16},{16,0},{32,48},{48,32},{64,80},{80,64},{96,112},{112,96},{1... | collective-permute-start | bytes 884744 | tf_op jit(solution)/shard_map/ppermute | solution.py:388
  78.3 7.6 %collective-permute-start.14 = (bf16[4,144,256]{2,1,0:T(8,128)(2,1)S(1)}, bf16[4,144,256]{2,1,0:T(8,128)(2,1)S(1)}, u32[]{:S(2)}, u32[]{:S(2)}) collective-permute-start(bf16[4,144,256]{2,1,0:T(8,128)(2,1)S(1)} %join.7.refs_2_), channel_id=1, source_target_pairs={{0,64},{16,208},{32,96},{48,240},{64,0},{80,144},{96,32},{112,176}... | collective-permute-start | bytes 884744 | tf_op jit(solution)/shard_map/ppermute | solution.py:384
  82.8 3.2 %collective-permute-start.12 = (bf16[4,144,256]{2,1,0:T(8,128)(2,1)S(1)}, bf16[4,144,256]{2,1,0:T(8,128)(2,1)S(1)}, u32[]{:S(2)}, u32[]{:S(2)}) collective-permute-start(bf16[4,144,256]{2,1,0:T(8,128)(2,1)S(1)} %collective-permute-done.11.a), channel_id=1, source_target_pairs={{0,16},{16,0},{32,48},{48,32},{64,80},{80,64},{96,112},{112,96},{1... | collective-permute-start | bytes 884744 | tf_op jit(solution)/shard_map/ppermute | solution.py:388
  85.9 1.6 %collective-permute-start.17 = (bf16[4,144,256]{2,1,0:T(8,128)(2,1)S(1)}, bf16[4,144,256]{2,1,0:T(8,128)(2,1)S(1)}, u32[]{:S(2)}, u32[]{:S(2)}) collective-permute-start(bf16[4,144,256]{2,1,0:T(8,128)(2,1)S(1)} %collective-permute-done.14.c), channel_id=1, source_target_pairs={{0,16},{16,0},{32,48},{48,32},{64,80},{80,64},{96,112},{112,96},{1... | collective-permute-start | bytes 884744 | tf_op jit(solution)/shard_map/ppermute | solution.py:388
